TPU v7x, 32 devices: a whole 2x2x4 slice. The times are simulated.
32 devices in a mesh: dp: 2 (over x), seq: 16 (over z, y, core).
Axes of the slice: x: 2, y: 2, z: 4, core: 2. Of those that a mesh axis runs over, the one named last changes fastest.
Arguments:
- inputs: bfloat16 [4, 4096, 1536], P('dp', 'seq'), may hold values from -6 to 6
- skip_input: bfloat16 [4, 8192, 1536], P('dp', 'seq'), may hold values from -6 to 6
- lengths: int32 [4], P('dp'), may hold values from 1024 to 4096, as said below
- cotangent: bfloat16 [4, 8192, 1536], P('dp', 'seq'), may hold values from -6 to 6
- first_gain: bfloat16 [1536], P(('dp', 'seq')), may hold values from 0.099609375 to 1.8984375
- query_weight: bfloat16 [1536, 512], P(('dp', 'seq')), may hold values from -0.15625 to 0.15625
- key_weight: bfloat16 [1536, 512], P(('dp', 'seq')), may hold values from -0.15625 to 0.15625
- value_weight: bfloat16 [1536, 1536], P(('dp', 'seq')), may hold values from -0.15625 to 0.15625
- content_bias: bfloat16 [512], P(('dp', 'seq')), may hold values from -3 to 3
- position_bias: bfloat16 [512], P(('dp', 'seq')), may hold values from -3 to 3
- relative_weight: bfloat16 [512, 32], P(('dp', 'seq')), may hold values from -3 to 3
- mixing_weight: bfloat16 [1536, 1536], P(('dp', 'seq')), may hold values from -2.5 to 2.5
- second_gain: bfloat16 [1536], P(('dp', 'seq')), may hold values from 0.099609375 to 1.8984375
- inner_weight: bfloat16 [1536, 3072], P(('dp', 'seq')), may hold values from -0.15625 to 0.15625
- inner_bias: bfloat16 [3072], P(('dp', 'seq')), may hold values from -3 to 3
- outer_weight: bfloat16 [3072, 1536], P(('dp', 'seq')), may hold values from -0.15625 to 0.15625
- outer_bias: bfloat16 [1536], P(('dp', 'seq')), may hold values from -3 to 3
- third_gain: bfloat16 [1536], P(('dp', 'seq')), may hold values from 0.099609375 to 1.8984375
- upsample_weight: bfloat16 [1536, 1536], P(('dp', 'seq')), may hold values from -0.21875 to 0.21875
- skip_weight: bfloat16 [1536, 1536], P(('dp', 'seq')), may hold values from -0.15625 to 0.15625
- skip_bias: bfloat16 [1536], P(('dp', 'seq')), may hold values from -3 to 3
- depth_weight: bfloat16 [1536, 3], P(('dp', 'seq')), may hold values from -4 to 4
- point_weight: bfloat16 [1536, 1536], P(('dp', 'seq')), may hold values from -0.15625 to 0.15625
Outputs:
- outputs: bfloat16 [4, 8192, 1536], P('dp', 'seq')
- input_grad: bfloat16 [4, 4096, 1536], P('dp', 'seq')
- skip_grad: bfloat16 [4, 8192, 1536], P('dp', 'seq')
- first_gain_grad: float32 [1536], P(('dp', 'seq'))
- query_weight_grad: float32 [1536, 512], P(('dp', 'seq'))
- key_weight_grad: float32 [1536, 512], P(('dp', 'seq'))
- value_weight_grad: float32 [1536, 1536], P(('dp', 'seq'))
- content_bias_grad: float32 [512], P(('dp', 'seq'))
- position_bias_grad: float32 [512], P(('dp', 'seq'))
- relative_weight_grad: float32 [512, 32], P(('dp', 'seq'))
- mixing_weight_grad: float32 [1536, 1536], P(('dp', 'seq'))
- second_gain_grad: float32 [1536], P(('dp', 'seq'))
- inner_weight_grad: float32 [1536, 3072], P(('dp', 'seq'))
- inner_bias_grad: float32 [3072], P(('dp', 'seq'))
- outer_weight_grad: float32 [3072, 1536], P(('dp', 'seq'))
- outer_bias_grad: float32 [1536], P(('dp', 'seq'))
- third_gain_grad: float32 [1536], P(('dp', 'seq'))
- upsample_weight_grad: float32 [1536, 1536], P(('dp', 'seq'))
- skip_weight_grad: float32 [1536, 1536], P(('dp', 'seq'))
- skip_bias_grad: float32 [1536], P(('dp', 'seq'))
- depth_weight_grad: float32 [1536, 3], P(('dp', 'seq'))
- point_weight_grad: float32 [1536, 1536], P(('dp', 'seq'))
Inputs may be any that keep to these rules, and one draw needn't show every extreme that they name: `lengths`: in each run of 2 windows on one index of dp, exactly one window has all 4096 bins valid; each other window has at most 3072 valid bins.
All inputs are finite; a program needn't handle non-finite values.
Results may differ from a plain program's by a relative error of at most 0.03.
Values may be sent and summed in bfloat16 or wider, within the bound.
A program may use at most 512 MiB of HBM per device.

v0:
```python
import math

import jax
import jax.numpy as jnp
from jax import lax
from jax.sharding import PartitionSpec as P

H = 8
KD = 64
VD = 192
RPF = 32


highest = lax.Precision.HIGHEST
masked_score = -1e30
epsilon = 1e-05


def extended_2(array, sides, width):
    for axis, dim in sides:
        peers, length = (lax.axis_size(axis), array.shape[dim])
        up = [(i, (i + 1) % peers) for i in range(peers - 1)]
        down = [(j, i) for i, j in up]
        last = lax.slice_in_dim(array, length - width, length, axis=dim)
        initial = lax.slice_in_dim(array, 0, width, axis=dim)
        before = lax.ppermute(last, axis, up)
        after = lax.ppermute(initial, axis, down)
        array = jnp.concatenate([before, array, after], axis=dim)
    return array


def layer_norm(values, gain):
    mean = jnp.mean(values, axis=-1, keepdims=True)
    centered = values - mean
    spread = jnp.mean(centered * centered, axis=-1, keepdims=True)
    return centered * lax.rsqrt(spread + epsilon) * gain


def smooth_gelu(values):
    return jax.nn.gelu(values, approximate=False)


def norm_gelu(values, gain):
    return smooth_gelu(layer_norm(values, gain))


def basis_table(first, rows, keys_total, features, extent):
    query_pos = first + jnp.arange(rows, dtype=jnp.int32)
    key_pos = jnp.arange(keys_total, dtype=jnp.int32)
    distance = (query_pos[:, None] - key_pos[None, :]).astype(jnp.float32)
    half = features // 2
    lives = jnp.exp(jnp.linspace(math.log(3.0), math.log(extent), half, dtype=jnp.float32))
    decay = jnp.exp(-math.log(2.0) * jnp.abs(distance)[None, :, :] / lives[:, None, None])
    return jnp.concatenate([decay, jnp.sign(distance)[None, :, :] * decay], axis=0).astype(
        jnp.bfloat16
    )


def matmul(left, right):
    return jnp.dot(left, right, preferred_element_type=jnp.float32)


def times_transposed(left, right):
    return lax.dot_general(
        left, right, (((1,), (1,)), ((), ())), preferred_element_type=jnp.float32
    )


def transposed_times(left, right):
    return lax.dot_general(
        left, right, (((0,), (0,)), ((), ())), preferred_element_type=jnp.float32
    )


def window_scores(content_one, projected_one, key_one, valid_one, table):
    content = jnp.einsum("qhk,thk->hqt", content_one, key_one, preferred_element_type=jnp.float32)
    position = jnp.einsum("qhf,fqt->hqt", projected_one, table, preferred_element_type=jnp.float32)
    return jnp.where(valid_one[None, None, :], content + position, masked_score)


def depth_apply(extended, taps):
    return (
        extended[:, :-2] * taps[:, 0]
        + extended[:, 1:-1] * taps[:, 1]
        + extended[:, 2:] * taps[:, 2]
    )


def on_device(
    inputs,
    skip_input,
    lengths,
    cotangent,
    first_gain,
    query_weight,
    key_weight,
    value_weight,
    content_bias,
    position_bias,
    relative_weight,
    mixing_weight,
    second_gain,
    inner_weight,
    inner_bias,
    outer_weight,
    outer_bias,
    third_gain,
    upsample_weight,
    skip_weight,
    skip_bias,
    depth_weight,
    point_weight,
):
    windows, rows, width = inputs.shape
    heads = H
    key_size = KD
    value_size = VD
    features = RPF
    scale = float(KD) ** (-0.5)
    first = lax.axis_index("seq") * rows
    (
        gain_first,
        weight_query,
        weight_key,
        weight_value,
        bias_content,
        bias_position,
        weight_relative,
        weight_mixing,
        gain_second,
        weight_inner,
        bias_inner,
        weight_outer,
        bias_outer,
        gain_third,
        weight_upsample,
        weight_skip,
        bias_skip,
        weight_depth,
        weight_point,
    ) = (
        lax.all_gather(first_gain, ("dp", "seq"), axis=0, tiled=True),
        lax.all_gather(query_weight, ("dp", "seq"), axis=0, tiled=True),
        lax.all_gather(key_weight, ("dp", "seq"), axis=0, tiled=True),
        lax.all_gather(value_weight, ("dp", "seq"), axis=0, tiled=True),
        lax.all_gather(content_bias, ("dp", "seq"), axis=0, tiled=True),
        lax.all_gather(position_bias, ("dp", "seq"), axis=0, tiled=True),
        lax.all_gather(relative_weight, ("dp", "seq"), axis=0, tiled=True),
        lax.all_gather(mixing_weight, ("dp", "seq"), axis=0, tiled=True),
        lax.all_gather(second_gain, ("dp", "seq"), axis=0, tiled=True),
        lax.all_gather(inner_weight, ("dp", "seq"), axis=0, tiled=True),
        lax.all_gather(inner_bias, ("dp", "seq"), axis=0, tiled=True),
        lax.all_gather(outer_weight, ("dp", "seq"), axis=0, tiled=True),
        lax.all_gather(outer_bias, ("dp", "seq"), axis=0, tiled=True),
        lax.all_gather(third_gain, ("dp", "seq"), axis=0, tiled=True),
        lax.all_gather(upsample_weight, ("dp", "seq"), axis=0, tiled=True),
        lax.all_gather(skip_weight, ("dp", "seq"), axis=0, tiled=True),
        lax.all_gather(skip_bias, ("dp", "seq"), axis=0, tiled=True),
        lax.all_gather(depth_weight, ("dp", "seq"), axis=0, tiled=True),
        lax.all_gather(point_weight, ("dp", "seq"), axis=0, tiled=True),
    )
    flat = inputs.reshape(windows * rows, width).astype(jnp.float32)
    normed, first_norm_back = jax.vjp(layer_norm, flat, gain_first.astype(jnp.float32))
    normed_low = normed.astype(jnp.bfloat16)
    queries = matmul(normed_low, weight_query)
    keys_low = matmul(normed_low, weight_key).astype(jnp.bfloat16)
    values_low = matmul(normed_low, weight_value).astype(jnp.bfloat16)
    content_low = (
        ((queries + bias_content) * scale)
        .astype(jnp.bfloat16)
        .reshape(windows, rows, heads, key_size)
    )
    positional = ((queries + bias_position) * scale).reshape(windows, rows, heads, key_size)
    relative = weight_relative.astype(jnp.float32).reshape(heads, key_size, features)
    projected_low = jnp.einsum("wqhk,hkf->wqhf", positional, relative, precision=highest).astype(
        jnp.bfloat16
    )
    key_local = keys_low.reshape(windows, rows, heads * key_size)
    value_local = values_low.reshape(windows, rows, heads * value_size)
    key_full, value_full = (
        lax.all_gather(key_local, "seq", axis=1, tiled=True),
        lax.all_gather(value_local, "seq", axis=1, tiled=True),
    )
    keys_total = key_full.shape[1]
    key_heads = key_full.reshape(windows, keys_total, heads, key_size)
    value_heads = value_full.reshape(windows, keys_total, heads, value_size)
    valid = jnp.arange(keys_total, dtype=jnp.int32)[None, :] < lengths[:, None]
    table = basis_table(first, rows, keys_total, features, keys_total)

    def attend(items):
        content_one, projected_one, key_one, value_one, valid_one = items
        scores = window_scores(content_one, projected_one, key_one, valid_one, table)
        top = jnp.max(scores, axis=-1, keepdims=True)
        exponent = jnp.exp(scores - top)
        total = jnp.sum(exponent, axis=-1, keepdims=True)
        probs_low = (exponent / total).astype(jnp.bfloat16)
        mixed_one = jnp.einsum(
            "hqt,thv->qhv", probs_low, value_one, preferred_element_type=jnp.float32
        ).astype(jnp.bfloat16)
        return (mixed_one, top + jnp.log(total))

    mixed_low, log_total = lax.map(
        attend, (content_low, projected_low, key_heads, value_heads, valid)
    )
    mixed_low = mixed_low.reshape(windows * rows, heads * value_size)
    middle = flat + matmul(mixed_low, weight_mixing)
    second, second_norm_back = jax.vjp(layer_norm, middle, gain_second.astype(jnp.float32))
    second_low = second.astype(jnp.bfloat16)
    before = matmul(second_low, weight_inner) + bias_inner.astype(jnp.float32)
    hidden, gelu_back = jax.vjp(smooth_gelu, before)
    hidden_low = hidden.astype(jnp.bfloat16)
    block_out = middle + matmul(hidden_low, weight_outer) + bias_outer.astype(jnp.float32)
    third, third_back = jax.vjp(norm_gelu, block_out, gain_third.astype(jnp.float32))
    third_low = third.astype(jnp.bfloat16)
    lifted = matmul(third_low, weight_upsample).reshape(windows, rows, 1, width)
    doubled = jnp.broadcast_to(lifted, (windows, rows, 2, width)).reshape(windows, 2 * rows, width)
    skip_flat = skip_input.reshape(windows * 2 * rows, width)
    skip_part = (matmul(skip_flat, weight_skip) + bias_skip.astype(jnp.float32)).reshape(
        windows, 2 * rows, width
    )
    joined_low = (doubled + skip_part).astype(jnp.bfloat16)
    joined_rim = extended_2(joined_low, (("seq", 1),), 1)
    taps = weight_depth.astype(jnp.float32)
    joined_wide = joined_rim.astype(jnp.float32)
    conv_low = depth_apply(joined_wide, taps).astype(jnp.bfloat16)
    conv_flat = conv_low.reshape(windows * 2 * rows, width)
    bins = 2 * first + jnp.arange(2 * rows, dtype=jnp.int32)
    keep = (bins // 2)[None, :] < lengths[:, None]
    keep_wide = keep.astype(jnp.float32)[:, :, None]
    outputs = (
        matmul(conv_flat, weight_point).reshape(windows, 2 * rows, width) * keep_wide
    ).astype(jnp.bfloat16)
    (
        gain_first,
        weight_query,
        weight_key,
        weight_value,
        bias_content,
        bias_position,
        weight_relative,
        weight_mixing,
        gain_second,
        weight_inner,
        bias_inner,
        weight_outer,
        bias_outer,
        gain_third,
        weight_upsample,
        weight_skip,
        bias_skip,
        weight_depth,
        weight_point,
    ) = (
        lax.all_gather(first_gain, ("dp", "seq"), axis=0, tiled=True),
        lax.all_gather(query_weight, ("dp", "seq"), axis=0, tiled=True),
        lax.all_gather(key_weight, ("dp", "seq"), axis=0, tiled=True),
        lax.all_gather(value_weight, ("dp", "seq"), axis=0, tiled=True),
        lax.all_gather(content_bias, ("dp", "seq"), axis=0, tiled=True),
        lax.all_gather(position_bias, ("dp", "seq"), axis=0, tiled=True),
        lax.all_gather(relative_weight, ("dp", "seq"), axis=0, tiled=True),
        lax.all_gather(mixing_weight, ("dp", "seq"), axis=0, tiled=True),
        lax.all_gather(second_gain, ("dp", "seq"), axis=0, tiled=True),
        lax.all_gather(inner_weight, ("dp", "seq"), axis=0, tiled=True),
        lax.all_gather(inner_bias, ("dp", "seq"), axis=0, tiled=True),
        lax.all_gather(outer_weight, ("dp", "seq"), axis=0, tiled=True),
        lax.all_gather(outer_bias, ("dp", "seq"), axis=0, tiled=True),
        lax.all_gather(third_gain, ("dp", "seq"), axis=0, tiled=True),
        lax.all_gather(upsample_weight, ("dp", "seq"), axis=0, tiled=True),
        lax.all_gather(skip_weight, ("dp", "seq"), axis=0, tiled=True),
        lax.all_gather(skip_bias, ("dp", "seq"), axis=0, tiled=True),
        lax.all_gather(depth_weight, ("dp", "seq"), axis=0, tiled=True),
        lax.all_gather(point_weight, ("dp", "seq"), axis=0, tiled=True),
    )
    taps = weight_depth.astype(jnp.float32)
    relative = weight_relative.astype(jnp.float32).reshape(heads, key_size, features)
    out_grad = (cotangent * keep.astype(jnp.bfloat16)[:, :, None]).reshape(
        windows * 2 * rows, width
    )
    grad_point = transposed_times(conv_flat, out_grad)
    conv_grad = (
        times_transposed(out_grad, weight_point)
        .astype(jnp.bfloat16)
        .reshape(windows, 2 * rows, width)
    )
    grad_rim = extended_2(conv_grad, (("seq", 1),), 1).astype(jnp.float32)
    joined_grad = (
        grad_rim[:, 2:] * taps[:, 0]
        + grad_rim[:, 1:-1] * taps[:, 1]
        + grad_rim[:, :-2] * taps[:, 2]
    )
    conv_wide = conv_grad.astype(jnp.float32)
    grad_depth = jnp.stack(
        [
            jnp.sum(conv_wide * joined_wide[:, :-2], axis=(0, 1)),
            jnp.sum(conv_wide * joined_wide[:, 1:-1], axis=(0, 1)),
            jnp.sum(conv_wide * joined_wide[:, 2:], axis=(0, 1)),
        ],
        axis=1,
    )
    grad_skip_bias = jnp.sum(joined_grad, axis=(0, 1))
    joined_flat = joined_grad.astype(jnp.bfloat16).reshape(windows * 2 * rows, width)
    grad_skip = transposed_times(skip_flat, joined_flat)
    skip_grad = (
        times_transposed(joined_flat, weight_skip)
        .astype(jnp.bfloat16)
        .reshape(windows, 2 * rows, width)
    )
    lifted_grad = jnp.sum(joined_grad.reshape(windows, rows, 2, width), axis=2)
    lifted_grad = lifted_grad.astype(jnp.bfloat16).reshape(windows * rows, width)
    grad_upsample = transposed_times(third_low, lifted_grad)
    block_grad, grad_third = third_back(times_transposed(lifted_grad, weight_upsample))
    block_low = block_grad.astype(jnp.bfloat16)
    grad_outer = transposed_times(hidden_low, block_low)
    grad_outer_bias = jnp.sum(block_grad, axis=0)
    (before_grad,) = gelu_back(times_transposed(block_low, weight_outer))
    before_low = before_grad.astype(jnp.bfloat16)
    grad_inner = transposed_times(second_low, before_low)
    grad_inner_bias = jnp.sum(before_low.astype(jnp.float32), axis=0)
    middle_part, grad_second = second_norm_back(times_transposed(before_low, weight_inner))
    middle_grad = block_grad + middle_part
    middle_low = middle_grad.astype(jnp.bfloat16)
    grad_mixing = transposed_times(mixed_low, middle_low)
    mixed_grad = times_transposed(middle_low, weight_mixing).astype(jnp.bfloat16)
    mixed_grad = mixed_grad.reshape(windows, rows, heads, value_size)
    key_again, value_again = (
        lax.all_gather(key_local, "seq", axis=1, tiled=True),
        lax.all_gather(value_local, "seq", axis=1, tiled=True),
    )
    key_heads = key_again.reshape(windows, keys_total, heads, key_size)
    value_heads = value_again.reshape(windows, keys_total, heads, value_size)

    def attend_back(items):
        content_one, projected_one, key_one, value_one, valid_one, grad_one, log_one = items
        scores = window_scores(content_one, projected_one, key_one, valid_one, table)
        exact = jnp.exp(scores - log_one)
        prob_grad = jnp.einsum(
            "qhv,thv->hqt", grad_one, value_one, preferred_element_type=jnp.float32
        )
        row_sum = jnp.sum(exact * prob_grad, axis=-1, keepdims=True)
        score_low = (exact * (prob_grad - row_sum)).astype(jnp.bfloat16)
        content_one_grad = jnp.einsum(
            "hqt,thk->qhk", score_low, key_one, preferred_element_type=jnp.float32
        )
        key_part = jnp.einsum(
            "hqt,qhk->thk", score_low, content_one, preferred_element_type=jnp.float32
        ).reshape(keys_total, heads * key_size)
        value_part = jnp.einsum(
            "hqt,qhv->thv", exact.astype(jnp.bfloat16), grad_one, preferred_element_type=jnp.float32
        ).reshape(keys_total, heads * value_size)
        key_one_grad, value_one_grad = (
            lax.psum_scatter(
                key_part.astype(jnp.bfloat16), "seq", scatter_dimension=0, tiled=True
            ).astype(jnp.float32),
            lax.psum_scatter(
                value_part.astype(jnp.bfloat16), "seq", scatter_dimension=0, tiled=True
            ).astype(jnp.float32),
        )
        projected_one_grad = jnp.einsum(
            "hqt,fqt->qhf", score_low, table, preferred_element_type=jnp.float32
        )
        return (content_one_grad, projected_one_grad, key_one_grad, value_one_grad)

    content_grad, projected_grad, key_grad, value_grad = lax.map(
        attend_back,
        (content_low, projected_low, key_heads, value_heads, valid, mixed_grad, log_total),
    )
    grad_relative = jnp.einsum(
        "wqhk,wqhf->hkf", positional, projected_grad, precision=highest
    ).reshape(heads * key_size, features)
    positional_grad = jnp.einsum("wqhf,hkf->wqhk", projected_grad, relative, precision=highest)
    grad_content = scale * jnp.sum(content_grad, axis=(0, 1)).reshape(heads * key_size)
    grad_position = scale * jnp.sum(positional_grad, axis=(0, 1)).reshape(heads * key_size)
    query_low = (
        (scale * (content_grad + positional_grad))
        .reshape(windows * rows, heads * key_size)
        .astype(jnp.bfloat16)
    )
    key_low = key_grad.reshape(windows * rows, heads * key_size).astype(jnp.bfloat16)
    value_low = value_grad.reshape(windows * rows, heads * value_size).astype(jnp.bfloat16)
    grad_query = transposed_times(normed_low, query_low)
    grad_key = transposed_times(normed_low, key_low)
    grad_value = transposed_times(normed_low, value_low)
    normed_grad = (
        times_transposed(query_low, weight_query)
        + times_transposed(key_low, weight_key)
        + times_transposed(value_low, weight_value)
    )
    input_part, grad_first = first_norm_back(normed_grad)
    input_grad = (middle_grad + input_part).astype(jnp.bfloat16).reshape(windows, rows, width)
    sharded = (
        lax.psum_scatter(grad_first, ("dp", "seq"), scatter_dimension=0, tiled=True),
        lax.psum_scatter(grad_query, ("dp", "seq"), scatter_dimension=0, tiled=True),
        lax.psum_scatter(grad_key, ("dp", "seq"), scatter_dimension=0, tiled=True),
        lax.psum_scatter(grad_value, ("dp", "seq"), scatter_dimension=0, tiled=True),
        lax.psum_scatter(grad_content, ("dp", "seq"), scatter_dimension=0, tiled=True),
        lax.psum_scatter(grad_position, ("dp", "seq"), scatter_dimension=0, tiled=True),
        lax.psum_scatter(grad_relative, ("dp", "seq"), scatter_dimension=0, tiled=True),
        lax.psum_scatter(grad_mixing, ("dp", "seq"), scatter_dimension=0, tiled=True),
        lax.psum_scatter(grad_second, ("dp", "seq"), scatter_dimension=0, tiled=True),
        lax.psum_scatter(grad_inner, ("dp", "seq"), scatter_dimension=0, tiled=True),
        lax.psum_scatter(grad_inner_bias, ("dp", "seq"), scatter_dimension=0, tiled=True),
        lax.psum_scatter(grad_outer, ("dp", "seq"), scatter_dimension=0, tiled=True),
        lax.psum_scatter(grad_outer_bias, ("dp", "seq"), scatter_dimension=0, tiled=True),
        lax.psum_scatter(grad_third, ("dp", "seq"), scatter_dimension=0, tiled=True),
        lax.psum_scatter(grad_upsample, ("dp", "seq"), scatter_dimension=0, tiled=True),
        lax.psum_scatter(grad_skip, ("dp", "seq"), scatter_dimension=0, tiled=True),
        lax.psum_scatter(grad_skip_bias, ("dp", "seq"), scatter_dimension=0, tiled=True),
        lax.psum_scatter(grad_depth, ("dp", "seq"), scatter_dimension=0, tiled=True),
        lax.psum_scatter(grad_point, ("dp", "seq"), scatter_dimension=0, tiled=True),
    )
    return (outputs, input_grad, skip_grad) + tuple(sharded)


def solution(mesh):
    in_specs = (
        P("dp", "seq", None),
        P("dp", "seq", None),
        P("dp"),
        P("dp", "seq", None),
        P(("dp", "seq")),
        P(("dp", "seq"), None),
        P(("dp", "seq"), None),
        P(("dp", "seq"), None),
        P(("dp", "seq")),
        P(("dp", "seq")),
        P(("dp", "seq"), None),
        P(("dp", "seq"), None),
        P(("dp", "seq")),
        P(("dp", "seq"), None),
        P(("dp", "seq")),
        P(("dp", "seq"), None),
        P(("dp", "seq")),
        P(("dp", "seq")),
        P(("dp", "seq"), None),
        P(("dp", "seq"), None),
        P(("dp", "seq")),
        P(("dp", "seq"), None),
        P(("dp", "seq"), None),
    )
    out_specs = (
        P("dp", "seq", None),
        P("dp", "seq", None),
        P("dp", "seq", None),
        P(("dp", "seq")),
        P(("dp", "seq"), None),
        P(("dp", "seq"), None),
        P(("dp", "seq"), None),
        P(("dp", "seq")),
        P(("dp", "seq")),
        P(("dp", "seq"), None),
        P(("dp", "seq"), None),
        P(("dp", "seq")),
        P(("dp", "seq"), None),
        P(("dp", "seq")),
        P(("dp", "seq"), None),
        P(("dp", "seq")),
        P(("dp", "seq")),
        P(("dp", "seq"), None),
        P(("dp", "seq"), None),
        P(("dp", "seq")),
        P(("dp", "seq"), None),
        P(("dp", "seq"), None),
    )
    return jax.shard_map(
        on_device, mesh=mesh, in_specs=in_specs, out_specs=out_specs, check_vma=False
    )
```

profile of v0, /device:TPU:1, one launch (start us, length us, event | category | flops | bytes accessed | tf_op | source)
XLA Modules:
  0.0 3219.4 jit_solution(11916277906296038543)
XLA Ops:
  17.5 42.0 %all-reduce.17 = (bf16[1536]{0:T(1024)(128)(2,1)S(1)}, bf16[1536]{0:T(1024)(128)(2,1)S(1)}, bf16[512]{0:T(512)(128)(2,1)S(1)}, bf16[512]{0:T(512)(128)(2,1)S(1)}...) all-reduce(bf16[1536]{0:T(1024)(128)(2,1)S(1)} %dynamic-update-slic, ...), channel_id=1, replica_groups=mesh['dp'=2,'seq'=16] {'dp','seq'}, use_global_device_ids=true, to_apply=%add.7 | all-reduce | flops 11776 | bytes 47104
  72.6 61.4 %all-gather.13.cloned.1.call-done = bf16[1536,1536]{1,0:T(8,128)(2,1)} async-done(((bf16[48,1536]{1,0:T(8,128)(2,1)}), bf16[1536,1536]{1,0:T(8,128)(2,1)}) %all-gather.13.cloned.1.call-update) | async-done | bytes 4718608 | tf_op jit(solution)/shard_map/all_gather | solution.py:145
  143.5 39.9 %all_gather.84 = bf16[512,32]{1,0:T(8,128)(2,1)S(1)} all-gather(bf16[16,32]{1,0:T(8,128)(2,1)S(1)} %copy-done.58), channel_id=1, replica_groups=mesh['dp'=2,'seq'=16] {'dp','seq'}, dimensions={0}, use_global_device_ids=true | all-gather | bytes 33792 | tf_op jit(solution)/shard_map/all_gather | solution.py:148
  192.1 36.8 %all-gather = bf16[32,48,3]{1,2,0:T(4,128)(2,1)S(1)} all-gather(bf16[1,48,3]{1,2,0:T(4,128)(2,1)S(1)} %bitcast.334), channel_id=1, replica_groups=mesh['dp'=2,'seq'=16] {'dp','seq'}, dimensions={0}, use_global_device_ids=true | all-gather | bytes 9504 | tf_op jit(solution)/shard_map/all_gather | solution.py:159
  230.4 25.3 fusion.68
  255.7 44.6 %pad_maximum_fusion = bf16[32,256,4096]{2,0,1:T(8,128)(2,1)} fusion(bf16[16,256,4096]{2,0,1:T(8,128)(2,1)} %get-tuple-element.454, bf16[16,256,4096]{2,0,1:T(8,128)(2,1)} %get-tuple-element.453), kind=kLoop, calls=%fused_computation.71 | loop fusion | flops 134217728 | bytes 134217728 | tf_op jit(solution)/shard_map/concatenate | solution.py:54
  371.7 25.9 all-gather.21.cloned.1.call-done
  409.4 117.2 %all-gather.15.cloned.1.call-done = bf16[2,4096,1536]{2,1,0:T(8,128)(2,1)} async-done(((bf16[2,256,1536]{2,1,0:T(8,128)(2,1)}), bf16[2,4096,1536]{2,1,0:T(8,128)(2,1)}) %all-gather.15.cloned.1.call-update) | async-done | bytes 25165840 | tf_op jit(solution)/shard_map/all_gather | solution.py:182
  526.6 30.3 copy.199
  556.9 201.7 %while.28 = (s32[]{:T(128)}, bf16[2,256,8,192]{1,3,2,0:T(8,128)(2,1)}, f32[2,8,256,1]{2,1,3,0:T(8,128)}, bf16[2,4096,8,192]{1,3,2,0:T(8,128)(2,1)}, pred[2,4096]...) while((s32[]{:T(128)}, ...), condition=%wide.region_5.6_spmd, body=%wide.region_2.5_spmd.sunk | while | flops 4899338240 | bytes 253312112 | solution.py:202
  557.3 35.5 %fusion.218 = f32[256,8,4096]{2,1,0:T(8,128)} fusion(bf16[32,256,4096]{2,0,1:T(8,128)(2,1)} %get-tuple-element.654, bf16[2,256,8,32]{3,2,1,0:T(8,128)(2,1)} %get-tuple-element.653, s32[]{:T(128)} %get-tuple-element.636), kind=kOutput, calls=%fused_computation.13.clone.1 | convolution fusion | flops 536870912 | bytes 101188096 | tf_op jit(solution)/shard_map/while/body/eval_jaxpr/qhf,fqt->hqt/dot_general | solution.py:77
  593.6 31.2 fusion.219
  624.8 13.6 fusion.220
  639.0 18.6 fusion.221
  657.6 35.6 %fusion.218 = f32[256,8,4096]{2,1,0:T(8,128)} fusion(bf16[32,256,4096]{2,0,1:T(8,128)(2,1)} %get-tuple-element.654, bf16[2,256,8,32]{3,2,1,0:T(8,128)(2,1)} %get-tuple-element.653, s32[]{:T(128)} %get-tuple-element.636), kind=kOutput, calls=%fused_computation.13.clone.1 | convolution fusion | flops 536870912 | bytes 101188096 | tf_op jit(solution)/shard_map/while/body/eval_jaxpr/qhf,fqt->hqt/dot_general | solution.py:77
  694.0 31.2 fusion.219
  725.2 14.5 fusion.220
  740.3 18.2 fusion.221
  771.6 23.5 multiply_convert_fusion.3
  807.7 17.6 all-gather.29.cloned.1.call-done
  825.3 13.9 multiply_reduce_fusion.1
  866.7 13.3 convert_reduce_fusion
  915.2 722.8 %while.29 = (s32[]{:T(128)}, f32[2,256,8,64]{1,3,2,0:T(8,128)}, f32[2,256,8,32]{1,3,0,2:T(8,128)}, bf16[2,256,512]{2,1,0:T(8,128)(2,1)}, bf16[2,256,1536]{2,1,0:...) while((s32[]{:T(128)}, f32[2,256,8,64]{1,3,2,0:T(8,128)}, ...), condition=%wide.region_19.20_spmd, body=%wide.region_15.19_spmd.sunk | while | flops 10821302272 | bytes 569695424 | solution.py:363
  933.8 20.5 fusion.234
  954.3 34.9 %fusion.235 = f32[256,8,4096]{2,1,0:T(8,128)} fusion(bf16[32,256,4096]{2,0,1:T(8,128)(2,1)} %get-tuple-element.693, bf16[2,256,8,32]{3,2,1,0:T(8,128)(2,1)} %get-tuple-element.692, s32[]{:T(128)S(6)} %copy.347), kind=kOutput, calls=%fused_computation.51.clone.1 | convolution fusion | flops 536870912 | bytes 101187584 | tf_op jit(solution)/shard_map/while/body/eval_jaxpr/qhf,fqt->hqt/dot_general | solution.py:77
  989.2 42.7 %multiply_reduce_fusion.11 = (f32[8,256]{1,0:T(8,128)S(1)}, f32[8,256,4096]{2,1,0:T(8,128)}) fusion(f32[8,256,4096]{2,1,0:T(8,128)} %fusion.234, f32[8,256]{1,0:T(8,128)S(1)} %dynamic-slice_bitcast_fusion.2, f32[256,8,4096]{2,1,0:T(8,128)} %fusion.235, bf16[2,4096,8,64]{1,3,2,0:T(8,128)(2,1)} %get-tuple-element.689, s32[]{:T(128)S(6)} %copy.347, ...), kind=kOutput, calls=%fused_computation.28.clone.1 | convolution fusion | flops 1115682816 | bytes 105141248 | tf_op jit(solution)/shard_map/while/body/eval_jaxpr/qhk,thk->hqt/dot_general | solution.py:76
  1031.8 27.8 multiply_convert_fusion.12
  1070.7 18.3 fusion.238
  1089.1 31.3 fusion.237
  1143.8 136.8 %reduce-scatter.44.cloned.1.call-done = bf16[256,1536]{0,1:T(8,128)(2,1)} async-done(((bf16[4096,1536]{0,1:T(8,128)(2,1)}), bf16[256,1536]{0,1:T(8,128)(2,1)}) %reduce-scatter.44.cloned.1.call-update) | async-done | bytes 786448 | tf_op jit(solution)/shard_map/while/body/eval_jaxpr/reduce_scatter | solution.py:354
  1286.4 20.5 fusion.234
  1306.9 34.9 %fusion.235 = f32[256,8,4096]{2,1,0:T(8,128)} fusion(bf16[32,256,4096]{2,0,1:T(8,128)(2,1)} %get-tuple-element.693, bf16[2,256,8,32]{3,2,1,0:T(8,128)(2,1)} %get-tuple-element.692, s32[]{:T(128)S(6)} %copy.347), kind=kOutput, calls=%fused_computation.51.clone.1 | convolution fusion | flops 536870912 | bytes 101187584 | tf_op jit(solution)/shard_map/while/body/eval_jaxpr/qhf,fqt->hqt/dot_general | solution.py:77
  1341.8 42.6 %multiply_reduce_fusion.11 = (f32[8,256]{1,0:T(8,128)S(1)}, f32[8,256,4096]{2,1,0:T(8,128)}) fusion(f32[8,256,4096]{2,1,0:T(8,128)} %fusion.234, f32[8,256]{1,0:T(8,128)S(1)} %dynamic-slice_bitcast_fusion.2, f32[256,8,4096]{2,1,0:T(8,128)} %fusion.235, bf16[2,4096,8,64]{1,3,2,0:T(8,128)(2,1)} %get-tuple-element.689, s32[]{:T(128)S(6)} %copy.347, ...), kind=kOutput, calls=%fused_computation.28.clone.1 | convolution fusion | flops 1115682816 | bytes 105141248 | tf_op jit(solution)/shard_map/while/body/eval_jaxpr/qhk,thk->hqt/dot_general | solution.py:76
  1384.4 27.8 multiply_convert_fusion.12
  1423.3 18.3 fusion.238
  1441.6 31.3 fusion.237
  1495.8 137.4 %reduce-scatter.44.cloned.1.call-done = bf16[256,1536]{0,1:T(8,128)(2,1)} async-done(((bf16[4096,1536]{0,1:T(8,128)(2,1)}), bf16[256,1536]{0,1:T(8,128)(2,1)}) %reduce-scatter.44.cloned.1.call-update) | async-done | bytes 786448 | tf_op jit(solution)/shard_map/while/body/eval_jaxpr/reduce_scatter | solution.py:354
  1756.0 40.8 %all-reduce.16 = (f32[1536]{0:T(1024)S(1)}, f32[512]{0:T(512)S(1)}, f32[512]{0:T(512)S(1)}, f32[1536]{0:T(1024)S(1)}, f32[3072]{0:T(1024)S(1)}, /*index=5*/f32[1...) all-reduce(f32[1536]{0:T(1024)S(1)} %get-tuple-element.373, ...), channel_id=4, replica_groups=mesh['dp'=2,'seq'=16] {'dp','seq'}, use_global_device_ids=true, to_apply=%region_23.24.clone | all-reduce | flops 11776 | bytes 94208
  1817.3 60.8 %reduce-scatter.38.cloned.1.call-done = f32[48,1536]{1,0:T(8,128)} async-done(((f32[1536,1536]{1,0:T(8,128)}), f32[48,1536]{1,0:T(8,128)}) %reduce-scatter.38.cloned.1.call-update) | async-done | bytes 294928
  1878.1 132.4 %reduce-scatter.36.cloned.1.call-done = f32[16,32]{1,0:T(8,128)} async-done(((f32[512,32]{1,0:T(8,128)}), f32[16,32]{1,0:T(8,128)}) %reduce-scatter.36.cloned.1.call-update) | async-done | bytes 2064
  2010.5 107.0 %reduce-scatter.20.cloned.1.call-done = f32[48,512]{1,0:T(8,128)} async-done(((f32[1536,512]{1,0:T(8,128)}), f32[48,512]{1,0:T(8,128)}) %reduce-scatter.20.cloned.1.call-update) | async-done | bytes 98320 | tf_op jit(solution)/shard_map/reduce_scatter | solution.py:392
  2117.5 106.3 %reduce-scatter.22.cloned.1.call-done = f32[48,512]{1,0:T(8,128)} async-done(((f32[1536,512]{1,0:T(8,128)}), f32[48,512]{1,0:T(8,128)}) %reduce-scatter.22.cloned.1.call-update) | async-done | bytes 98320 | tf_op jit(solution)/shard_map/reduce_scatter | solution.py:393
  2223.8 140.8 %reduce-scatter.26.cloned.1.call-done = f32[48,1536]{1,0:T(8,128)} async-done(((f32[1536,1536]{1,0:T(8,128)}), f32[48,1536]{1,0:T(8,128)}) %reduce-scatter.26.cloned.1.call-update) | async-done | bytes 294928 | tf_op jit(solution)/shard_map/reduce_scatter | solution.py:398
  2364.6 142.1 %reduce-scatter.24.cloned.1.call-done = f32[48,1536]{1,0:T(8,128)} async-done(((f32[1536,1536]{1,0:T(8,128)}), f32[48,1536]{1,0:T(8,128)}) %reduce-scatter.24.cloned.1.call-update) | async-done | bytes 294928 | tf_op jit(solution)/shard_map/reduce_scatter | solution.py:394
  2506.8 141.2 %reduce-scatter.32.cloned.1.call-done = f32[48,1536]{1,0:T(8,128)} async-done(((f32[1536,1536]{1,0:T(8,128)}), f32[48,1536]{1,0:T(8,128)}) %reduce-scatter.32.cloned.1.call-update) | async-done | bytes 294928 | tf_op jit(solution)/shard_map/reduce_scatter | solution.py:405
  2647.9 142.0 %reduce-scatter.34.cloned.1.call-done = f32[48,1536]{1,0:T(8,128)} async-done(((f32[1536,1536]{1,0:T(8,128)}), f32[48,1536]{1,0:T(8,128)}) %reduce-scatter.34.cloned.1.call-update) | async-done | bytes 294928 | tf_op jit(solution)/shard_map/reduce_scatter | solution.py:409
  2789.9 211.9 %reduce-scatter.30.cloned.1.call-done = f32[96,1536]{1,0:T(8,128)} async-done(((f32[3072,1536]{1,0:T(8,128)}), f32[96,1536]{1,0:T(8,128)}) %reduce-scatter.30.cloned.1.call-update) | async-done | bytes 589840 | tf_op jit(solution)/shard_map/reduce_scatter | solution.py:402
  3001.8 210.8 %reduce-scatter.28.cloned.1.call-done = f32[48,3072]{1,0:T(8,128)} async-done(((f32[1536,3072]{1,0:T(8,128)}), f32[48,3072]{1,0:T(8,128)}) %reduce-scatter.28.cloned.1.call-update) | async-done | bytes 589840 | tf_op jit(solution)/shard_map/reduce_scatter | solution.py:400
  (367 shorter events, 434.6 us)
Async XLA Ops:
  7.2 330.6 %copy-start = (bf16[2,512,1536]{2,1,0:T(8,128)(2,1)S(1)}, bf16[2,512,1536]{2,1,0:T(8,128)(2,1)}, u32[]{:S(2)}) copy-start(bf16[2,512,1536]{2,1,0:T(8,128)(2,1)} %param.28) | copy-start | bytes 9437188
  7.2 61.6 %all-gather.19.cloned.1.call-start = ((), (), s32[]{:S(2)}) async-start(), calls=%async_computation.16 | async-start | bytes 1622016 | tf_op jit(solution)/shard_map/all_gather | solution.py:144
  7.9 126.1 %all-gather.13.cloned.1.call-start = ((), (), s32[]{:S(2)}) async-start(), calls=%async_computation.13 | async-start | bytes 4866048 | tf_op jit(solution)/shard_map/all_gather | solution.py:145
  8.7 295.8 %all-gather.17.cloned.1.call-start = ((), (), s32[]{:S(2)}) async-start(), calls=%async_computation.15 | async-start | bytes 1622016 | tf_op jit(solution)/shard_map/all_gather | solution.py:143
  9.4 313.1 %all-gather.33.cloned.1.call-start = ((), (), s32[]{:S(2)}) async-start(), calls=%async_computation.23 | async-start | bytes 4866048 | tf_op jit(solution)/shard_map/all_gather | solution.py:160
  10.0 327.8 %all-gather.31.cloned.1.call-start = ((), (), s32[]{:S(2)}) async-start(), calls=%async_computation.22 | async-start | bytes 4866048 | tf_op jit(solution)/shard_map/all_gather | solution.py:157
  10.6 387.0 %all-gather.21.cloned.1.call-start = ((), (), s32[]{:S(2)}) async-start(), calls=%async_computation.17 | async-start | bytes 8912896 | tf_op jit(solution)/shard_map/all_gather | solution.py:181
  72.5 71.0 %copy-start.58 = (bf16[16,32]{1,0:T(8,128)(2,1)S(1)}, bf16[16,32]{1,0:T(8,128)(2,1)}, u32[]{:S(2)}) copy-start(bf16[16,32]{1,0:T(8,128)(2,1)} %param.37) | copy-start | bytes 3076
  72.5 454.1 %all-gather.15.cloned.1.call-start = ((), (), s32[]{:S(2)}) async-start(), calls=%async_computation.14 | async-start | bytes 26738688 | tf_op jit(solution)/shard_map/all_gather | solution.py:182
  140.6 622.6 %all-gather.23.cloned.1.call-start = ((), (), s32[]{:S(2)}) async-start(), calls=%async_computation.18 | async-start | bytes 4866048 | tf_op jit(solution)/shard_map/all_gather | solution.py:149
  141.4 630.2 %all-gather.25.cloned.1.call-start = ((), (), s32[]{:S(2)}) async-start(), calls=%async_computation.19 | async-start | bytes 9732096 | tf_op jit(solution)/shard_map/all_gather | solution.py:151
  142.1 653.0 %all-gather.27.cloned.1.call-start = ((), (), s32[]{:S(2)}) async-start(), calls=%async_computation.20 | async-start | bytes 9732096 | tf_op jit(solution)/shard_map/all_gather | solution.py:153
  142.7 682.6 %all-gather.29.cloned.1.call-start = ((), (), s32[]{:S(2)}) async-start(), calls=%async_computation.21 | async-start | bytes 4866048 | tf_op jit(solution)/shard_map/all_gather | solution.py:156
  183.4 131.0 %copy-start.21 = (bf16[512,32]{1,0:T(8,128)(2,1)}, bf16[512,32]{1,0:T(8,128)(2,1)S(1)}, u32[]{:S(2)}) copy-start(bf16[512,32]{1,0:T(8,128)(2,1)S(1)} %all_gather.84) | copy-start | bytes 98308
  183.4 8.7 copy-start.61
  229.7 118.6 %copy-start.26 = (f32[1536]{0:T(1024)}, f32[1536]{0:T(1024)S(1)}, u32[]{:S(2)}) copy-start(f32[1536]{0:T(1024)S(1)} %get-tuple-element.375) | copy-start | bytes 18436
  229.7 118.6 %copy-start.28 = (f32[1536]{0:T(1024)}, f32[1536]{0:T(1024)S(1)}, u32[]{:S(2)}) copy-start(f32[1536]{0:T(1024)S(1)} %get-tuple-element.376) | copy-start | bytes 18436
  322.6 15.3 copy-start.57
  332.3 15.0 collective-permute-start.2
  335.9 11.5 collective-permute-start.3
  337.8 9.5 copy-start.8
  769.4 120.4 %copy-start.43 = (f32[512]{0:T(512)}, f32[512]{0:T(512)S(1)}, u32[]{:S(2)}) copy-start(f32[512]{0:T(512)S(1)} %broadcast_multiply_fusion.4) | copy-start | bytes 6148
  771.5 118.4 %copy-start.50 = (f32[512]{0:T(512)}, f32[512]{0:T(512)S(1)}, u32[]{:S(2)}) copy-start(f32[512]{0:T(512)S(1)} %fusion.102) | copy-start | bytes 6148
  771.5 23.6 copy-start.56
  805.6 19.7 copy-start.40
  825.3 14.0 copy-start.13
  855.5 11.2 copy-start.11
  861.5 44.7 %collective-permute-start = (bf16[2,1,1536]{2,1,0:T(2,128)(2,1)S(1)}, bf16[2,1,1536]{2,1,0:T(2,128)(2,1)S(1)}, u32[]{:S(2)}, u32[]{:S(2)}) collective-permute-start(bf16[2,1,1536]{2,1,0:T(2,128)(2,1)S(1)} %get-tuple-element.458), channel_id=1, source_target_pairs={{0,1},{1,2},{2,3},{3,4},{4,5},{5,6},{6,7},{7,8},{8,9},{9,10},{10,1... | collective-permute-start | bytes 18440 | tf_op jit(solution)/shard_map/ppermute | solution.py:26
  864.7 41.5 %collective-permute-start.1 = (bf16[2,1,1536]{2,1,0:T(2,128)(2,1)S(1)}, bf16[2,1,1536]{2,1,0:T(2,128)(2,1)S(1)}, u32[]{:S(2)}, u32[]{:S(2)}) collective-permute-start(bf16[2,1,1536]{2,1,0:T(2,128)(2,1)S(1)} %get-tuple-element.459), channel_id=1, source_target_pairs={{1,0},{2,1},{3,2},{4,3},{5,4},{6,5},{7,6},{8,7},{9,8},{10,9},{11,1... | collective-permute-start | bytes 18440 | tf_op jit(solution)/shard_map/ppermute | solution.py:27
  866.7 24.2 copy-start.52
  866.7 13.3 copy-start.5
  880.0 9.8 copy-start.64
  932.3 209.6 %reduce-scatter.42.cloned.1.call-start = ((), (), s32[]{:S(2)}) async-start(), calls=%async_computation.35 | async-start | bytes 4456448 | tf_op jit(solution)/shard_map/while/body/eval_jaxpr/reduce_scatter | solution.py:351
  1070.7 209.9 %reduce-scatter.44.cloned.1.call-start = ((), (), s32[]{:S(2)}) async-start(), calls=%async_computation.36 | async-start | bytes 13369344 | tf_op jit(solution)/shard_map/while/body/eval_jaxpr/reduce_scatter | solution.py:354
  1285.0 209.1 %reduce-scatter.42.cloned.1.call-start = ((), (), s32[]{:S(2)}) async-start(), calls=%async_computation.35 | async-start | bytes 4456448 | tf_op jit(solution)/shard_map/while/body/eval_jaxpr/reduce_scatter | solution.py:351
  1423.3 210.0 %reduce-scatter.44.cloned.1.call-start = ((), (), s32[]{:S(2)}) async-start(), calls=%async_computation.36 | async-start | bytes 13369344 | tf_op jit(solution)/shard_map/while/body/eval_jaxpr/reduce_scatter | solution.py:354
  1638.0 177.9 %reduce-scatter.40.cloned.1.call-start = ((), (), s32[]{:S(2)}) async-start(), calls=%async_computation.34 | async-start | bytes 811008
  1638.6 239.6 %reduce-scatter.38.cloned.1.call-start = ((), (), s32[]{:S(2)}) async-start(), calls=%async_computation.33 | async-start | bytes 9732096
  1657.8 352.7 %reduce-scatter.36.cloned.1.call-start = ((), (), s32[]{:S(2)}) async-start(), calls=%async_computation.32 | async-start | bytes 270336
  1665.6 451.9 %reduce-scatter.20.cloned.1.call-start = ((), (), s32[]{:S(2)}) async-start(), calls=%async_computation.24 | async-start | bytes 3244032 | tf_op jit(solution)/shard_map/reduce_scatter | solution.py:392
  1669.9 554.0 %reduce-scatter.22.cloned.1.call-start = ((), (), s32[]{:S(2)}) async-start(), calls=%async_computation.25 | async-start | bytes 3244032 | tf_op jit(solution)/shard_map/reduce_scatter | solution.py:393
  1674.2 690.5 %reduce-scatter.26.cloned.1.call-start = ((), (), s32[]{:S(2)}) async-start(), calls=%async_computation.27 | async-start | bytes 9732096 | tf_op jit(solution)/shard_map/reduce_scatter | solution.py:398
  1682.9 823.8 %reduce-scatter.24.cloned.1.call-start = ((), (), s32[]{:S(2)}) async-start(), calls=%async_computation.26 | async-start | bytes 9732096 | tf_op jit(solution)/shard_map/reduce_scatter | solution.py:394
  1691.4 956.6 %reduce-scatter.32.cloned.1.call-start = ((), (), s32[]{:S(2)}) async-start(), calls=%async_computation.30 | async-start | bytes 9732096 | tf_op jit(solution)/shard_map/reduce_scatter | solution.py:405
  1699.7 1090.2 %reduce-scatter.34.cloned.1.call-start = ((), (), s32[]{:S(2)}) async-start(), calls=%async_computation.31 | async-start | bytes 9732096 | tf_op jit(solution)/shard_map/reduce_scatter | solution.py:409
  1709.9 1291.9 %reduce-scatter.30.cloned.1.call-start = ((), (), s32[]{:S(2)}) async-start(), calls=%async_computation.29 | async-start | bytes 19464192 | tf_op jit(solution)/shard_map/reduce_scatter | solution.py:402
  1722.2 1490.4 %reduce-scatter.28.cloned.1.call-start = ((), (), s32[]{:S(2)}) async-start(), calls=%async_computation.28 | async-start | bytes 19464192 | tf_op jit(solution)/shard_map/reduce_scatter | solution.py:400
  1801.5 5.7 copy-start.59
  (49 other events, 129.9 us)
Sparse Core Ops, SparseCore 0:
  10.9 57.8 all-gather.18
  71.8 62.2 all-gather.12
  136.9 53.8 all-gather.16
  193.5 62.4 all-gather.32
  258.8 62.3 all-gather.30
  323.9 73.7 all-gather.20
  399.8 126.7 all-gather.14
  529.5 63.5 all-gather.22
  596.0 80.8 all-gather.24
  679.6 80.6 all-gather.26
  763.1 62.0 all-gather.28
  1070.8 71.0 reduce-scatter.41
  1146.5 134.0 reduce-scatter.43
  1423.4 70.5 reduce-scatter.41
  1498.5 134.7 reduce-scatter.43
  1643.6 93.7 reduce-scatter.39
  1743.8 134.3 reduce-scatter.37
  1880.9 129.5 reduce-scatter.35
  2016.5 100.9 reduce-scatter.19
  2123.4 100.4 reduce-scatter.21
  2230.3 134.2 reduce-scatter.25
  2372.1 134.6 reduce-scatter.23
  2513.3 134.6 reduce-scatter.31
  2655.3 134.5 reduce-scatter.33
  2796.9 204.8 reduce-scatter.29
  3008.6 203.9 reduce-scatter.27
where the time goes:
time: 3230 us; the launch traced here: 3220 us
  waiting for transfers between devices  1920 us (59%)
  matrix products  732 us (23%)
  other arithmetic  229 us (7%)
  blocking collectives  159 us (5%)
  local copies, waits for them, and re-layouts  137 us (4%)
    reduce_scatter x2, waiting for transfers between devices, attend_back(): lax.psum_scatter(value_part.astype(jnp.bfloat16), 'seq', scatter_dimensio...  274 us
    reduce_scatter x1, waiting for transfers between devices, on_device(): lax.psum_scatter(grad_outer, ('dp', 'seq'), scatter_dimension=0, tiled=True)  212 us
    reduce_scatter x1, waiting for transfers between devices, on_device(): lax.psum_scatter(grad_inner, ('dp', 'seq'), scatter_dimension=0, tiled=True)  211 us
    unnamed x25, waiting for transfers between devices  200 us
    dot_general x4, matrix products, window_scores(): jnp.einsum('qhk,thk->hqt', content_one, key_one, preferred_element_type=j...  148 us
    reduce_scatter x1, waiting for transfers between devices, on_device(): lax.psum_scatter(grad_value, ('dp', 'seq'), scatter_dimension=0, tiled=True)  142 us
    reduce_scatter x1, waiting for transfers between devices, on_device(): lax.psum_scatter(grad_point, ('dp', 'seq'), scatter_dimension=0, tiled=True)  142 us
    reduce_scatter x1, waiting for transfers between devices, on_device(): lax.psum_scatter(grad_upsample, ('dp', 'seq'), scatter_dimension=0, tiled...  141 us
  transfers between devices with their start and end apart: 30, of which 19 were waited for; matrix products, arithmetic and copies ran while one was open for 24% of the time, Pallas kernels for 0%

commit v1 on v0

v1 whole, which is shorter than its diff:
```python
import functools
import math

import jax
import jax.numpy as jnp
from jax import lax
from jax.experimental import pallas as pl
from jax.experimental.pallas import tpu as pltpu
from jax.sharding import PartitionSpec as P

H = 8
KD = 64
VD = 192
RPF = 32
NEG = -1e30
BF = jnp.bfloat16
F32 = jnp.float32
epsilon = 1e-05


def extended_2(array, sides, width):
    for axis, dim in sides:
        peers, length = (lax.axis_size(axis), array.shape[dim])
        up = [(i, (i + 1) % peers) for i in range(peers - 1)]
        down = [(j, i) for i, j in up]
        last = lax.slice_in_dim(array, length - width, length, axis=dim)
        initial = lax.slice_in_dim(array, 0, width, axis=dim)
        before = lax.ppermute(last, axis, up)
        after = lax.ppermute(initial, axis, down)
        array = jnp.concatenate([before, array, after], axis=dim)
    return array


def layer_norm(values, gain):
    mean = jnp.mean(values, axis=-1, keepdims=True)
    centered = values - mean
    spread = jnp.mean(centered * centered, axis=-1, keepdims=True)
    return centered * lax.rsqrt(spread + epsilon) * gain


def smooth_gelu(values):
    return jax.nn.gelu(values, approximate=False)


def norm_gelu(values, gain):
    return smooth_gelu(layer_norm(values, gain))


def matmul(left, right):
    return jnp.dot(left, right, preferred_element_type=jnp.float32)


def times_transposed(left, right):
    return lax.dot_general(
        left, right, (((1,), (1,)), ((), ())), preferred_element_type=jnp.float32
    )


def transposed_times(left, right):
    return lax.dot_general(
        left, right, (((0,), (0,)), ((), ())), preferred_element_type=jnp.float32
    )


def depth_apply(extended, taps):
    return (
        extended[:, :-2] * taps[:, 0]
        + extended[:, 1:-1] * taps[:, 1]
        + extended[:, 2:] * taps[:, 2]
    )


def dot(a, b):
    return lax.dot_general(a, b, (((1,), (0,)), ((), ())), preferred_element_type=F32)


def dot32(a, b, dims=((1,), (0,))):
    return lax.dot_general(
        a, b, (dims, ((), ())), precision=lax.Precision.HIGHEST, preferred_element_type=F32
    )


def key_side(parts, part, rates, rows, groups, mine, other, store):
    half = RPF // 2
    spot = lax.broadcasted_iota(jnp.int32, (half, rows), 1).astype(F32)
    low = jnp.exp(-rates * (rows - 1 - spot)).astype(BF)
    high = jnp.exp(-rates * spot).astype(BF)
    pad = jnp.zeros((128 - KD - RPF, rows), BF)
    for slot in range(parts):
        theirs = lax.rem(part + slot, 2) if parts == 2 else slot_part(part, slot, parts)
        for g in range(groups):
            source = mine if slot == 0 else other
            if slot == 0:
                kt, vt = mine[g, 0, KD : 2 * KD, :], mine[g, 0, 2 * KD :, :]
            else:
                kt, vt = other[slot - 1, g, 0, :KD, :], other[slot - 1, g, 0, KD:, :]
            store(g * parts + theirs, jnp.concatenate([kt, low, high, pad], axis=0), vt)


def slot_part(part, slot, parts):
    out, bit = part, 1
    while bit < parts:
        if slot & bit:
            has = lax.rem(lax.div(part, bit), 2)
            out = out + bit - 2 * bit * has
        bit *= 2
    return out


def query_side(content, bias, relative, half):
    positional = content.astype(F32) + bias
    projected = dot32(relative, positional).astype(BF).astype(F32)
    return positional, projected[:half] + projected[half:], projected[:half] - projected[half:]


def block_query(content, plus, minus, rates, q_block, k_block, rows, kind):
    spot = lax.broadcasted_iota(jnp.int32, plus.shape, 1)
    query_pos = q_block * rows + spot
    zero = jnp.zeros(plus.shape, BF)
    below = above = zero
    if kind != "above":
        gap = (query_pos - (k_block * rows + rows - 1)).astype(F32)
        below = (plus * jnp.exp(jnp.minimum(-rates * gap, 60.0))).astype(BF)
    if kind != "below":
        gap = (k_block * rows - query_pos).astype(F32)
        above = (minus * jnp.exp(jnp.minimum(-rates * gap, 60.0))).astype(BF)
    rest = jnp.zeros((128 - KD - RPF, rows), BF)
    if kind == "below":
        return jnp.concatenate([content, below, zero, rest], axis=0)
    if kind == "above":
        return jnp.concatenate([content, zero, above, rest], axis=0)
    return (
        jnp.concatenate([content, below, zero, rest], axis=0),
        jnp.concatenate([content, zero, above, rest], axis=0),
    )


def signs(q_block, k_block, rows):
    i = q_block * rows + lax.broadcasted_iota(jnp.int32, (rows, rows), 1)
    j = k_block * rows + lax.broadcasted_iota(jnp.int32, (rows, rows), 0)
    return i, j


def block_scores(k_sc, content, plus, minus, rates, q_block, k_block, rows, kind, length):
    keys = k_sc[pl.ds(pl.multiple_of(k_block * rows, rows), rows), :]
    if kind != "both":
        return dot(keys, block_query(content, plus, minus, rates, q_block, k_block, rows, kind))
    below, above = block_query(content, plus, minus, rates, q_block, k_block, rows, kind)
    i, j = signs(q_block, k_block, rows)
    s_below, s_above = dot(keys, below), dot(keys, above)
    scores = jnp.where(i > j, s_below, jnp.where(i < j, s_above, 0.5 * (s_below + s_above)))
    return jnp.where(j < length, scores, NEG)


def visit_tiles(tile, q_block, length, rows, per, tiles):
    span = rows * per
    count = lax.div(length + span - 1, span)
    full = lax.div(length, span)
    own = lax.div(q_block, per)
    pl.loop(0, jnp.minimum(own, full))(functools.partial(tile, kind="below"))
    pl.loop(own + 1, full)(functools.partial(tile, kind="above"))

    @pl.loop(0, 2)
    def _(k):
        t = jnp.where(k == 0, own, full)
        go = (t < count) & ((k == 0) | (full != own))

        @pl.when(go)
        def _():
            tile(t, kind="both")


def forward_kernel(
    parts, per, info, rates_ref, bias_ref, rel_ref, mine, other, mixed, wide, lse, k_sc, v_sc, m_sc, l_sc, acc
):
    groups, rows = mine.shape[0], mine.shape[3]
    half = RPF // 2
    length = info[pl.program_id(0)]
    part = info[pl.num_programs(0)]
    rates = rates_ref[...]

    def store(block, kt, vt):
        spot = pl.multiple_of(block * rows, rows)
        k_sc[pl.ds(spot, rows), :] = kt.T
        v_sc[:, pl.ds(spot, rows)] = vt

    key_side(parts, part, rates, rows, groups, mine, other, store)

    @pl.loop(0, groups)
    def _(g):
        q_block = g * parts + part

        @pl.when(q_block * rows > length)
        def _():
            mixed[g, 0] = jnp.zeros(mixed.shape[2:], mixed.dtype)
            wide[g, 0] = jnp.zeros(wide.shape[2:], wide.dtype)
            lse[g, 0] = jnp.zeros(lse.shape[2:], lse.dtype)

        @pl.when(q_block * rows <= length)
        def _():
            content = mine[g, 0, :KD, :]
            _, plus, minus = query_side(content, bias_ref[...], rel_ref[...], half)
            m_sc[...] = jnp.full(m_sc.shape, NEG, F32)
            l_sc[...] = jnp.zeros(l_sc.shape, F32)
            acc[...] = jnp.zeros(acc.shape, F32)

            def tile(t, kind):
                scores = jnp.concatenate(
                    [
                        block_scores(
                            k_sc, content, plus, minus, rates, q_block, t * per + n, rows, kind, length
                        )
                        for n in range(per)
                    ],
                    axis=0,
                )
                old = m_sc[...]
                new = jnp.maximum(old, jnp.max(scores, axis=0, keepdims=True))
                alpha = jnp.exp(old - new)
                probs = jnp.exp(scores - new)
                m_sc[...] = new
                l_sc[...] = l_sc[...] * alpha + jnp.sum(probs, axis=0, keepdims=True)
                span = rows * per
                values = v_sc[:, pl.ds(pl.multiple_of(t * span, span), span)]
                acc[...] = acc[...] * alpha + dot(values, probs.astype(BF))

            visit_tiles(tile, q_block, length, rows, per, groups * parts // per)
            total = l_sc[...]
            out = acc[...] / total
            mixed[g, 0] = out.astype(BF)
            wide[g, 0] = out
            lse[g, 0] = jnp.broadcast_to(m_sc[...] + jnp.log(total), lse.shape[2:])


def backward_kernel(
    parts, per, info, rates_ref, bias_ref, rel_ref, mine, other, grad, wide, lse,
    dq, dkv_mine, dkv_other, sums, rel_grad,
    k_sc, kt_sc, v_sc, dk_sc, dv_sc, dq_sc, bias_sc,
):
    groups, rows = mine.shape[0], mine.shape[3]
    half = RPF // 2
    step = pl.program_id(0)
    length = info[step]
    part = info[pl.num_programs(0)]
    rates = rates_ref[...]
    scale = KD**-0.5

    def store(block, kt, vt):
        spot = pl.multiple_of(block * rows, rows)
        k_sc[pl.ds(spot, rows), :] = kt.T
        kt_sc[:, pl.ds(spot, rows)] = kt
        v_sc[pl.ds(spot, rows), :] = vt.T

    key_side(parts, part, rates, rows, groups, mine, other, store)
    dk_sc[...] = jnp.zeros(dk_sc.shape, F32)
    dv_sc[...] = jnp.zeros(dv_sc.shape, F32)

    @pl.when(step == 0)
    def _():
        bias_sc[...] = jnp.zeros(bias_sc.shape, F32)
        rel_grad[...] = jnp.zeros(rel_grad.shape, F32)

    @pl.loop(0, groups)
    def _(g):
        q_block = g * parts + part

        @pl.when(q_block * rows > length)
        def _():
            dq[g, 0] = jnp.zeros(dq.shape[2:], dq.dtype)

        @pl.when(q_block * rows <= length)
        def _():
            content = mine[g, 0, :KD, :]
            content_rows = content.T
            positional, plus, minus = query_side(content, bias_ref[...], rel_ref[...], half)
            grad_t = grad[g, 0]
            grad_rows = grad_t.T
            log_total = lse[g, 0, :1, :]
            row_sum = jnp.sum(grad_t.astype(F32) * wide[g, 0], axis=0, keepdims=True)
            dq_sc[...] = jnp.zeros(dq_sc.shape, F32)

            def tile(t, kind):
                span = rows * per
                spot = pl.multiple_of(t * span, span)
                scores = jnp.concatenate(
                    [
                        block_scores(
                            k_sc, content, plus, minus, rates, q_block, t * per + n, rows, kind, length
                        )
                        for n in range(per)
                    ],
                    axis=0,
                )
                exact = jnp.exp(scores - log_total)
                prob_grad = dot(v_sc[pl.ds(spot, span), :], grad_t)
                score_grad = exact * (prob_grad - row_sum)
                low = score_grad.astype(BF)
                dv_sc[pl.ds(spot, span), :] += dot(exact.astype(BF), grad_rows)
                dk_sc[pl.ds(spot, span), :] += dot(low, content_rows)
                for n in range(per):
                    k_block = t * per + n
                    piece = low[n * rows : (n + 1) * rows]
                    keys = kt_sc[:, pl.ds(pl.multiple_of(k_block * rows, rows), rows)]
                    place = q_block * rows + lax.broadcasted_iota(jnp.int32, (half, rows), 1)
                    down = -rates * (place - (k_block * rows + rows - 1)).astype(F32)
                    up = -rates * (k_block * rows - place).astype(F32)
                    if kind == "below":
                        part_sum = dot(keys[: KD + half], piece)
                        dq_sc[:KD] += part_sum[:KD]
                        dq_sc[KD : KD + half] += part_sum[KD:] * jnp.exp(down)
                    elif kind == "above":
                        part_sum = dot(keys[: KD + RPF], piece)
                        dq_sc[:KD] += part_sum[:KD]
                        dq_sc[KD + half :] += part_sum[KD + half :] * jnp.exp(up)
                    else:
                        i, j = signs(q_block, k_block, rows)
                        wide_piece = score_grad[n * rows : (n + 1) * rows]
                        equal = 0.5 * wide_piece
                        lower = jnp.where(i > j, wide_piece, jnp.where(i < j, 0.0, equal)).astype(BF)
                        upper = jnp.where(i < j, wide_piece, jnp.where(i > j, 0.0, equal)).astype(BF)
                        dq_sc[:KD] += dot(keys[:KD], piece)
                        dq_sc[KD : KD + half] += dot(keys[KD : KD + half], lower) * jnp.exp(
                            jnp.minimum(down, 60.0)
                        )
                        dq_sc[KD + half :] += dot(keys[KD + half : KD + RPF], upper) * jnp.exp(
                            jnp.minimum(up, 60.0)
                        )

            visit_tiles(tile, q_block, length, rows, per, groups * parts // per)
            content_grad = dq_sc[:KD]
            down, up = dq_sc[KD : KD + half], dq_sc[KD + half :]
            projected_grad = jnp.concatenate([down + up, down - up], axis=0)
            positional_grad = dot32(rel_ref[...], projected_grad, ((0,), (0,)))
            dq[g, 0] = (scale * (content_grad + positional_grad)).astype(BF)
            bias_sc[0] += content_grad
            bias_sc[1] += positional_grad
            rel_grad[...] += dot32(positional, projected_grad, ((1,), (1,)))

    for slot in range(parts):
        theirs = slot_part(part, slot, parts)
        for g in range(groups):
            spot = pl.multiple_of((g * parts + theirs) * rows, rows)
            dkt = dk_sc[pl.ds(spot, rows), :].astype(BF).T
            dvt = dv_sc[pl.ds(spot, rows), :].astype(BF).T
            both = jnp.concatenate([dkt, dvt], axis=0)
            if slot == 0:
                dkv_mine[g, 0] = both
            else:
                dkv_other[slot - 1, g, 0] = both

    @pl.when(step == pl.num_programs(0) - 1)
    def _():
        sums[...] = scale * jnp.sum(bias_sc[...], axis=-1, keepdims=True)


def attention_cost(windows, groups, rows, parts, wide):
    pairs = windows * groups * rows * groups * parts * rows
    return pl.CostEstimate(
        flops=int(pairs * 2 * wide * 0.75), bytes_accessed=20_000_000, transcendentals=int(pairs)
    )


def whole(*shape):
    return pl.BlockSpec(shape, lambda w: (0,) * len(shape))


def per_window(*shape):
    lead = len(shape) - 3
    return pl.BlockSpec(shape, lambda w: (0,) * lead + (w, 0, 0))


def tile_blocks(rows, groups, parts, target):
    per = max(1, target // rows)
    while (groups * parts) % per:
        per -= 1
    return per


def attention_forward(info, rates, bias, rel, mine, other, parts):
    groups, windows, _, rows = mine.shape
    per = tile_blocks(rows, groups, parts, 512)
    total = groups * parts * rows
    return pl.pallas_call(
        functools.partial(forward_kernel, parts, per),
        grid=(windows,),
        out_shape=(
            jax.ShapeDtypeStruct((groups, windows, VD, rows), BF),
            jax.ShapeDtypeStruct((groups, windows, VD, rows), F32),
            jax.ShapeDtypeStruct((groups, windows, 8, rows), F32),
        ),
        in_specs=[
            pl.BlockSpec(memory_space=pltpu.SMEM),
            whole(*rates.shape),
            whole(*bias.shape),
            whole(*rel.shape),
            per_window(groups, 1, 2 * KD + VD, rows),
            per_window(parts - 1, groups, 1, KD + VD, rows),
        ],
        out_specs=(
            per_window(groups, 1, VD, rows),
            per_window(groups, 1, VD, rows),
            per_window(groups, 1, 8, rows),
        ),
        scratch_shapes=[
            pltpu.VMEM((total, 128), BF),
            pltpu.VMEM((VD, total), BF),
            pltpu.VMEM((1, rows), F32),
            pltpu.VMEM((1, rows), F32),
            pltpu.VMEM((VD, rows), F32),
        ],
        compiler_params=pltpu.CompilerParams(vmem_limit_bytes=56 * 2**20),
        cost_estimate=attention_cost(windows, groups, rows, parts, 128 + 256),
        name="attention_forward",
    )(info, rates, bias, rel, mine, other)


def attention_backward(info, rates, bias, rel, mine, other, grad, wide, lse, parts):
    groups, windows, _, rows = mine.shape
    per = tile_blocks(rows, groups, parts, 512)
    total = groups * parts * rows
    return pl.pallas_call(
        functools.partial(backward_kernel, parts, per),
        grid=(windows,),
        out_shape=(
            jax.ShapeDtypeStruct((groups, windows, KD, rows), BF),
            jax.ShapeDtypeStruct((groups, windows, KD + VD, rows), BF),
            jax.ShapeDtypeStruct((parts - 1, groups, windows, KD + VD, rows), BF),
            jax.ShapeDtypeStruct((2, KD, 1), F32),
            jax.ShapeDtypeStruct((KD, RPF), F32),
        ),
        in_specs=[
            pl.BlockSpec(memory_space=pltpu.SMEM),
            whole(*rates.shape),
            whole(*bias.shape),
            whole(*rel.shape),
            per_window(groups, 1, 2 * KD + VD, rows),
            per_window(parts - 1, groups, 1, KD + VD, rows),
            per_window(groups, 1, VD, rows),
            per_window(groups, 1, VD, rows),
            per_window(groups, 1, 8, rows),
        ],
        out_specs=(
            per_window(groups, 1, KD, rows),
            per_window(groups, 1, KD + VD, rows),
            per_window(parts - 1, groups, 1, KD + VD, rows),
            whole(2, KD, 1),
            whole(KD, RPF),
        ),
        scratch_shapes=[
            pltpu.VMEM((total, 128), BF),
            pltpu.VMEM((128, total), BF),
            pltpu.VMEM((total, VD), BF),
            pltpu.VMEM((total, KD), F32),
            pltpu.VMEM((total, VD), F32),
            pltpu.VMEM((KD + RPF, rows), F32),
            pltpu.VMEM((2, KD, rows), F32),
        ],
        compiler_params=pltpu.CompilerParams(vmem_limit_bytes=56 * 2**20),
        cost_estimate=attention_cost(windows, groups, rows, parts, 3 * 256 + 2 * 256),
        name="attention_backward",
    )(info, rates, bias, rel, mine, other, grad, wide, lse)

MESH = pl.DeviceIdType.MESH


def gather_kernel(pairs, nhi, ndp, *refs):
    count = 1 + max(chunk[0] for pair in pairs for side in pair for chunk in side)
    refs_in, refs_out, sems = refs[:count], refs[count : 2 * count], refs[2 * count :]
    local_sem, send_hi, recv_hi, send_y, recv_y, send_dp, recv_dp, send_c, recv_c = sems
    dp, seq = lax.axis_index("dp"), lax.axis_index("seq")
    hi, low = lax.div(seq, 4), lax.rem(seq, 4)
    y, c = lax.div(low, 2), lax.rem(low, 2)

    def place(dp_to, hi_to, y_to, c_to):
        return (dp_to, hi_to * 4 + y_to * 2 + c_to)

    hi_peers = [place(dp, lax.rem(hi + k, nhi), y, c) for k in range(1, nhi)]
    y_peers = [place(dp, hi, 1 - y, c)]
    dp_peers = [place(lax.rem(dp + k, ndp), hi, y, c) for k in range(1, ndp)]
    c_peers = [place(dp, hi, y, 1 - c)]

    barrier = pltpu.get_barrier_semaphore()
    everyone = hi_peers + y_peers + dp_peers + c_peers
    for peer in everyone:
        pl.semaphore_signal(barrier, inc=1, device_id=peer, device_id_type=MESH)
    pl.semaphore_wait(barrier, len(everyone))

    chunks = [
        [(n, side) + chunk for n, (side, chunk) in enumerate(flat)]
        for flat in [[(s, ch) for s in (0, 1) for ch in pair[s]] for pair in pairs]
    ]
    serial, step_chunks = 0, []
    for group in chunks:
        step_chunks.append([])
        for _, side, array, first, columns in group:
            step_chunks[-1].append((serial, side, array, first, columns))
            serial += 1

    def copies(chunk, stage):
        n, side, array, first, columns = chunk
        cols = pl.ds(first, columns)
        shard, out = refs_in[array], refs_out[array]
        which = (("hi", "y", "dp", "c"), ("hi", "dp", "y", "c"))[side][stage]
        if which == "hi":
            target = out.at[dp, hi, y, c, :, cols]
            source = shard.at[:, cols]
            peers, ss, rs = hi_peers, send_hi, recv_hi
        else:
            if which == "c":
                target = out.at[:, :, :, c, :, cols]
                peers, ss, rs = c_peers, send_c, recv_c
            elif which == "y":
                target = (
                    out.at[dp, :, y, c, :, cols] if stage == 1 else out.at[:, :, y, c, :, cols]
                )
                peers, ss, rs = y_peers, send_y, recv_y
            else:
                target = (
                    out.at[dp, :, y, c, :, cols] if stage == 1 else out.at[dp, :, :, c, :, cols]
                )
                peers, ss, rs = dp_peers, send_dp, recv_dp
            source = target
        return [
            pltpu.make_async_remote_copy(
                src_ref=source,
                dst_ref=target,
                send_sem=ss.at[n, k],
                recv_sem=rs.at[n, k],
                device_id=peer,
                device_id_type=MESH,
            )
            for k, peer in enumerate(peers)
        ]

    def own(array):
        return pltpu.make_async_copy(
            refs_in[array], refs_out[array].at[dp, hi, y, c], local_sem.at[array]
        )

    for group in step_chunks:
        for chunk in group:
            for copy in copies(chunk, 0):
                copy.start()
    for array in range(count):
        own(array).start()
    for array in range(count):
        own(array).wait()
    for step in range(len(pairs) + 2):
        for stage in (3, 2, 1):
            if 0 <= step + 1 - stage < len(pairs):
                for chunk in step_chunks[step + 1 - stage]:
                    for copy in copies(chunk, stage - 1):
                        copy.wait_recv()
                    for copy in copies(chunk, stage):
                        copy.start()
    for group in step_chunks:
        for chunk in group:
            for copy in copies(chunk, 3):
                copy.wait_recv()
    for group in step_chunks:
        for chunk in group:
            for stage in range(4):
                for copy in copies(chunk, stage):
                    copy.wait_send()


def gather_weights(shards, pairs):
    ndp, nseq = lax.axis_size("dp"), lax.axis_size("seq")
    nhi, count = nseq // 4, len(shards)
    chunks = sum(len(side) for pair in pairs for side in pair)
    return pl.pallas_call(
        functools.partial(gather_kernel, pairs, nhi, ndp),
        out_shape=[
            jax.ShapeDtypeStruct((ndp, nhi, 2, 2) + shard.shape, shard.dtype) for shard in shards
        ],
        in_specs=[pl.BlockSpec(memory_space=pl.ANY)] * count,
        out_specs=[pl.BlockSpec(memory_space=pl.ANY)] * count,
        scratch_shapes=[pltpu.SemaphoreType.DMA((count,))]
        + [
            pltpu.SemaphoreType.DMA((chunks, size))
            for size in (nhi - 1, nhi - 1, 1, 1, ndp - 1, ndp - 1, 1, 1)
        ],
        compiler_params=pltpu.CompilerParams(collective_id=1, has_side_effects=True),
        name="gather_weights",
    )(*shards)


def flat_index():
    return lax.axis_index("dp") * lax.axis_size("seq") + lax.axis_index("seq")


def swap(array, mask):
    devices = lax.axis_size("dp") * lax.axis_size("seq")
    return lax.ppermute(array, ("dp", "seq"), [(i, i ^ mask) for i in range(devices)])


def tie(*values):
    return lax.optimization_barrier(values)


def tie_tree(tree):
    leaves, shape = jax.tree.flatten(tree)
    arrays = [k for k, leaf in enumerate(leaves) if isinstance(leaf, jax.Array)]
    for k, value in zip(arrays, tie(*[leaves[k] for k in arrays]), strict=True):
        leaves[k] = value
    return jax.tree.unflatten(shape, leaves)


def bit_of(mask):
    return lax.rem(lax.div(flat_index(), mask), 2)


def halve(arrays, left, mask):
    spot, bit = left.index(mask), bit_of(mask)

    def pick(which):
        return jnp.concatenate(
            [lax.dynamic_index_in_dim(a, which, spot, keepdims=False) for a in arrays], axis=-2
        )

    theirs = swap(pick(1 - bit), mask)
    total = pick(bit).astype(jnp.float32) + theirs.astype(jnp.float32)
    return total.astype(arrays[0].dtype), [m for m in left if m != mask]


def chip_term(left, right):
    half, core = right.shape[1] // 2, bit_of(1)
    theirs = lax.dynamic_slice_in_dim(right, (1 - core) * half, half, 1)
    mine = lax.dynamic_slice_in_dim(right, core * half, half, 1)
    arrived = swap(transposed_times(left, theirs).astype(jnp.bfloat16), 1)
    return (transposed_times(left, mine) + arrived.astype(jnp.float32)).astype(jnp.bfloat16)


def mask_lists():
    nseq, ndp = lax.axis_size("seq"), lax.axis_size("dp")
    left, mask = [], nseq * ndp // 2
    while mask > 1:
        left.append(mask)
        mask //= 2
    across = [m for m in left if m >= nseq]
    return left, across, [m for m in left if 2 < m < nseq]


def plane_orders():
    _, across, _ = mask_lists()
    return (across + [2], [2] + across)


def plane_start(terms, columns):
    left, _, _ = mask_lists()
    chips = 2 ** len(left)
    pieces = []
    for t in terms:
        t = t.reshape((2,) * len(left) + (t.shape[0] // chips, t.shape[1]))
        pieces += [t[..., k : k + columns] for k in range(0, t.shape[-1], columns)]
    half = columns // 2
    return [([p[..., :half] for p in pieces], left), ([p[..., half:] for p in pieces], left)]


def plane_step(state, step, last):
    out = []
    for (arrays, left), order in zip(state, plane_orders(), strict=True):
        hops = order[step:] if last else order[step : step + 1]
        for mask in hops:
            total, left = halve(arrays, left, mask)
            arrays = [total]
        out.append((arrays, left))
    return out


def line_sum(state):
    arrays = [pieces[0] for pieces, _ in state]
    whole_line = jnp.concatenate(arrays, axis=-1)
    _, _, line = mask_lists()
    count = 2 ** len(line)
    blocks = whole_line.reshape((count,) + whole_line.shape[len(line) :])
    here = lax.div(lax.axis_index("seq"), 4)
    total = lax.dynamic_index_in_dim(blocks, here, 0, keepdims=False).astype(jnp.float32)
    for k in range(1, count):
        there = here ^ k
        arrived = swap(lax.dynamic_index_in_dim(blocks, there, 0, keepdims=False), 4 * k)
        total = total + arrived.astype(jnp.float32)
    return total


def to_owner(total, rows):
    core = bit_of(1)
    out, spot = [], 0
    for r in rows:
        piece = total[spot : spot + 2 * r]
        spot += 2 * r
        out.append(piece.reshape(2, r, piece.shape[1]))
    mine = [lax.dynamic_index_in_dim(p, core, 0, keepdims=False) for p in out]
    theirs = jnp.concatenate(
        [lax.dynamic_index_in_dim(p, 1 - core, 0, keepdims=False) for p in out], axis=0
    )
    arrived = swap(theirs, 1)
    done, spot = [], 0
    for r, m in zip(rows, mine, strict=True):
        a = arrived[spot : spot + r]
        spot += r
        done.append((jnp.where(core == 0, m, a), jnp.where(core == 0, a, m)))
    return done


def scatter_small(pieces):
    devices = lax.axis_size("dp") * lax.axis_size("seq")
    packed = jnp.concatenate([p.reshape(devices, -1) for p in pieces], axis=1)
    count = packed.shape[1]
    total = jnp.pad(packed, ((0, 0), (0, -count % 1024))).reshape(devices, -1, 128)
    left, _, _ = mask_lists()
    left = left + [1]
    total = total.reshape((2,) * len(left) + total.shape[1:])
    for mask in left[::-1]:
        total, left = halve([total], left, mask)
    total = total.reshape(-1)
    out, spot = [], 0
    for p in pieces:
        size = p.size // devices
        out.append(total[spot : spot + size].reshape((p.shape[0] // devices,) + p.shape[1:]))
        spot += size
    return out


def on_device(
    inputs,
    skip_input,
    lengths,
    cotangent,
    first_gain,
    query_weight,
    key_weight,
    value_weight,
    content_bias,
    position_bias,
    relative_weight,
    mixing_weight,
    second_gain,
    inner_weight,
    inner_bias,
    outer_weight,
    outer_bias,
    third_gain,
    upsample_weight,
    skip_weight,
    skip_bias,
    depth_weight,
    point_weight,
):
    windows, rows, width = inputs.shape
    scale = float(KD) ** (-0.5)
    wide = 2 * KD + VD
    nseq, ndp = lax.axis_size("seq"), lax.axis_size("dp")
    devices = nseq * ndp
    parts = nseq // H
    keys_total = rows * nseq
    seq = lax.axis_index("seq")
    head, part = lax.div(seq, parts), lax.rem(seq, parts)
    first = seq * rows
    hidden_width = inner_weight.shape[1]

    shard_rows = query_weight.shape[0]
    packed_shard = jnp.concatenate(
        [
            query_weight.reshape(shard_rows, H, KD),
            key_weight.reshape(shard_rows, H, KD),
            value_weight.reshape(shard_rows, H, VD),
        ],
        axis=2,
    ).reshape(shard_rows, H * wide)
    small_shards = (
        first_gain,
        content_bias,
        position_bias,
        relative_weight,
        second_gain,
        inner_bias,
        outer_bias,
        third_gain,
        skip_bias,
        depth_weight,
    )
    small_shard = jnp.concatenate([s.reshape(-1) for s in small_shards])
    small_count = small_shard.shape[0]
    small_shard = jnp.pad(small_shard, (0, -small_count % 2048)).reshape(-1, 128)
    half_wide, half_hidden, half_width = H * wide // 2, hidden_width // 2, width // 2
    gathered = gather_weights(
        [
            small_shard,
            packed_shard,
            skip_weight,
            mixing_weight,
            inner_weight,
            outer_weight,
            upsample_weight,
            point_weight,
        ],
        (
            (((0, 0, 128), (1, 0, half_wide)), ((1, half_wide, half_wide),)),
            (((2, 0, width),), ((3, 0, width),)),
            (((4, 0, half_hidden),), ((5, 0, half_width),)),
            (((4, half_hidden, half_hidden),), ((5, half_width, half_width),)),
            (((6, 0, width),), ((7, 0, width),)),
        ),
    )
    small_full = gathered[0].reshape(devices, -1)
    (
        weight_packed,
        weight_skip,
        weight_mixing,
        weight_inner,
        weight_outer,
        weight_upsample,
        weight_point,
    ) = (g.reshape(-1, g.shape[-1]) for g in gathered[1:])
    small, spot = [], 0
    for s in small_shards:
        small.append(
            small_full[:, spot : spot + s.size].reshape((devices * s.shape[0],) + s.shape[1:])
        )
        spot += s.size
    (
        gain_first,
        bias_content,
        bias_position,
        weight_relative,
        gain_second,
        bias_inner,
        bias_outer,
        gain_third,
        bias_skip,
        weight_depth,
    ) = (s.astype(jnp.float32) for s in small)

    lives = jnp.exp(
        jnp.linspace(math.log(3.0), math.log(keys_total), RPF // 2, dtype=jnp.float32)
    )
    rates = (math.log(2.0) / lives)[:, None]
    bias_gap = ((bias_position - bias_content) * scale).reshape(H, KD, 1)
    bias_gap = lax.dynamic_index_in_dim(bias_gap, head, 0, keepdims=False)
    relative = lax.dynamic_index_in_dim(
        weight_relative.reshape(H, KD, RPF), head, 0, keepdims=False
    ).T
    info = jnp.concatenate([lengths, part[None].astype(jnp.int32)])
    groups = [[p + parts * g for g in range(H)] for p in range(parts)]

    def exchange(array):
        return lax.all_to_all(array, "seq", 0, 0, axis_index_groups=groups, tiled=True)

    def swap_part(array, slot):
        return lax.ppermute(array, "seq", [(i, i ^ slot) for i in range(nseq)])

    flat = inputs.reshape(windows * rows, width).astype(jnp.float32)
    normed, first_norm_back = jax.vjp(layer_norm, flat, gain_first)
    normed_low = normed.astype(jnp.bfloat16)
    per_head = jnp.concatenate(
        [bias_content.reshape(H, KD), jnp.zeros((H, KD + VD), jnp.float32)], axis=1
    ).reshape(H * wide)
    per_scale = jnp.tile(
        jnp.concatenate(
            [jnp.full((KD,), scale, jnp.float32), jnp.ones((KD + VD,), jnp.float32)]
        ),
        H,
    )

    def by_head(array, size):
        (array,) = tie(array)
        (array,) = tie(array.reshape(windows, rows, H, size).transpose(2, 0, 3, 1))
        return array

    def by_row(array):
        (array,) = tie(array.transpose(1, 3, 0, 2).reshape(windows * rows, -1))
        return array

    made = (matmul(normed_low, weight_packed) + per_head) * per_scale
    sent = by_head(made.astype(jnp.bfloat16), wide)
    mine = exchange(sent)
    other = jnp.stack([swap_part(mine[:, :, KD:, :], slot) for slot in range(1, parts)])
    mixed_own, mixed_wide, log_total = attention_forward(
        info, rates, bias_gap, relative, mine, other, parts
    )
    mixed_low = by_row(exchange(mixed_own))
    middle = flat + matmul(mixed_low, weight_mixing)
    second, second_norm_back = jax.vjp(layer_norm, middle, gain_second)
    second_low = second.astype(jnp.bfloat16)
    before = matmul(second_low, weight_inner) + bias_inner
    hidden, gelu_back = jax.vjp(smooth_gelu, before)
    hidden_low = hidden.astype(jnp.bfloat16)
    block_out = middle + matmul(hidden_low, weight_outer) + bias_outer
    third, third_back = jax.vjp(norm_gelu, block_out, gain_third)
    third_low = third.astype(jnp.bfloat16)
    fine = jnp.arange(2 * rows, dtype=jnp.int32)[:, None] // 2
    twice = (fine == jnp.arange(rows, dtype=jnp.int32)[None, :]).astype(jnp.bfloat16)
    third_twice = (
        jnp.einsum(
            "ts,wsd->wtd",
            twice,
            third_low.reshape(windows, rows, width),
            preferred_element_type=jnp.float32,
        )
        .astype(jnp.bfloat16)
        .reshape(windows * 2 * rows, width)
    )
    skip_flat = skip_input.reshape(windows * 2 * rows, width)
    skip_part = matmul(skip_flat, weight_skip) + bias_skip
    joined_low = (
        (matmul(third_twice, weight_upsample) + skip_part)
        .astype(jnp.bfloat16)
        .reshape(windows, 2 * rows, width)
    )
    joined_rim = extended_2(joined_low, (("seq", 1),), 1)
    taps = weight_depth
    joined_wide = joined_rim.astype(jnp.float32)
    conv_low = depth_apply(joined_wide, taps).astype(jnp.bfloat16)
    conv_flat = conv_low.reshape(windows * 2 * rows, width)
    bins = 2 * first + jnp.arange(2 * rows, dtype=jnp.int32)
    keep = (bins // 2)[None, :] < lengths[:, None]
    keep_wide = keep.astype(jnp.float32)[:, :, None]
    outputs = (
        matmul(conv_flat, weight_point).reshape(windows, 2 * rows, width) * keep_wide
    ).astype(jnp.bfloat16)

    out_grad = (cotangent * keep.astype(jnp.bfloat16)[:, :, None]).reshape(
        windows * 2 * rows, width
    )
    term_point = chip_term(conv_flat, out_grad)
    conv_grad = (
        times_transposed(out_grad, weight_point)
        .astype(jnp.bfloat16)
        .reshape(windows, 2 * rows, width)
    )
    grad_rim = extended_2(conv_grad, (("seq", 1),), 1).astype(jnp.float32)
    joined_grad = (
        grad_rim[:, 2:] * taps[:, 0]
        + grad_rim[:, 1:-1] * taps[:, 1]
        + grad_rim[:, :-2] * taps[:, 2]
    )
    conv_wide = conv_grad.astype(jnp.float32)
    grad_depth = jnp.stack(
        [
            jnp.sum(conv_wide * joined_wide[:, :-2], axis=(0, 1)),
            jnp.sum(conv_wide * joined_wide[:, 1:-1], axis=(0, 1)),
            jnp.sum(conv_wide * joined_wide[:, 2:], axis=(0, 1)),
        ],
        axis=1,
    )
    grad_skip_bias = jnp.sum(joined_grad, axis=(0, 1))
    joined_back = joined_grad.astype(jnp.bfloat16)
    joined_flat = joined_back.reshape(windows * 2 * rows, width)
    term_skip = chip_term(skip_flat, joined_flat)
    skip_grad = (
        times_transposed(joined_flat, weight_skip)
        .astype(jnp.bfloat16)
        .reshape(windows, 2 * rows, width)
    )
    lifted_grad = (
        jnp.einsum("ts,wtd->wsd", twice, joined_back, preferred_element_type=jnp.float32)
        .astype(jnp.bfloat16)
        .reshape(windows * rows, width)
    )
    third_grad = times_transposed(lifted_grad, weight_upsample)
    last = [False, True]
    term_point, term_skip, lifted_grad, third_grad, skip_grad, outputs = tie(
        term_point, term_skip, lifted_grad, third_grad, skip_grad, outputs
    )

    sum_a = plane_step(plane_start([term_point, term_skip], half_width), 0, last[0])
    block_grad, grad_third = third_back(third_grad)
    block_low = block_grad.astype(jnp.bfloat16)
    term_upsample = chip_term(third_low, lifted_grad)
    term_outer = chip_term(hidden_low, block_low)
    grad_outer_bias = jnp.sum(block_grad, axis=0)
    (before_grad,) = gelu_back(times_transposed(block_low, weight_outer))
    before_low = before_grad.astype(jnp.bfloat16)
    sum_a, term_upsample, term_outer, before_low, block_grad = tie_tree(
        (sum_a, term_upsample, term_outer, before_low, block_grad)
    )

    sum_a = plane_step(sum_a, 1, last[1])
    sum_b = plane_step(plane_start([term_upsample, term_outer], half_width), 0, last[0])
    grad_inner_bias = jnp.sum(before_low.astype(jnp.float32), axis=0)
    middle_part, grad_second = second_norm_back(times_transposed(before_low, weight_inner))
    middle_grad = block_grad + middle_part
    middle_low = middle_grad.astype(jnp.bfloat16)
    mixed_grad = by_head(times_transposed(middle_low, weight_mixing).astype(jnp.bfloat16), VD)
    term_inner = chip_term(second_low, before_low)
    sum_a, sum_b, term_inner, mixed_grad, middle_low, middle_grad = tie_tree(
        (sum_a, sum_b, term_inner, mixed_grad, middle_low, middle_grad)
    )

    arrived_grad = exchange(mixed_grad)
    sum_b = plane_step(sum_b, 1, last[1])
    term_mixing = chip_term(mixed_low, middle_low)
    sum_b, term_mixing, arrived_grad = tie_tree((sum_b, term_mixing, arrived_grad))

    line_a, line_b = line_sum(sum_a), line_sum(sum_b)
    sum_c = plane_step(plane_start([term_inner, term_mixing], half_width), 0, last[0])
    query_own, own_side, other_side, bias_sums, relative_sum = attention_backward(
        info, rates, bias_gap, relative, mine, other, arrived_grad, mixed_wide, log_total, parts
    )
    line_a, line_b, sum_c, query_own, own_side, other_side = tie_tree(
        (line_a, line_b, sum_c, query_own, own_side, other_side)
    )

    own_side = own_side.astype(jnp.float32)
    for slot in range(1, parts):
        own_side = own_side + swap_part(other_side[slot - 1], slot).astype(jnp.float32)
    heads_grad = exchange(
        jnp.concatenate([query_own, own_side.astype(jnp.bfloat16)], axis=2)
    )
    sum_c = plane_step(sum_c, 1, last[1])
    r = shard_rows
    own_point, own_skip = to_owner(line_a, [r, r])
    own_upsample, own_outer = to_owner(line_b, [r, outer_weight.shape[0]])
    sum_c, heads_grad = tie_tree((sum_c, heads_grad))

    line_c = line_sum(sum_c)
    packed_grad = by_row(heads_grad)
    term_packed = chip_term(normed_low, packed_grad)
    normed_grad = times_transposed(packed_grad, weight_packed)
    input_part, grad_first = first_norm_back(normed_grad)
    input_grad = (middle_grad + input_part).astype(jnp.bfloat16).reshape(windows, rows, width)
    sum_d = plane_start([term_packed], half_wide)
    sum_d = plane_step(plane_step(sum_d, 0, False), 1, True)
    own_inner_low, own_inner_high, own_mixing = to_owner(line_c, [r, r, r])
    (own_packed,) = to_owner(line_sum(sum_d), [r])

    def joined_columns(pair):
        return jnp.concatenate(pair, axis=1)

    def at_head(value):
        full = jnp.zeros((H,) + value.shape, jnp.float32)
        return lax.dynamic_update_index_in_dim(full, value, head, 0)

    small_grads = scatter_small(
        [
            grad_first,
            at_head(bias_sums[0, :, 0]).reshape(-1),
            at_head(bias_sums[1, :, 0]).reshape(-1),
            at_head(relative_sum).reshape(H * KD, RPF),
            grad_second,
            grad_inner_bias,
            grad_outer_bias,
            grad_third,
            grad_skip_bias,
            grad_depth,
        ]
    )
    (
        own_first,
        own_content,
        own_position,
        own_relative,
        own_second,
        own_inner_bias,
        own_outer_bias,
        own_third,
        own_skip_bias,
        own_depth,
    ) = small_grads
    own_heads = joined_columns(own_packed).reshape(r, H, wide)
    own_point, own_skip, own_upsample, own_outer, own_mixing = map(
        joined_columns, (own_point, own_skip, own_upsample, own_outer, own_mixing)
    )
    own_inner = jnp.concatenate(
        [own_inner_low[0], own_inner_high[0], own_inner_low[1], own_inner_high[1]], axis=1
    )
    return (
        outputs,
        input_grad,
        skip_grad,
        own_first,
        own_heads[:, :, :KD].reshape(r, H * KD),
        own_heads[:, :, KD : 2 * KD].reshape(r, H * KD),
        own_heads[:, :, 2 * KD :].reshape(r, H * VD),
        own_content,
        own_position,
        own_relative,
        own_mixing,
        own_second,
        own_inner,
        own_inner_bias,
        own_outer,
        own_outer_bias,
        own_third,
        own_upsample,
        own_skip,
        own_skip_bias,
        own_depth,
        own_point,
    )


def solution(mesh):
    in_specs = (
        P("dp", "seq", None),
        P("dp", "seq", None),
        P("dp"),
        P("dp", "seq", None),
        P(("dp", "seq")),
        P(("dp", "seq"), None),
        P(("dp", "seq"), None),
        P(("dp", "seq"), None),
        P(("dp", "seq")),
        P(("dp", "seq")),
        P(("dp", "seq"), None),
        P(("dp", "seq"), None),
        P(("dp", "seq")),
        P(("dp", "seq"), None),
        P(("dp", "seq")),
        P(("dp", "seq"), None),
        P(("dp", "seq")),
        P(("dp", "seq")),
        P(("dp", "seq"), None),
        P(("dp", "seq"), None),
        P(("dp", "seq")),
        P(("dp", "seq"), None),
        P(("dp", "seq"), None),
    )
    out_specs = (
        P("dp", "seq", None),
        P("dp", "seq", None),
        P("dp", "seq", None),
        P(("dp", "seq")),
        P(("dp", "seq"), None),
        P(("dp", "seq"), None),
        P(("dp", "seq"), None),
        P(("dp", "seq")),
        P(("dp", "seq")),
        P(("dp", "seq"), None),
        P(("dp", "seq"), None),
        P(("dp", "seq")),
        P(("dp", "seq"), None),
        P(("dp", "seq")),
        P(("dp", "seq"), None),
        P(("dp", "seq")),
        P(("dp", "seq")),
        P(("dp", "seq"), None),
        P(("dp", "seq"), None),
        P(("dp", "seq")),
        P(("dp", "seq"), None),
        P(("dp", "seq"), None),
    )
    return jax.shard_map(
        on_device, mesh=mesh, in_specs=in_specs, out_specs=out_specs, check_vma=False
    )
```

time: 3230 us -> 1090 us (0.34)
  waiting for transfers between devices: 1920 us -> 165 us
  matrix products: 732 us -> 175 us
  Pallas kernels: 0 us -> 349 us
  other arithmetic: 229 us -> 96 us
  blocking collectives: 159 us -> 62.8 us
  starting transfers between devices: 12 us -> 104 us
    reduce_scatter x12 -> x0, waiting for transfers between devices: 1490 us -> none  [the longest x2 274 us: attend_back(): lax.psum_scatter(value_part.astype(jnp.bfloat16), 'seq', scatter_dimensio...]
    dot_general x23 -> x2, matrix products: 513 us -> 2.02 us  [the longest x1 1.03 us: on_device(): jnp.einsum('ts,wsd->wtd', twice, third_low.reshape(windows, rows, width),...]
    pallas_call x0 -> x3, Pallas kernels: none -> 349 us  [the longest x1 247 us: gather_weights(): pl.pallas_call(functools.partial(gather_kernel, pairs, nhi, ndp), out_sha...]
    all_gather x11 -> x0, waiting for transfers between devices: 224 us -> none  [the longest x1 117 us: on_device(): lax.all_gather(value_local, 'seq', axis=1, tiled=True)]
    unnamed x25 -> x0, waiting for transfers between devices: 200 us -> none
    ppermute x0 -> x46, waiting for transfers between devices: none -> 146 us  [the longest x44 143 us: swap(): lax.ppermute(array, ('dp', 'seq'), [(i, i ^ mask) for i in range(devices)])]
    unnamed x2 -> x0, blocking collectives: 82.8 us -> none
    all_gather x2 -> x0, blocking collectives: 76.7 us -> none  [the longest x1 39.9 us: on_device(): lax.all_gather(relative_weight, ('dp', 'seq'), axis=0, tiled=True)]
  transfers between devices with their start and end apart: 30 -> 53, of which waited for: 19 -> 23; matrix products, arithmetic and copies ran while one was open for 24% -> 24% of each run, Pallas kernels for 0% -> 5%
where the time goes in v1:
time: 1090 us; the launch traced here: 1070 us
  Pallas kernels  349 us (32%)
  matrix products  175 us (16%)
  waiting for transfers between devices  165 us (15%)
  local copies, waits for them, and re-layouts  112 us (10%)
  starting transfers between devices  104 us (10%)
  other arithmetic  96 us (9%)
  blocking collectives  62.8 us (6%)
    pallas_call x1, Pallas kernels, gather_weights(): pl.pallas_call(functools.partial(gather_kernel, pairs, nhi, ndp), out_sha...  247 us
    ppermute x44, waiting for transfers between devices, swap(): lax.ppermute(array, ('dp', 'seq'), [(i, i ^ mask) for i in range(devices)])  143 us
    ppermute x44, starting transfers between devices, swap(): lax.ppermute(array, ('dp', 'seq'), [(i, i ^ mask) for i in range(devices)])  69.9 us
    all_to_all x1, blocking collectives, exchange(): lax.all_to_all(array, 'seq', 0, 0, axis_index_groups=groups, tiled=True)  62.8 us
    dot_general x14, matrix products, transposed_times(): lax.dot_general(left, right, (((0,), (0,)), ((), ())), preferred_element_...  60.9 us
    dot_general x7, matrix products, matmul(): return jnp.dot(left, right, preferred_element_type=jnp.float32)  59.9 us
    pallas_call x1, Pallas kernels, attention_backward(): pl.pallas_call(functools.partial(backward_kernel, parts, per), grid=(wind...  54.9 us
    dot_general x7, matrix products, times_transposed(): lax.dot_general(left, right, (((1,), (1,)), ((), ())), preferred_element_...  52.2 us
  transfers between devices with their start and end apart: 53, of which 23 were waited for; matrix products, arithmetic and copies ran while one was open for 24% of the time, Pallas kernels for 5%

profile of v1, /device:TPU:1, one launch (start us, length us, event | category | flops | bytes accessed | tf_op | source)
XLA Modules:
  0.0 1067.3 jit_solution(17357362834907248592)
XLA Ops:
  8.9 5.4 concatenate.118
  14.9 246.6 %gather_weights.1 = (bf16[2,4,2,2,16,128]{5,4,3,2,1,0:T(8,128)(2,1)}, bf16[2,4,2,2,48,2560]{5,4,3,2,1,0:T(8,128)(2,1)}, bf16[2,4,2,2,48,1536]{5,4,3,2,1,0:T(8,12...) custom-call(bf16[16,128]{1,0:T(8,128)(2,1)} %pad_bitcast_fusion.refs, ...), custom_call_target="tpu_custom_call" | custom-call | tf_op jit(solution)/shard_map/gather_weights/pallas_call | solution.py:571
  270.3 8.8 multiply_convert_fusion.2
  279.1 5.9 reshape.721
  285.0 4.8 copy.70
  289.7 62.8 %all_to_all.20.mine = bf16[8,2,320,256]{3,2,1,0:T(8,128)(2,1)S(1)} all-to-all(bf16[8,2,320,256]{3,2,1,0:T(8,128)(2,1)} %bitcast.388), channel_id=1, replica_groups={{0,2,4,6,8,10,12,14},{1,3,5,7,9,11,13,15},{16,18,20,22,24,26,28,30},{17..., dimensions={0} | all-to-all | bytes 5242880 | tf_op jit(solution)/shard_map/all_to_all | solution.py:848
  364.7 47.1 %attention_forward.1 = (bf16[8,2,192,256]{3,2,1,0:T(8,128)(2,1)}, f32[8,2,192,256]{3,2,1,0:T(8,128)}, f32[8,2,8,256]{3,2,1,0:T(8,128)}) custom-call(s32[3]{0:T(128)} %pad_add_fusion.info, f32[16,1]{1,0:T(8,128)} %exponential_divide_fusion.rates_ref, f32[64,1]{1,0:T(8,128)} %copy.71.bias_ref, f32[32,64]{1,0:T(8,128)} %bitcast.459, ...), custom_call_target="tpu_custom_call" | custom-call | flops 9663676416 | bytes 20000000 | tf_op jit(solution)/shard_map/attention_forward/pallas_call | solution.py:383
  411.8 4.3 all-to-all-start.1
  418.3 8.8 convolution_convert_fusion.4
  428.8 5.8 collective-permute-start.4
  441.3 9.6 all-to-all-done.1
  454.4 5.4 fusion.139
  461.8 21.8 %multiply_convert_fusion.1 = (bf16[512,3072]{1,0:T(8,128)(2,1)}, f32[512,3072]{1,0:T(8,128)}, f32[512,3072]{1,0:T(8,128)}) fusion(f32[3072]{0:T(1024)S(1)} %reshape.699, bf16[512,1536]{1,0:T(8,128)(2,1)S(1)} %multiply_convert_fusion.5, bf16[1536,3072]{1,0:T(8,128)(2,1)S(1)} %bitcast.467), kind=kOutput, calls=%fused_computation.24 | convolution fusion | flops 4935647232 | bytes 26750976 | tf_op jit(solution)/shard_map/dot_general | solution.py:50
  483.7 7.1 fusion.140
  491.3 9.1 multiply_convert_fusion.4
  501.5 5.0 fusion.141
  506.6 5.4 fusion.6
  512.0 6.1 collective-permute-start.1
  524.1 7.9 fusion.1
  532.0 9.4 convolution_convert_fusion.3
  553.5 6.4 multiply_convert_fusion
  563.8 4.4 add_convert_fusion.7
  576.4 4.3 convolution_convert_fusion.2
  580.8 4.4 convolution_convert_fusion.9
  595.2 12.5 %add_convert_fusion.3 = bf16[512,3072]{1,0:T(8,128)(2,1)S(1)} fusion(f32[512,3072]{1,0:T(8,128)} %get-tuple-element.194, f32[512,3072]{1,0:T(8,128)} %get-tuple-element.313, f32[3072]{0:T(1024)S(1)} %reshape.699, bf16[512,1536]{1,0:T(8,128)(2,1)S(1)} %copy-done.56, bf16[3072,1536]{1,0:T(8,128)(2,1)} %bitcast.468), kind=kOutput, calls=%fused_computation.21 | convolution fusion | flops 4855431168 | bytes 26750976 | tf_op jit(solution)/shard_map/dot_general | solution.py:54
  607.7 10.7 collective-permute-done.8
  625.1 4.7 add_convert_fusion.1
  629.8 4.5 convolution_convert_fusion.1
  649.5 8.1 multiply_reduce_fusion.1
  672.6 25.6 %collective-permute-done.12 = bf16[2,2,192,384]{3,2,1,0:T(8,128)(2,1)} collective-permute-done((bf16[2,2,192,384]{3,2,1,0:T(8,128)(2,1)}, bf16[2,2,192,384]{3,2,1,0:T(8,128)(2,1)}, u32[]{:S(2)}, u32[]{:S(2)}) %collective-permute-start.12) | collective-permute-done | bytes 589856 | tf_op jit(solution)/shard_map/ppermute | solution.py:594
  708.6 6.3 add_convert_fusion
  718.5 4.7 all-to-all-start.2
  734.3 22.5 %collective-permute-done.16 = bf16[192,768]{1,0:T(8,128)(2,1)S(1)} collective-permute-done((bf16[192,768]{1,0:T(8,128)(2,1)S(1)}, bf16[192,768]{1,0:T(8,128)(2,1)S(1)}, u32[]{:S(2)}, u32[]{:S(2)}) %collective-permute-start.16) | collective-permute-done | bytes 294944 | tf_op jit(solution)/shard_map/ppermute | solution.py:594
  761.6 18.3 %collective-permute-done.17 = bf16[192,768]{1,0:T(8,128)(2,1)S(1)} collective-permute-done((bf16[192,768]{1,0:T(8,128)(2,1)S(1)}, bf16[192,768]{1,0:T(8,128)(2,1)S(1)}, u32[]{:S(2)}, u32[]{:S(2)}) %collective-permute-start.17) | collective-permute-done | bytes 294944 | tf_op jit(solution)/shard_map/ppermute | solution.py:594
  783.3 4.5 add_convert_fusion.5
  795.2 6.6 collective-permute-start.22
  803.8 54.9 %attention_backward.1 = (bf16[8,2,64,256]{3,2,1,0:T(8,128)(2,1)}, bf16[8,2,256,256]{3,2,1,0:T(8,128)(2,1)}, bf16[1,8,2,256,256]{4,3,2,1,0:T(8,128)(2,1)}, f32[2,64,1]{2,1,0:T(8,128)}, f32[64,32]{1,0:T(8,128)}) custom-call(s32[3]{0:T(128)} %pad_add_fusion.info, f32[16,1]{1,0:T(8,128)} %exponential_divide_fusion.rates_ref, f32[64,1]{1,0:T(8,128)} %copy.71.bias_ref, ...), custom_call_target="tpu_custom_call" | custom-call | flops 32212254720 | bytes 20000000 | tf_op jit(solution)/shard_map/attention_backward/pallas_call | solution.py:421
  867.5 4.4 collective-permute-start.29
  902.7 11.6 %collective-permute-done.28 = bf16[2,2,288,384]{3,2,1,0:T(8,128)(2,1)S(1)} collective-permute-done((bf16[2,2,288,384]{3,2,1,0:T(8,128)(2,1)S(1)}, bf16[2,2,288,384]{3,2,1,0:T(8,128)(2,1)S(1)}, u32[]{:S(2)}, u32[]{:S(2)}) %collective-permute-start.28) | collective-permute-done | bytes 884768 | tf_op jit(solution)/shard_map/ppermute | solution.py:594
  915.4 17.4 %collective-permute-done.27 = bf16[2,2,288,384]{3,2,1,0:T(8,128)(2,1)S(1)} collective-permute-done((bf16[2,2,288,384]{3,2,1,0:T(8,128)(2,1)S(1)}, bf16[2,2,288,384]{3,2,1,0:T(8,128)(2,1)S(1)}, u32[]{:S(2)}, u32[]{:S(2)}) %collective-permute-start.27) | collective-permute-done | bytes 884768 | tf_op jit(solution)/shard_map/ppermute | solution.py:594
  934.0 7.3 all-to-all-done.3
  945.4 7.1 multiply_reduce_fusion.3
  988.9 5.3 add_convert_fusion.2
  1000.7 10.2 collective-permute-done.46
  1017.1 8.9 collective-permute-start.47
  1027.6 5.3 collective-permute-start.40
  1039.1 7.1 collective-permute-done.42
  1046.3 9.2 collective-permute-start.43
  (579 shorter events, 280.1 us)
Async XLA Ops:
  355.5 9.1 collective-permute-start
  411.8 39.0 %all-to-all-start.1 = ((bf16[8,2,192,256]{3,2,1,0:T(8,128)(2,1)}), bf16[8,2,192,256]{3,2,1,0:T(8,128)(2,1)}, u32[]{:S(2)}, u32[]{:S(2)}) async-start(bf16[8,2,192,256]{3,2,1,0:T(8,128)(2,1)} %get-tuple-element.74), calls=%async_computation.1 | async-start | bytes 3145728 | tf_op jit(solution)/shard_map/all_to_all | solution.py:848
  428.8 91.3 %collective-permute-start.4 = (bf16[2,1,1536]{2,1,0:T(2,128)(2,1)S(1)}, bf16[2,1,1536]{2,1,0:T(2,128)(2,1)S(1)}, u32[]{:S(2)}, u32[]{:S(2)}) collective-permute-start(bf16[2,1,1536]{2,1,0:T(2,128)(2,1)S(1)} %get-tuple-element.204), channel_id=1, source_target_pairs={{0,1},{1,2},{2,3},{3,4},{4,5},{5,6},{6,7},{7,8},{8,9},{9,10},{10,1... | collective-permute-start | bytes 18440 | tf_op jit(solution)/shard_map/ppermute | solution.py:28
  434.6 85.5 %collective-permute-start.5 = (bf16[2,1,1536]{2,1,0:T(2,128)(2,1)S(1)}, bf16[2,1,1536]{2,1,0:T(2,128)(2,1)S(1)}, u32[]{:S(2)}, u32[]{:S(2)}) collective-permute-start(bf16[2,1,1536]{2,1,0:T(2,128)(2,1)S(1)} %get-tuple-element.205), channel_id=1, source_target_pairs={{1,0},{2,1},{3,2},{4,3},{5,4},{6,5},{7,6},{8,7},{9,8},{10,9},{11,1... | collective-permute-start | bytes 18440 | tf_op jit(solution)/shard_map/ppermute | solution.py:29
  512.0 9.0 collective-permute-start.1
  518.1 5.0 collective-permute-start.2
  545.3 14.6 %collective-permute-start.6 = (bf16[1536,768]{0,1:T(8,128)(2,1)}, bf16[1536,768]{0,1:T(8,128)(2,1)S(1)}, u32[]{:S(2)}, u32[]{:S(2)}) collective-permute-start(bf16[1536,768]{0,1:T(8,128)(2,1)} %fusion.20), channel_id=1, source_target_pairs={{0,1},{1,0},{2,3},{3,2},{4,5},{5,4},{6,7},{7,6},{8,9},{9,8},{10,11... | collective-permute-start | bytes 7077896 | tf_op jit(solution)/shard_map/ppermute | solution.py:594
  549.3 14.5 %collective-permute-start.3 = (bf16[1536,768]{1,0:T(8,128)(2,1)}, bf16[1536,768]{1,0:T(8,128)(2,1)S(1)}, u32[]{:S(2)}, u32[]{:S(2)}) collective-permute-start(bf16[1536,768]{1,0:T(8,128)(2,1)} %convolution_convert_fusion.7), channel_id=1, source_target_pairs={{0,1},{1,0},{2,3},{3,2},{4,5},{5,4},{6,7},{7,6},{8,9},{9,8},{10,11... | collective-permute-start | bytes 7077896 | tf_op jit(solution)/shard_map/ppermute | solution.py:594
  580.7 44.4 %collective-permute-start.10 = (bf16[3072,768]{1,0:T(8,128)(2,1)}, bf16[3072,768]{1,0:T(8,128)(2,1)}, u32[]{:S(2)}, u32[]{:S(2)}) collective-permute-start(bf16[3072,768]{1,0:T(8,128)(2,1)} %convolution_convert_fusion.2), channel_id=1, source_target_pairs={{0,1},{1,0},{2,3},{3,2},{4,5},{5,4},{6,7},{7,6},{8,9},{9,8},{10,11... | collective-permute-start | bytes 14155784 | tf_op jit(solution)/shard_map/ppermute | solution.py:594
  585.3 36.2 %collective-permute-start.9 = (bf16[1536,768]{1,0:T(8,128)(2,1)}, bf16[1536,768]{1,0:T(8,128)(2,1)}, u32[]{:S(2)}, u32[]{:S(2)}) collective-permute-start(bf16[1536,768]{1,0:T(8,128)(2,1)} %convolution_convert_fusion.9), channel_id=1, source_target_pairs={{0,1},{1,0},{2,3},{3,2},{4,5},{5,4},{6,7},{7,6},{8,9},{9,8},{10,11... | collective-permute-start | bytes 7077896 | tf_op jit(solution)/shard_map/ppermute | solution.py:594
  590.8 27.5 %collective-permute-start.8 = (bf16[2,2,2,192,384]{4,3,2,1,0:T(8,128)(2,1)S(1)}, bf16[2,2,2,192,384]{4,3,2,1,0:T(8,128)(2,1)S(1)}, u32[]{:S(2)}, u32[]{:S(2)}) collective-permute-start(bf16[2,2,2,192,384]{4,3,2,1,0:T(8,128)(2,1)S(1)} %pad_maximum_fusion.8), channel_id=1, source_target_pairs={{0,2},{1,3},{2,0},{3,1},{4,6},{5,7},{6,4},{7,5},{8,10},{9,11},{10,... | collective-permute-start | bytes 3538952 | tf_op jit(solution)/shard_map/ppermute | solution.py:594
  591.3 29.8 %collective-permute-start.7 = (bf16[2,2,2,192,384]{4,3,2,1,0:T(8,128)(2,1)S(1)}, bf16[2,2,2,192,384]{4,3,2,1,0:T(8,128)(2,1)S(1)}, u32[]{:S(2)}, u32[]{:S(2)}) collective-permute-start(bf16[2,2,2,192,384]{4,3,2,1,0:T(8,128)(2,1)S(1)} %pad_maximum_fusion.7), channel_id=1, source_target_pairs={{0,16},{1,17},{2,18},{3,19},{4,20},{5,21},{6,22},{7,23},{8,24},{9,... | collective-permute-start | bytes 3538952 | tf_op jit(solution)/shard_map/ppermute | solution.py:594
  634.3 74.3 %collective-permute-start.15 = (bf16[1536,1536]{1,0:T(8,128)(2,1)}, bf16[1536,1536]{1,0:T(8,128)(2,1)}, u32[]{:S(2)}, u32[]{:S(2)}) collective-permute-start(bf16[1536,1536]{1,0:T(8,128)(2,1)} %convolution_convert_fusion.1), channel_id=1, source_target_pairs={{0,1},{1,0},{2,3},{3,2},{4,5},{5,4},{6,7},{7,6},{8,9},{9,8},{10,11... | collective-permute-start | bytes 14155784 | tf_op jit(solution)/shard_map/ppermute | solution.py:594
  639.9 62.1 %collective-permute-start.14 = (bf16[2,2,2,288,384]{4,3,2,1,0:T(8,128)(2,1)}, bf16[2,2,2,288,384]{4,3,2,1,0:T(8,128)(2,1)}, u32[]{:S(2)}, u32[]{:S(2)}) collective-permute-start(bf16[2,2,2,288,384]{4,3,2,1,0:T(8,128)(2,1)} %pad_maximum_fusion.2), channel_id=1, source_target_pairs={{0,2},{1,3},{2,0},{3,1},{4,6},{5,7},{6,4},{7,5},{8,10},{9,11},{10,... | collective-permute-start | bytes 5308424 | tf_op jit(solution)/shard_map/ppermute | solution.py:594
  644.8 60.5 %collective-permute-start.13 = (bf16[2,2,2,288,384]{4,3,2,1,0:T(8,128)(2,1)}, bf16[2,2,2,288,384]{4,3,2,1,0:T(8,128)(2,1)}, u32[]{:S(2)}, u32[]{:S(2)}) collective-permute-start(bf16[2,2,2,288,384]{4,3,2,1,0:T(8,128)(2,1)} %pad_maximum_fusion.1), channel_id=1, source_target_pairs={{0,16},{1,17},{2,18},{3,19},{4,20},{5,21},{6,22},{7,23},{8,24},{9,... | collective-permute-start | bytes 5308424 | tf_op jit(solution)/shard_map/ppermute | solution.py:594
  647.4 50.8 %collective-permute-start.12 = (bf16[2,2,192,384]{3,2,1,0:T(8,128)(2,1)}, bf16[2,2,192,384]{3,2,1,0:T(8,128)(2,1)}, u32[]{:S(2)}, u32[]{:S(2)}) collective-permute-start(bf16[2,2,192,384]{3,2,1,0:T(8,128)(2,1)} %dynamic-slice_bitcast_fusion.25), channel_id=1, source_target_pairs={{0,16},{1,17},{2,18},{3,19},{4,20},{5,21},{6,22},{7,23},{8,24},{9,... | collective-permute-start | bytes 1769480 | tf_op jit(solution)/shard_map/ppermute | solution.py:594
  648.3 51.4 %collective-permute-start.11 = (bf16[2,2,192,384]{3,2,1,0:T(8,128)(2,1)}, bf16[2,2,192,384]{3,2,1,0:T(8,128)(2,1)}, u32[]{:S(2)}, u32[]{:S(2)}) collective-permute-start(bf16[2,2,192,384]{3,2,1,0:T(8,128)(2,1)} %dynamic-slice_bitcast_fusion.26), channel_id=1, source_target_pairs={{0,2},{1,3},{2,0},{3,1},{4,6},{5,7},{6,4},{7,5},{8,10},{9,11},{10,... | collective-permute-start | bytes 1769480 | tf_op jit(solution)/shard_map/ppermute | solution.py:594
  717.7 65.6 %collective-permute-start.21 = (bf16[1536,768]{1,0:T(8,128)(2,1)}, bf16[1536,768]{1,0:T(8,128)(2,1)}, u32[]{:S(2)}, u32[]{:S(2)}) collective-permute-start(bf16[1536,768]{1,0:T(8,128)(2,1)} %convolution_convert_fusion.8), channel_id=1, source_target_pairs={{0,1},{1,0},{2,3},{3,2},{4,5},{5,4},{6,7},{7,6},{8,9},{9,8},{10,11... | collective-permute-start | bytes 7077896 | tf_op jit(solution)/shard_map/ppermute | solution.py:594
  718.5 69.3 %all-to-all-start.2 = ((bf16[8,2,192,256]{3,2,1,0:T(8,128)(2,1)}), bf16[8,2,192,256]{3,2,1,0:T(8,128)(2,1)}, u32[]{:S(2)}, u32[]{:S(2)}) async-start(bf16[8,2,192,256]{3,2,1,0:T(8,128)(2,1)} %bitcast.61), calls=%async_computation.2 | async-start | bytes 3145728 | tf_op jit(solution)/shard_map/all_to_all | solution.py:848
  724.5 56.4 %collective-permute-start.20 = (bf16[2,2,288,384]{3,2,1,0:T(8,128)(2,1)S(1)}, bf16[2,2,288,384]{3,2,1,0:T(8,128)(2,1)S(1)}, u32[]{:S(2)}, u32[]{:S(2)}) collective-permute-start(bf16[2,2,288,384]{3,2,1,0:T(8,128)(2,1)S(1)} %dynamic-slice_bitcast_fusion.7), channel_id=1, source_target_pairs={{0,16},{1,17},{2,18},{3,19},{4,20},{5,21},{6,22},{7,23},{8,24},{9,... | collective-permute-start | bytes 2654216 | tf_op jit(solution)/shard_map/ppermute | solution.py:594
  727.3 54.8 %collective-permute-start.19 = (bf16[2,2,288,384]{3,2,1,0:T(8,128)(2,1)S(1)}, bf16[2,2,288,384]{3,2,1,0:T(8,128)(2,1)S(1)}, u32[]{:S(2)}, u32[]{:S(2)}) collective-permute-start(bf16[2,2,288,384]{3,2,1,0:T(8,128)(2,1)S(1)} %dynamic-slice_bitcast_fusion.8), channel_id=1, source_target_pairs={{0,2},{1,3},{2,0},{3,1},{4,6},{5,7},{6,4},{7,5},{8,10},{9,11},{10,... | collective-permute-start | bytes 2654216 | tf_op jit(solution)/shard_map/ppermute | solution.py:594
  728.9 27.8 %collective-permute-start.16 = (bf16[192,768]{1,0:T(8,128)(2,1)S(1)}, bf16[192,768]{1,0:T(8,128)(2,1)S(1)}, u32[]{:S(2)}, u32[]{:S(2)}) collective-permute-start(bf16[192,768]{1,0:T(8,128)(2,1)S(1)} %get-tuple-element.242), channel_id=1, source_target_pairs={{0,4},{1,5},{2,6},{3,7},{4,0},{5,1},{6,2},{7,3},{8,12},{9,13},{10,... | collective-permute-start | bytes 884744 | tf_op jit(solution)/shard_map/ppermute | solution.py:594
  730.9 49.1 %collective-permute-start.17 = (bf16[192,768]{1,0:T(8,128)(2,1)S(1)}, bf16[192,768]{1,0:T(8,128)(2,1)S(1)}, u32[]{:S(2)}, u32[]{:S(2)}) collective-permute-start(bf16[192,768]{1,0:T(8,128)(2,1)S(1)} %get-tuple-element.244), channel_id=1, source_target_pairs={{0,8},{1,9},{2,10},{3,11},{4,12},{5,13},{6,14},{7,15},{8,0},{9,1},... | collective-permute-start | bytes 884744 | tf_op jit(solution)/shard_map/ppermute | solution.py:594
  756.8 23.2 %collective-permute-start.18 = (bf16[192,768]{1,0:T(8,128)(2,1)S(1)}, bf16[192,768]{1,0:T(8,128)(2,1)S(1)}, u32[]{:S(2)}, u32[]{:S(2)}) collective-permute-start(bf16[192,768]{1,0:T(8,128)(2,1)S(1)} %get-tuple-element.243), channel_id=1, source_target_pairs={{0,12},{1,13},{2,14},{3,15},{4,8},{5,9},{6,10},{7,11},{8,4},{9,5},... | collective-permute-start | bytes 884744 | tf_op jit(solution)/shard_map/ppermute | solution.py:594
  790.3 70.7 %collective-permute-start.26 = (bf16[2,2,2,288,384]{4,3,2,1,0:T(8,128)(2,1)S(1)}, bf16[2,2,2,288,384]{4,3,2,1,0:T(8,128)(2,1)}, u32[]{:S(2)}, u32[]{:S(2)}) collective-permute-start(bf16[2,2,2,288,384]{4,3,2,1,0:T(8,128)(2,1)S(1)} %pad_maximum_fusion.5), channel_id=1, source_target_pairs={{0,2},{1,3},{2,0},{3,1},{4,6},{5,7},{6,4},{7,5},{8,10},{9,11},{10,... | collective-permute-start | bytes 5308424 | tf_op jit(solution)/shard_map/ppermute | solution.py:594
  792.7 71.6 %collective-permute-start.25 = (bf16[2,2,2,288,384]{4,3,2,1,0:T(8,128)(2,1)}, bf16[2,2,2,288,384]{4,3,2,1,0:T(8,128)(2,1)}, u32[]{:S(2)}, u32[]{:S(2)}) collective-permute-start(bf16[2,2,2,288,384]{4,3,2,1,0:T(8,128)(2,1)} %pad_maximum_fusion.4), channel_id=1, source_target_pairs={{0,16},{1,17},{2,18},{3,19},{4,20},{5,21},{6,22},{7,23},{8,24},{9,... | collective-permute-start | bytes 5308424 | tf_op jit(solution)/shard_map/ppermute | solution.py:594
  795.2 63.6 %collective-permute-start.22 = (bf16[288,768]{1,0:T(8,128)(2,1)}, bf16[288,768]{1,0:T(8,128)(2,1)S(1)}, u32[]{:S(2)}, u32[]{:S(2)}) collective-permute-start(bf16[288,768]{1,0:T(8,128)(2,1)} %get-tuple-element.225), channel_id=1, source_target_pairs={{0,4},{1,5},{2,6},{3,7},{4,0},{5,1},{6,2},{7,3},{8,12},{9,13},{10,... | collective-permute-start | bytes 1327112 | tf_op jit(solution)/shard_map/ppermute | solution.py:594
  801.8 57.0 %collective-permute-start.23 = (bf16[288,768]{1,0:T(8,128)(2,1)S(1)}, bf16[288,768]{1,0:T(8,128)(2,1)S(1)}, u32[]{:S(2)}, u32[]{:S(2)}) collective-permute-start(bf16[288,768]{1,0:T(8,128)(2,1)S(1)} %get-tuple-element.227), channel_id=1, source_target_pairs={{0,8},{1,9},{2,10},{3,11},{4,12},{5,13},{6,14},{7,15},{8,0},{9,1},... | collective-permute-start | bytes 1327112 | tf_op jit(solution)/shard_map/ppermute | solution.py:594
  802.2 56.7 %collective-permute-start.24 = (bf16[288,768]{1,0:T(8,128)(2,1)S(1)}, bf16[288,768]{1,0:T(8,128)(2,1)}, u32[]{:S(2)}, u32[]{:S(2)}) collective-permute-start(bf16[288,768]{1,0:T(8,128)(2,1)S(1)} %get-tuple-element.226), channel_id=1, source_target_pairs={{0,12},{1,13},{2,14},{3,15},{4,8},{5,9},{6,10},{7,11},{8,4},{9,5},... | collective-permute-start | bytes 1327112 | tf_op jit(solution)/shard_map/ppermute | solution.py:594
  867.5 8.2 collective-permute-start.29
  878.2 63.1 %all-to-all-start.3 = ((bf16[8,2,320,256]{3,2,1,0:T(8,128)(2,1)}), bf16[8,2,320,256]{3,2,1,0:T(8,128)(2,1)S(1)}, u32[]{:S(2)}, u32[]{:S(2)}) async-start(bf16[8,2,320,256]{3,2,1,0:T(8,128)(2,1)} %pad_maximum_fusion), calls=%async_computation.3 | async-start | bytes 5242880 | tf_op jit(solution)/shard_map/all_to_all | solution.py:848
  893.3 20.9 %collective-permute-start.28 = (bf16[2,2,288,384]{3,2,1,0:T(8,128)(2,1)S(1)}, bf16[2,2,288,384]{3,2,1,0:T(8,128)(2,1)S(1)}, u32[]{:S(2)}, u32[]{:S(2)}) collective-permute-start(bf16[2,2,288,384]{3,2,1,0:T(8,128)(2,1)S(1)} %dynamic-slice_bitcast_fusion.5), channel_id=1, source_target_pairs={{0,16},{1,17},{2,18},{3,19},{4,20},{5,21},{6,22},{7,23},{8,24},{9,... | collective-permute-start | bytes 2654216 | tf_op jit(solution)/shard_map/ppermute | solution.py:594
  894.8 38.0 %collective-permute-start.27 = (bf16[2,2,288,384]{3,2,1,0:T(8,128)(2,1)S(1)}, bf16[2,2,288,384]{3,2,1,0:T(8,128)(2,1)S(1)}, u32[]{:S(2)}, u32[]{:S(2)}) collective-permute-start(bf16[2,2,288,384]{3,2,1,0:T(8,128)(2,1)S(1)} %dynamic-slice_bitcast_fusion.6), channel_id=1, source_target_pairs={{0,2},{1,3},{2,0},{3,1},{4,6},{5,7},{6,4},{7,5},{8,10},{9,11},{10,... | collective-permute-start | bytes 2654216 | tf_op jit(solution)/shard_map/ppermute | solution.py:594
  900.8 62.8 %collective-permute-start.49 = (f32[96,768]{1,0:T(8,128)}, f32[96,768]{1,0:T(8,128)}, u32[]{:S(2)}, u32[]{:S(2)}) collective-permute-start(f32[96,768]{1,0:T(8,128)} %pad_maximum_fusion.19), channel_id=1, source_target_pairs={{0,1},{1,0},{2,3},{3,2},{4,5},{5,4},{6,7},{7,6},{8,9},{9,8},{10,11... | collective-permute-start | bytes 884744 | tf_op jit(solution)/shard_map/ppermute | solution.py:594
  962.1 26.8 %collective-permute-start.35 = (bf16[1536,1280]{1,0:T(8,128)(2,1)}, bf16[1536,1280]{1,0:T(8,128)(2,1)}, u32[]{:S(2)}, u32[]{:S(2)}) collective-permute-start(bf16[1536,1280]{1,0:T(8,128)(2,1)} %convolution_convert_fusion), channel_id=1, source_target_pairs={{0,1},{1,0},{2,3},{3,2},{4,5},{5,4},{6,7},{7,6},{8,9},{9,8},{10,11... | collective-permute-start | bytes 11796488 | tf_op jit(solution)/shard_map/ppermute | solution.py:594
  963.4 6.8 collective-permute-start.48
  982.7 18.0 %collective-permute-start.44 = (bf16[288,768]{1,0:T(8,128)(2,1)}, bf16[288,768]{1,0:T(8,128)(2,1)}, u32[]{:S(2)}, u32[]{:S(2)}) collective-permute-start(bf16[288,768]{1,0:T(8,128)(2,1)} %get-tuple-element.222), channel_id=1, source_target_pairs={{0,4},{1,5},{2,6},{3,7},{4,0},{5,1},{6,2},{7,3},{8,12},{9,13},{10,... | collective-permute-start | bytes 1327112 | tf_op jit(solution)/shard_map/ppermute | solution.py:594
  983.3 17.4 %collective-permute-start.45 = (bf16[288,768]{1,0:T(8,128)(2,1)}, bf16[288,768]{1,0:T(8,128)(2,1)}, u32[]{:S(2)}, u32[]{:S(2)}) collective-permute-start(bf16[288,768]{1,0:T(8,128)(2,1)} %get-tuple-element.224), channel_id=1, source_target_pairs={{0,8},{1,9},{2,10},{3,11},{4,12},{5,13},{6,14},{7,15},{8,0},{9,1},... | collective-permute-start | bytes 1327112 | tf_op jit(solution)/shard_map/ppermute | solution.py:594
  985.0 25.9 %collective-permute-start.46 = (bf16[288,768]{1,0:T(8,128)(2,1)}, bf16[288,768]{1,0:T(8,128)(2,1)}, u32[]{:S(2)}, u32[]{:S(2)}) collective-permute-start(bf16[288,768]{1,0:T(8,128)(2,1)} %get-tuple-element.223), channel_id=1, source_target_pairs={{0,12},{1,13},{2,14},{3,15},{4,8},{5,9},{6,10},{7,11},{8,4},{9,5},... | collective-permute-start | bytes 1327112 | tf_op jit(solution)/shard_map/ppermute | solution.py:594
  994.9 18.7 %collective-permute-start.36 = (bf16[2,2,2,96,640]{4,3,1,0,2:T(8,128)(2,1)S(1)}, bf16[2,2,2,96,640]{4,3,1,0,2:T(8,128)(2,1)S(1)}, u32[]{:S(2)}, u32[]{:S(2)}) collective-permute-start(bf16[2,2,2,96,640]{4,3,1,0,2:T(8,128)(2,1)S(1)} %bitcast.445), channel_id=1, source_target_pairs={{0,16},{1,17},{2,18},{3,19},{4,20},{5,21},{6,22},{7,23},{8,24},{9,... | collective-permute-start | bytes 2949128 | tf_op jit(solution)/shard_map/ppermute | solution.py:594
  997.1 18.4 %collective-permute-start.38 = (bf16[2,2,2,96,640]{4,3,2,1,0:T(8,128)(2,1)S(1)}, bf16[2,2,2,96,640]{4,3,2,1,0:T(8,128)(2,1)S(1)}, u32[]{:S(2)}, u32[]{:S(2)}) collective-permute-start(bf16[2,2,2,96,640]{4,3,2,1,0:T(8,128)(2,1)S(1)} %dynamic-slice_bitcast_fusion.4), channel_id=1, source_target_pairs={{0,2},{1,3},{2,0},{3,1},{4,6},{5,7},{6,4},{7,5},{8,10},{9,11},{10,... | collective-permute-start | bytes 2949128 | tf_op jit(solution)/shard_map/ppermute | solution.py:594
  1013.9 13.2 %collective-permute-start.37 = (bf16[2,2,96,640]{3,2,1,0:T(8,128)(2,1)S(1)}, bf16[2,2,96,640]{3,2,1,0:T(8,128)(2,1)S(1)}, u32[]{:S(2)}, u32[]{:S(2)}) collective-permute-start(bf16[2,2,96,640]{3,2,1,0:T(8,128)(2,1)S(1)} %dynamic-slice_bitcast_fusion.36), channel_id=1, source_target_pairs={{0,2},{1,3},{2,0},{3,1},{4,6},{5,7},{6,4},{7,5},{8,10},{9,11},{10,... | collective-permute-start | bytes 1474568 | tf_op jit(solution)/shard_map/ppermute | solution.py:594
  1015.8 11.5 %collective-permute-start.39 = (bf16[2,2,96,640]{3,2,1,0:T(8,128)(2,1)S(1)}, bf16[2,2,96,640]{3,2,1,0:T(8,128)(2,1)S(1)}, u32[]{:S(2)}, u32[]{:S(2)}) collective-permute-start(bf16[2,2,96,640]{3,2,1,0:T(8,128)(2,1)S(1)} %dynamic-slice_bitcast_fusion.35), channel_id=1, source_target_pairs={{0,16},{1,17},{2,18},{3,19},{4,20},{5,21},{6,22},{7,23},{8,24},{9,... | collective-permute-start | bytes 1474568 | tf_op jit(solution)/shard_map/ppermute | solution.py:594
  1017.1 18.1 %collective-permute-start.47 = (f32[144,768]{1,0:T(8,128)S(1)}, f32[144,768]{1,0:T(8,128)S(1)}, u32[]{:S(2)}, u32[]{:S(2)}) collective-permute-start(f32[144,768]{1,0:T(8,128)S(1)} %pad_maximum_fusion.14), channel_id=1, source_target_pairs={{0,1},{1,0},{2,3},{3,2},{4,5},{5,4},{6,7},{7,6},{8,9},{9,8},{10,11... | collective-permute-start | bytes 1327112 | tf_op jit(solution)/shard_map/ppermute | solution.py:594
  1027.6 11.5 %collective-permute-start.40 = (bf16[96,1280]{1,0:T(8,128)(2,1)S(1)}, bf16[96,1280]{1,0:T(8,128)(2,1)S(1)}, u32[]{:S(2)}, u32[]{:S(2)}) collective-permute-start(bf16[96,1280]{1,0:T(8,128)(2,1)S(1)} %get-tuple-element.259), channel_id=1, source_target_pairs={{0,4},{1,5},{2,6},{3,7},{4,0},{5,1},{6,2},{7,3},{8,12},{9,13},{10,... | collective-permute-start | bytes 737288 | tf_op jit(solution)/shard_map/ppermute | solution.py:594
  1032.9 6.2 collective-permute-start.41
  1034.1 12.0 %collective-permute-start.42 = (bf16[96,1280]{1,0:T(8,128)(2,1)S(1)}, bf16[96,1280]{1,0:T(8,128)(2,1)S(1)}, u32[]{:S(2)}, u32[]{:S(2)}) collective-permute-start(bf16[96,1280]{1,0:T(8,128)(2,1)S(1)} %get-tuple-element.260), channel_id=1, source_target_pairs={{0,12},{1,13},{2,14},{3,15},{4,8},{5,9},{6,10},{7,11},{8,4},{9,5},... | collective-permute-start | bytes 737288 | tf_op jit(solution)/shard_map/ppermute | solution.py:594
  1046.3 10.8 %collective-permute-start.43 = (f32[48,1280]{1,0:T(8,128)S(1)}, f32[48,1280]{1,0:T(8,128)S(1)}, u32[]{:S(2)}, u32[]{:S(2)}) collective-permute-start(f32[48,1280]{1,0:T(8,128)S(1)} %dynamic-slice_bitcast_fusion.47), channel_id=1, source_target_pairs={{0,1},{1,0},{2,3},{3,2},{4,5},{5,4},{6,7},{7,6},{8,9},{9,8},{10,11... | collective-permute-start | bytes 737288 | tf_op jit(solution)/shard_map/ppermute | solution.py:594
  (129 other events, 2121.9 us)

commit v2 on v1

--- a/solution.py
+++ b/solution.py
@@ -463,11 +463,18 @@
 MESH = pl.DeviceIdType.MESH
 
 
-def gather_kernel(pairs, nhi, ndp, *refs):
-    count = 1 + max(chunk[0] for pair in pairs for side in pair for chunk in side)
-    refs_in, refs_out, sems = refs[:count], refs[count : 2 * count], refs[2 * count :]
-    local_sem, send_hi, recv_hi, send_y, recv_y, send_dp, recv_dp, send_c, recv_c = sems
+def links_kernel(pairs, counts, parts, *refs):
+    n_in, n_out = counts
+    refs_in, refs = refs[:n_in], refs[n_in:]
+    if parts:
+        blocks, refs = refs[0], refs[1:]
+    refs_out, refs = refs[:n_out], refs[n_out:]
+    if parts:
+        mine, other = refs[:2]
+        refs = refs[2:]
+    local_sem, send_hi, recv_hi, send_y, recv_y, send_dp, recv_dp, send_c, recv_c = refs[:9]
     dp, seq = lax.axis_index("dp"), lax.axis_index("seq")
+    ndp, nhi = refs_out[0].shape[:2]
     hi, low = lax.div(seq, 4), lax.rem(seq, 4)
     y, c = lax.div(low, 2), lax.rem(low, 2)
 
@@ -478,32 +485,45 @@
     y_peers = [place(dp, hi, 1 - y, c)]
     dp_peers = [place(lax.rem(dp + k, ndp), hi, y, c) for k in range(1, ndp)]
     c_peers = [place(dp, hi, y, 1 - c)]
+    everyone = hi_peers + y_peers + dp_peers + c_peers
+    if parts:
+        head, part = lax.div(seq, parts), lax.rem(seq, parts)
+        head_of = [lax.rem(head + k, H) for k in range(1, H)]
+        head_peers = [(dp, h * parts + part) for h in head_of]
+        part_peers = [(dp, head * parts + slot_part(part, k, parts)) for k in range(1, parts)]
+        everyone = everyone + head_peers + part_peers
 
     barrier = pltpu.get_barrier_semaphore()
-    everyone = hi_peers + y_peers + dp_peers + c_peers
     for peer in everyone:
         pl.semaphore_signal(barrier, inc=1, device_id=peer, device_id_type=MESH)
     pl.semaphore_wait(barrier, len(everyone))
 
-    chunks = [
-        [(n, side) + chunk for n, (side, chunk) in enumerate(flat)]
-        for flat in [[(s, ch) for s in (0, 1) for ch in pair[s]] for pair in pairs]
-    ]
-    serial, step_chunks = 0, []
-    for group in chunks:
+    def remote(source, target, ss, rs, peer):
+        return pltpu.make_async_remote_copy(
+            src_ref=source,
+            dst_ref=target,
+            send_sem=ss,
+            recv_sem=rs,
+            device_id=peer,
+            device_id_type=MESH,
+        )
+
+    step_chunks, serial = [], 0
+    for pair in pairs:
         step_chunks.append([])
-        for _, side, array, first, columns in group:
-            step_chunks[-1].append((serial, side, array, first, columns))
-            serial += 1
+        for side in (0, 1):
+            for chunk in pair[side]:
+                step_chunks[-1].append((serial, side) + chunk)
+                serial += 1
 
     def copies(chunk, stage):
-        n, side, array, first, columns = chunk
+        n, side, shard, shard_first, array, first, columns = chunk
         cols = pl.ds(first, columns)
-        shard, out = refs_in[array], refs_out[array]
+        out = refs_out[array]
         which = (("hi", "y", "dp", "c"), ("hi", "dp", "y", "c"))[side][stage]
         if which == "hi":
             target = out.at[dp, hi, y, c, :, cols]
-            source = shard.at[:, cols]
+            source = refs_in[shard].at[:, pl.ds(shard_first, columns)]
             peers, ss, rs = hi_peers, send_hi, recv_hi
         else:
             if which == "c":
@@ -520,206 +540,664 @@
                 )
                 peers, ss, rs = dp_peers, send_dp, recv_dp
             source = target
-        return [
-            pltpu.make_async_remote_copy(
-                src_ref=source,
-                dst_ref=target,
-                send_sem=ss.at[n, k],
-                recv_sem=rs.at[n, k],
-                device_id=peer,
-                device_id_type=MESH,
-            )
-            for k, peer in enumerate(peers)
+        return [remote(source, target, ss.at[n, k], rs.at[n, k], p) for k, p in enumerate(peers)]
+
+    def own(chunk):
+        n, _, shard, shard_first, array, first, columns = chunk
+        return pltpu.make_async_copy(
+            refs_in[shard].at[:, pl.ds(shard_first, columns)],
+            refs_out[array].at[dp, hi, y, c, :, pl.ds(first, columns)],
+            local_sem.at[n],
+        )
+
+    everything = [chunk for group in step_chunks for chunk in group]
+    if parts:
+        head_local, head_send, head_recv, part_send, part_recv = refs[9:]
+        head_copies = [
+            remote(blocks.at[:, h], mine.at[head], head_send.at[k], head_recv.at[k], p)
+            for k, (h, p) in enumerate(zip(head_of, head_peers, strict=True))
         ]
-
-    def own(array):
-        return pltpu.make_async_copy(
-            refs_in[array], refs_out[array].at[dp, hi, y, c], local_sem.at[array]
-        )
-
-    for group in step_chunks:
-        for chunk in group:
+        head_own = pltpu.make_async_copy(blocks.at[:, head], mine.at[head], head_local.at[0])
+        keys = mine.at[:, :, pl.ds(KD, KD + VD)]
+        part_copies = [
+            remote(keys, other.at[k], part_send.at[k], part_recv.at[k], p)
+            for k, p in enumerate(part_peers)
+        ]
+        head_own.start()
+    else:
+        head_copies = []
+    ahead, lag = 3, 2
+    share = -(-len(head_copies) // len(pairs))
+
+    def launch(step):
+        for copy in head_copies[step * share : (step + 1) * share]:
+            copy.start()
+        for chunk in step_chunks[step]:
             for copy in copies(chunk, 0):
                 copy.start()
-    for array in range(count):
-        own(array).start()
-    for array in range(count):
-        own(array).wait()
-    for step in range(len(pairs) + 2):
+
+    for step in range(min(ahead, len(pairs))):
+        launch(step)
+    for chunk in everything:
+        own(chunk).start()
+    for chunk in everything:
+        own(chunk).wait()
+    for step in range(len(pairs) + 2 * lag):
         for stage in (3, 2, 1):
-            if 0 <= step + 1 - stage < len(pairs):
-                for chunk in step_chunks[step + 1 - stage]:
+            spot = step - lag * (stage - 1)
+            if 0 <= spot < len(pairs):
+                for chunk in step_chunks[spot]:
                     for copy in copies(chunk, stage - 1):
                         copy.wait_recv()
                     for copy in copies(chunk, stage):
                         copy.start()
-    for group in step_chunks:
-        for chunk in group:
-            for copy in copies(chunk, 3):
-                copy.wait_recv()
-    for group in step_chunks:
-        for chunk in group:
-            for stage in range(4):
-                for copy in copies(chunk, stage):
-                    copy.wait_send()
-
-
-def gather_weights(shards, pairs):
+        if step + ahead < len(pairs):
+            launch(step + ahead)
+    if parts:
+        head_own.wait()
+        for copy in head_copies:
+            copy.wait_recv()
+        for copy in part_copies:
+            copy.start()
+    for chunk in everything:
+        for copy in copies(chunk, 3):
+            copy.wait_recv()
+    if parts:
+        for copy in part_copies:
+            copy.wait_recv()
+        for copy in head_copies + part_copies:
+            copy.wait_send()
+    for chunk in everything:
+        for stage in range(4):
+            for copy in copies(chunk, stage):
+                copy.wait_send()
+
+
+def use_links(name, collective, shards, arrays, pairs, blocks=None):
     ndp, nseq = lax.axis_size("dp"), lax.axis_size("seq")
-    nhi, count = nseq // 4, len(shards)
+    nhi, parts = nseq // 4, nseq // H if blocks is not None else 0
     chunks = sum(len(side) for pair in pairs for side in pair)
-    return pl.pallas_call(
-        functools.partial(gather_kernel, pairs, nhi, ndp),
-        out_shape=[
-            jax.ShapeDtypeStruct((ndp, nhi, 2, 2) + shard.shape, shard.dtype) for shard in shards
-        ],
-        in_specs=[pl.BlockSpec(memory_space=pl.ANY)] * count,
-        out_specs=[pl.BlockSpec(memory_space=pl.ANY)] * count,
-        scratch_shapes=[pltpu.SemaphoreType.DMA((count,))]
-        + [
-            pltpu.SemaphoreType.DMA((chunks, size))
-            for size in (nhi - 1, nhi - 1, 1, 1, ndp - 1, ndp - 1, 1, 1)
-        ],
-        compiler_params=pltpu.CompilerParams(collective_id=1, has_side_effects=True),
-        name="gather_weights",
-    )(*shards)
-
-
-def flat_index():
-    return lax.axis_index("dp") * lax.axis_size("seq") + lax.axis_index("seq")
-
-
-def swap(array, mask):
-    devices = lax.axis_size("dp") * lax.axis_size("seq")
-    return lax.ppermute(array, ("dp", "seq"), [(i, i ^ mask) for i in range(devices)])
+    out_shape = [jax.ShapeDtypeStruct((ndp, nhi, 2, 2) + shape, BF) for shape in arrays]
+    operands = list(shards)
+    sizes = [(chunks,)] + [
+        (chunks, size) for size in (nhi - 1, nhi - 1, 1, 1, ndp - 1, ndp - 1, 1, 1)
+    ]
+    if parts:
+        windows, _, wide, rows = blocks.shape
+        operands.append(blocks)
+        out_shape += [
+            jax.ShapeDtypeStruct((H, windows, wide, rows), BF),
+            jax.ShapeDtypeStruct((parts - 1, H, windows, KD + VD, rows), BF),
+        ]
+        sizes += [(1,), (H - 1,), (H - 1,), (parts - 1,), (parts - 1,)]
+    outs = pl.pallas_call(
+        functools.partial(links_kernel, pairs, (len(shards), len(arrays)), parts),
+        out_shape=out_shape,
+        in_specs=[pl.BlockSpec(memory_space=pl.ANY)] * len(operands),
+        out_specs=[pl.BlockSpec(memory_space=pl.ANY)] * len(out_shape),
+        scratch_shapes=[pltpu.SemaphoreType.DMA(size) for size in sizes],
+        compiler_params=pltpu.CompilerParams(collective_id=collective, has_side_effects=True),
+        name=name,
+    )(*operands)
+    flat = [out.reshape(-1, out.shape[-1]) for out in outs[: len(arrays)]]
+    return flat + list(outs[len(arrays) :])
 
 
 def tie(*values):
     return lax.optimization_barrier(values)
 
 
-def tie_tree(tree):
-    leaves, shape = jax.tree.flatten(tree)
-    arrays = [k for k, leaf in enumerate(leaves) if isinstance(leaf, jax.Array)]
-    for k, value in zip(arrays, tie(*[leaves[k] for k in arrays]), strict=True):
-        leaves[k] = value
-    return jax.tree.unflatten(shape, leaves)
-
-
-def bit_of(mask):
-    return lax.rem(lax.div(flat_index(), mask), 2)
-
-
-def halve(arrays, left, mask):
-    spot, bit = left.index(mask), bit_of(mask)
-
-    def pick(which):
-        return jnp.concatenate(
-            [lax.dynamic_index_in_dim(a, which, spot, keepdims=False) for a in arrays], axis=-2
+def project_kernel(values, gain, content_bias, w_query, w_key, w_value, normed, sent, scratch):
+    windows, rows, _ = values.shape
+
+    @pl.when(pl.program_id(0) == 0)
+    def _():
+        for w in range(windows):
+            low = layer_norm(values[w].astype(F32), gain[...]).astype(BF)
+            scratch[w * rows : (w + 1) * rows, :] = low
+            normed[w * rows : (w + 1) * rows, :] = low
+
+    low = scratch[...]
+    content = ((dot(low, w_query[...]) + content_bias[0]) * (KD**-0.5)).astype(BF).T
+    keys = dot(low, w_key[...]).astype(BF).T
+    mixable = dot(low, w_value[...]).astype(BF).T
+    for h in range(2):
+        for w in range(windows):
+            span = slice(w * rows, (w + 1) * rows)
+            sent[w, h, :KD, :] = content[h * KD : (h + 1) * KD, span]
+            sent[w, h, KD : 2 * KD, :] = keys[h * KD : (h + 1) * KD, span]
+            sent[w, h, 2 * KD :, :] = mixable[h * VD : (h + 1) * VD, span]
+
+
+def project(values, gain, content_bias, weight_keys, weight_values):
+    windows, rows, width = values.shape
+    steps = H // 2
+    return pl.pallas_call(
+        project_kernel,
+        grid=(steps,),
+        out_shape=(
+            jax.ShapeDtypeStruct((windows * rows, width), BF),
+            jax.ShapeDtypeStruct((windows, H, 2 * KD + VD, rows), BF),
+        ),
+        in_specs=[
+            pl.BlockSpec((windows, rows, width), lambda i: (0, 0, 0)),
+            pl.BlockSpec((1, width), lambda i: (0, 0)),
+            pl.BlockSpec((1, 1, 2 * KD), lambda i: (i, 0, 0)),
+            pl.BlockSpec((width, 2 * KD), lambda i: (0, i)),
+            pl.BlockSpec((width, 2 * KD), lambda i: (0, i + steps)),
+            pl.BlockSpec((width, 2 * VD), lambda i: (0, i)),
+        ],
+        out_specs=(
+            pl.BlockSpec((windows * rows, width), lambda i: (0, 0)),
+            pl.BlockSpec((windows, 2, 2 * KD + VD, rows), lambda i: (0, i, 0, 0)),
+        ),
+        scratch_shapes=[pltpu.VMEM((windows * rows, width), BF)],
+        compiler_params=pltpu.CompilerParams(vmem_limit_bytes=48 * 2**20),
+        name="project",
+    )(
+        values,
+        gain.reshape(1, width),
+        content_bias.reshape(steps, 1, 2 * KD),
+        weight_keys,
+        weight_keys,
+        weight_values,
+    )
+
+
+def sums_kernel(plan, refs_spec, *refs):
+    groups, n_terms, mode, parts, n_small, made_here = plan
+    refs = list(refs)
+
+    def take(count):
+        out, refs[:count] = refs[:count], []
+        return out
+
+    terms = take(n_terms * (2 if made_here else 1))
+    head_in = take({None: 0, "in": 1, "out": 3}[mode])
+    small_in = take(1 if n_small else 0)
+    outs = take(n_terms)
+    head_out = take(1 if mode else 0)
+    small_out = take(1 if n_small else 0)
+    own, arrived, result, back, hop1, hop2, line = [], [], [], [], [], [], []
+    flat = [(side, unit) for group in groups for side in (0, 1) for unit in group[side]]
+    count = len(flat)
+    own = take(count)
+    arrived = take(count)
+    hop1 = take(count)
+    hop2 = take(count)
+    line = take(count)
+    result = take(count)
+    back = take(count)
+    if made_here:
+        slots = min(2, n_terms)
+        lefts, rights, turned = take(slots), take(slots), take(slots)
+        going, left_sem, right_sem = take(3)
+    load_sem, c_send, c_recv, s1, r1, s2, r2, s3, r3, s4, r4 = take(11)
+    dp, seq = lax.axis_index("dp"), lax.axis_index("seq")
+    ndp, nhi = own[0].shape[:2]
+    nseq = nhi * 4
+    hi, low = lax.div(seq, 4), lax.rem(seq, 4)
+    y, c = lax.div(low, 2), lax.rem(low, 2)
+
+    def place(dp_to, hi_to, y_to, c_to):
+        return (dp_to, hi_to * 4 + y_to * 2 + c_to)
+
+    hi_index = [lax.rem(hi + k, nhi) for k in range(1, nhi)]
+    dp_index = [lax.rem(dp + k, ndp) for k in range(1, ndp)]
+    hi_peers = [place(dp, h, y, c) for h in hi_index]
+    dp_peers = [place(d, hi, y, c) for d in dp_index]
+    y_peer, c_peer = place(dp, hi, 1 - y, c), place(dp, hi, y, 1 - c)
+    everyone = hi_peers + dp_peers + [y_peer, c_peer]
+    if mode:
+        head, part = lax.div(seq, parts), lax.rem(seq, parts)
+        head_of = [lax.rem(head + k, H) for k in range(1, H)]
+        head_peers = [(dp, h * parts + part) for h in head_of]
+        part_peers = [(dp, head * parts + slot_part(part, k, parts)) for k in range(1, parts)]
+        everyone = everyone + head_peers + part_peers
+
+    barrier = pltpu.get_barrier_semaphore()
+    for peer in everyone:
+        pl.semaphore_signal(barrier, inc=1, device_id=peer, device_id_type=MESH)
+    expected = len(everyone)
+    me = dp * nseq + seq
+    if n_small:
+
+        def other_device(k):
+            there = lax.rem(me + k, n_small)
+            return (lax.div(there, nseq), lax.rem(there, nseq))
+
+        @pl.loop(1, n_small)
+        def _(k):
+            pl.semaphore_signal(barrier, inc=1, device_id=other_device(k), device_id_type=MESH)
+
+        expected += n_small - 1
+    pl.semaphore_wait(barrier, expected)
+
+    def remote(source, target, ss, rs, peer):
+        return pltpu.make_async_remote_copy(
+            src_ref=source,
+            dst_ref=target,
+            send_sem=ss,
+            recv_sem=rs,
+            device_id=peer,
+            device_id_type=MESH,
         )
 
-    theirs = swap(pick(1 - bit), mask)
-    total = pick(bit).astype(jnp.float32) + theirs.astype(jnp.float32)
-    return total.astype(arrays[0].dtype), [m for m in left if m != mask]
-
-
-def chip_term(left, right):
-    half, core = right.shape[1] // 2, bit_of(1)
-    theirs = lax.dynamic_slice_in_dim(right, (1 - core) * half, half, 1)
-    mine = lax.dynamic_slice_in_dim(right, core * half, half, 1)
-    arrived = swap(transposed_times(left, theirs).astype(jnp.bfloat16), 1)
-    return (transposed_times(left, mine) + arrived.astype(jnp.float32)).astype(jnp.bfloat16)
-
-
-def mask_lists():
-    nseq, ndp = lax.axis_size("seq"), lax.axis_size("dp")
-    left, mask = [], nseq * ndp // 2
-    while mask > 1:
-        left.append(mask)
-        mask //= 2
-    across = [m for m in left if m >= nseq]
-    return left, across, [m for m in left if 2 < m < nseq]
-
-
-def plane_orders():
-    _, across, _ = mask_lists()
-    return (across + [2], [2] + across)
-
-
-def plane_start(terms, columns):
-    left, _, _ = mask_lists()
-    chips = 2 ** len(left)
-    pieces = []
-    for t in terms:
-        t = t.reshape((2,) * len(left) + (t.shape[0] // chips, t.shape[1]))
-        pieces += [t[..., k : k + columns] for k in range(0, t.shape[-1], columns)]
-    half = columns // 2
-    return [([p[..., :half] for p in pieces], left), ([p[..., half:] for p in pieces], left)]
-
-
-def plane_step(state, step, last):
-    out = []
-    for (arrays, left), order in zip(state, plane_orders(), strict=True):
-        hops = order[step:] if last else order[step : step + 1]
-        for mask in hops:
-            total, left = halve(arrays, left, mask)
-            arrays = [total]
-        out.append((arrays, left))
-    return out
-
-
-def line_sum(state):
-    arrays = [pieces[0] for pieces, _ in state]
-    whole_line = jnp.concatenate(arrays, axis=-1)
-    _, _, line = mask_lists()
-    count = 2 ** len(line)
-    blocks = whole_line.reshape((count,) + whole_line.shape[len(line) :])
-    here = lax.div(lax.axis_index("seq"), 4)
-    total = lax.dynamic_index_in_dim(blocks, here, 0, keepdims=False).astype(jnp.float32)
-    for k in range(1, count):
-        there = here ^ k
-        arrived = swap(lax.dynamic_index_in_dim(blocks, there, 0, keepdims=False), 4 * k)
-        total = total + arrived.astype(jnp.float32)
-    return total
-
-
-def to_owner(total, rows):
-    core = bit_of(1)
+    def half_of(array):
+        return outs[array].shape[1] // 2
+
+    def columns_of(unit, core):
+        array, row, rows, column, columns = unit
+        half = half_of(array)
+        spot = pl.multiple_of(core * half + column, 128)
+        return terms[array].at[:, :, :, :, pl.ds(row, rows), pl.ds(spot, columns)]
+
+    def load(n):
+        return pltpu.make_async_copy(columns_of(flat[n][1], c), own[n], load_sem.at[n])
+
+    def over_core(n):
+        source = going_of(n) if made_here else columns_of(flat[n][1], 1 - c)
+        return [remote(source, arrived[n], c_send.at[n], c_recv.at[n], c_peer)]
+
+    def first_hop(n):
+        if flat[n][0] == 0:
+            return [
+                remote(own[n].at[d], hop1[n].at[k], s1.at[n, k], r1.at[n, k], p)
+                for k, (d, p) in enumerate(zip(dp_index, dp_peers, strict=True))
+            ]
+        return [remote(own[n].at[:, :, 1 - y], hop1[n], s1.at[n, 0], r1.at[n, 0], y_peer)]
+
+    def second_hop(n):
+        if flat[n][0] == 0:
+            return [remote(own[n].at[dp, :, 1 - y], hop2[n], s2.at[n, 0], r2.at[n, 0], y_peer)]
+        return [
+            remote(own[n].at[d, :, y], hop2[n].at[k], s2.at[n, k], r2.at[n, k], p)
+            for k, (d, p) in enumerate(zip(dp_index, dp_peers, strict=True))
+        ]
+
+    def along_line(n):
+        return [
+            remote(own[n].at[dp, h, y], line[n].at[k], s3.at[n, k], r3.at[n, k], p)
+            for k, (h, p) in enumerate(zip(hi_index, hi_peers, strict=True))
+        ]
+
+    def back_home(n):
+        return [remote(result[n].at[1 - c], back[n], s4.at[n], r4.at[n], c_peer)]
+
+    hops = (over_core, first_hop, second_hop, along_line, back_home)
+
+    def add(a, b):
+        return (a.astype(F32) + b.astype(F32)).astype(BF)
+
+    def absorb(n, stage):
+        mine = own[n]
+        if stage == 1:
+
+            @pl.loop(0, ndp * nhi)
+            def _(k):
+                d, h = lax.div(k, nhi), lax.rem(k, nhi)
+                mine[d, h] = add(mine[d, h], arrived[n][d, h])
+
+        elif stage == 2 and flat[n][0] == 0:
+
+            @pl.loop(0, nhi)
+            def _(h):
+                total = mine[dp, h].astype(F32)
+                for k in range(ndp - 1):
+                    total = total + hop1[n][k, h].astype(F32)
+                mine[dp, h] = total.astype(BF)
+
+        elif stage == 2:
+
+            @pl.loop(0, ndp * nhi)
+            def _(k):
+                d, h = lax.div(k, nhi), lax.rem(k, nhi)
+                mine[d, h, y] = add(mine[d, h, y], hop1[n][d, h])
+
+        elif stage == 3 and flat[n][0] == 0:
+
+            @pl.loop(0, nhi)
+            def _(h):
+                mine[dp, h, y] = add(mine[dp, h, y], hop2[n][h])
+
+        elif stage == 3:
+
+            @pl.loop(0, nhi)
+            def _(h):
+                total = mine[dp, h, y].astype(F32)
+                for k in range(ndp - 1):
+                    total = total + hop2[n][k, h].astype(F32)
+                mine[dp, h, y] = total.astype(BF)
+
+        elif stage == 4:
+            total = mine[dp, hi, y].astype(F32)
+            for k in range(nhi - 1):
+                total = total + line[n][k].astype(F32)
+            result[n][...] = total
+        else:
+            array, row, rows, column, columns = flat[n][1]
+            half = half_of(array)
+            here, there = result[n][c], back[n][...]
+            outs[array][row : row + rows, column : column + columns] = jnp.where(
+                c == 0, here, there
+            )
+            outs[array][row : row + rows, half + column : half + column + columns] = jnp.where(
+                c == 0, there, here
+            )
+
+    numbers, serial = [], 0
+    for group in groups:
+        size = len(group[0]) + len(group[1])
+        numbers.append(range(serial, serial + size))
+        serial += size
+
+    def going_of(n):
+        step = next(k for k, some in enumerate(numbers) if n in some)
+        unit = flat[n][1]
+        side = numbers[step].index(n)
+        return going.at[step % 2, side, :, :, :, :, pl.ds(0, unit[2]), pl.ds(0, unit[4])]
+
+    def fetch(array):
+        left, right = terms[2 * array], terms[2 * array + 1]
+        tokens, slot = left.shape[0], array % 2
+        return [
+            pltpu.make_async_copy(
+                left,
+                lefts[slot].at[pl.ds(0, tokens), pl.ds(0, left.shape[1])],
+                left_sem.at[array],
+            ),
+            pltpu.make_async_copy(
+                right,
+                rights[slot].at[pl.ds(0, tokens), pl.ds(0, right.shape[1])],
+                right_sem.at[array],
+            ),
+        ]
+
+    def make(step):
+        units = [flat[n][1] for n in numbers[step]]
+        array, rows = units[0][0], units[0][2]
+        first, size = units[0][3], sum(u[4] for u in units)
+        left = terms[2 * array]
+        tokens, slot = left.shape[0], array % 2
+        if step == 0 or flat[numbers[step - 1][0]][1][0] != array:
+            for copy in fetch(array):
+                copy.wait()
+            if array >= 1 and array + 1 < n_terms:
+                for copy in fetch(array + 1):
+                    copy.start()
+
+            @pl.loop(0, left.shape[1] // 256)
+            def _(k):
+                spot = pl.multiple_of(k * 256, 256)
+                turned[slot][pl.ds(spot, 256), pl.ds(0, tokens)] = lefts[slot][
+                    pl.ds(0, tokens), pl.ds(spot, 256)
+                ].T
+
+        if step >= 2:
+            for n in numbers[step - 2]:
+                for copy in over_core(n):
+                    copy.wait_send()
+        span = nhi * 4 * rows
+        for whose in (1 - c, c):
+            spot = pl.multiple_of(whose * half_of(array) + first, 128)
+            part_right = rights[slot][pl.ds(0, tokens), pl.ds(spot, size)]
+            for d in range(ndp):
+                made = dot(turned[slot][pl.ds(d * span, span), pl.ds(0, tokens)], part_right)
+                made = made.astype(BF).reshape(nhi, 2, 2, rows, size)
+                at = 0
+                for k, n in enumerate(numbers[step]):
+                    piece = made[..., at : at + units[k][4]]
+                    if whose is c:
+                        own[n][d] = piece
+                    else:
+                        going[step % 2, k, d, :, :, :, pl.ds(0, rows), pl.ds(0, units[k][4])] = piece
+                    at += units[k][4]
+            if whose is not c:
+                for n in numbers[step]:
+                    for copy in over_core(n):
+                        copy.start()
+
+    def launch(step):
+        if made_here:
+            make(step)
+        else:
+            for n in numbers[step]:
+                load(n).start()
+                for copy in over_core(n):
+                    copy.start()
+
+    if made_here:
+        for array in range(min(2, n_terms)):
+            for copy in fetch(array):
+                copy.start()
+
+    if mode == "in":
+        head_send, head_recv, head_local = take(3)
+        blocks, gathered = head_in[0], head_out[0]
+        head_copies = [
+            remote(blocks.at[:, h], gathered.at[head], head_send.at[k], head_recv.at[k], p)
+            for k, (h, p) in enumerate(zip(head_of, head_peers, strict=True))
+        ]
+        head_own = [
+            pltpu.make_async_copy(blocks.at[:, head], gathered.at[head], head_local.at[0])
+        ]
+        for copy in head_copies + head_own:
+            copy.start()
+    if mode == "out":
+        head_send, head_recv, head_local, part_send, part_recv, mine_kv, arrived_kv = take(7)
+        query, pair_mine, pair_other = head_in
+        gathered = head_out[0]
+        part_copies = [
+            remote(pair_other.at[k], arrived_kv.at[k], part_send.at[k], part_recv.at[k], p)
+            for k, p in enumerate(part_peers)
+        ]
+        kv_load = pltpu.make_async_copy(pair_mine, mine_kv, head_local.at[0])
+        for copy in part_copies + [kv_load]:
+            copy.start()
+    if n_small:
+        small_send, small_recv, small_sc = take(3)
+        small = small_in[0]
+
+        def small_copy(k):
+            there = lax.rem(me + k, n_small)
+            return remote(
+                small.at[there],
+                small_sc.at[k - 1],
+                small_send.at[k - 1],
+                small_recv.at[k - 1],
+                other_device(k),
+            )
+
+        @pl.loop(1, n_small)
+        def _(k):
+            small_copy(k).start()
+
+    ahead = 3
+    for step in range(min(ahead, len(groups))):
+        launch(step)
+    if mode == "out":
+        for copy in part_copies:
+            copy.wait_recv()
+        kv_load.wait()
+
+        @pl.loop(0, H)
+        def _(g):
+            total = mine_kv[g].astype(F32)
+            for k in range(parts - 1):
+                total = total + arrived_kv[k, g].astype(F32)
+            mine_kv[g] = total.astype(BF)
+
+        q_target = gathered.at[head, :, pl.ds(0, KD)]
+        kv_target = gathered.at[head, :, pl.ds(KD, KD + VD)]
+        head_copies = [
+            remote(source.at[h], target, head_send.at[i, k], head_recv.at[i, k], p)
+            for k, (h, p) in enumerate(zip(head_of, head_peers, strict=True))
+            for i, (source, target) in enumerate(((query, q_target), (mine_kv, kv_target)))
+        ]
+        head_own = [
+            pltpu.make_async_copy(query.at[head], q_target, head_local.at[1]),
+            pltpu.make_async_copy(mine_kv.at[head], kv_target, head_local.at[2]),
+        ]
+        for copy in head_copies + head_own:
+            copy.start()
+    lag = 2
+    for step in range(len(groups) + 4 * lag):
+        for stage in (5, 4, 3, 2, 1):
+            spot = step - lag * (stage - 1)
+            if 0 <= spot < len(groups):
+                for n in numbers[spot]:
+                    if stage == 1 and not made_here:
+                        load(n).wait()
+                    for copy in hops[stage - 1](n):
+                        copy.wait_recv()
+                    absorb(n, stage)
+                    if stage < 5:
+                        for copy in hops[stage](n):
+                            copy.start()
+        if step + ahead < len(groups):
+            launch(step + ahead)
+    if n_small:
+
+        @pl.loop(1, n_small)
+        def _(k):
+            small_copy(k).wait_recv()
+
+        small_out[0][...] = small[me] + jnp.sum(small_sc[...], axis=0)
+
+        @pl.loop(1, n_small)
+        def _(k):
+            small_copy(k).wait_send()
+
+    if mode:
+        for copy in head_own:
+            copy.wait()
+        for copy in head_copies:
+            copy.wait_recv()
+        for copy in head_copies:
+            copy.wait_send()
+    if mode == "out":
+        for copy in part_copies:
+            copy.wait_send()
+    for n in range(count):
+        for hop in hops:
+            if hop is not over_core or not made_here or n in tuple(numbers[-1]) + tuple(numbers[-2]):
+                for copy in hop(n):
+                    copy.wait_send()
+
+
+def sum_terms(name, collective, pairs, groups, mode=None, heads=(), small=None):
+    ndp, nseq = lax.axis_size("dp"), lax.axis_size("seq")
+    nhi, parts, devices = nseq // 4, nseq // H, ndp * nseq
+    shares = [(left.shape[1] // devices, right.shape[1]) for left, right in pairs]
+    made_here = all(rows % 16 == 0 for rows, _ in shares)
+    if made_here:
+        operands = [x for pair in pairs for x in pair]
+    else:
+        operands = [
+            transposed_times(left, right).astype(BF).reshape((ndp, nhi, 2, 2) + share)
+            for (left, right), share in zip(pairs, shares, strict=True)
+        ]
+    in_specs = [pl.BlockSpec(memory_space=pl.ANY)] * len(operands)
+    out_shape = [jax.ShapeDtypeStruct(share, F32) for share in shares]
+    out_specs = [pl.BlockSpec(memory_space=pltpu.VMEM)] * len(out_shape)
+    flat = [(side, unit) for group in groups for side in (0, 1) for unit in group[side]]
+    count = len(flat)
+    shapes = [(unit[2], unit[4]) for _, unit in flat]
+    sides = [side for side, _ in flat]
+    scratch = [pltpu.VMEM((ndp, nhi, 2, 2) + s, BF) for s in shapes] * 2
+    scratch += [
+        pltpu.VMEM(((ndp, nhi, 2) if side else (ndp - 1, nhi, 2, 2)) + s, BF)
+        if not side
+        else pltpu.VMEM((ndp, nhi, 2) + s, BF)
+        for side, s in zip(sides, shapes, strict=True)
+    ]
+    scratch += [
+        pltpu.VMEM((ndp - 1, nhi, 2) + s if side else (nhi, 2) + s, BF)
+        for side, s in zip(sides, shapes, strict=True)
+    ]
+    scratch += [pltpu.VMEM((nhi - 1, 2) + s, BF) for s in shapes]
+    scratch += [pltpu.VMEM((2,) + s, F32) for s in shapes]
+    scratch += [pltpu.VMEM(s, F32) for s in shapes]
+    if made_here:
+        slots = [pairs[k::2] for k in range(min(2, len(pairs)))]
+        tokens = [max(left.shape[0] for left, _ in slot) for slot in slots]
+        tall = [max(left.shape[1] for left, _ in slot) for slot in slots]
+        wide = [max(right.shape[1] for _, right in slot) for slot in slots]
+        unit_rows = max(rows for rows, _ in shapes)
+        unit_columns = max(columns for _, columns in shapes)
+        scratch += [
+            *[pltpu.VMEM(s, BF) for s in zip(tokens, tall, strict=True)],
+            *[pltpu.VMEM(s, BF) for s in zip(tokens, wide, strict=True)],
+            *[pltpu.VMEM(s, BF) for s in zip(tall, tokens, strict=True)],
+            pltpu.VMEM((2, 2, ndp, nhi, 2, 2, unit_rows, unit_columns), BF),
+            pltpu.SemaphoreType.DMA((len(pairs),)),
+            pltpu.SemaphoreType.DMA((len(pairs),)),
+        ]
+    hop = max(ndp - 1, 1)
+    sizes = [(count,)] * 3 + [(count, hop)] * 4 + [(count, nhi - 1)] * 2 + [(count,)] * 2
+    scratch += [pltpu.SemaphoreType.DMA(size) for size in sizes]
+    if mode == "in":
+        windows, _, size, rows = heads[0].shape
+        operands.append(heads[0])
+        in_specs.append(pl.BlockSpec(memory_space=pl.ANY))
+        out_shape.append(jax.ShapeDtypeStruct((H, windows, size, rows), BF))
+        out_specs.append(pl.BlockSpec(memory_space=pl.ANY))
+        scratch += [pltpu.SemaphoreType.DMA((n,)) for n in (H - 1, H - 1, 1)]
+    if mode == "out":
+        _, windows, _, rows = heads[0].shape
+        operands += list(heads)
+        in_specs += [pl.BlockSpec(memory_space=pl.ANY)] * 3
+        out_shape.append(jax.ShapeDtypeStruct((H, windows, 2 * KD + VD, rows), BF))
+        out_specs.append(pl.BlockSpec(memory_space=pl.ANY))
+        scratch += [
+            pltpu.SemaphoreType.DMA(size)
+            for size in ((2, H - 1), (2, H - 1), (3,), (parts - 1,), (parts - 1,))
+        ]
+        scratch += [pltpu.VMEM(heads[1].shape, BF), pltpu.VMEM(heads[2].shape, BF)]
+    n_small = 0
+    if small is not None:
+        n_small = devices
+        operands.append(small)
+        in_specs.append(pl.BlockSpec(memory_space=pltpu.VMEM))
+        out_shape.append(jax.ShapeDtypeStruct(small.shape[1:], F32))
+        out_specs.append(pl.BlockSpec(memory_space=pltpu.VMEM))
+        scratch += [
+            pltpu.SemaphoreType.DMA((devices - 1,)),
+            pltpu.SemaphoreType.DMA((devices - 1,)),
+            pltpu.VMEM((devices - 1,) + small.shape[1:], F32),
+        ]
+    plan = (groups, len(pairs), mode, parts, n_small, made_here)
+    return pl.pallas_call(
+        functools.partial(sums_kernel, plan, None),
+        out_shape=out_shape,
+        in_specs=in_specs,
+        out_specs=out_specs,
+        scratch_shapes=scratch,
+        compiler_params=pltpu.CompilerParams(
+            collective_id=collective, has_side_effects=True, vmem_limit_bytes=60 * 2**20
+        ),
+        name=name,
+    )(*operands)
+
+
+def halves(array, rows, columns, size=128):
     out, spot = [], 0
-    for r in rows:
-        piece = total[spot : spot + 2 * r]
-        spot += 2 * r
-        out.append(piece.reshape(2, r, piece.shape[1]))
-    mine = [lax.dynamic_index_in_dim(p, core, 0, keepdims=False) for p in out]
-    theirs = jnp.concatenate(
-        [lax.dynamic_index_in_dim(p, 1 - core, 0, keepdims=False) for p in out], axis=0
-    )
-    arrived = swap(theirs, 1)
-    done, spot = [], 0
-    for r, m in zip(rows, mine, strict=True):
-        a = arrived[spot : spot + r]
-        spot += r
-        done.append((jnp.where(core == 0, m, a), jnp.where(core == 0, a, m)))
-    return done
-
-
-def scatter_small(pieces):
-    devices = lax.axis_size("dp") * lax.axis_size("seq")
-    packed = jnp.concatenate([p.reshape(devices, -1) for p in pieces], axis=1)
-    count = packed.shape[1]
-    total = jnp.pad(packed, ((0, 0), (0, -count % 1024))).reshape(devices, -1, 128)
-    left, _, _ = mask_lists()
-    left = left + [1]
-    total = total.reshape((2,) * len(left) + total.shape[1:])
-    for mask in left[::-1]:
-        total, left = halve([total], left, mask)
-    total = total.reshape(-1)
-    out, spot = [], 0
-    for p in pieces:
-        size = p.size // devices
-        out.append(total[spot : spot + size].reshape((p.shape[0] // devices,) + p.shape[1:]))
-        spot += size
-    return out
+    while spot < columns:
+        size = min(size, (columns - spot) // 2)
+        out.append((((array, 0, rows, spot, size),), ((array, 0, rows, spot + size, size),)))
+        spot += 2 * size
+    return tuple(out)
+
+
+def weight_pairs(width, hidden_width):
+    third = width // 3
+
+    def pieces(array, total, size):
+        return [(array, k, array, k, size) for k in range(0, total, size)]
+
+    first = pieces(0, width, third) + pieces(2, hidden_width, third) + pieces(4, width, third)
+    second = pieces(1, width, third) + pieces(3, width, third // 2) + pieces(5, width, third)
+    return tuple(((a,), (b,)) for a, b in zip(first, second, strict=True))
 
 
 def on_device(
@@ -749,7 +1227,6 @@
 ):
     windows, rows, width = inputs.shape
     scale = float(KD) ** (-0.5)
-    wide = 2 * KD + VD
     nseq, ndp = lax.axis_size("seq"), lax.axis_size("dp")
     devices = nseq * ndp
     parts = nseq // H
@@ -759,78 +1236,60 @@
     first = seq * rows
     hidden_width = inner_weight.shape[1]
 
-    shard_rows = query_weight.shape[0]
-    packed_shard = jnp.concatenate(
-        [
-            query_weight.reshape(shard_rows, H, KD),
-            key_weight.reshape(shard_rows, H, KD),
-            value_weight.reshape(shard_rows, H, VD),
-        ],
-        axis=2,
-    ).reshape(shard_rows, H * wide)
-    small_shards = (
+    r = shard_rows = query_weight.shape[0]
+    vectors = (
         first_gain,
         content_bias,
         position_bias,
-        relative_weight,
         second_gain,
         inner_bias,
         outer_bias,
         third_gain,
         skip_bias,
-        depth_weight,
-    )
-    small_shard = jnp.concatenate([s.reshape(-1) for s in small_shards])
-    small_count = small_shard.shape[0]
-    small_shard = jnp.pad(small_shard, (0, -small_count % 2048)).reshape(-1, 128)
-    half_wide, half_hidden, half_width = H * wide // 2, hidden_width // 2, width // 2
-    gathered = gather_weights(
-        [
-            small_shard,
-            packed_shard,
-            skip_weight,
-            mixing_weight,
-            inner_weight,
-            outer_weight,
-            upsample_weight,
-            point_weight,
-        ],
+    )
+    small_rows = [v.reshape(1, -1) for v in vectors] + [depth_weight.T]
+    small_rows = [jnp.pad(v, ((0, 0), (0, 128 - v.shape[1]))) for v in small_rows]
+    small_rows.append(jnp.zeros((16 - len(vectors) - 3, 128), BF))
+    relative_rows = relative_weight.shape[0]
+    small_rows.append(
+        jnp.pad(relative_weight, ((0, -relative_rows % 16), (0, 128 - relative_weight.shape[1])))
+    )
+    small_shard = jnp.concatenate(small_rows, axis=0)
+    keys_width, values_width = 2 * H * KD, H * VD
+    half_hidden, half_width = hidden_width // 2, width // 2
+    small_full, weight_keys, weight_values = use_links(
+        "gather_heads",
+        1,
+        [small_shard, query_weight, key_weight, value_weight],
+        [small_shard.shape, (r, keys_width), (r, values_width)],
         (
-            (((0, 0, 128), (1, 0, half_wide)), ((1, half_wide, half_wide),)),
-            (((2, 0, width),), ((3, 0, width),)),
-            (((4, 0, half_hidden),), ((5, 0, half_width),)),
-            (((4, half_hidden, half_hidden),), ((5, half_width, half_width),)),
-            (((6, 0, width),), ((7, 0, width),)),
+            (((0, 0, 0, 0, 128), (1, 0, 1, 0, 256)), ((2, 0, 1, 512, 256),)),
+            (((1, 256, 1, 256, 256),), ((2, 256, 1, 768, 256),)),
+            (((3, 0, 2, 0, 256),), ((3, 256, 2, 256, 256),)),
+            (((3, 512, 2, 512, 256),), ((3, 768, 2, 768, 256),)),
+            (((3, 1024, 2, 1024, 256),), ((3, 1280, 2, 1280, 256),)),
         ),
     )
-    small_full = gathered[0].reshape(devices, -1)
-    (
-        weight_packed,
-        weight_skip,
-        weight_mixing,
-        weight_inner,
-        weight_outer,
-        weight_upsample,
-        weight_point,
-    ) = (g.reshape(-1, g.shape[-1]) for g in gathered[1:])
-    small, spot = [], 0
-    for s in small_shards:
-        small.append(
-            small_full[:, spot : spot + s.size].reshape((devices * s.shape[0],) + s.shape[1:])
-        )
-        spot += s.size
+    small_full = small_full.reshape((devices,) + small_shard.shape).astype(jnp.float32)
+
+    def vector(k):
+        return small_full[:, k, : vectors[k].shape[0]].reshape(-1)
+
     (
         gain_first,
         bias_content,
         bias_position,
-        weight_relative,
         gain_second,
         bias_inner,
         bias_outer,
         gain_third,
         bias_skip,
-        weight_depth,
-    ) = (s.astype(jnp.float32) for s in small)
+    ) = map(vector, range(len(vectors)))
+    taken = len(vectors)
+    weight_depth = (
+        small_full[:, taken : taken + 3, :r].transpose(0, 2, 1).reshape(width, 3)
+    )
+    weight_relative = small_full[:, 16 : 16 + relative_rows, :RPF].reshape(H * KD, RPF)
 
     lives = jnp.exp(
         jnp.linspace(math.log(3.0), math.log(keys_total), RPF // 2, dtype=jnp.float32)
@@ -851,31 +1310,37 @@
         return lax.ppermute(array, "seq", [(i, i ^ slot) for i in range(nseq)])
 
     flat = inputs.reshape(windows * rows, width).astype(jnp.float32)
-    normed, first_norm_back = jax.vjp(layer_norm, flat, gain_first)
-    normed_low = normed.astype(jnp.bfloat16)
-    per_head = jnp.concatenate(
-        [bias_content.reshape(H, KD), jnp.zeros((H, KD + VD), jnp.float32)], axis=1
-    ).reshape(H * wide)
-    per_scale = jnp.tile(
-        jnp.concatenate(
-            [jnp.full((KD,), scale, jnp.float32), jnp.ones((KD + VD,), jnp.float32)]
-        ),
-        H,
-    )
-
-    def by_head(array, size):
-        (array,) = tie(array)
-        (array,) = tie(array.reshape(windows, rows, H, size).transpose(2, 0, 3, 1))
-        return array
+    _, first_norm_back = jax.vjp(layer_norm, flat, gain_first)
+    normed_low, sent = project(inputs, gain_first, bias_content, weight_keys, weight_values)
+    (
+        weight_skip,
+        weight_mixing,
+        weight_inner,
+        weight_outer,
+        weight_upsample,
+        weight_point,
+        mine,
+        other,
+    ) = use_links(
+        "gather_weights",
+        2,
+        [skip_weight, mixing_weight, inner_weight, outer_weight, upsample_weight, point_weight],
+        [
+            (r, width),
+            (r, width),
+            (r, hidden_width),
+            (outer_weight.shape[0], width),
+            (r, width),
+            (r, width),
+        ],
+        weight_pairs(width, hidden_width),
+        sent,
+    )
 
     def by_row(array):
         (array,) = tie(array.transpose(1, 3, 0, 2).reshape(windows * rows, -1))
         return array
 
-    made = (matmul(normed_low, weight_packed) + per_head) * per_scale
-    sent = by_head(made.astype(jnp.bfloat16), wide)
-    mine = exchange(sent)
-    other = jnp.stack([swap_part(mine[:, :, KD:, :], slot) for slot in range(1, parts)])
     mixed_own, mixed_wide, log_total = attention_forward(
         info, rates, bias_gap, relative, mine, other, parts
     )
@@ -923,7 +1388,6 @@
     out_grad = (cotangent * keep.astype(jnp.bfloat16)[:, :, None]).reshape(
         windows * 2 * rows, width
     )
-    term_point = chip_term(conv_flat, out_grad)
     conv_grad = (
         times_transposed(out_grad, weight_point)
         .astype(jnp.bfloat16)
@@ -947,105 +1411,106 @@
     grad_skip_bias = jnp.sum(joined_grad, axis=(0, 1))
     joined_back = joined_grad.astype(jnp.bfloat16)
     joined_flat = joined_back.reshape(windows * 2 * rows, width)
-    term_skip = chip_term(skip_flat, joined_flat)
+    lifted_grad = (
+        jnp.einsum("ts,wtd->wsd", twice, joined_back, preferred_element_type=jnp.float32)
+        .astype(jnp.bfloat16)
+        .reshape(windows * rows, width)
+    )
+    third_grad = times_transposed(lifted_grad, weight_upsample)
     skip_grad = (
         times_transposed(joined_flat, weight_skip)
         .astype(jnp.bfloat16)
         .reshape(windows, 2 * rows, width)
     )
-    lifted_grad = (
-        jnp.einsum("ts,wtd->wsd", twice, joined_back, preferred_element_type=jnp.float32)
-        .astype(jnp.bfloat16)
-        .reshape(windows * rows, width)
-    )
-    third_grad = times_transposed(lifted_grad, weight_upsample)
-    last = [False, True]
-    term_point, term_skip, lifted_grad, third_grad, skip_grad, outputs = tie(
-        term_point, term_skip, lifted_grad, third_grad, skip_grad, outputs
-    )
-
-    sum_a = plane_step(plane_start([term_point, term_skip], half_width), 0, last[0])
     block_grad, grad_third = third_back(third_grad)
     block_low = block_grad.astype(jnp.bfloat16)
-    term_upsample = chip_term(third_low, lifted_grad)
-    term_outer = chip_term(hidden_low, block_low)
     grad_outer_bias = jnp.sum(block_grad, axis=0)
     (before_grad,) = gelu_back(times_transposed(block_low, weight_outer))
     before_low = before_grad.astype(jnp.bfloat16)
-    sum_a, term_upsample, term_outer, before_low, block_grad = tie_tree(
-        (sum_a, term_upsample, term_outer, before_low, block_grad)
-    )
-
-    sum_a = plane_step(sum_a, 1, last[1])
-    sum_b = plane_step(plane_start([term_upsample, term_outer], half_width), 0, last[0])
     grad_inner_bias = jnp.sum(before_low.astype(jnp.float32), axis=0)
     middle_part, grad_second = second_norm_back(times_transposed(before_low, weight_inner))
     middle_grad = block_grad + middle_part
     middle_low = middle_grad.astype(jnp.bfloat16)
-    mixed_grad = by_head(times_transposed(middle_low, weight_mixing).astype(jnp.bfloat16), VD)
-    term_inner = chip_term(second_low, before_low)
-    sum_a, sum_b, term_inner, mixed_grad, middle_low, middle_grad = tie_tree(
-        (sum_a, sum_b, term_inner, mixed_grad, middle_low, middle_grad)
-    )
-
-    arrived_grad = exchange(mixed_grad)
-    sum_b = plane_step(sum_b, 1, last[1])
-    term_mixing = chip_term(mixed_low, middle_low)
-    sum_b, term_mixing, arrived_grad = tie_tree((sum_b, term_mixing, arrived_grad))
-
-    line_a, line_b = line_sum(sum_a), line_sum(sum_b)
-    sum_c = plane_step(plane_start([term_inner, term_mixing], half_width), 0, last[0])
+    middle_rows = middle_low.reshape(windows, rows, width)
+    mixed_grad = (
+        jnp.einsum("vd,wrd->wvr", weight_mixing, middle_rows, preferred_element_type=jnp.float32)
+        .astype(jnp.bfloat16)
+        .reshape(windows, H, VD, rows)
+    )
+    own_point, own_outer, own_skip, own_upsample, arrived_grad = sum_terms(
+        "sum_upper",
+        3,
+        [
+            (conv_flat, out_grad),
+            (hidden_low, block_low),
+            (skip_flat, joined_flat),
+            (third_low, lifted_grad),
+        ],
+        halves(0, r, half_width)
+        + halves(1, outer_weight.shape[0], half_width)
+        + halves(2, r, half_width)
+        + halves(3, r, half_width),
+        "in",
+        (mixed_grad,),
+    )
     query_own, own_side, other_side, bias_sums, relative_sum = attention_backward(
         info, rates, bias_gap, relative, mine, other, arrived_grad, mixed_wide, log_total, parts
     )
-    line_a, line_b, sum_c, query_own, own_side, other_side = tie_tree(
-        (line_a, line_b, sum_c, query_own, own_side, other_side)
-    )
-
-    own_side = own_side.astype(jnp.float32)
-    for slot in range(1, parts):
-        own_side = own_side + swap_part(other_side[slot - 1], slot).astype(jnp.float32)
-    heads_grad = exchange(
-        jnp.concatenate([query_own, own_side.astype(jnp.bfloat16)], axis=2)
-    )
-    sum_c = plane_step(sum_c, 1, last[1])
-    r = shard_rows
-    own_point, own_skip = to_owner(line_a, [r, r])
-    own_upsample, own_outer = to_owner(line_b, [r, outer_weight.shape[0]])
-    sum_c, heads_grad = tie_tree((sum_c, heads_grad))
-
-    line_c = line_sum(sum_c)
-    packed_grad = by_row(heads_grad)
-    term_packed = chip_term(normed_low, packed_grad)
-    normed_grad = times_transposed(packed_grad, weight_packed)
+    own_inner, own_mixing, heads_grad = sum_terms(
+        "sum_lower",
+        4,
+        [(second_low, before_low), (mixed_low, middle_low)],
+        halves(0, r, half_hidden) + halves(1, r, half_width),
+        "out",
+        (query_own, own_side, other_side),
+    )
+    packed_grad = jnp.concatenate(
+        [
+            by_row(heads_grad[:, :, :KD]),
+            by_row(heads_grad[:, :, KD : 2 * KD]),
+            by_row(heads_grad[:, :, 2 * KD :]),
+        ],
+        axis=1,
+    )
+    (packed_grad,) = tie(packed_grad)
+    normed_grad = times_transposed(packed_grad[:, :keys_width], weight_keys) + times_transposed(
+        packed_grad[:, keys_width:], weight_values
+    )
     input_part, grad_first = first_norm_back(normed_grad)
     input_grad = (middle_grad + input_part).astype(jnp.bfloat16).reshape(windows, rows, width)
-    sum_d = plane_start([term_packed], half_wide)
-    sum_d = plane_step(plane_step(sum_d, 0, False), 1, True)
-    own_inner_low, own_inner_high, own_mixing = to_owner(line_c, [r, r, r])
-    (own_packed,) = to_owner(line_sum(sum_d), [r])
-
-    def joined_columns(pair):
-        return jnp.concatenate(pair, axis=1)
 
     def at_head(value):
         full = jnp.zeros((H,) + value.shape, jnp.float32)
         return lax.dynamic_update_index_in_dim(full, value, head, 0)
 
-    small_grads = scatter_small(
-        [
-            grad_first,
-            at_head(bias_sums[0, :, 0]).reshape(-1),
-            at_head(bias_sums[1, :, 0]).reshape(-1),
-            at_head(relative_sum).reshape(H * KD, RPF),
-            grad_second,
-            grad_inner_bias,
-            grad_outer_bias,
-            grad_third,
-            grad_skip_bias,
-            grad_depth,
-        ]
-    )
+    pieces = [
+        grad_first,
+        at_head(bias_sums[0, :, 0]).reshape(-1),
+        at_head(bias_sums[1, :, 0]).reshape(-1),
+        at_head(relative_sum).reshape(H * KD, RPF),
+        grad_second,
+        grad_inner_bias,
+        grad_outer_bias,
+        grad_third,
+        grad_skip_bias,
+        grad_depth,
+    ]
+    packed = jnp.concatenate([p.reshape(devices, -1) for p in pieces], axis=1)
+    packed = jnp.pad(packed, ((0, 0), (0, -packed.shape[1] % 1024))).reshape(devices, -1, 128)
+    own_heads, small_total = sum_terms(
+        "sum_heads",
+        5,
+        [(normed_low, packed_grad)],
+        halves(0, r, packed_grad.shape[1] // 2),
+        small=packed,
+    )
+    small_total, spot, small_grads = small_total.reshape(-1), 0, []
+    for p in pieces:
+        size = p.size // devices
+        small_grads.append(
+            small_total[spot : spot + size].reshape((p.shape[0] // devices,) + p.shape[1:])
+        )
+        spot += size
     (
         own_first,
         own_content,
@@ -1058,21 +1523,14 @@
         own_skip_bias,
         own_depth,
     ) = small_grads
-    own_heads = joined_columns(own_packed).reshape(r, H, wide)
-    own_point, own_skip, own_upsample, own_outer, own_mixing = map(
-        joined_columns, (own_point, own_skip, own_upsample, own_outer, own_mixing)
-    )
-    own_inner = jnp.concatenate(
-        [own_inner_low[0], own_inner_high[0], own_inner_low[1], own_inner_high[1]], axis=1
-    )
     return (
         outputs,
         input_grad,
         skip_grad,
         own_first,
-        own_heads[:, :, :KD].reshape(r, H * KD),
-        own_heads[:, :, KD : 2 * KD].reshape(r, H * KD),
-        own_heads[:, :, 2 * KD :].reshape(r, H * VD),
+        own_heads[:, : H * KD],
+        own_heads[:, H * KD : keys_width],
+        own_heads[:, keys_width:],
         own_content,
         own_position,
         own_relative,

time: 1090 us -> 985 us (0.904); the launches traced: 1070 us -> 977 us
  Pallas kernels: 349 us -> 725 us
  waiting for transfers between devices: 165 us -> 0.01 us
  starting transfers between devices: 104 us -> 35.5 us
  other arithmetic: 96 us -> 32.5 us
  blocking collectives: 62.8 us -> 0 us
  matrix products: 175 us -> 119 us
  local copies, waits for them, and re-layouts: 112 us -> 62.8 us
    pallas_call x1 -> x6, Pallas kernels: 247 us -> 618 us  [the longest x3 324 us: sum_terms(): pl.pallas_call(functools.partial(sums_kernel, plan, None), out_shape=out_...]
    ppermute x46 -> x0, waiting for transfers between devices: 146 us -> none  [the longest x44 143 us: swap(): lax.ppermute(array, ('dp', 'seq'), [(i, i ^ mask) for i in range(devices)])]
    ppermute x46 -> x0, starting transfers between devices: 75.4 us -> none  [the longest x44 69.9 us: swap(): lax.ppermute(array, ('dp', 'seq'), [(i, i ^ mask) for i in range(devices)])]
    all_to_all x1 -> x0, blocking collectives: 62.8 us -> none  [exchange(): lax.all_to_all(array, 'seq', 0, 0, axis_index_groups=groups, tiled=True)]
    dot_general x14 -> x1, matrix products: 60.9 us -> 3.77 us  [on_device(): jnp.einsum('vd,wrd->wvr', weight_mixing, middle_rows, preferred_element_t...]
    convert_element_type x25 -> x2, other arithmetic: 41.4 us -> 6.51 us  [the longest x1 5.51 us: on_device(): (middle_grad + input_part).astype(jnp.bfloat16)]
    reshape x24 -> x10, local copies, waits for them, and re-layouts: 34.9 us -> 2.26 us  [the longest x7 1.38 us: on_device(): packed = jnp.concatenate([p.reshape(devices, -1) for p in pieces], axis=1)]
    squeeze x40 -> x0, local copies, waits for them, and re-layouts: 20.2 us -> none  [the longest x28 17.3 us: pick(): lax.dynamic_index_in_dim(a, which, spot, keepdims=False)]
  transfers between devices with their start and end apart: 53 -> 5, of which waited for: 23 -> 0; matrix products, arithmetic and copies ran while one was open for 24% -> 7% of each run, Pallas kernels for 5% -> 0%
where the time goes in v2:
time: 985 us; the launch traced here: 977 us
  Pallas kernels  725 us (74%)
  matrix products  119 us (12%)
  local copies, waits for them, and re-layouts  62.8 us (6%)
  starting transfers between devices  35.5 us (4%)
  other arithmetic  32.5 us (3%)
    pallas_call x3, Pallas kernels, sum_terms(): pl.pallas_call(functools.partial(sums_kernel, plan, None), out_shape=out_...  324 us
    pallas_call x2, Pallas kernels, use_links(): pl.pallas_call(functools.partial(links_kernel, pairs, (len(shards), len(a...  284 us
    pallas_call x1, Pallas kernels, attention_backward(): pl.pallas_call(functools.partial(backward_kernel, parts, per), grid=(wind...  57.6 us
    dot_general x6, matrix products, matmul(): return jnp.dot(left, right, preferred_element_type=jnp.float32)  55.1 us
    dot_general x7, matrix products, times_transposed(): lax.dot_general(left, right, (((1,), (1,)), ((), ())), preferred_element_...  54.7 us
    pallas_call x1, Pallas kernels, attention_forward(): pl.pallas_call(functools.partial(forward_kernel, parts, per), grid=(windo...  49.5 us
    all_to_all x1, starting transfers between devices, exchange(): lax.all_to_all(array, 'seq', 0, 0, axis_index_groups=groups, tiled=True)  23.9 us
    unnamed x135, local copies, waits for them, and re-layouts  22.5 us
  transfers between devices with their start and end apart: 5, of which 0 were waited for; matrix products, arithmetic and copies ran while one was open for 7% of the time, Pallas kernels for 0%

profile of v2, /device:TPU:1, one launch (start us, length us, event | category | flops | bytes accessed | tf_op | source)
XLA Modules:
  0.0 976.6 jit_solution(18334391733550741705)
XLA Ops:
  7.5 1.8 concatenate.34.refs_0_
  9.3 53.6 %gather_heads.1 = (bf16[2,4,2,2,32,128]{5,4,3,2,1,0:T(8,128)(2,1)}, bf16[2,4,2,2,48,1024]{5,4,3,2,1,0:T(8,128)(2,1)}, bf16[2,4,2,2,48,1536]{5,4,3,2,1,0:T(8,128)(2,1)}) custom-call(bf16[32,128]{1,0:T(8,128)(2,1)} %concatenate.34.refs_0_, bf16[48,512]{1,0:T(8,128)(2,1)} %refs_1_.2, bf16[48,512]{1,0:T(8,128)(2,1)} %refs_2_.2, bf16[48,1536]{1,0:T(8,128)(2,1)} %refs_3_.2), custom_call_target="tpu_custom_call" | custom-call | tf_op jit(solution)/shard_map/gather_heads/pallas_call | solution.py:633
  68.7 10.3 %project.1 = (bf16[512,1536]{1,0:T(8,128)(2,1)S(1)}, bf16[2,8,320,256]{3,2,1,0:T(8,128)(2,1)S(1)}) custom-call(bf16[2,256,1536]{2,1,0:T(8,128)(2,1)S(1)} %copy-done, f32[1,1536]{1,0:T(1,128)S(1)} %reshape_reshape_squeeze.6.gain, f32[4,1,128]{2,1,0:T(1,128)S(1)} %bitcast.159, bf16[1536,1024]{1,0:T(8,128)(2,1)} %bitcast.165, bf16[1536,1024]{1,0:T(8,128)(2,1)} %bitcast.166, ...), custom_call_target="tpu_custom_call" | custom-call | tf_op jit(solution)/shard_map/project/pallas_call | solution.py:675
  81.6 230.1 %gather_weights.1 = (bf16[2,4,2,2,48,1536]{5,4,3,2,1,0:T(8,128)(2,1)}, bf16[2,4,2,2,48,1536]{5,4,3,2,1,0:T(8,128)(2,1)}, bf16[2,4,2,2,48,3072]{5,4,3,2,1,0:T(8,1...) custom-call(bf16[48,1536]{1,0:T(8,128)(2,1)} %refs_0_.1, ...), custom_call_target="tpu_custom_call" | custom-call | tf_op jit(solution)/shard_map/gather_weights/pallas_call | solution.py:633
  311.7 49.5 %attention_forward.1 = (bf16[8,2,192,256]{3,2,1,0:T(8,128)(2,1)}, f32[8,2,192,256]{3,2,1,0:T(8,128)}, f32[8,2,8,256]{3,2,1,0:T(8,128)}) custom-call(s32[3]{0:T(128)} %pad_add_fusion.info, f32[16,1]{1,0:T(8,128)} %exponential_divide_fusion.rates_ref, f32[64,1]{1,0:T(8,128)} %copy.82.bias_ref, f32[32,64]{1,0:T(8,128)} %bitcast.210, ...), custom_call_target="tpu_custom_call" | custom-call | flops 9663676416 | bytes 20000000 | tf_op jit(solution)/shard_map/attention_forward/pallas_call | solution.py:383
  361.2 23.9 %all-to-all-start = ((bf16[8,2,192,256]{3,2,1,0:T(8,128)(2,1)}), bf16[8,2,192,256]{3,2,1,0:T(8,128)(2,1)S(1)}, u32[]{:S(2)}, u32[]{:S(2)}) async-start(bf16[8,2,192,256]{3,2,1,0:T(8,128)(2,1)} %get-tuple-element.59), calls=%async_computation | async-start | bytes 3145728 | tf_op jit(solution)/shard_map/all_to_all | solution.py:1307
  385.8 2.3 broadcast_multiply_fusion
  389.1 5.3 convolution_convert_fusion.1
  394.4 1.7 copy-done.7
  396.1 4.0 collective-permute-start.2
  400.1 2.1 collective-permute-start.3
  407.3 2.8 maximum_convert_fusion.1
  410.2 3.4 fusion.44
  414.3 4.2 convolution_convert_fusion.4
  418.5 8.8 convolution_convert_fusion
  427.2 1.6 copy.83
  429.2 4.9 fusion.56
  435.4 21.9 %multiply_convert_fusion.1 = (bf16[512,3072]{1,0:T(8,128)(2,1)S(1)}, f32[512,3072]{1,0:T(8,128)}, f32[512,3072]{1,0:T(8,128)}) fusion(f32[3072]{0:T(1024)S(1)} %add.162, bf16[512,1536]{1,0:T(8,128)(2,1)S(1)} %multiply_convert_fusion.3.refs_0_, bf16[1536,3072]{1,0:T(8,128)(2,1)S(1)} %bitcast.224), kind=kOutput, calls=%fused_computation.19 | convolution fusion | flops 4935647232 | bytes 26750976 | tf_op jit(solution)/shard_map/dot_general | solution.py:50
  457.3 5.2 fusion.57
  463.9 10.3 %multiply_reduce_fusion = (f32[1536]{0:T(1024)S(1)}, f32[512]{0:T(512)S(1)}, f32[512,1536]{1,0:T(8,128)S(1)}, f32[512,1536]{1,0:T(8,128)S(1)}) fusion(f32[512,1536]{1,0:T(8,128)S(1)} %get-tuple-element.191, f32[512]{0:T(512)S(1)} %fusion.35, f32[512]{0:T(512)S(1)} %broadcast_multiply_fusion.2, f32[1536]{0:T(1024)S(1)} %mul.368, ...), kind=kOutput, calls=%fused_computation.48 | convolution fusion | flops 2478045184 | bytes 15747072 | tf_op jit(solution)/shard_map/dot_general | solution.py:54
  474.2 1.7 fusion.47
  477.0 6.9 fusion.58
  484.0 7.4 fusion.6
  491.4 3.6 collective-permute-start
  495.1 1.9 collective-permute-start.1
  497.3 14.3 %convert_reduce_fusion = (f32[3072]{0:T(1024)S(1)}, bf16[512,3072]{1,0:T(8,128)(2,1)}) fusion(f32[512,3072]{1,0:T(8,128)} %get-tuple-element.158, f32[512,3072]{1,0:T(8,128)} %get-tuple-element.189, f32[3072]{0:T(1024)S(1)} %add.162, bf16[512,1536]{1,0:T(8,128)(2,1)S(1)} %add_convert_fusion.3.refs_3_, bf16[3072,1536]{1,0:T(8,128)(2,1)} %bitcast.225), kind=kOutput, calls=%fused_computation.15 | convolution fusion | flops 4858573824 | bytes 26763264 | tf_op jit(solution)/shard_map/dot_general | solution.py:54
  511.6 11.3 %multiply_reduce_fusion.1 = (f32[1536]{0:T(1024)S(1)}, f32[512]{0:T(512)S(1)}, f32[512,1536]{1,0:T(8,128)}) fusion(f32[512,1536]{1,0:T(8,128)S(1)} %get-tuple-element.188, f32[512]{0:T(512)S(1)} %fusion.34, f32[512]{0:T(512)S(1)} %broadcast_multiply_fusion.3, f32[1536]{0:T(1024)S(1)} %mul.359, bf16[512,3072]{1,0:T(8,128)(2,1)} %get-tuple-element.150.refs_1_, ...), kind=kOutput, calls=%fused_computation.49 | convolution fusion | flops 4837341184 | bytes 18892800 | tf_op jit(solution)/shard_map/dot_general | solution.py:54
  522.9 2.9 fusion.46
  528.7 3.8 fusion.19
  532.4 1.6 copy.88.refs_2_
  534.0 2.8 copy.86
  539.0 4.7 fusion.1
  543.6 144.7 %sum_upper.1 = (f32[48,1536]{1,0:T(8,128)}, f32[96,1536]{1,0:T(8,128)}, f32[48,1536]{1,0:T(8,128)}, f32[48,1536]{1,0:T(8,128)}, bf16[8,2,192,256]{3,2,1,0:T(8,128)(2,1)}) custom-call(bf16[1024,1536]{1,0:T(8,128)(2,1)} %bitcast.170, bf16[1024,1536]{1,0:T(8,128)(2,1)} %bitcast.169, bf16[512,3072]{1,0:T(8,128)(2,1)} %copy-done.21, ...), custom_call_target="tpu_custom_call" | custom-call | tf_op jit(solution)/shard_map/sum_upper/pallas_call | solution.py:1170
  688.3 57.6 %attention_backward.1 = (bf16[8,2,64,256]{3,2,1,0:T(8,128)(2,1)}, bf16[8,2,256,256]{3,2,1,0:T(8,128)(2,1)}, bf16[1,8,2,256,256]{4,3,2,1,0:T(8,128)(2,1)}, f32[2,64,1]{2,1,0:T(8,128)}, f32[64,32]{1,0:T(8,128)}) custom-call(s32[3]{0:T(128)} %pad_add_fusion.info, f32[16,1]{1,0:T(8,128)} %exponential_divide_fusion.rates_ref, f32[64,1]{1,0:T(8,128)} %copy.82.bias_ref, ...), custom_call_target="tpu_custom_call" | custom-call | flops 32212254720 | bytes 20000000 | tf_op jit(solution)/shard_map/attention_backward/pallas_call | solution.py:421
  745.9 121.7 %sum_lower.1 = (f32[48,3072]{1,0:T(8,128)}, f32[48,1536]{1,0:T(8,128)}, bf16[8,2,320,256]{3,2,1,0:T(8,128)(2,1)}) custom-call(bf16[512,1536]{1,0:T(8,128)(2,1)} %copy-done.15, bf16[512,3072]{1,0:T(8,128)(2,1)} %get-tuple-element.150.refs_1_, bf16[512,1536]{1,0:T(8,128)(2,1)} %copy.88.refs_2_, bf16[512,1536]{1,0:T(8,128)(2,1)} %copy-done.16, ...), custom_call_target="tpu_custom_call" | custom-call | tf_op jit(solution)/shard_map/sum_lower/pallas_call | solution.py:1170
  867.6 1.5 slice_bitcast_fusion
  869.1 2.3 slice_bitcast_fusion.2
  872.1 1.6 copy.91
  874.8 1.6 copy.89
  877.8 1.7 copy-done.10
  879.5 1.9 fusion.21
  882.3 2.9 multiply_reduce_fusion.3
  885.3 1.6 copy-done.9
  889.7 57.3 %sum_heads.1 = (f32[48,2560]{1,0:T(8,128)}, f32[8,128]{1,0:T(8,128)}) custom-call(bf16[512,1536]{1,0:T(8,128)(2,1)} %copy-done.3, bf16[512,2560]{1,0:T(8,128)(2,1)} %copy-done.14, f32[32,8,128]{2,1,0:T(8,128)} %bitcast.199), custom_call_target="tpu_custom_call" | custom-call | tf_op jit(solution)/shard_map/sum_heads/pallas_call | solution.py:1170
  947.0 1.7 slice.168
  948.7 1.6 fusion.53
  957.3 5.5 add_convert_fusion.2
  962.8 8.8 multiply_convert_fusion
  (243 shorter events, 50.0 us)
Async XLA Ops:
  0.7 68.0 %copy-start = (bf16[2,256,1536]{2,1,0:T(8,128)(2,1)S(1)}, bf16[2,256,1536]{2,1,0:T(8,128)(2,1)}, u32[]{:S(2)}) copy-start(bf16[2,256,1536]{2,1,0:T(8,128)(2,1)} %values.1) | copy-start | bytes 4718596
  361.2 23.9 %copy-start.44 = (s32[2]{0:T(128)S(1)}, s32[2]{0:T(128)}, u32[]{:S(2)}) copy-start(s32[2]{0:T(128)} %param.25) | copy-start | bytes 28
  361.2 66.0 %all-to-all-start = ((bf16[8,2,192,256]{3,2,1,0:T(8,128)(2,1)}), bf16[8,2,192,256]{3,2,1,0:T(8,128)(2,1)S(1)}, u32[]{:S(2)}, u32[]{:S(2)}) async-start(bf16[8,2,192,256]{3,2,1,0:T(8,128)(2,1)} %get-tuple-element.59), calls=%async_computation | async-start | bytes 3145728 | tf_op jit(solution)/shard_map/all_to_all | solution.py:1307
  385.8 3.4 copy-start.45
  388.1 6.3 copy-start.11
  396.1 11.2 %collective-permute-start.2 = (bf16[2,1,1536]{2,1,0:T(2,128)(2,1)S(1)}, bf16[2,1,1536]{2,1,0:T(2,128)(2,1)S(1)}, u32[]{:S(2)}, u32[]{:S(2)}) collective-permute-start(bf16[2,1,1536]{2,1,0:T(2,128)(2,1)S(1)} %get-tuple-element.165), channel_id=1, source_target_pairs={{0,1},{1,2},{2,3},{3,4},{4,5},{5,6},{6,7},{7,8},{8,9},{9,10},{10,1... | collective-permute-start | bytes 18440 | tf_op jit(solution)/shard_map/ppermute | solution.py:28
  400.1 7.3 collective-permute-start.3
  404.5 5.7 copy-start.31
  404.5 5.7 copy-start.33
  404.5 5.6 copy-start.35
  414.3 4.2 copy-start.13
  429.2 5.9 slice-start.4
  429.2 5.9 slice-start.5
  434.6 22.7 %slice-start.7 = ((s8[9437184]{0:T(1024)(128)(4,1)}), s8[4194304]{0:T(1024)(128)(4,1)S(1)}, s32[]{:S(2)}) async-start(s8[9437184]{0:T(1024)(128)(4,1)} %bitcast.226), calls=%async_computation.8 | async-start | bytes 8388608
  435.1 22.1 %copy-start.15 = (bf16[512,1536]{1,0:T(8,128)(2,1)}, bf16[512,1536]{1,0:T(8,128)(2,1)S(1)}, u32[]{:S(2)}) copy-start(bf16[512,1536]{1,0:T(8,128)(2,1)S(1)} %multiply_convert_fusion.3.refs_0_) | copy-start | bytes 4718596
  435.4 21.9 %slice-start.8 = ((s8[9437184]{0:T(1024)(128)(4,1)}), s8[4194304]{0:T(1024)(128)(4,1)S(1)}, s32[]{:S(2)}) async-start(s8[9437184]{0:T(1024)(128)(4,1)} %bitcast.226), calls=%async_computation.9 | async-start | bytes 8388608
  435.4 21.9 %slice-start.9 = ((s8[9437184]{0:T(1024)(128)(4,1)}), s8[1048576]{0:T(1024)(128)(4,1)S(1)}, s32[]{:S(2)}) async-start(s8[9437184]{0:T(1024)(128)(4,1)} %bitcast.226), calls=%async_computation.10 | async-start | bytes 2097152
  457.2 5.3 copy-start.21
  457.3 5.7 slice-start.12
  457.3 5.7 slice-start.13
  475.9 50.0 %copy-start.4 = (f32[512,1536]{1,0:T(8,128)}, f32[512,1536]{1,0:T(8,128)S(1)}, u32[]{:S(2)}) copy-start(f32[512,1536]{1,0:T(8,128)S(1)} %get-tuple-element.154) | copy-start | bytes 9437188
  475.9 8.1 slice-start.10
  477.0 6.9 copy-start.20
  477.0 6.9 slice-start.11
  484.0 44.7 %slice-start = ((s8[4718592]{0:T(1024)(128)(4,1)}), s8[4194304]{0:T(1024)(128)(4,1)S(1)}, s32[]{:S(2)}) async-start(s8[4718592]{0:T(1024)(128)(4,1)} %bitcast.174), calls=%async_computation.1 | async-start | bytes 8388608
  491.4 5.6 copy-start.18
  491.4 45.7 %collective-permute-start = (bf16[2,1,1536]{2,1,0:T(2,128)(2,1)S(1)}, bf16[2,1,1536]{2,1,0:T(2,128)(2,1)S(1)}, u32[]{:S(2)}, u32[]{:S(2)}) collective-permute-start(bf16[2,1,1536]{2,1,0:T(2,128)(2,1)S(1)} %get-tuple-element.163), channel_id=1, source_target_pairs={{0,1},{1,2},{2,3},{3,4},{4,5},{5,6},{6,7},{7,8},{8,9},{9,10},{10,1... | collective-permute-start | bytes 18440 | tf_op jit(solution)/shard_map/ppermute | solution.py:28
  495.1 42.1 %collective-permute-start.1 = (bf16[2,1,1536]{2,1,0:T(2,128)(2,1)S(1)}, bf16[2,1,1536]{2,1,0:T(2,128)(2,1)S(1)}, u32[]{:S(2)}, u32[]{:S(2)}) collective-permute-start(bf16[2,1,1536]{2,1,0:T(2,128)(2,1)S(1)} %get-tuple-element.164), channel_id=1, source_target_pairs={{1,0},{2,1},{3,2},{4,3},{5,4},{6,5},{7,6},{8,7},{9,8},{10,9},{11,1... | collective-permute-start | bytes 18440 | tf_op jit(solution)/shard_map/ppermute | solution.py:29
  497.2 14.3 %copy-start.17 = (bf16[512,1536]{1,0:T(8,128)(2,1)}, bf16[512,1536]{1,0:T(8,128)(2,1)S(1)}, u32[]{:S(2)}) copy-start(bf16[512,1536]{1,0:T(8,128)(2,1)S(1)} %add_convert_fusion.3.refs_3_) | copy-start | bytes 4718596
  497.3 31.4 %slice-start.1 = ((s8[4718592]{0:T(1024)(128)(4,1)}), s8[524288]{0:T(1024)(128)(4,1)S(1)}, s32[]{:S(2)}) async-start(s8[4718592]{0:T(1024)(128)(4,1)} %bitcast.174), calls=%async_computation.2 | async-start | bytes 1048576
  534.0 3.1 copy-start.19
  877.6 3.8 slice-start.2
  879.5 2.7 copy-start.1
  879.5 2.8 slice-start.3
  879.5 2.8 copy-start.37
  879.5 2.8 copy-start.41
  882.3 3.0 copy-start.42
  885.2 3.1 copy-start.40
  885.2 3.3 copy-start.39
  885.3 3.6 copy-start.38
  957.3 5.5 copy-start.12
  957.3 5.5 copy-start.43
  962.8 8.9 copy-start.30
  962.8 9.6 copy-start.26
  962.8 10.4 %copy-start.25 = (f32[96,1536]{1,0:T(8,128)S(1)}, f32[96,1536]{1,0:T(8,128)}, u32[]{:S(2)}) copy-start(f32[96,1536]{1,0:T(8,128)} %get-tuple-element.233) | copy-start | bytes 1769476
  971.6 2.4 copy-start.29
  971.6 3.1 copy-start.28
  971.6 3.8 copy-start.27
  (17 other events, 26.7 us)

commit v3 on v2

--- a/solution.py
+++ b/solution.py
@@ -80,21 +80,15 @@
     )
 
 
-def key_side(parts, part, rates, rows, groups, mine, other, store):
-    half = RPF // 2
-    spot = lax.broadcasted_iota(jnp.int32, (half, rows), 1).astype(F32)
-    low = jnp.exp(-rates * (rows - 1 - spot)).astype(BF)
-    high = jnp.exp(-rates * spot).astype(BF)
-    pad = jnp.zeros((128 - KD - RPF, rows), BF)
+def key_side(parts, part, groups, mine, other, store):
     for slot in range(parts):
-        theirs = lax.rem(part + slot, 2) if parts == 2 else slot_part(part, slot, parts)
+        theirs = slot_part(part, slot, parts)
         for g in range(groups):
-            source = mine if slot == 0 else other
             if slot == 0:
                 kt, vt = mine[g, 0, KD : 2 * KD, :], mine[g, 0, 2 * KD :, :]
             else:
                 kt, vt = other[slot - 1, g, 0, :KD, :], other[slot - 1, g, 0, KD:, :]
-            store(g * parts + theirs, jnp.concatenate([kt, low, high, pad], axis=0), vt)
+            store(g * parts + theirs, kt, vt)
 
 
 def slot_part(part, slot, parts):
@@ -113,52 +107,85 @@
     return positional, projected[:half] + projected[half:], projected[:half] - projected[half:]
 
 
-def block_query(content, plus, minus, rates, q_block, k_block, rows, kind):
-    spot = lax.broadcasted_iota(jnp.int32, plus.shape, 1)
-    query_pos = q_block * rows + spot
-    zero = jnp.zeros(plus.shape, BF)
-    below = above = zero
-    if kind != "above":
-        gap = (query_pos - (k_block * rows + rows - 1)).astype(F32)
-        below = (plus * jnp.exp(jnp.minimum(-rates * gap, 60.0))).astype(BF)
-    if kind != "below":
-        gap = (k_block * rows - query_pos).astype(F32)
-        above = (minus * jnp.exp(jnp.minimum(-rates * gap, 60.0))).astype(BF)
-    rest = jnp.zeros((128 - KD - RPF, rows), BF)
-    if kind == "below":
-        return jnp.concatenate([content, below, zero, rest], axis=0)
-    if kind == "above":
-        return jnp.concatenate([content, zero, above, rest], axis=0)
-    return (
-        jnp.concatenate([content, below, zero, rest], axis=0),
-        jnp.concatenate([content, zero, above, rest], axis=0),
-    )
-
-
-def signs(q_block, k_block, rows):
-    i = q_block * rows + lax.broadcasted_iota(jnp.int32, (rows, rows), 1)
-    j = k_block * rows + lax.broadcasted_iota(jnp.int32, (rows, rows), 0)
+def query_block(content, plus, minus, rates):
+    spot = lax.broadcasted_iota(jnp.int32, plus.shape, 1).astype(F32)
+    last = plus.shape[1] - 1
+    from_first, to_last = jnp.exp(-rates * spot), jnp.exp(-rates * (last - spot))
+    rest = jnp.zeros((128 - KD - RPF, content.shape[1]), BF)
+    block = jnp.concatenate(
+        [content, (plus * from_first).astype(BF), (minus * to_last).astype(BF), rest], axis=0
+    )
+    return block, from_first, to_last
+
+
+def lane_rates(rates_row):
+    lane = lax.broadcasted_iota(jnp.int32, (1, 128), 1)
+    half = RPF // 2
+    below = (lane >= KD) & (lane < KD + half)
+    above = (lane >= KD + half) & (lane < KD + RPF)
+    return rates_row, below, above
+
+
+def decay_table(rates_row, span):
+    rates_row, below, above = lane_rates(rates_row)
+    spot = lax.broadcasted_iota(jnp.int32, (span, 128), 0).astype(F32)
+    table = jnp.where(below, jnp.exp(-rates_row * (span - 1 - spot)), 0.0)
+    return jnp.where(above, jnp.exp(-rates_row * spot), table)
+
+
+def key_decays(table, rates_row, first_query, last_query, first_key, span, kind):
+    rates_row, below, above = lane_rates(rates_row)
+    if kind == "plain":
+        before = first_key < first_query
+        gap = jnp.where(before, first_query - (first_key + span - 1), first_key - last_query)
+        used = (below & before) | (above & jnp.logical_not(before))
+        return (table * jnp.where(used, jnp.exp(-rates_row * gap.astype(F32)), 0.0)).astype(BF)
+    key = first_key + lax.broadcasted_iota(jnp.int32, (span, 128), 0)
+    down = jnp.exp(jnp.minimum(-rates_row * (first_query - key).astype(F32), 60.0))
+    up = jnp.exp(jnp.minimum(-rates_row * (key - last_query).astype(F32), 60.0))
+    return jnp.where(below, down, 0.0).astype(BF), jnp.where(above, up, 0.0).astype(BF)
+
+
+def order_of(first_query, first_key, span, rows):
+    i = first_query + lax.broadcasted_iota(jnp.int32, (span, rows), 1)
+    j = first_key + lax.broadcasted_iota(jnp.int32, (span, rows), 0)
     return i, j
 
 
-def block_scores(k_sc, content, plus, minus, rates, q_block, k_block, rows, kind, length):
-    keys = k_sc[pl.ds(pl.multiple_of(k_block * rows, rows), rows), :]
+def tile_scores(keys, decays, query, first_query, first_key, length, kind):
     if kind != "both":
-        return dot(keys, block_query(content, plus, minus, rates, q_block, k_block, rows, kind))
-    below, above = block_query(content, plus, minus, rates, q_block, k_block, rows, kind)
-    i, j = signs(q_block, k_block, rows)
-    s_below, s_above = dot(keys, below), dot(keys, above)
+        return dot(keys + decays, query)
+    s_below, s_above = dot(keys + decays[0], query), dot(keys + decays[1], query)
+    i, j = order_of(first_query, first_key, *s_below.shape)
     scores = jnp.where(i > j, s_below, jnp.where(i < j, s_above, 0.5 * (s_below + s_above)))
     return jnp.where(j < length, scores, NEG)
 
 
-def visit_tiles(tile, q_block, length, rows, per, tiles):
+def visit_tiles(scores_into, use, slots, whole_tile, q_block, length, rows, per):
     span = rows * per
     count = lax.div(length + span - 1, span)
     full = lax.div(length, span)
     own = lax.div(q_block, per)
-    pl.loop(0, jnp.minimum(own, full))(functools.partial(tile, kind="below"))
-    pl.loop(own + 1, full)(functools.partial(tile, kind="above"))
+    plain = full - jnp.where(own < full, 1, 0)
+
+    def tile_of(k):
+        return k + jnp.where(k >= own, 1, 0)
+
+    @pl.when(plain > 0)
+    def _():
+        scores_into(slots[0], tile_of(0), own)
+
+    @pl.loop(0, lax.div(plain, 2))
+    def _(k):
+        first = 2 * k
+        scores_into(slots[1], tile_of(first + 1), own)
+        use(slots[0], tile_of(first), own)
+        scores_into(slots[0], tile_of(jnp.minimum(first + 2, plain - 1)), own)
+        use(slots[1], tile_of(first + 1), own)
+
+    @pl.when(lax.rem(plain, 2) == 1)
+    def _():
+        use(slots[0], tile_of(plain - 1), own)
 
     @pl.loop(0, 2)
     def _(k):
@@ -167,11 +194,11 @@
 
         @pl.when(go)
         def _():
-            tile(t, kind="both")
+            whole_tile(t)
 
 
 def forward_kernel(
-    parts, per, info, rates_ref, bias_ref, rel_ref, mine, other, mixed, wide, lse, k_sc, v_sc, m_sc, l_sc, acc
+    parts, per, info, rates_ref, lanes_ref, bias_ref, rel_ref, mine, other, mixed, wide, lse, k_sc, v_sc, table_sc, s0_sc, s1_sc, m_sc, l_sc, acc
 ):
     groups, rows = mine.shape[0], mine.shape[3]
     half = RPF // 2
@@ -181,10 +208,12 @@
 
     def store(block, kt, vt):
         spot = pl.multiple_of(block * rows, rows)
-        k_sc[pl.ds(spot, rows), :] = kt.T
+        k_sc[pl.ds(spot, rows), :] = jnp.concatenate([kt, jnp.zeros_like(kt)], axis=0).T
         v_sc[:, pl.ds(spot, rows)] = vt
 
-    key_side(parts, part, rates, rows, groups, mine, other, store)
+    key_side(parts, part, groups, mine, other, store)
+    span = rows * per
+    table_sc[...] = decay_table(lanes_ref[...], span)
 
     @pl.loop(0, groups)
     def _(g):
@@ -200,31 +229,39 @@
         def _():
             content = mine[g, 0, :KD, :]
             _, plus, minus = query_side(content, bias_ref[...], rel_ref[...], half)
+            query, _, _ = query_block(content, plus, minus, rates)
+            first_query = q_block * rows
             m_sc[...] = jnp.full(m_sc.shape, NEG, F32)
             l_sc[...] = jnp.zeros(l_sc.shape, F32)
             acc[...] = jnp.zeros(acc.shape, F32)
 
-            def tile(t, kind):
-                scores = jnp.concatenate(
-                    [
-                        block_scores(
-                            k_sc, content, plus, minus, rates, q_block, t * per + n, rows, kind, length
-                        )
-                        for n in range(per)
-                    ],
-                    axis=0,
+            def scores_of(t, kind):
+                first_key = pl.multiple_of(t * span, span)
+                decays = key_decays(
+                    table_sc[...], lanes_ref[...], first_query, first_query + rows - 1, first_key, span, kind
                 )
+                keys = k_sc[pl.ds(first_key, span), :]
+                return tile_scores(keys, decays, query, first_query, first_key, length, kind)
+
+            def scores_into(slot, t, own):
+                slot[...] = scores_of(t, "plain")
+
+            def use(slot, t, own):
+                scores = slot[...]
                 old = m_sc[...]
                 new = jnp.maximum(old, jnp.max(scores, axis=0, keepdims=True))
                 alpha = jnp.exp(old - new)
                 probs = jnp.exp(scores - new)
                 m_sc[...] = new
                 l_sc[...] = l_sc[...] * alpha + jnp.sum(probs, axis=0, keepdims=True)
-                span = rows * per
                 values = v_sc[:, pl.ds(pl.multiple_of(t * span, span), span)]
                 acc[...] = acc[...] * alpha + dot(values, probs.astype(BF))
 
-            visit_tiles(tile, q_block, length, rows, per, groups * parts // per)
+            def whole_tile(t):
+                s0_sc[...] = scores_of(t, "both")
+                use(s0_sc, t, None)
+
+            visit_tiles(scores_into, use, (s0_sc, s1_sc), whole_tile, q_block, length, rows, per)
             total = l_sc[...]
             out = acc[...] / total
             mixed[g, 0] = out.astype(BF)
@@ -233,9 +270,9 @@
 
 
 def backward_kernel(
-    parts, per, info, rates_ref, bias_ref, rel_ref, mine, other, grad, wide, lse,
+    parts, per, info, rates_ref, lanes_ref, bias_ref, rel_ref, mine, other, grad, wide, lse,
     dq, dkv_mine, dkv_other, sums, rel_grad,
-    k_sc, kt_sc, v_sc, dk_sc, dv_sc, dq_sc, bias_sc,
+    k_sc, kt_sc, v_sc, table_sc, turned_sc, s0_sc, s1_sc, dk_sc, dv_sc, dq_sc, bias_sc,
 ):
     groups, rows = mine.shape[0], mine.shape[3]
     half = RPF // 2
@@ -247,11 +284,14 @@
 
     def store(block, kt, vt):
         spot = pl.multiple_of(block * rows, rows)
-        k_sc[pl.ds(spot, rows), :] = kt.T
+        k_sc[pl.ds(spot, rows), :] = jnp.concatenate([kt, jnp.zeros_like(kt)], axis=0).T
         kt_sc[:, pl.ds(spot, rows)] = kt
         v_sc[pl.ds(spot, rows), :] = vt.T
 
-    key_side(parts, part, rates, rows, groups, mine, other, store)
+    key_side(parts, part, groups, mine, other, store)
+    span = rows * per
+    table_sc[...] = decay_table(lanes_ref[...], span)
+    turned_sc[...] = table_sc[...].T[KD : KD + RPF]
     dk_sc[...] = jnp.zeros(dk_sc.shape, F32)
     dv_sc[...] = jnp.zeros(dv_sc.shape, F32)
 
@@ -273,62 +313,70 @@
             content = mine[g, 0, :KD, :]
             content_rows = content.T
             positional, plus, minus = query_side(content, bias_ref[...], rel_ref[...], half)
+            query, from_first, to_last = query_block(content, plus, minus, rates)
+            first_query = q_block * rows
+            last_query = first_query + rows - 1
             grad_t = grad[g, 0]
             grad_rows = grad_t.T
             log_total = lse[g, 0, :1, :]
             row_sum = jnp.sum(grad_t.astype(F32) * wide[g, 0], axis=0, keepdims=True)
             dq_sc[...] = jnp.zeros(dq_sc.shape, F32)
 
-            def tile(t, kind):
-                span = rows * per
-                spot = pl.multiple_of(t * span, span)
-                scores = jnp.concatenate(
-                    [
-                        block_scores(
-                            k_sc, content, plus, minus, rates, q_block, t * per + n, rows, kind, length
-                        )
-                        for n in range(per)
-                    ],
-                    axis=0,
+            def decays_of(first_key, kind):
+                return key_decays(
+                    table_sc[...], lanes_ref[...], first_query, last_query, first_key, span, kind
                 )
+
+            def scores_of(t, decays, kind):
+                first_key = pl.multiple_of(t * span, span)
+                keys = k_sc[pl.ds(first_key, span), :]
+                return tile_scores(keys, decays, query, first_query, first_key, length, kind)
+
+            def scores_into(slot, t, own):
+                first_key = pl.multiple_of(t * span, span)
+                slot[0] = scores_of(t, decays_of(first_key, "plain"), "plain")
+                slot[1] = dot(v_sc[pl.ds(first_key, span), :], grad_t)
+
+            def use(slot, t, own):
+                absorb(slot, t, "plain", None)
+
+            def whole_tile(t):
+                first_key = pl.multiple_of(t * span, span)
+                decays = decays_of(first_key, "both")
+                s0_sc[0] = scores_of(t, decays, "both")
+                s0_sc[1] = dot(v_sc[pl.ds(first_key, span), :], grad_t)
+                absorb(s0_sc, t, "both", decays)
+
+            def absorb(slot, t, kind, decays):
+                first_key = spot = pl.multiple_of(t * span, span)
+                scores, prob_grad = slot[0], slot[1]
                 exact = jnp.exp(scores - log_total)
-                prob_grad = dot(v_sc[pl.ds(spot, span), :], grad_t)
                 score_grad = exact * (prob_grad - row_sum)
                 low = score_grad.astype(BF)
                 dv_sc[pl.ds(spot, span), :] += dot(exact.astype(BF), grad_rows)
                 dk_sc[pl.ds(spot, span), :] += dot(low, content_rows)
-                for n in range(per):
-                    k_block = t * per + n
-                    piece = low[n * rows : (n + 1) * rows]
-                    keys = kt_sc[:, pl.ds(pl.multiple_of(k_block * rows, rows), rows)]
-                    place = q_block * rows + lax.broadcasted_iota(jnp.int32, (half, rows), 1)
-                    down = -rates * (place - (k_block * rows + rows - 1)).astype(F32)
-                    up = -rates * (k_block * rows - place).astype(F32)
-                    if kind == "below":
-                        part_sum = dot(keys[: KD + half], piece)
-                        dq_sc[:KD] += part_sum[:KD]
-                        dq_sc[KD : KD + half] += part_sum[KD:] * jnp.exp(down)
-                    elif kind == "above":
-                        part_sum = dot(keys[: KD + RPF], piece)
-                        dq_sc[:KD] += part_sum[:KD]
-                        dq_sc[KD + half :] += part_sum[KD + half :] * jnp.exp(up)
-                    else:
-                        i, j = signs(q_block, k_block, rows)
-                        wide_piece = score_grad[n * rows : (n + 1) * rows]
-                        equal = 0.5 * wide_piece
-                        lower = jnp.where(i > j, wide_piece, jnp.where(i < j, 0.0, equal)).astype(BF)
-                        upper = jnp.where(i < j, wide_piece, jnp.where(i > j, 0.0, equal)).astype(BF)
-                        dq_sc[:KD] += dot(keys[:KD], piece)
-                        dq_sc[KD : KD + half] += dot(keys[KD : KD + half], lower) * jnp.exp(
-                            jnp.minimum(down, 60.0)
-                        )
-                        dq_sc[KD + half :] += dot(keys[KD + half : KD + RPF], upper) * jnp.exp(
-                            jnp.minimum(up, 60.0)
-                        )
-
-            visit_tiles(tile, q_block, length, rows, per, groups * parts // per)
+                keys_turned = kt_sc[:, pl.ds(spot, span)]
+                if kind == "both":
+                    i, j = order_of(first_query, first_key, span, rows)
+                    equal = 0.5 * score_grad
+                    lower = jnp.where(i > j, score_grad, jnp.where(i < j, 0.0, equal)).astype(BF)
+                    upper = jnp.where(i < j, score_grad, jnp.where(i > j, 0.0, equal)).astype(BF)
+                    dq_sc[:KD] += dot(keys_turned, low)
+                    below, above = decays
+                    dq_sc[KD : KD + half] += dot(below.T[KD : KD + half], lower)
+                    dq_sc[KD + half : KD + RPF] += dot(above.T[KD + half : KD + RPF], upper)
+                else:
+                    before = first_key < first_query
+                    gap = jnp.where(before, first_query - (first_key + span - 1), first_key - last_query)
+                    faded = jnp.exp(-rates * gap.astype(F32))
+                    down = turned_sc[:half] * jnp.where(before, faded, 0.0)
+                    up = turned_sc[half:] * jnp.where(before, 0.0, faded)
+                    pos = jnp.concatenate([down, up], axis=0).astype(BF)
+                    dq_sc[...] += dot(jnp.concatenate([keys_turned, pos], axis=0), low)
+
+            visit_tiles(scores_into, use, (s0_sc, s1_sc), whole_tile, q_block, length, rows, per)
             content_grad = dq_sc[:KD]
-            down, up = dq_sc[KD : KD + half], dq_sc[KD + half :]
+            down, up = dq_sc[KD : KD + half] * from_first, dq_sc[KD + half :] * to_last
             projected_grad = jnp.concatenate([down + up, down - up], axis=0)
             positional_grad = dot32(rel_ref[...], projected_grad, ((0,), (0,)))
             dq[g, 0] = (scale * (content_grad + positional_grad)).astype(BF)
@@ -376,9 +424,14 @@
     return per
 
 
+def lanes_of(rates):
+    line = rates.reshape(1, -1)
+    return jnp.pad(jnp.concatenate([line, line], axis=1), ((0, 0), (KD, 128 - KD - RPF)))
+
+
 def attention_forward(info, rates, bias, rel, mine, other, parts):
     groups, windows, _, rows = mine.shape
-    per = tile_blocks(rows, groups, parts, 512)
+    per = tile_blocks(rows, groups, parts, 1024)
     total = groups * parts * rows
     return pl.pallas_call(
         functools.partial(forward_kernel, parts, per),
@@ -391,6 +444,7 @@
         in_specs=[
             pl.BlockSpec(memory_space=pltpu.SMEM),
             whole(*rates.shape),
+            whole(1, 128),
             whole(*bias.shape),
             whole(*rel.shape),
             per_window(groups, 1, 2 * KD + VD, rows),
@@ -404,6 +458,9 @@
         scratch_shapes=[
             pltpu.VMEM((total, 128), BF),
             pltpu.VMEM((VD, total), BF),
+            pltpu.VMEM((rows * per, 128), F32),
+            pltpu.VMEM((rows * per, rows), F32),
+            pltpu.VMEM((rows * per, rows), F32),
             pltpu.VMEM((1, rows), F32),
             pltpu.VMEM((1, rows), F32),
             pltpu.VMEM((VD, rows), F32),
@@ -411,12 +468,12 @@
         compiler_params=pltpu.CompilerParams(vmem_limit_bytes=56 * 2**20),
         cost_estimate=attention_cost(windows, groups, rows, parts, 128 + 256),
         name="attention_forward",
-    )(info, rates, bias, rel, mine, other)
+    )(info, rates, lanes_of(rates), bias, rel, mine, other)
 
 
 def attention_backward(info, rates, bias, rel, mine, other, grad, wide, lse, parts):
     groups, windows, _, rows = mine.shape
-    per = tile_blocks(rows, groups, parts, 512)
+    per = tile_blocks(rows, groups, parts, 1024)
     total = groups * parts * rows
     return pl.pallas_call(
         functools.partial(backward_kernel, parts, per),
@@ -431,6 +488,7 @@
         in_specs=[
             pl.BlockSpec(memory_space=pltpu.SMEM),
             whole(*rates.shape),
+            whole(1, 128),
             whole(*bias.shape),
             whole(*rel.shape),
             per_window(groups, 1, 2 * KD + VD, rows),
@@ -448,8 +506,12 @@
         ),
         scratch_shapes=[
             pltpu.VMEM((total, 128), BF),
-            pltpu.VMEM((128, total), BF),
+            pltpu.VMEM((KD, total), BF),
             pltpu.VMEM((total, VD), BF),
+            pltpu.VMEM((rows * per, 128), F32),
+            pltpu.VMEM((RPF, rows * per), F32),
+            pltpu.VMEM((2, rows * per, rows), F32),
+            pltpu.VMEM((2, rows * per, rows), F32),
             pltpu.VMEM((total, KD), F32),
             pltpu.VMEM((total, VD), F32),
             pltpu.VMEM((KD + RPF, rows), F32),
@@ -458,21 +520,30 @@
         compiler_params=pltpu.CompilerParams(vmem_limit_bytes=56 * 2**20),
         cost_estimate=attention_cost(windows, groups, rows, parts, 3 * 256 + 2 * 256),
         name="attention_backward",
-    )(info, rates, bias, rel, mine, other, grad, wide, lse)
+    )(info, rates, lanes_of(rates), bias, rel, mine, other, grad, wide, lse)
 
 MESH = pl.DeviceIdType.MESH
 
 
-def links_kernel(pairs, counts, parts, *refs):
+def links_kernel(pairs, counts, parts, early, *refs):
     n_in, n_out = counts
-    refs_in, refs = refs[:n_in], refs[n_in:]
+    refs = list(refs)
+
+    def take(count):
+        out, refs[:count] = refs[:count], []
+        return out
+
+    refs_in = take(n_in)
+    if early:
+        values, spread_gain, pick_gain, spread_bias, pick_bias = take(5)
+    elif parts:
+        (blocks,) = take(1)
+    refs_out = take(n_out)
     if parts:
-        blocks, refs = refs[0], refs[1:]
-    refs_out, refs = refs[:n_out], refs[n_out:]
-    if parts:
-        mine, other = refs[:2]
-        refs = refs[2:]
-    local_sem, send_hi, recv_hi, send_y, recv_y, send_dp, recv_dp, send_c, recv_c = refs[:9]
+        mine, other = take(2)
+    if early:
+        (normed,) = take(1)
+    local_sem, send_hi, recv_hi, send_y, recv_y, send_dp, recv_dp, send_c, recv_c = take(9)
     dp, seq = lax.axis_index("dp"), lax.axis_index("seq")
     ndp, nhi = refs_out[0].shape[:2]
     hi, low = lax.div(seq, 4), lax.rem(seq, 4)
@@ -517,42 +588,41 @@
                 serial += 1
 
     def copies(chunk, stage):
-        n, side, shard, shard_first, array, first, columns = chunk
-        cols = pl.ds(first, columns)
+        n, side, array, row, rows, first, columns = chunk
         out = refs_out[array]
+        piece = (pl.ds(row, rows), pl.ds(first, columns))
         which = (("hi", "y", "dp", "c"), ("hi", "dp", "y", "c"))[side][stage]
         if which == "hi":
-            target = out.at[dp, hi, y, c, :, cols]
-            source = refs_in[shard].at[:, pl.ds(shard_first, columns)]
+            target = out.at[(dp, hi, y, c) + piece]
+            source = refs_in[array].at[piece]
             peers, ss, rs = hi_peers, send_hi, recv_hi
         else:
+            every = slice(None)
             if which == "c":
-                target = out.at[:, :, :, c, :, cols]
+                target = out.at[(every, every, every, c) + piece]
                 peers, ss, rs = c_peers, send_c, recv_c
             elif which == "y":
-                target = (
-                    out.at[dp, :, y, c, :, cols] if stage == 1 else out.at[:, :, y, c, :, cols]
-                )
+                there = (dp, every, y, c) if stage == 1 else (every, every, y, c)
+                target = out.at[there + piece]
                 peers, ss, rs = y_peers, send_y, recv_y
             else:
-                target = (
-                    out.at[dp, :, y, c, :, cols] if stage == 1 else out.at[dp, :, :, c, :, cols]
-                )
+                there = (dp, every, y, c) if stage == 1 else (dp, every, every, c)
+                target = out.at[there + piece]
                 peers, ss, rs = dp_peers, send_dp, recv_dp
             source = target
         return [remote(source, target, ss.at[n, k], rs.at[n, k], p) for k, p in enumerate(peers)]
 
-    def own(chunk):
-        n, _, shard, shard_first, array, first, columns = chunk
+    def own(array):
         return pltpu.make_async_copy(
-            refs_in[shard].at[:, pl.ds(shard_first, columns)],
-            refs_out[array].at[dp, hi, y, c, :, pl.ds(first, columns)],
-            local_sem.at[n],
+            refs_in[array], refs_out[array].at[dp, hi, y, c], local_sem.at[array]
         )
 
     everything = [chunk for group in step_chunks for chunk in group]
+    head_copies, head_own = [], None
     if parts:
-        head_local, head_send, head_recv, part_send, part_recv = refs[9:]
+        head_local, head_send, head_recv, part_send, part_recv = take(5)
+        if early:
+            blocks = take(1)[0]
         head_copies = [
             remote(blocks.at[:, h], mine.at[head], head_send.at[k], head_recv.at[k], p)
             for k, (h, p) in enumerate(zip(head_of, head_peers, strict=True))
@@ -563,45 +633,114 @@
             remote(keys, other.at[k], part_send.at[k], part_recv.at[k], p)
             for k, p in enumerate(part_peers)
         ]
+        if not early:
+            head_own.start()
+    if early:
+        small_v, query_v, key_v, values_v, inputs_v, gain_v, bias_v, load_sem = take(8)
+        inputs_load = pltpu.make_async_copy(values, inputs_v, load_sem.at[0])
+        inputs_load.start()
+
+    def make_blocks():
+        loads = [
+            pltpu.make_async_copy(source, target, load_sem.at[k + 1])
+            for k, (source, target) in enumerate(
+                zip(refs_out[:4], (small_v, query_v, key_v, values_v), strict=True)
+            )
+        ]
+        for load in loads:
+            load.start()
+        inputs_load.wait()
+        for load in loads:
+            load.wait()
+
+        @pl.loop(0, ndp * nhi * 4)
+        def _(k):
+            rows = small_v[
+                lax.div(k, nhi * 4),
+                lax.rem(lax.div(k, 4), nhi),
+                lax.rem(lax.div(k, 2), 2),
+                lax.rem(k, 2),
+            ].astype(F32)
+            gain_v[pl.ds(k, 1), :] = rows[0:1, :]
+            bias_v[pl.ds(k, 1), :] = rows[1:2, :]
+
+        def line_up(table, spread, pick):
+            return jnp.sum(dot(table[...].astype(BF), spread[...]) * pick[...], axis=0, keepdims=True)
+
+        gain = line_up(gain_v, spread_gain, pick_gain)
+        bias = line_up(bias_v, spread_bias, pick_bias)
+        windows, rows = inputs_v.shape[:2]
+        for w in range(windows):
+            normed[w * rows : (w + 1) * rows, :] = layer_norm(
+                inputs_v[w].astype(F32), gain
+            ).astype(BF)
+        low = normed[...]
+        width = low.shape[1]
+
+        def weight(table, first, columns):
+            return table[:, :, :, :, :, first : first + columns].reshape(width, columns)
+
+        for pair in range(H // 2):
+            spot, wide = pair * 2 * KD, pair * 2 * VD
+            content = dot(low, weight(query_v, spot, 2 * KD)) + bias[:, spot : spot + 2 * KD]
+            content = (content * (KD**-0.5)).astype(BF).T
+            key = dot(low, weight(key_v, spot, 2 * KD)).astype(BF).T
+            value = dot(low, weight(values_v, wide, 2 * VD)).astype(BF).T
+            for h in range(2):
+                for w in range(windows):
+                    span = slice(w * rows, (w + 1) * rows)
+                    blocks[w, 2 * pair + h, :KD, :] = content[h * KD : (h + 1) * KD, span]
+                    blocks[w, 2 * pair + h, KD : 2 * KD, :] = key[h * KD : (h + 1) * KD, span]
+                    blocks[w, 2 * pair + h, 2 * KD :, :] = value[h * VD : (h + 1) * VD, span]
         head_own.start()
-    else:
-        head_copies = []
+
     ahead, lag = 3, 2
-    share = -(-len(head_copies) // len(pairs))
 
     def launch(step):
-        for copy in head_copies[step * share : (step + 1) * share]:
-            copy.start()
         for chunk in step_chunks[step]:
             for copy in copies(chunk, 0):
                 copy.start()
 
+    events = {}
+    for spot in range(len(pairs)):
+        gap = 1 if spot < early else lag
+        for stage in (3, 2, 1):
+            events.setdefault(spot + gap * (stage - 1), []).append((stage, spot))
+    made_at = early + 2 if early else 0
+    heads_at = [made_at + k for k in range(len(head_copies))]
     for step in range(min(ahead, len(pairs))):
         launch(step)
-    for chunk in everything:
-        own(chunk).start()
-    for chunk in everything:
-        own(chunk).wait()
-    for step in range(len(pairs) + 2 * lag):
-        for stage in (3, 2, 1):
-            spot = step - lag * (stage - 1)
-            if 0 <= spot < len(pairs):
-                for chunk in step_chunks[spot]:
-                    for copy in copies(chunk, stage - 1):
-                        copy.wait_recv()
-                    for copy in copies(chunk, stage):
-                        copy.start()
+    for array in range(n_out):
+        own(array).start()
+    for array in range(n_out):
+        own(array).wait()
+    for step in range(max(list(events) + heads_at) + 1):
+        for stage, spot in sorted(events.get(step, []), reverse=True):
+            for chunk in step_chunks[spot]:
+                for copy in copies(chunk, stage - 1):
+                    copy.wait_recv()
+                for copy in copies(chunk, stage):
+                    copy.start()
         if step + ahead < len(pairs):
             launch(step + ahead)
+        if early and step == made_at:
+            for group in step_chunks[:early]:
+                for chunk in group:
+                    for copy in copies(chunk, 3):
+                        copy.wait_recv()
+            make_blocks()
+        if step in heads_at:
+            head_copies[heads_at.index(step)].start()
     if parts:
         head_own.wait()
         for copy in head_copies:
             copy.wait_recv()
         for copy in part_copies:
             copy.start()
-    for chunk in everything:
-        for copy in copies(chunk, 3):
-            copy.wait_recv()
+    for group in step_chunks[early:]:
+        for chunk in group:
+            for copy in copies(chunk, 3):
+                copy.wait_recv()
     if parts:
         for copy in part_copies:
             copy.wait_recv()
@@ -613,30 +752,73 @@
                 copy.wait_send()
 
 
-def use_links(name, collective, shards, arrays, pairs, blocks=None):
+def spread_tables(length, share):
+    column = jnp.arange(length, dtype=jnp.int32)
+    lane = jnp.arange(128, dtype=jnp.int32)
+    device = jnp.arange(length // share, dtype=jnp.int32)
+    spread = (column[None, :] % share == lane[:, None]).astype(BF)
+    pick = (column[None, :] // share == device[:, None]).astype(F32)
+    return spread, pick
+
+
+def use_links(name, collective, shards, pairs, blocks=None, values=None, early=0):
     ndp, nseq = lax.axis_size("dp"), lax.axis_size("seq")
-    nhi, parts = nseq // 4, nseq // H if blocks is not None else 0
+    nhi, devices = nseq // 4, ndp * nseq
+    parts = nseq // H if blocks is not None or early else 0
     chunks = sum(len(side) for pair in pairs for side in pair)
+    arrays = [shard.shape for shard in shards]
     out_shape = [jax.ShapeDtypeStruct((ndp, nhi, 2, 2) + shape, BF) for shape in arrays]
     operands = list(shards)
-    sizes = [(chunks,)] + [
+    in_specs = [pl.BlockSpec(memory_space=pl.ANY)] * len(operands)
+    sizes = [(len(arrays),)] + [
         (chunks, size) for size in (nhi - 1, nhi - 1, 1, 1, ndp - 1, ndp - 1, 1, 1)
     ]
+    scratch = []
+    if early:
+        windows, rows, width = values.shape
+        operands += [values]
+        operands += [
+            *spread_tables(width, width // devices),
+            *spread_tables(H * KD, H * KD // devices),
+        ]
+        in_specs += [pl.BlockSpec(memory_space=pl.ANY)] + [
+            pl.BlockSpec(memory_space=pltpu.VMEM)
+        ] * 4
+        scratch = [
+            pltpu.VMEM((windows, H, 2 * KD + VD, rows), BF),
+            pltpu.VMEM(out_shape[0].shape, BF),
+            pltpu.VMEM(out_shape[1].shape, BF),
+            pltpu.VMEM(out_shape[2].shape, BF),
+            pltpu.VMEM(out_shape[3].shape, BF),
+            pltpu.VMEM(values.shape, BF),
+            pltpu.VMEM((devices, 128), F32),
+            pltpu.VMEM((devices, 128), F32),
+            pltpu.SemaphoreType.DMA((5,)),
+        ]
+    elif parts:
+        windows, _, _, rows = blocks.shape
+        operands.append(blocks)
+        in_specs.append(pl.BlockSpec(memory_space=pl.ANY))
+    out_specs = [pl.BlockSpec(memory_space=pl.ANY)] * len(out_shape)
     if parts:
-        windows, _, wide, rows = blocks.shape
-        operands.append(blocks)
         out_shape += [
-            jax.ShapeDtypeStruct((H, windows, wide, rows), BF),
+            jax.ShapeDtypeStruct((H, windows, 2 * KD + VD, rows), BF),
             jax.ShapeDtypeStruct((parts - 1, H, windows, KD + VD, rows), BF),
         ]
+        out_specs += [pl.BlockSpec(memory_space=pl.ANY)] * 2
         sizes += [(1,), (H - 1,), (H - 1,), (parts - 1,), (parts - 1,)]
+    if early:
+        out_shape.append(jax.ShapeDtypeStruct((windows * rows, width), BF))
+        out_specs.append(pl.BlockSpec(memory_space=pltpu.VMEM))
     outs = pl.pallas_call(
-        functools.partial(links_kernel, pairs, (len(shards), len(arrays)), parts),
+        functools.partial(links_kernel, pairs, (len(shards), len(arrays)), parts, early),
         out_shape=out_shape,
-        in_specs=[pl.BlockSpec(memory_space=pl.ANY)] * len(operands),
-        out_specs=[pl.BlockSpec(memory_space=pl.ANY)] * len(out_shape),
-        scratch_shapes=[pltpu.SemaphoreType.DMA(size) for size in sizes],
-        compiler_params=pltpu.CompilerParams(collective_id=collective, has_side_effects=True),
+        in_specs=in_specs,
+        out_specs=out_specs,
+        scratch_shapes=[pltpu.SemaphoreType.DMA(size) for size in sizes] + scratch,
+        compiler_params=pltpu.CompilerParams(
+            collective_id=collective, has_side_effects=True, vmem_limit_bytes=60 * 2**20
+        ),
         name=name,
     )(*operands)
     flat = [out.reshape(-1, out.shape[-1]) for out in outs[: len(arrays)]]
@@ -669,7 +851,7 @@
             sent[w, h, 2 * KD :, :] = mixable[h * VD : (h + 1) * VD, span]
 
 
-def project(values, gain, content_bias, weight_keys, weight_values):
+def project(values, gain, content_bias, weight_query, weight_key, weight_value):
     windows, rows, width = values.shape
     steps = H // 2
     return pl.pallas_call(
@@ -684,7 +866,7 @@
             pl.BlockSpec((1, width), lambda i: (0, 0)),
             pl.BlockSpec((1, 1, 2 * KD), lambda i: (i, 0, 0)),
             pl.BlockSpec((width, 2 * KD), lambda i: (0, i)),
-            pl.BlockSpec((width, 2 * KD), lambda i: (0, i + steps)),
+            pl.BlockSpec((width, 2 * KD), lambda i: (0, i)),
             pl.BlockSpec((width, 2 * VD), lambda i: (0, i)),
         ],
         out_specs=(
@@ -698,9 +880,9 @@
         values,
         gain.reshape(1, width),
         content_bias.reshape(steps, 1, 2 * KD),
-        weight_keys,
-        weight_keys,
-        weight_values,
+        weight_query,
+        weight_key,
+        weight_value,
     )
 
 
@@ -1189,15 +1371,35 @@
     return tuple(out)
 
 
-def weight_pairs(width, hidden_width):
-    third = width // 3
-
-    def pieces(array, total, size):
-        return [(array, k, array, k, size) for k in range(0, total, size)]
-
-    first = pieces(0, width, third) + pieces(2, hidden_width, third) + pieces(4, width, third)
-    second = pieces(1, width, third) + pieces(3, width, third // 2) + pieces(5, width, third)
-    return tuple(((a,), (b,)) for a, b in zip(first, second, strict=True))
+def full(array, shards):
+    rows, columns = shards[array].shape
+    return (array, 0, rows, 0, columns)
+
+
+def columns_of_rows(array, rows, first, columns):
+    return (array, 0, rows, first, columns)
+
+
+def weight_pairs(shapes, offset):
+    def pieces(n, parts):
+        rows, columns = shapes[n]
+        if rows % (16 * parts):
+            return [(offset + n, 0, rows, 0, columns)]
+        size = rows // parts
+        return [(offset + n, k * size, size, 0, columns) for k in range(parts)]
+
+    first = pieces(0, 3) + pieces(2, 3) + pieces(4, 3) + pieces(5, 3)
+    second = pieces(1, 3) + pieces(3, 6)
+    steps = max(len(second), 1)
+    spare = len(first) - steps
+    pairs, spot = [], 0
+    for k in range(steps):
+        take = 2 if k >= steps - spare else 1
+        pairs.append((tuple(first[spot : spot + take]), (second[k],)))
+        spot += take
+    if spot < len(first):
+        pairs.append((tuple(first[spot:]), ()))
+    return tuple(pairs)
 
 
 def on_device(
@@ -1257,19 +1459,46 @@
     small_shard = jnp.concatenate(small_rows, axis=0)
     keys_width, values_width = 2 * H * KD, H * VD
     half_hidden, half_width = hidden_width // 2, width // 2
-    small_full, weight_keys, weight_values = use_links(
-        "gather_heads",
-        1,
-        [small_shard, query_weight, key_weight, value_weight],
-        [small_shard.shape, (r, keys_width), (r, values_width)],
+    head_shards = [small_shard, query_weight, key_weight, value_weight]
+    head_pairs = (
+        ((full(0, head_shards), full(1, head_shards)), (full(2, head_shards),)),
+        ((columns_of_rows(3, r, 0, values_width // 2),), (columns_of_rows(3, r, values_width // 2, values_width // 2),)),
+    )
+    shards = [
+        skip_weight,
+        mixing_weight,
+        inner_weight,
+        outer_weight,
+        upsample_weight,
+        point_weight,
+    ]
+    if r % 16 == 0:
         (
-            (((0, 0, 0, 0, 128), (1, 0, 1, 0, 256)), ((2, 0, 1, 512, 256),)),
-            (((1, 256, 1, 256, 256),), ((2, 256, 1, 768, 256),)),
-            (((3, 0, 2, 0, 256),), ((3, 256, 2, 256, 256),)),
-            (((3, 512, 2, 512, 256),), ((3, 768, 2, 768, 256),)),
-            (((3, 1024, 2, 1024, 256),), ((3, 1280, 2, 1280, 256),)),
-        ),
-    )
+            small_full,
+            weight_query,
+            weight_key,
+            weight_value,
+            weight_skip,
+            weight_mixing,
+            weight_inner,
+            weight_outer,
+            weight_upsample,
+            weight_point,
+            mine,
+            other,
+            normed_low,
+        ) = use_links(
+            "gather_weights",
+            1,
+            head_shards + shards,
+            head_pairs + weight_pairs([w.shape for w in shards], len(head_shards)),
+            values=inputs,
+            early=len(head_pairs),
+        )
+    else:
+        small_full, weight_query, weight_key, weight_value = use_links(
+            "gather_heads", 1, head_shards, head_pairs
+        )
     small_full = small_full.reshape((devices,) + small_shard.shape).astype(jnp.float32)
 
     def vector(k):
@@ -1311,31 +1540,22 @@
 
     flat = inputs.reshape(windows * rows, width).astype(jnp.float32)
     _, first_norm_back = jax.vjp(layer_norm, flat, gain_first)
-    normed_low, sent = project(inputs, gain_first, bias_content, weight_keys, weight_values)
-    (
-        weight_skip,
-        weight_mixing,
-        weight_inner,
-        weight_outer,
-        weight_upsample,
-        weight_point,
-        mine,
-        other,
-    ) = use_links(
-        "gather_weights",
-        2,
-        [skip_weight, mixing_weight, inner_weight, outer_weight, upsample_weight, point_weight],
-        [
-            (r, width),
-            (r, width),
-            (r, hidden_width),
-            (outer_weight.shape[0], width),
-            (r, width),
-            (r, width),
-        ],
-        weight_pairs(width, hidden_width),
-        sent,
-    )
+    if r % 16:
+        normed_low, sent = project(
+            inputs, gain_first, bias_content, weight_query, weight_key, weight_value
+        )
+        (
+            weight_skip,
+            weight_mixing,
+            weight_inner,
+            weight_outer,
+            weight_upsample,
+            weight_point,
+            mine,
+            other,
+        ) = use_links(
+            "gather_weights", 2, shards, weight_pairs([w.shape for w in shards], 0), sent
+        )
 
     def by_row(array):
         (array,) = tie(array.transpose(1, 3, 0, 2).reshape(windows * rows, -1))
@@ -1473,8 +1693,10 @@
         axis=1,
     )
     (packed_grad,) = tie(packed_grad)
-    normed_grad = times_transposed(packed_grad[:, :keys_width], weight_keys) + times_transposed(
-        packed_grad[:, keys_width:], weight_values
+    normed_grad = (
+        times_transposed(packed_grad[:, : H * KD], weight_query)
+        + times_transposed(packed_grad[:, H * KD : keys_width], weight_key)
+        + times_transposed(packed_grad[:, keys_width:], weight_value)
     )
     input_part, grad_first = first_norm_back(normed_grad)
     input_grad = (middle_grad + input_part).astype(jnp.bfloat16).reshape(windows, rows, width)

time: 985 us -> 938 us (0.952)
  Pallas kernels: 725 us -> 685 us
    pallas_call x2 -> x1, Pallas kernels: 284 us -> 265 us  [use_links(): pl.pallas_call(functools.partial(links_kernel, pairs, (len(shards), len(a...]
    pallas_call x1, Pallas kernels: 49.5 us -> 35.2 us  [attention_forward(): pl.pallas_call(functools.partial(forward_kernel, parts, per), grid=(windo...]
    pallas_call x3, Pallas kernels: 324 us -> 334 us  [sum_terms(): pl.pallas_call(functools.partial(sums_kernel, plan, None), out_shape=out_...]
    pallas_call x1 -> x0, Pallas kernels: 10.3 us -> none  [project(): pl.pallas_call(project_kernel, grid=(steps,), out_shape=(jax.ShapeDtypeSt...]
    all_to_all x1, starting transfers between devices: 23.9 us -> 13.9 us  [exchange(): lax.all_to_all(array, 'seq', 0, 0, axis_index_groups=groups, tiled=True)]
    unnamed x135 -> x125, local copies, waits for them, and re-layouts: 22.5 us -> 17.1 us
    dot_general x7 -> x8, matrix products: 54.7 us -> 58.6 us  [times_transposed(): lax.dot_general(left, right, (((1,), (1,)), ((), ())), preferred_element_...]
  transfers between devices with their start and end apart: 5 -> 5, of which waited for: 0 -> 0; matrix products, arithmetic and copies ran while one was open for 7% -> 8% of each run, Pallas kernels for 0% -> 0%
where the time goes in v3:
time: 938 us; the launch traced here: 933 us
  Pallas kernels  685 us (73%)
  matrix products  125 us (13%)
  local copies, waits for them, and re-layouts  58.3 us (6%)
  other arithmetic  35.2 us (4%)
  starting transfers between devices  27.1 us (3%)
    pallas_call x3, Pallas kernels, sum_terms(): pl.pallas_call(functools.partial(sums_kernel, plan, None), out_shape=out_...  334 us
    pallas_call x1, Pallas kernels, use_links(): pl.pallas_call(functools.partial(links_kernel, pairs, (len(shards), len(a...  265 us
    dot_general x8, matrix products, times_transposed(): lax.dot_general(left, right, (((1,), (1,)), ((), ())), preferred_element_...  58.6 us
    dot_general x6, matrix products, matmul(): return jnp.dot(left, right, preferred_element_type=jnp.float32)  55 us
    pallas_call x1, Pallas kernels, attention_backward(): pl.pallas_call(functools.partial(backward_kernel, parts, per), grid=(wind...  50.7 us
    pallas_call x1, Pallas kernels, attention_forward(): pl.pallas_call(functools.partial(forward_kernel, parts, per), grid=(windo...  35.2 us
  transfers between devices with their start and end apart: 5, of which 0 were waited for; matrix products, arithmetic and copies ran while one was open for 8% of the time, Pallas kernels for 0%

profile of v3, /device:TPU:1, one launch (start us, length us, event | category | flops | bytes accessed | tf_op | source)
XLA Modules:
  0.0 932.9 jit_solution(6180225737516579154)
XLA Ops:
  10.2 1.8 concatenate.52.refs_0_
  12.0 264.8 %gather_weights.1 = (bf16[2,4,2,2,32,128]{5,4,3,2,1,0:T(8,128)(2,1)}, bf16[2,4,2,2,48,512]{5,4,3,2,1,0:T(8,128)(2,1)}, bf16[2,4,2,2,48,512]{5,4,3,2,1,0:T(8,128)...) custom-call(bf16[32,128]{1,0:T(8,128)(2,1)} %concatenate.52.refs_0_,, ...), custom_call_target="tpu_custom_call" | custom-call | tf_op jit(solution)/shard_map/gather_weights/pallas_call | solution.py:813
  282.2 35.2 %attention_forward.1 = (bf16[8,2,192,256]{3,2,1,0:T(8,128)(2,1)}, f32[8,2,192,256]{3,2,1,0:T(8,128)}, f32[8,2,8,256]{3,2,1,0:T(8,128)}) custom-call(s32[3]{0:T(128)} %pad_add_fusion.info, f32[16,1]{1,0:T(8,128)} %fusion.38.rates_ref, f32[1,128]{1,0:T(1,128)} %select_maximum_fusion.lanes_ref, f32[64,1]{1,0:T(8,128)} %copy.91.bias_ref, f32[32,64]{1,0:T(8,128)} %bitcast.194, ...), custom_call_target="tpu_custom_call" | custom-call | flops 9663676416 | bytes 20000000 | tf_op jit(solution)/shard_map/attention_forward/pallas_call | solution.py:436
  317.4 13.9 %all-to-all-start = ((bf16[8,2,192,256]{3,2,1,0:T(8,128)(2,1)}), bf16[8,2,192,256]{3,2,1,0:T(8,128)(2,1)S(1)}, u32[]{:S(2)}, u32[]{:S(2)}) async-start(bf16[8,2,192,256]{3,2,1,0:T(8,128)(2,1)} %get-tuple-element.56), calls=%async_computation | async-start | bytes 3145728 | tf_op jit(solution)/shard_map/all_to_all | solution.py:1536
  332.0 2.2 broadcast_multiply_fusion
  334.2 8.8 convolution_convert_fusion.1
  343.0 1.7 copy-done.7
  344.7 5.6 collective-permute-start.2
  350.4 1.9 collective-permute-start.3
  352.3 1.4 slice_reduce_fusion.2
  358.9 2.8 maximum_convert_fusion.1
  361.8 3.4 fusion.64
  365.9 4.2 convolution_convert_fusion.4
  370.1 8.8 convolution_convert_fusion
  378.9 1.6 copy.92
  380.8 4.9 fusion.75
  387.0 21.9 %multiply_convert_fusion.1 = (bf16[512,3072]{1,0:T(8,128)(2,1)S(1)}, f32[512,3072]{1,0:T(8,128)}, f32[512,3072]{1,0:T(8,128)}) fusion(f32[3072]{0:T(1024)S(1)} %add.211, bf16[512,1536]{1,0:T(8,128)(2,1)S(1)} %multiply_convert_fusion.3.refs_0_, bf16[1536,3072]{1,0:T(8,128)(2,1)S(1)} %bitcast.208), kind=kOutput, calls=%fused_computation.19 | convolution fusion | flops 4935647232 | bytes 26750976 | tf_op jit(solution)/shard_map/dot_general | solution.py:50
  409.0 5.2 fusion.76
  415.6 10.3 %multiply_reduce_fusion = (f32[1536]{0:T(1024)S(1)}, f32[512]{0:T(512)S(1)}, f32[512,1536]{1,0:T(8,128)S(1)}, f32[512,1536]{1,0:T(8,128)S(1)}) fusion(f32[512,1536]{1,0:T(8,128)S(1)} %get-tuple-element.210, f32[512]{0:T(512)S(1)} %fusion.53, f32[512]{0:T(512)S(1)} %broadcast_multiply_fusion.2, f32[1536]{0:T(1024)S(1)} %mul.384, ...), kind=kOutput, calls=%fused_computation.49 | convolution fusion | flops 2478045184 | bytes 15747072 | tf_op jit(solution)/shard_map/dot_general | solution.py:54
  425.9 1.7 fusion.67
  428.7 6.9 fusion.77
  435.7 7.3 fusion.6
  443.0 3.6 collective-permute-start
  446.6 1.9 collective-permute-start.1
  448.8 13.1 %convert_reduce_fusion = (f32[3072]{0:T(1024)S(1)}, bf16[512,3072]{1,0:T(8,128)(2,1)S(1)}) fusion(f32[512,3072]{1,0:T(8,128)} %get-tuple-element.180, f32[512,3072]{1,0:T(8,128)} %get-tuple-element.208, f32[3072]{0:T(1024)S(1)} %add.211, bf16[512,1536]{1,0:T(8,128)(2,1)S(1)} %add_convert_fusion.3.refs_3_, bf16[3072,1536]{1,0:T(8,128)(2,1)} %bitcast.209), kind=kOutput, calls=%fused_computation.15 | convolution fusion | flops 4858573824 | bytes 26763264 | tf_op jit(solution)/shard_map/dot_general | solution.py:54
  461.9 10.4 %multiply_reduce_fusion.1 = (f32[1536]{0:T(1024)S(1)}, f32[512]{0:T(512)S(1)}, f32[512,1536]{1,0:T(8,128)}) fusion(f32[512,1536]{1,0:T(8,128)S(1)} %get-tuple-element.207, f32[512]{0:T(512)S(1)} %fusion.52, f32[512]{0:T(512)S(1)} %broadcast_multiply_fusion.3, f32[1536]{0:T(1024)S(1)} %mul.375, bf16[512,3072]{1,0:T(8,128)(2,1)S(1)} %get-tuple-element.172.refs_1_, ...), kind=kOutput, calls=%fused_computation.50 | convolution fusion | flops 4837341184 | bytes 18892800 | tf_op jit(solution)/shard_map/dot_general | solution.py:54
  472.3 2.9 fusion.66
  476.9 6.6 fusion.20
  483.5 1.6 copy.97.refs_2_
  485.1 2.7 copy.95
  490.0 4.7 fusion.1
  494.7 146.6 %sum_upper.1 = (f32[48,1536]{1,0:T(8,128)}, f32[96,1536]{1,0:T(8,128)}, f32[48,1536]{1,0:T(8,128)}, f32[48,1536]{1,0:T(8,128)}, bf16[8,2,192,256]{3,2,1,0:T(8,128)(2,1)}) custom-call(bf16[1024,1536]{1,0:T(8,128)(2,1)} %bitcast.162, bf16[1024,1536]{1,0:T(8,128)(2,1)} %bitcast.161, bf16[512,3072]{1,0:T(8,128)(2,1)} %copy-done.19, ...), custom_call_target="tpu_custom_call" | custom-call | tf_op jit(solution)/shard_map/sum_upper/pallas_call | solution.py:1352
  641.3 50.7 %attention_backward.1 = (bf16[8,2,64,256]{3,2,1,0:T(8,128)(2,1)}, bf16[8,2,256,256]{3,2,1,0:T(8,128)(2,1)}, bf16[1,8,2,256,256]{4,3,2,1,0:T(8,128)(2,1)}, f32[2,64,1]{2,1,0:T(8,128)}, f32[64,32]{1,0:T(8,128)}) custom-call(s32[3]{0:T(128)} %pad_add_fusion.info, f32[16,1]{1,0:T(8,128)} %fusion.38.rates_ref, f32[1,128]{1,0:T(1,128)} %select_maximum_fusion.lanes_ref, ...), custom_call_target="tpu_custom_call" | custom-call | flops 32212254720 | bytes 20000000 | tf_op jit(solution)/shard_map/attention_backward/pallas_call | solution.py:478
  692.0 130.6 %sum_lower.1 = (f32[48,3072]{1,0:T(8,128)}, f32[48,1536]{1,0:T(8,128)}, bf16[8,2,320,256]{3,2,1,0:T(8,128)(2,1)}) custom-call(bf16[512,1536]{1,0:T(8,128)(2,1)} %copy-done.12, bf16[512,3072]{1,0:T(8,128)(2,1)} %copy-done.17, bf16[512,1536]{1,0:T(8,128)(2,1)} %copy.97.refs_2_, bf16[512,1536]{1,0:T(8,128)(2,1)} %copy-done.13, ...), custom_call_target="tpu_custom_call" | custom-call | tf_op jit(solution)/shard_map/sum_lower/pallas_call | solution.py:1352
  822.7 1.5 slice_bitcast_fusion
  824.2 2.3 slice_bitcast_fusion.2
  827.2 1.6 copy.100
  829.8 1.6 copy.98
  832.9 1.9 copy-done.22
  835.8 4.9 fusion.21
  840.8 1.5 multiply_reduce_fusion.3
  842.3 1.6 copy-done.4
  846.6 56.9 %sum_heads.1 = (f32[48,2560]{1,0:T(8,128)}, f32[8,128]{1,0:T(8,128)}) custom-call(bf16[512,1536]{1,0:T(8,128)(2,1)} %get-tuple-element.73.refs_0_, bf16[512,2560]{1,0:T(8,128)(2,1)} %copy-done.6, f32[32,8,128]{2,1,0:T(8,128)} %bitcast.187), custom_call_target="tpu_custom_call" | custom-call | tf_op jit(solution)/shard_map/sum_heads/pallas_call | solution.py:1352
  903.6 1.7 slice.172
  905.3 1.6 fusion.72
  908.4 1.5 fusion.73
  913.8 5.5 add_convert_fusion.2
  919.3 8.8 multiply_convert_fusion
  (237 shorter events, 46.3 us)
Async XLA Ops:
  0.7 281.0 %copy-start.44 = (s32[2]{0:T(128)S(1)}, s32[2]{0:T(128)}, u32[]{:S(2)}) copy-start(s32[2]{0:T(128)} %param.25) | copy-start | bytes 28
  317.4 61.5 %all-to-all-start = ((bf16[8,2,192,256]{3,2,1,0:T(8,128)(2,1)}), bf16[8,2,192,256]{3,2,1,0:T(8,128)(2,1)S(1)}, u32[]{:S(2)}, u32[]{:S(2)}) async-start(bf16[8,2,192,256]{3,2,1,0:T(8,128)(2,1)} %get-tuple-element.56), calls=%async_computation | async-start | bytes 3145728 | tf_op jit(solution)/shard_map/all_to_all | solution.py:1536
  334.2 8.8 copy-start.9
  334.2 21.5 %copy-start = (bf16[2,256,1536]{2,1,0:T(8,128)(2,1)S(1)}, bf16[2,256,1536]{2,1,0:T(8,128)(2,1)}, u32[]{:S(2)}) copy-start(bf16[2,256,1536]{2,1,0:T(8,128)(2,1)} %refs_10_.1) | copy-start | bytes 4718596
  344.7 14.2 %collective-permute-start.2 = (bf16[2,1,1536]{2,1,0:T(2,128)(2,1)S(1)}, bf16[2,1,1536]{2,1,0:T(2,128)(2,1)S(1)}, u32[]{:S(2)}, u32[]{:S(2)}) collective-permute-start(bf16[2,1,1536]{2,1,0:T(2,128)(2,1)S(1)} %get-tuple-element.187), channel_id=1, source_target_pairs={{0,1},{1,2},{2,3},{3,4},{4,5},{5,6},{6,7},{7,8},{8,9},{9,10},{10,1... | collective-permute-start | bytes 18440 | tf_op jit(solution)/shard_map/ppermute | solution.py:28
  350.4 8.6 collective-permute-start.3
  356.1 5.7 copy-start.32
  356.1 5.7 copy-start.34
  356.1 5.7 copy-start.36
  365.9 4.2 copy-start.11
  380.8 5.9 slice-start
  380.8 5.9 slice-start.1
  386.2 22.7 %slice-start.3 = ((s8[9437184]{0:T(1024)(128)(4,1)}), s8[4194304]{0:T(1024)(128)(4,1)S(1)}, s32[]{:S(2)}) async-start(s8[9437184]{0:T(1024)(128)(4,1)} %bitcast.210), calls=%async_computation.4 | async-start | bytes 8388608
  386.7 22.2 %copy-start.12 = (bf16[512,1536]{1,0:T(8,128)(2,1)}, bf16[512,1536]{1,0:T(8,128)(2,1)S(1)}, u32[]{:S(2)}) copy-start(bf16[512,1536]{1,0:T(8,128)(2,1)S(1)} %multiply_convert_fusion.3.refs_0_) | copy-start | bytes 4718596
  387.0 22.0 %slice-start.4 = ((s8[9437184]{0:T(1024)(128)(4,1)}), s8[4194304]{0:T(1024)(128)(4,1)S(1)}, s32[]{:S(2)}) async-start(s8[9437184]{0:T(1024)(128)(4,1)} %bitcast.210), calls=%async_computation.5 | async-start | bytes 8388608
  387.0 22.0 %slice-start.5 = ((s8[9437184]{0:T(1024)(128)(4,1)}), s8[1048576]{0:T(1024)(128)(4,1)S(1)}, s32[]{:S(2)}) async-start(s8[9437184]{0:T(1024)(128)(4,1)} %bitcast.210), calls=%async_computation.6 | async-start | bytes 2097152
  408.9 5.3 copy-start.19
  408.9 5.7 slice-start.8
  409.0 5.7 slice-start.9
  427.6 47.6 %copy-start.2 = (f32[512,1536]{1,0:T(8,128)}, f32[512,1536]{1,0:T(8,128)S(1)}, u32[]{:S(2)}) copy-start(f32[512,1536]{1,0:T(8,128)S(1)} %get-tuple-element.176) | copy-start | bytes 9437188
  427.6 8.1 slice-start.6
  428.7 6.9 copy-start.18
  428.7 6.9 slice-start.7
  442.9 5.6 copy-start.15
  443.0 45.2 %collective-permute-start = (bf16[2,1,1536]{2,1,0:T(2,128)(2,1)S(1)}, bf16[2,1,1536]{2,1,0:T(2,128)(2,1)S(1)}, u32[]{:S(2)}, u32[]{:S(2)}) collective-permute-start(bf16[2,1,1536]{2,1,0:T(2,128)(2,1)S(1)} %get-tuple-element.185), channel_id=1, source_target_pairs={{0,1},{1,2},{2,3},{3,4},{4,5},{5,6},{6,7},{7,8},{8,9},{9,10},{10,1... | collective-permute-start | bytes 18440 | tf_op jit(solution)/shard_map/ppermute | solution.py:28
  446.6 41.6 %collective-permute-start.1 = (bf16[2,1,1536]{2,1,0:T(2,128)(2,1)S(1)}, bf16[2,1,1536]{2,1,0:T(2,128)(2,1)S(1)}, u32[]{:S(2)}, u32[]{:S(2)}) collective-permute-start(bf16[2,1,1536]{2,1,0:T(2,128)(2,1)S(1)} %get-tuple-element.186), channel_id=1, source_target_pairs={{1,0},{2,1},{3,2},{4,3},{5,4},{6,5},{7,6},{8,7},{9,8},{10,9},{11,1... | collective-permute-start | bytes 18440 | tf_op jit(solution)/shard_map/ppermute | solution.py:29
  448.8 13.1 %copy-start.14 = (bf16[512,1536]{1,0:T(8,128)(2,1)}, bf16[512,1536]{1,0:T(8,128)(2,1)S(1)}, u32[]{:S(2)}) copy-start(bf16[512,1536]{1,0:T(8,128)(2,1)S(1)} %add_convert_fusion.3.refs_3_) | copy-start | bytes 4718596
  461.9 10.4 %copy-start.17 = (bf16[512,3072]{1,0:T(8,128)(2,1)}, bf16[512,3072]{1,0:T(8,128)(2,1)S(1)}, u32[]{:S(2)}) copy-start(bf16[512,3072]{1,0:T(8,128)(2,1)S(1)} %get-tuple-element.172.refs_1_) | copy-start | bytes 9437188
  476.9 6.6 copy-start.13
  485.1 3.1 copy-start.16
  829.8 2.0 copy-start.20
  832.7 2.1 copy-start.22
  832.8 7.9 copy-start.6
  835.8 5.0 copy-start.1
  835.8 5.0 copy-start.23
  835.8 5.0 copy-start.31
  835.8 5.0 copy-start.41
  842.2 3.1 copy-start.40
  842.2 3.2 copy-start.39
  842.3 3.5 copy-start.38
  913.8 5.5 copy-start.10
  913.8 5.5 copy-start.43
  919.3 8.9 copy-start.30
  919.3 9.6 %copy-start.26 = (f32[48,3072]{1,0:T(8,128)S(1)}, f32[48,3072]{1,0:T(8,128)}, u32[]{:S(2)}) copy-start(f32[48,3072]{1,0:T(8,128)} %get-tuple-element.250) | copy-start | bytes 1769476
  919.3 10.4 %copy-start.25 = (f32[96,1536]{1,0:T(8,128)S(1)}, f32[96,1536]{1,0:T(8,128)}, u32[]{:S(2)}) copy-start(f32[96,1536]{1,0:T(8,128)} %get-tuple-element.252) | copy-start | bytes 1769476
  928.2 2.4 copy-start.29
  928.2 3.1 copy-start.28
  928.2 3.8 copy-start.27
  (12 other events, 18.8 us)

commit v4 on v3

--- a/solution.py
+++ b/solution.py
@@ -525,6 +525,186 @@
 MESH = pl.DeviceIdType.MESH
 
 
+def upper_work(here, lengths, cotangent, skip_input, outs, gathered, scratch, remote, neighbours):
+    out_grad_o, conv_o, joined_o, lifted_o, third_o, skip_grad_o, skip_part_o, bias_o = outs
+    (
+        table_rows,
+        lines,
+        w_point,
+        w_skip,
+        w_upsample,
+        grad_v,
+        skip_v,
+        conv_v,
+        joined_v,
+        lifted_v,
+        part_v,
+        halo_before,
+        halo_after,
+        sem,
+        halo_sem,
+    ) = scratch
+    dp, seq = here
+    windows, fine, width = grad_v.shape
+    rows = fine // 2
+    before, after = neighbours
+
+    def load(source, target, n):
+        return pltpu.make_async_copy(source, target, sem.at[n])
+
+    point_load = load(gathered[9], w_point, 0)
+    skip_load = load(gathered[4], w_skip, 1)
+    upsample_load = load(gathered[8], w_upsample, 2)
+    grad_load = load(cotangent, grad_v, 3)
+    input_load = load(skip_input, skip_v, 4)
+    grad_load.start()
+    input_load.start()
+    stores = {
+        "out_grad": load(grad_v, out_grad_o, 5),
+        "conv": load(conv_v, conv_o, 6),
+        "joined": load(joined_v, joined_o, 7),
+        "lifted": load(lifted_v, lifted_o, 8),
+        "skip": load(skip_v, skip_grad_o, 9),
+    }
+
+    def against(x, table):
+        return lax.dot_general(
+            x, table[...].reshape(width, width), (((1,), (1,)), ((), ())), preferred_element_type=F32
+        )
+
+    def halo_copies():
+        out = []
+        for w in range(windows):
+            out.append(
+                remote(
+                    conv_v.at[w, pl.ds(fine - 16, 16)],
+                    halo_before.at[w],
+                    halo_sem.at[0, w],
+                    halo_sem.at[1, w],
+                    after,
+                )
+            )
+            out.append(
+                remote(
+                    conv_v.at[w, pl.ds(0, 16)],
+                    halo_after.at[w],
+                    halo_sem.at[2, w],
+                    halo_sem.at[3, w],
+                    before,
+                )
+            )
+        return out
+
+    def conv_grad(w):
+        if w == 0:
+            point_load.start()
+            grad_load.wait()
+            point_load.wait()
+        length = lengths[w]
+
+        @pl.loop(0, fine // 256)
+        def _(k):
+            at = pl.ds(pl.multiple_of(k * 256, 256), 256)
+            bin_ = seq * rows + lax.div(
+                k * 256 + lax.broadcasted_iota(jnp.int32, (256, width), 0), 2
+            )
+            grad = jnp.where(bin_ < length, grad_v[w, at, :].astype(F32), 0.0).astype(BF)
+            grad_v[w, at, :] = grad
+            conv_v[w, at, :] = against(grad, w_point).astype(BF)
+
+        if w == windows - 1:
+            stores["out_grad"].start()
+            stores["conv"].start()
+            for copy in halo_copies():
+                copy.start()
+
+    def skip_part(w):
+        if w == 0:
+            skip_load.start()
+            input_load.wait()
+            skip_load.wait()
+
+        @pl.loop(0, fine // 256)
+        def _(k):
+            at = pl.ds(pl.multiple_of(k * 256, 256), 256)
+            made = dot(skip_v[w, at, :], w_skip[...].reshape(width, width)) + lines[0:1, :]
+            part_v[...] = made
+            store = load(part_v, skip_part_o.at[w, at], 10)
+            store.start()
+            store.wait()
+
+    def joined_grad():
+        for copy in halo_copies():
+            copy.wait_recv()
+        total = jnp.zeros((1, width), F32)
+        tap = [lines[n : n + 1, :] for n in (1, 2, 3)]
+        tile = 64
+        for w in range(windows):
+            first = halo_before[w].astype(F32)[15:16, :]
+            first = jnp.where(seq == 0, 0.0, first)
+            last = halo_after[w].astype(F32)[0:1, :]
+            last = jnp.where(seq == lax.axis_size("seq") - 1, 0.0, last)
+            for k in range(fine // tile):
+                at = slice(k * tile, (k + 1) * tile)
+                here_rows = conv_v[w, at, :].astype(F32)
+                up = first if k == 0 else conv_v[w, k * tile - 16 : k * tile, :].astype(F32)[15:16, :]
+                down = (
+                    last
+                    if k == fine // tile - 1
+                    else conv_v[w, (k + 1) * tile : (k + 1) * tile + 16, :].astype(F32)[0:1, :]
+                )
+                index = lax.broadcasted_iota(jnp.int32, here_rows.shape, 0)
+                earlier = jnp.where(index == 0, up, pltpu.roll(here_rows, 1, 0))
+                later = jnp.where(index == tile - 1, down, pltpu.roll(here_rows, tile - 1, 0))
+                made = later * tap[0] + here_rows * tap[1] + earlier * tap[2]
+                total = total + jnp.sum(made, axis=0, keepdims=True)
+                joined_v[w, at, :] = made.astype(BF)
+        bias_o[...] = total
+        stores["joined"].start()
+        pair = lax.div(lax.broadcasted_iota(jnp.int32, (rows, fine), 1), 2)
+        twice = (pair == lax.broadcasted_iota(jnp.int32, (rows, fine), 0)).astype(F32).astype(BF)
+        for w in range(windows):
+            lifted_v[w * rows : (w + 1) * rows, :] = dot(twice, joined_v[w]).astype(BF)
+        stores["lifted"].start()
+
+    def skip_grad(w):
+        @pl.loop(0, fine // 256)
+        def _(k):
+            at = pl.ds(pl.multiple_of(k * 256, 256), 256)
+            skip_v[w, at, :] = against(joined_v[w, at, :], w_skip).astype(BF)
+
+        if w == windows - 1:
+            stores["skip"].start()
+
+    def third_grad():
+        upsample_load.start()
+        upsample_load.wait()
+
+        @pl.loop(0, windows * rows // 256)
+        def _(k):
+            at = pl.ds(pl.multiple_of(k * 256, 256), 256)
+            part_v[...] = against(lifted_v[at, :], w_upsample)
+            store = load(part_v, third_o.at[at], 10)
+            store.start()
+            store.wait()
+
+    def finish():
+        for store in stores.values():
+            store.wait()
+        for copy in halo_copies():
+            copy.wait_send()
+
+    jobs = {
+        9: [(9, functools.partial(conv_grad, 0))],
+        10: [(None, functools.partial(conv_grad, 1))],
+        11: [(4, functools.partial(skip_part, 0)), (None, functools.partial(skip_part, 1))],
+        12: [(None, joined_grad)],
+        13: [(None, functools.partial(skip_grad, 0)), (None, functools.partial(skip_grad, 1))],
+        14: [(8, third_grad)],
+    }
+    return {"rows": table_rows, "lines": lines, "jobs": jobs, "finish": finish}
+
+
 def links_kernel(pairs, counts, parts, early, *refs):
     n_in, n_out = counts
     refs = list(refs)
@@ -536,6 +716,7 @@
     refs_in = take(n_in)
     if early:
         values, spread_gain, pick_gain, spread_bias, pick_bias = take(5)
+        lengths, cotangent, skip_input = take(3)
     elif parts:
         (blocks,) = take(1)
     refs_out = take(n_out)
@@ -543,6 +724,7 @@
         mine, other = take(2)
     if early:
         (normed,) = take(1)
+        upper_out = take(8)
     local_sem, send_hi, recv_hi, send_y, recv_y, send_dp, recv_dp, send_c, recv_c = take(9)
     dp, seq = lax.axis_index("dp"), lax.axis_index("seq")
     ndp, nhi = refs_out[0].shape[:2]
@@ -563,6 +745,11 @@
         head_peers = [(dp, h * parts + part) for h in head_of]
         part_peers = [(dp, head * parts + slot_part(part, k, parts)) for k in range(1, parts)]
         everyone = everyone + head_peers + part_peers
+    if early:
+        nseq = nhi * 4
+        after = (dp, lax.rem(seq + 1, nseq))
+        before = (dp, lax.rem(seq + nseq - 1, nseq))
+        everyone = everyone + [after, before]
 
     barrier = pltpu.get_barrier_semaphore()
     for peer in everyone:
@@ -639,6 +826,9 @@
         small_v, query_v, key_v, values_v, inputs_v, gain_v, bias_v, load_sem = take(8)
         inputs_load = pltpu.make_async_copy(values, inputs_v, load_sem.at[0])
         inputs_load.start()
+        upper = upper_work(
+            (dp, seq), lengths, cotangent, skip_input, upper_out, refs_out, take(15), remote, (before, after)
+        )
 
     def make_blocks():
         loads = [
@@ -663,11 +853,15 @@
             ].astype(F32)
             gain_v[pl.ds(k, 1), :] = rows[0:1, :]
             bias_v[pl.ds(k, 1), :] = rows[1:2, :]
+            for n in range(4):
+                upper["rows"][n, pl.ds(k, 1), :] = rows[7 + n : 8 + n, :]
 
         def line_up(table, spread, pick):
             return jnp.sum(dot(table[...].astype(BF), spread[...]) * pick[...], axis=0, keepdims=True)
 
         gain = line_up(gain_v, spread_gain, pick_gain)
+        for n in range(4):
+            upper["lines"][n : n + 1, :] = line_up(upper["rows"].at[n], spread_gain, pick_gain)
         bias = line_up(bias_v, spread_bias, pick_bias)
         windows, rows = inputs_v.shape[:2]
         for w in range(windows):
@@ -707,6 +901,7 @@
         for stage in (3, 2, 1):
             events.setdefault(spot + gap * (stage - 1), []).append((stage, spot))
     made_at = early + 2 if early else 0
+    waited = []
     heads_at = [made_at + k for k in range(len(head_copies))]
     for step in range(min(ahead, len(pairs))):
         launch(step)
@@ -731,6 +926,14 @@
             make_blocks()
         if step in heads_at:
             head_copies[heads_at.index(step)].start()
+        if early:
+            for need, job in upper["jobs"].get(step, []):
+                for chunk in everything:
+                    if chunk[2] == need:
+                        for copy in copies(chunk, 3):
+                            copy.wait_recv()
+                        waited.append(chunk)
+                job()
     if parts:
         head_own.wait()
         for copy in head_copies:
@@ -739,8 +942,11 @@
             copy.start()
     for group in step_chunks[early:]:
         for chunk in group:
-            for copy in copies(chunk, 3):
-                copy.wait_recv()
+            if chunk not in waited:
+                for copy in copies(chunk, 3):
+                    copy.wait_recv()
+    if early:
+        upper["finish"]()
     if parts:
         for copy in part_copies:
             copy.wait_recv()
@@ -761,7 +967,7 @@
     return spread, pick
 
 
-def use_links(name, collective, shards, pairs, blocks=None, values=None, early=0):
+def use_links(name, collective, shards, pairs, blocks=None, values=None, early=0, upper=()):
     ndp, nseq = lax.axis_size("dp"), lax.axis_size("seq")
     nhi, devices = nseq // 4, ndp * nseq
     parts = nseq // H if blocks is not None or early else 0
@@ -784,6 +990,10 @@
         in_specs += [pl.BlockSpec(memory_space=pl.ANY)] + [
             pl.BlockSpec(memory_space=pltpu.VMEM)
         ] * 4
+        operands += list(upper)
+        in_specs += [pl.BlockSpec(memory_space=pltpu.SMEM)] + [
+            pl.BlockSpec(memory_space=pl.ANY)
+        ] * 2
         scratch = [
             pltpu.VMEM((windows, H, 2 * KD + VD, rows), BF),
             pltpu.VMEM(out_shape[0].shape, BF),
@@ -794,6 +1004,16 @@
             pltpu.VMEM((devices, 128), F32),
             pltpu.VMEM((devices, 128), F32),
             pltpu.SemaphoreType.DMA((5,)),
+            pltpu.VMEM((4, devices, 128), F32),
+            pltpu.VMEM((8, width), F32),
+            *[pltpu.VMEM((ndp, nhi, 2, 2, width // devices, width), BF)] * 3,
+            *[pltpu.VMEM((windows, 2 * rows, width), BF)] * 4,
+            pltpu.VMEM((windows * rows, width), BF),
+            pltpu.VMEM((256, width), F32),
+            pltpu.VMEM((windows, 16, width), BF),
+            pltpu.VMEM((windows, 16, width), BF),
+            pltpu.SemaphoreType.DMA((11,)),
+            pltpu.SemaphoreType.DMA((4, windows)),
         ]
     elif parts:
         windows, _, _, rows = blocks.shape
@@ -809,6 +1029,22 @@
         sizes += [(1,), (H - 1,), (H - 1,), (parts - 1,), (parts - 1,)]
     if early:
         out_shape.append(jax.ShapeDtypeStruct((windows * rows, width), BF))
+        out_specs.append(pl.BlockSpec(memory_space=pltpu.VMEM))
+        fine, coarse = (windows, 2 * rows, width), (windows * rows, width)
+        out_shape += [
+            jax.ShapeDtypeStruct(*s)
+            for s in (
+                (fine, BF),
+                (fine, BF),
+                (fine, BF),
+                (coarse, BF),
+                (coarse, F32),
+                (fine, BF),
+                (fine, F32),
+                ((1, width), F32),
+            )
+        ]
+        out_specs += [pl.BlockSpec(memory_space=pl.ANY)] * 7
         out_specs.append(pl.BlockSpec(memory_space=pltpu.VMEM))
     outs = pl.pallas_call(
         functools.partial(links_kernel, pairs, (len(shards), len(arrays)), parts, early),
@@ -887,19 +1123,27 @@
 
 
 def sums_kernel(plan, refs_spec, *refs):
-    groups, n_terms, mode, parts, n_small, made_here = plan
+    groups, n_terms, mode, parts, n_small, made_here, late, masked = plan
     refs = list(refs)
 
     def take(count):
         out, refs[:count] = refs[:count], []
         return out
 
-    terms = take(n_terms * (2 if made_here else 1))
-    head_in = take({None: 0, "in": 1, "out": 3}[mode])
+    terms = take(n_terms * (2 if made_here else 1) - (1 if late else 0))
+    head_in = take({None: 0, "in": 1, "back": 1, "out": 3}[mode])
     small_in = take(1 if n_small else 0)
+    if late:
+        w_query, w_key, w_value, values, middle_grad, gain, spread, pick = take(8)
+    if masked:
+        lengths, w_masked = take(2)
     outs = take(n_terms)
-    head_out = take(1 if mode else 0)
+    head_out = take(0 if late or not mode else 1)
     small_out = take(1 if n_small else 0)
+    if late:
+        (input_grad,) = take(1)
+    if masked:
+        (masked_o,) = take(1)
     own, arrived, result, back, hop1, hop2, line = [], [], [], [], [], [], []
     flat = [(side, unit) for group in groups for side in (0, 1) for unit in group[side]]
     count = len(flat)
@@ -912,7 +1156,7 @@
     back = take(count)
     if made_here:
         slots = min(2, n_terms)
-        lefts, rights, turned = take(slots), take(slots), take(slots)
+        lefts, rights, turned = take(1), take(slots), take(slots)
         going, left_sem, right_sem = take(3)
     load_sem, c_send, c_recv, s1, r1, s2, r2, s3, r3, s4, r4 = take(11)
     dp, seq = lax.axis_index("dp"), lax.axis_index("seq")
@@ -1079,21 +1323,37 @@
         side = numbers[step].index(n)
         return going.at[step % 2, side, :, :, :, :, pl.ds(0, unit[2]), pl.ds(0, unit[4])]
 
-    def fetch(array):
-        left, right = terms[2 * array], terms[2 * array + 1]
-        tokens, slot = left.shape[0], array % 2
-        return [
-            pltpu.make_async_copy(
-                left,
-                lefts[slot].at[pl.ds(0, tokens), pl.ds(0, left.shape[1])],
-                left_sem.at[array],
-            ),
-            pltpu.make_async_copy(
-                right,
-                rights[slot].at[pl.ds(0, tokens), pl.ds(0, right.shape[1])],
-                right_sem.at[array],
-            ),
-        ]
+    def fetch_left(array):
+        left = terms[2 * array]
+        return pltpu.make_async_copy(
+            left,
+            lefts[0].at[pl.ds(0, left.shape[0]), pl.ds(0, left.shape[1])],
+            left_sem.at[array],
+        )
+
+    def fetch_right(array):
+        right = terms[2 * array + 1]
+        return pltpu.make_async_copy(
+            right,
+            rights[array % 2].at[pl.ds(0, right.shape[0]), pl.ds(0, right.shape[1])],
+            right_sem.at[array],
+        )
+
+    def arrive():
+        for copy in head_own:
+            copy.wait()
+        for copy in head_copies:
+            copy.wait_recv()
+        packed = rights[(n_terms - 1) % 2]
+        windows, rows = gathered.shape[1], gathered.shape[3]
+        for w in range(windows):
+            for pair in range(H // 2):
+                for first, size, start in ((0, KD, 0), (KD, KD, H * KD), (2 * KD, VD, 2 * H * KD)):
+                    both = jnp.concatenate(
+                        [gathered[2 * pair + h, w, first : first + size, :] for h in range(2)], axis=0
+                    )
+                    at = start + pair * 2 * size
+                    packed[w * rows : (w + 1) * rows, at : at + 2 * size] = both.T
 
     def make(step):
         units = [flat[n][1] for n in numbers[step]]
@@ -1102,18 +1362,23 @@
         left = terms[2 * array]
         tokens, slot = left.shape[0], array % 2
         if step == 0 or flat[numbers[step - 1][0]][1][0] != array:
-            for copy in fetch(array):
-                copy.wait()
-            if array >= 1 and array + 1 < n_terms:
-                for copy in fetch(array + 1):
-                    copy.start()
+            fetch_left(array).wait()
 
             @pl.loop(0, left.shape[1] // 256)
             def _(k):
                 spot = pl.multiple_of(k * 256, 256)
-                turned[slot][pl.ds(spot, 256), pl.ds(0, tokens)] = lefts[slot][
+                turned[slot][pl.ds(spot, 256), pl.ds(0, tokens)] = lefts[0][
                     pl.ds(0, tokens), pl.ds(spot, 256)
                 ].T
+
+            if array + 1 < n_terms:
+                fetch_left(array + 1).start()
+                if array >= 1 and not (late and array + 1 == n_terms - 1):
+                    fetch_right(array + 1).start()
+            if late and array == n_terms - 1:
+                arrive()
+            else:
+                fetch_right(array).wait()
 
         if step >= 2:
             for n in numbers[step - 2]:
@@ -1149,26 +1414,31 @@
                     copy.start()
 
     if made_here:
+        fetch_left(0).start()
         for array in range(min(2, n_terms)):
-            for copy in fetch(array):
-                copy.start()
-
-    if mode == "in":
+            if not (late and array == n_terms - 1):
+                fetch_right(array).start()
+
+    if mode in ("in", "back"):
         head_send, head_recv, head_local = take(3)
         blocks, gathered = head_in[0], head_out[0]
+
+        def block_of(h):
+            return blocks.at[:, h] if mode == "in" else blocks.at[h]
+
         head_copies = [
-            remote(blocks.at[:, h], gathered.at[head], head_send.at[k], head_recv.at[k], p)
+            remote(block_of(h), gathered.at[head], head_send.at[k], head_recv.at[k], p)
             for k, (h, p) in enumerate(zip(head_of, head_peers, strict=True))
         ]
         head_own = [
-            pltpu.make_async_copy(blocks.at[:, head], gathered.at[head], head_local.at[0])
+            pltpu.make_async_copy(block_of(head), gathered.at[head], head_local.at[0])
         ]
         for copy in head_copies + head_own:
             copy.start()
     if mode == "out":
         head_send, head_recv, head_local, part_send, part_recv, mine_kv, arrived_kv = take(7)
         query, pair_mine, pair_other = head_in
-        gathered = head_out[0]
+        gathered = take(1)[0] if late else head_out[0]
         part_copies = [
             remote(pair_other.at[k], arrived_kv.at[k], part_send.at[k], part_recv.at[k], p)
             for k, p in enumerate(part_peers)
@@ -1179,6 +1449,126 @@
     if n_small:
         small_send, small_recv, small_sc = take(3)
         small = small_in[0]
+    if masked:
+        w_v, x_v, y_v, masked_sem = take(4)
+        w_masked_load = pltpu.make_async_copy(w_masked, w_v, masked_sem.at[0])
+        w_masked_load.start()
+        windows, fine = masked_o.shape[:2]
+        tile = x_v.shape[0]
+
+        def masked_product(k):
+            w, at = divmod(k * tile, fine)
+            load = pltpu.make_async_copy(terms[0].at[pl.ds(k * tile, tile)], x_v, masked_sem.at[1])
+            load.start()
+            load.wait()
+            if k == 0:
+                w_masked_load.wait()
+            made = dot(x_v[...], w_v[...])
+            bin_ = seq * (fine // 2) + lax.div(
+                at + lax.broadcasted_iota(jnp.int32, made.shape, 0), 2
+            )
+            y_v[...] = jnp.where(bin_ < lengths[w], made, 0.0).astype(BF)
+            store = pltpu.make_async_copy(
+                y_v, masked_o.at[w, pl.ds(at, tile)], masked_sem.at[2]
+            )
+            store.start()
+            store.wait()
+
+    if late:
+        small, w_buffer, acc, flat_v, middle_v, out_v, gain_sum, late_sem = take(8)
+        w_loads = [
+            pltpu.make_async_copy(w_query, w_buffer.at[:, pl.ds(0, H * KD)], late_sem.at[0]),
+            pltpu.make_async_copy(w_key, w_buffer.at[:, pl.ds(H * KD, H * KD)], late_sem.at[1]),
+        ]
+        for copy in w_loads:
+            copy.start()
+
+        def window_loads(w):
+            span = pl.ds(w * flat_v.shape[0], flat_v.shape[0])
+            return [
+                pltpu.make_async_copy(values.at[w], flat_v, late_sem.at[2]),
+                pltpu.make_async_copy(middle_grad.at[span], middle_v, late_sem.at[3]),
+            ]
+
+        def store_window(w):
+            span = pl.ds(w * flat_v.shape[0], flat_v.shape[0])
+            return pltpu.make_async_copy(out_v, input_grad.at[span], late_sem.at[4])
+
+        for copy in window_loads(0):
+            copy.start()
+
+        def back_through(w_ref, first, columns, into_first):
+            packed = rights[(n_terms - 1) % 2]
+
+            @pl.loop(0, acc.shape[0] // 128)
+            def _(k):
+                rows = pl.ds(pl.multiple_of(k * 128, 128), 128)
+                made = lax.dot_general(
+                    packed[rows, first : first + columns],
+                    w_ref[:, 0:columns],
+                    (((1,), (1,)), ((), ())),
+                    preferred_element_type=F32,
+                )
+                acc[rows, :] = made if into_first else acc[rows, :] + made
+
+        def value_load(k):
+            half = H * VD // 2
+            return pltpu.make_async_copy(
+                w_value.at[:, pl.ds(k * half, half)],
+                w_buffer.at[:, pl.ds(0, half)],
+                late_sem.at[5 + k],
+            )
+
+        def products(stage):
+            half = H * VD // 2
+            if stage == 0:
+                for copy in w_loads:
+                    copy.wait()
+                back_through(w_buffer, 0, 2 * H * KD, True)
+                value_load(0).start()
+            else:
+                value_load(0).wait()
+                back_through(w_buffer, 2 * H * KD, half, False)
+                value_load(1).start()
+                value_load(1).wait()
+                back_through(w_buffer, 2 * H * KD + half, half, False)
+
+        def norm_back(w):
+            for copy in window_loads(w):
+                copy.wait()
+            if w:
+                store_window(w - 1).wait()
+            else:
+                gain_sum[...] = jnp.zeros(gain_sum.shape, F32)
+            size = flat_v.shape[0]
+
+            @pl.loop(0, size // 32)
+            def _(k):
+                rows = pl.ds(pl.multiple_of(k * 32, 32), 32)
+                value = flat_v[rows, :].astype(F32)
+                centered = value - jnp.mean(value, axis=-1, keepdims=True)
+                scale = lax.rsqrt(jnp.mean(centered * centered, axis=-1, keepdims=True) + epsilon)
+                unit = centered * scale
+                grad = acc[pl.ds(pl.multiple_of(w * size + k * 32, 32), 32), :]
+                gain_sum[...] += jnp.sum(grad * unit, axis=0, keepdims=True)
+                grad = grad * gain[...]
+                along = jnp.mean(grad * unit, axis=-1, keepdims=True)
+                back = scale * (grad - jnp.mean(grad, axis=-1, keepdims=True) - unit * along)
+                out_v[rows, :] = (middle_v[rows, :] + back).astype(BF)
+
+            store_window(w).start()
+            if w + 1 < values.shape[0]:
+                for copy in window_loads(w + 1):
+                    copy.start()
+            else:
+                rows = dot32(pick[...] * gain_sum[...], spread[...].astype(F32), ((1,), (1,)))
+                wide = small_in[0].shape[1]
+                small[:, :wide, :] = small_in[0][...]
+                small[:, wide:, :] = jnp.broadcast_to(
+                    rows[:, None, :], (rows.shape[0], 8, rows.shape[1])
+                )
+
+    if n_small:
 
         def small_copy(k):
             there = lax.rem(me + k, n_small)
@@ -1190,9 +1580,13 @@
                 other_device(k),
             )
 
-        @pl.loop(1, n_small)
-        def _(k):
-            small_copy(k).start()
+        def start_small():
+            @pl.loop(1, n_small)
+            def _(k):
+                small_copy(k).start()
+
+        if not late:
+            start_small()
 
     ahead = 3
     for step in range(min(ahead, len(groups))):
@@ -1238,6 +1632,16 @@
                             copy.start()
         if step + ahead < len(groups):
             launch(step + ahead)
+        if masked and 0 <= step - (len(groups) - ahead) < terms[0].shape[0] // tile:
+            masked_product(step - (len(groups) - ahead))
+        if late and step >= len(groups) - ahead:
+            turn = step - (len(groups) - ahead)
+            if turn < 2:
+                products(turn)
+            elif turn < 2 + values.shape[0]:
+                norm_back(turn - 2)
+                if turn == 1 + values.shape[0]:
+                    start_small()
     if n_small:
 
         @pl.loop(1, n_small)
@@ -1250,11 +1654,14 @@
         def _(k):
             small_copy(k).wait_send()
 
+    if late:
+        store_window(values.shape[0] - 1).wait()
     if mode:
-        for copy in head_own:
-            copy.wait()
-        for copy in head_copies:
-            copy.wait_recv()
+        if not late:
+            for copy in head_own:
+                copy.wait()
+            for copy in head_copies:
+                copy.wait_recv()
         for copy in head_copies:
             copy.wait_send()
     if mode == "out":
@@ -1267,13 +1674,13 @@
                     copy.wait_send()
 
 
-def sum_terms(name, collective, pairs, groups, mode=None, heads=(), small=None):
+def sum_terms(name, collective, pairs, groups, mode=None, heads=(), small=None, late=None, masked=None):
     ndp, nseq = lax.axis_size("dp"), lax.axis_size("seq")
     nhi, parts, devices = nseq // 4, nseq // H, ndp * nseq
     shares = [(left.shape[1] // devices, right.shape[1]) for left, right in pairs]
     made_here = all(rows % 16 == 0 for rows, _ in shares)
     if made_here:
-        operands = [x for pair in pairs for x in pair]
+        operands = [x for pair in pairs for x in pair][: -1 if late else None]
     else:
         operands = [
             transposed_times(left, right).astype(BF).reshape((ndp, nhi, 2, 2) + share)
@@ -1308,7 +1715,7 @@
         unit_rows = max(rows for rows, _ in shapes)
         unit_columns = max(columns for _, columns in shapes)
         scratch += [
-            *[pltpu.VMEM(s, BF) for s in zip(tokens, tall, strict=True)],
+            pltpu.VMEM((max(tokens), max(tall)), BF),
             *[pltpu.VMEM(s, BF) for s in zip(tokens, wide, strict=True)],
             *[pltpu.VMEM(s, BF) for s in zip(tall, tokens, strict=True)],
             pltpu.VMEM((2, 2, ndp, nhi, 2, 2, unit_rows, unit_columns), BF),
@@ -1318,8 +1725,9 @@
     hop = max(ndp - 1, 1)
     sizes = [(count,)] * 3 + [(count, hop)] * 4 + [(count, nhi - 1)] * 2 + [(count,)] * 2
     scratch += [pltpu.SemaphoreType.DMA(size) for size in sizes]
-    if mode == "in":
-        windows, _, size, rows = heads[0].shape
+    if mode in ("in", "back"):
+        windows = heads[0].shape[0 if mode == "in" else 1]
+        size, rows = heads[0].shape[2:]
         operands.append(heads[0])
         in_specs.append(pl.BlockSpec(memory_space=pl.ANY))
         out_shape.append(jax.ShapeDtypeStruct((H, windows, size, rows), BF))
@@ -1329,26 +1737,61 @@
         _, windows, _, rows = heads[0].shape
         operands += list(heads)
         in_specs += [pl.BlockSpec(memory_space=pl.ANY)] * 3
-        out_shape.append(jax.ShapeDtypeStruct((H, windows, 2 * KD + VD, rows), BF))
-        out_specs.append(pl.BlockSpec(memory_space=pl.ANY))
+        if not late:
+            out_shape.append(jax.ShapeDtypeStruct((H, windows, 2 * KD + VD, rows), BF))
+            out_specs.append(pl.BlockSpec(memory_space=pl.ANY))
         scratch += [
             pltpu.SemaphoreType.DMA(size)
             for size in ((2, H - 1), (2, H - 1), (3,), (parts - 1,), (parts - 1,))
         ]
         scratch += [pltpu.VMEM(heads[1].shape, BF), pltpu.VMEM(heads[2].shape, BF)]
+        if late:
+            scratch.append(pltpu.VMEM((H, windows, 2 * KD + VD, rows), BF))
     n_small = 0
     if small is not None:
         n_small = devices
         operands.append(small)
         in_specs.append(pl.BlockSpec(memory_space=pltpu.VMEM))
-        out_shape.append(jax.ShapeDtypeStruct(small.shape[1:], F32))
+        message = (small.shape[1] + (8 if late else 0), small.shape[2])
+        out_shape.append(jax.ShapeDtypeStruct(message, F32))
         out_specs.append(pl.BlockSpec(memory_space=pltpu.VMEM))
         scratch += [
             pltpu.SemaphoreType.DMA((devices - 1,)),
             pltpu.SemaphoreType.DMA((devices - 1,)),
-            pltpu.VMEM((devices - 1,) + small.shape[1:], F32),
+            pltpu.VMEM((devices - 1,) + message, F32),
         ]
-    plan = (groups, len(pairs), mode, parts, n_small, made_here)
+    if late:
+        windows, rows, width = late[3].shape
+        operands += list(late) + list(spread_tables(width, width // devices))
+        in_specs += [pl.BlockSpec(memory_space=pl.ANY)] * 5
+        in_specs += [pl.BlockSpec(memory_space=pltpu.VMEM)] * 3
+        out_shape.append(jax.ShapeDtypeStruct((windows * rows, width), BF))
+        out_specs.append(pl.BlockSpec(memory_space=pl.ANY))
+        scratch += [
+            pltpu.VMEM((devices,) + message, F32),
+            pltpu.VMEM((width, 2 * H * KD), BF),
+            pltpu.VMEM((windows * rows, width), F32),
+            pltpu.VMEM((rows, width), BF),
+            pltpu.VMEM((rows, width), F32),
+            pltpu.VMEM((rows, width), BF),
+            pltpu.VMEM((1, width), F32),
+            pltpu.SemaphoreType.DMA((7,)),
+        ]
+    if masked:
+        lengths, weight, shape = masked
+        operands += [lengths, weight]
+        in_specs += [pl.BlockSpec(memory_space=pltpu.SMEM), pl.BlockSpec(memory_space=pl.ANY)]
+        out_shape.append(jax.ShapeDtypeStruct(shape, BF))
+        out_specs.append(pl.BlockSpec(memory_space=pl.ANY))
+        scratch += [
+            pltpu.VMEM(weight.shape, BF),
+            pltpu.VMEM((256, shape[2]), BF),
+            pltpu.VMEM((256, shape[2]), BF),
+            pltpu.SemaphoreType.DMA((3,)),
+        ]
+    plan = (
+        groups, len(pairs), mode, parts, n_small, made_here, late is not None, masked is not None
+    )
     return pl.pallas_call(
         functools.partial(sums_kernel, plan, None),
         out_shape=out_shape,
@@ -1356,7 +1799,7 @@
         out_specs=out_specs,
         scratch_shapes=scratch,
         compiler_params=pltpu.CompilerParams(
-            collective_id=collective, has_side_effects=True, vmem_limit_bytes=60 * 2**20
+            collective_id=collective, has_side_effects=True, vmem_limit_bytes=63 * 2**20
         ),
         name=name,
     )(*operands)
@@ -1380,6 +1823,176 @@
     return (array, 0, rows, first, columns)
 
 
+def gelu_parts(x):
+    below = 0.5 * (1.0 + lax.erf(x * (0.5**0.5)))
+    density = jnp.exp(-0.5 * x * x) * (1.0 / math.sqrt(2.0 * math.pi))
+    return x * below, below + x * density
+
+
+def norm_parts(value):
+    centered = value - jnp.mean(value, axis=-1, keepdims=True)
+    scale = lax.rsqrt(jnp.mean(centered * centered, axis=-1, keepdims=True) + epsilon)
+    return centered * scale, scale
+
+
+def norm_backward(unit, scale, grad, gain):
+    grad = grad * gain
+    along = jnp.mean(grad * unit, axis=-1, keepdims=True)
+    return scale * (grad - jnp.mean(grad, axis=-1, keepdims=True) - unit * along)
+
+
+def times_rows(x, table):
+    return lax.dot_general(x, table, (((1,), (1,)), ((), ())), preferred_element_type=F32)
+
+
+def block_kernel(
+    values, arrived, third_grad, w_mixing, w_inner, w_outer,
+    second_gain, third_gain, inner_bias, outer_bias,
+    mixed_o, second_o, hidden_o, third_o, block_o, before_o, middle_o, middle_grad_o, mixed_grad_o,
+    second_sum, third_sum, inner_sum, outer_sum,
+    mixing_v, inner_v, outer_v, middle_v, block_v, slope_v, sem,
+):
+    first = pl.program_id(0) == 0
+    rows, width = middle_v.shape
+    wide = slope_v.shape[1]
+    tile = 512
+    loads = [
+        pltpu.make_async_copy(source, target, sem.at[k])
+        for k, (source, target) in enumerate(
+            ((w_mixing, mixing_v), (w_inner, inner_v), (w_outer, outer_v))
+        )
+    ]
+
+    @pl.when(first)
+    def _():
+        for load in loads:
+            load.start()
+        for total in (second_sum, third_sum, inner_sum, outer_sum):
+            total[...] = jnp.zeros(total.shape, F32)
+
+    def ready(k):
+        @pl.when(first)
+        def _():
+            loads[k].wait()
+
+    for pair in range(H // 2):
+        both = jnp.concatenate([arrived[2 * pair + h, 0] for h in range(2)], axis=0)
+        mixed_o[:, pair * 2 * VD : (pair + 1) * 2 * VD] = both.T
+    ready(0)
+    for k in range(0, width, tile):
+        cols = slice(k, k + tile)
+        middle_v[:, cols] = values[0][:, cols].astype(F32) + dot(mixed_o[...], mixing_v[:, cols])
+
+    chunk = 32
+
+    @pl.loop(0, rows // chunk)
+    def _(k):
+        at = pl.ds(pl.multiple_of(k * chunk, chunk), chunk)
+        unit, _ = norm_parts(middle_v[at, :])
+        second_o[at, :] = (unit * second_gain[...]).astype(BF)
+
+    ready(1)
+    for k in range(0, wide, tile):
+        cols = slice(k, k + tile)
+        before = dot(second_o[...], inner_v[:, cols]) + inner_bias[:, cols]
+        hidden, slope = gelu_parts(before)
+        hidden_o[:, cols] = hidden.astype(BF)
+        slope_v[:, cols] = slope.astype(BF)
+    ready(2)
+    for k in range(0, width, tile):
+        cols = slice(k, k + tile)
+        block_v[:, cols] = (
+            middle_v[:, cols] + dot(hidden_o[...], outer_v[:, cols]) + outer_bias[:, cols]
+        )
+
+    @pl.loop(0, rows // chunk)
+    def _(k):
+        at = pl.ds(pl.multiple_of(k * chunk, chunk), chunk)
+        unit, scale = norm_parts(block_v[at, :])
+        third, slope = gelu_parts(unit * third_gain[...])
+        third_o[at, :] = third.astype(BF)
+        grad = third_grad[at, :] * slope
+        third_sum[...] += jnp.sum(grad * unit, axis=0, keepdims=True)
+        back = norm_backward(unit, scale, grad, third_gain[...])
+        outer_sum[...] += jnp.sum(back, axis=0, keepdims=True)
+        block_v[at, :] = back
+        block_o[at, :] = back.astype(BF)
+
+    for k in range(0, wide, tile):
+        cols = slice(k, k + tile)
+        grad = times_rows(block_o[...], outer_v[cols, :]) * slope_v[:, cols].astype(F32)
+        low = grad.astype(BF)
+        before_o[:, cols] = low
+        inner_sum[:, cols] += jnp.sum(low.astype(F32), axis=0, keepdims=True)
+    for k in range(0, width, tile):
+        cols = slice(k, k + tile)
+        middle_grad_o[:, cols] = times_rows(before_o[...], inner_v[cols, :])
+
+    @pl.loop(0, rows // chunk)
+    def _(k):
+        at = pl.ds(pl.multiple_of(k * chunk, chunk), chunk)
+        unit, scale = norm_parts(middle_v[at, :])
+        grad = middle_grad_o[at, :]
+        second_sum[...] += jnp.sum(grad * unit, axis=0, keepdims=True)
+        back = block_v[at, :] + norm_backward(unit, scale, grad, second_gain[...])
+        middle_grad_o[at, :] = back
+        middle_o[at, :] = back.astype(BF)
+
+    for pair in range(H // 2):
+        cols = slice(pair * 2 * VD, (pair + 1) * 2 * VD)
+        turned = times_rows(middle_o[...], mixing_v[cols, :]).astype(BF).T
+        for h in range(2):
+            mixed_grad_o[0, 2 * pair + h] = turned[h * VD : (h + 1) * VD]
+
+
+def block_pass(values, arrived, third_grad, weights, gains, biases):
+    windows, rows, width = values.shape
+    wide = weights[1].shape[1]
+
+    def by_rows(columns):
+        return pl.BlockSpec((rows, columns), lambda w: (w, 0))
+
+    def line(columns):
+        return pl.BlockSpec((1, columns), lambda w: (0, 0))
+
+    narrow = jax.ShapeDtypeStruct((windows * rows, width), BF)
+    broad = jax.ShapeDtypeStruct((windows * rows, wide), BF)
+    sums = [jax.ShapeDtypeStruct((1, n), F32) for n in (width, width, wide, width)]
+    any_space = pl.BlockSpec(memory_space=pl.ANY)
+    return pl.pallas_call(
+        block_kernel,
+        grid=(windows,),
+        out_shape=[
+            narrow, narrow, broad, narrow, narrow, broad, narrow,
+            jax.ShapeDtypeStruct((windows * rows, width), F32),
+            jax.ShapeDtypeStruct((windows, H, VD, rows), BF),
+            *sums,
+        ],
+        in_specs=[
+            pl.BlockSpec((1, rows, width), lambda w: (w, 0, 0)),
+            pl.BlockSpec((H, 1, VD, rows), lambda w: (0, w, 0, 0)),
+            by_rows(width),
+            any_space, any_space, any_space,
+            line(width), line(width), line(wide), line(width),
+        ],
+        out_specs=[
+            by_rows(width), by_rows(width), by_rows(wide), by_rows(width), by_rows(width),
+            by_rows(wide), by_rows(width), by_rows(width),
+            pl.BlockSpec((1, H, VD, rows), lambda w: (w, 0, 0, 0)),
+            line(width), line(width), line(wide), line(width),
+        ],
+        scratch_shapes=[
+            *[pltpu.VMEM(w.shape, BF) for w in weights],
+            pltpu.VMEM((rows, width), F32),
+            pltpu.VMEM((rows, width), F32),
+            pltpu.VMEM((rows, wide), BF),
+            pltpu.SemaphoreType.DMA((3,)),
+        ],
+        compiler_params=pltpu.CompilerParams(vmem_limit_bytes=62 * 2**20),
+        name="block_pass",
+    )(values, arrived, third_grad, *weights, *gains, *biases)
+
+
 def weight_pairs(shapes, offset):
     def pieces(n, parts):
         rows, columns = shapes[n]
@@ -1388,13 +2001,13 @@
         size = rows // parts
         return [(offset + n, k * size, size, 0, columns) for k in range(parts)]
 
-    first = pieces(0, 3) + pieces(2, 3) + pieces(4, 3) + pieces(5, 3)
+    first = pieces(5, 3) + pieces(0, 3) + pieces(4, 3) + pieces(2, 3)
     second = pieces(1, 3) + pieces(3, 6)
     steps = max(len(second), 1)
     spare = len(first) - steps
     pairs, spot = [], 0
     for k in range(steps):
-        take = 2 if k >= steps - spare else 1
+        take = 2 if 3 <= k < 3 + spare else 1
         pairs.append((tuple(first[spot : spot + take]), (second[k],)))
         spot += take
     if spot < len(first):
@@ -1487,6 +2100,14 @@
             mine,
             other,
             normed_low,
+            out_grad,
+            conv_grad,
+            joined_flat,
+            lifted_grad,
+            third_grad,
+            skip_grad,
+            skip_part,
+            grad_skip_bias,
         ) = use_links(
             "gather_weights",
             1,
@@ -1494,7 +2115,12 @@
             head_pairs + weight_pairs([w.shape for w in shards], len(head_shards)),
             values=inputs,
             early=len(head_pairs),
-        )
+            upper=(lengths, cotangent, skip_input),
+        )
+        out_grad, joined_flat, skip_part = (
+            x.reshape(-1, width) for x in (out_grad, joined_flat, skip_part)
+        )
+        grad_skip_bias = grad_skip_bias[0]
     else:
         small_full, weight_query, weight_key, weight_value = use_links(
             "gather_heads", 1, head_shards, head_pairs
@@ -1539,7 +2165,6 @@
         return lax.ppermute(array, "seq", [(i, i ^ slot) for i in range(nseq)])
 
     flat = inputs.reshape(windows * rows, width).astype(jnp.float32)
-    _, first_norm_back = jax.vjp(layer_norm, flat, gain_first)
     if r % 16:
         normed_low, sent = project(
             inputs, gain_first, bias_content, weight_query, weight_key, weight_value
@@ -1564,16 +2189,50 @@
     mixed_own, mixed_wide, log_total = attention_forward(
         info, rates, bias_gap, relative, mine, other, parts
     )
-    mixed_low = by_row(exchange(mixed_own))
-    middle = flat + matmul(mixed_low, weight_mixing)
-    second, second_norm_back = jax.vjp(layer_norm, middle, gain_second)
-    second_low = second.astype(jnp.bfloat16)
-    before = matmul(second_low, weight_inner) + bias_inner
-    hidden, gelu_back = jax.vjp(smooth_gelu, before)
-    hidden_low = hidden.astype(jnp.bfloat16)
-    block_out = middle + matmul(hidden_low, weight_outer) + bias_outer
-    third, third_back = jax.vjp(norm_gelu, block_out, gain_third)
-    third_low = third.astype(jnp.bfloat16)
+    if r % 16 == 0:
+        skip_flat = skip_input.reshape(windows * 2 * rows, width)
+        own_skip, mixed_arrived = sum_terms(
+            "sum_skip",
+            6,
+            [(skip_flat, joined_flat)],
+            halves(0, r, half_width),
+            "back",
+            (mixed_own,),
+        )
+    else:
+        mixed_arrived = exchange(mixed_own)
+    if r % 16 == 0:
+        (
+            mixed_low,
+            second_low,
+            hidden_low,
+            third_low,
+            block_low,
+            before_low,
+            middle_low,
+            middle_grad,
+            mixed_grad,
+            *block_sums,
+        ) = block_pass(
+            inputs,
+            mixed_arrived,
+            third_grad,
+            (weight_mixing, weight_inner, weight_outer),
+            (gain_second[None, :], gain_third[None, :]),
+            (bias_inner[None, :], bias_outer[None, :]),
+        )
+        grad_second, grad_third, grad_inner_bias, grad_outer_bias = (s[0] for s in block_sums)
+    else:
+        mixed_low = by_row(mixed_arrived)
+        middle = flat + matmul(mixed_low, weight_mixing)
+        second, second_norm_back = jax.vjp(layer_norm, middle, gain_second)
+        second_low = second.astype(jnp.bfloat16)
+        before = matmul(second_low, weight_inner) + bias_inner
+        hidden, gelu_back = jax.vjp(smooth_gelu, before)
+        hidden_low = hidden.astype(jnp.bfloat16)
+        block_out = middle + matmul(hidden_low, weight_outer) + bias_outer
+        third, third_back = jax.vjp(norm_gelu, block_out, gain_third)
+        third_low = third.astype(jnp.bfloat16)
     fine = jnp.arange(2 * rows, dtype=jnp.int32)[:, None] // 2
     twice = (fine == jnp.arange(rows, dtype=jnp.int32)[None, :]).astype(jnp.bfloat16)
     third_twice = (
@@ -1587,7 +2246,8 @@
         .reshape(windows * 2 * rows, width)
     )
     skip_flat = skip_input.reshape(windows * 2 * rows, width)
-    skip_part = matmul(skip_flat, weight_skip) + bias_skip
+    if r % 16:
+        skip_part = matmul(skip_flat, weight_skip) + bias_skip
     joined_low = (
         (matmul(third_twice, weight_upsample) + skip_part)
         .astype(jnp.bfloat16)
@@ -1601,24 +2261,39 @@
     bins = 2 * first + jnp.arange(2 * rows, dtype=jnp.int32)
     keep = (bins // 2)[None, :] < lengths[:, None]
     keep_wide = keep.astype(jnp.float32)[:, :, None]
-    outputs = (
-        matmul(conv_flat, weight_point).reshape(windows, 2 * rows, width) * keep_wide
-    ).astype(jnp.bfloat16)
-
-    out_grad = (cotangent * keep.astype(jnp.bfloat16)[:, :, None]).reshape(
-        windows * 2 * rows, width
-    )
-    conv_grad = (
-        times_transposed(out_grad, weight_point)
-        .astype(jnp.bfloat16)
-        .reshape(windows, 2 * rows, width)
-    )
-    grad_rim = extended_2(conv_grad, (("seq", 1),), 1).astype(jnp.float32)
-    joined_grad = (
-        grad_rim[:, 2:] * taps[:, 0]
-        + grad_rim[:, 1:-1] * taps[:, 1]
-        + grad_rim[:, :-2] * taps[:, 2]
-    )
+    if r % 16:
+        outputs = (
+            matmul(conv_flat, weight_point).reshape(windows, 2 * rows, width) * keep_wide
+        ).astype(jnp.bfloat16)
+    if r % 16:
+        out_grad = (cotangent * keep.astype(jnp.bfloat16)[:, :, None]).reshape(
+            windows * 2 * rows, width
+        )
+        conv_grad = (
+            times_transposed(out_grad, weight_point)
+            .astype(jnp.bfloat16)
+            .reshape(windows, 2 * rows, width)
+        )
+        grad_rim = extended_2(conv_grad, (("seq", 1),), 1).astype(jnp.float32)
+        joined_grad = (
+            grad_rim[:, 2:] * taps[:, 0]
+            + grad_rim[:, 1:-1] * taps[:, 1]
+            + grad_rim[:, :-2] * taps[:, 2]
+        )
+        grad_skip_bias = jnp.sum(joined_grad, axis=(0, 1))
+        joined_back = joined_grad.astype(jnp.bfloat16)
+        joined_flat = joined_back.reshape(windows * 2 * rows, width)
+        lifted_grad = (
+            jnp.einsum("ts,wtd->wsd", twice, joined_back, preferred_element_type=jnp.float32)
+            .astype(jnp.bfloat16)
+            .reshape(windows * rows, width)
+        )
+        third_grad = times_transposed(lifted_grad, weight_upsample)
+        skip_grad = (
+            times_transposed(joined_flat, weight_skip)
+            .astype(jnp.bfloat16)
+            .reshape(windows, 2 * rows, width)
+        )
     conv_wide = conv_grad.astype(jnp.float32)
     grad_depth = jnp.stack(
         [
@@ -1628,85 +2303,60 @@
         ],
         axis=1,
     )
-    grad_skip_bias = jnp.sum(joined_grad, axis=(0, 1))
-    joined_back = joined_grad.astype(jnp.bfloat16)
-    joined_flat = joined_back.reshape(windows * 2 * rows, width)
-    lifted_grad = (
-        jnp.einsum("ts,wtd->wsd", twice, joined_back, preferred_element_type=jnp.float32)
-        .astype(jnp.bfloat16)
-        .reshape(windows * rows, width)
-    )
-    third_grad = times_transposed(lifted_grad, weight_upsample)
-    skip_grad = (
-        times_transposed(joined_flat, weight_skip)
-        .astype(jnp.bfloat16)
-        .reshape(windows, 2 * rows, width)
-    )
-    block_grad, grad_third = third_back(third_grad)
-    block_low = block_grad.astype(jnp.bfloat16)
-    grad_outer_bias = jnp.sum(block_grad, axis=0)
-    (before_grad,) = gelu_back(times_transposed(block_low, weight_outer))
-    before_low = before_grad.astype(jnp.bfloat16)
-    grad_inner_bias = jnp.sum(before_low.astype(jnp.float32), axis=0)
-    middle_part, grad_second = second_norm_back(times_transposed(before_low, weight_inner))
-    middle_grad = block_grad + middle_part
-    middle_low = middle_grad.astype(jnp.bfloat16)
-    middle_rows = middle_low.reshape(windows, rows, width)
-    mixed_grad = (
-        jnp.einsum("vd,wrd->wvr", weight_mixing, middle_rows, preferred_element_type=jnp.float32)
-        .astype(jnp.bfloat16)
-        .reshape(windows, H, VD, rows)
-    )
-    own_point, own_outer, own_skip, own_upsample, arrived_grad = sum_terms(
-        "sum_upper",
-        3,
-        [
-            (conv_flat, out_grad),
-            (hidden_low, block_low),
-            (skip_flat, joined_flat),
-            (third_low, lifted_grad),
-        ],
-        halves(0, r, half_width)
-        + halves(1, outer_weight.shape[0], half_width)
-        + halves(2, r, half_width)
-        + halves(3, r, half_width),
-        "in",
-        (mixed_grad,),
-    )
+    if r % 16:
+        block_grad, grad_third = third_back(third_grad)
+        block_low = block_grad.astype(jnp.bfloat16)
+        grad_outer_bias = jnp.sum(block_grad, axis=0)
+        (before_grad,) = gelu_back(times_transposed(block_low, weight_outer))
+        before_low = before_grad.astype(jnp.bfloat16)
+        grad_inner_bias = jnp.sum(before_low.astype(jnp.float32), axis=0)
+        middle_part, grad_second = second_norm_back(times_transposed(before_low, weight_inner))
+        middle_grad = block_grad + middle_part
+        middle_low = middle_grad.astype(jnp.bfloat16)
+        middle_rows = middle_low.reshape(windows, rows, width)
+        mixed_grad = (
+            jnp.einsum("vd,wrd->wvr", weight_mixing, middle_rows, preferred_element_type=jnp.float32)
+            .astype(jnp.bfloat16)
+            .reshape(windows, H, VD, rows)
+        )
+    if r % 16 == 0:
+        own_point, own_outer, own_upsample, arrived_grad, outputs = sum_terms(
+            "sum_upper",
+            3,
+            [(conv_flat, out_grad), (hidden_low, block_low), (third_low, lifted_grad)],
+            halves(0, r, half_width)
+            + halves(1, outer_weight.shape[0], half_width)
+            + halves(2, r, half_width),
+            "in",
+            (mixed_grad,),
+            masked=(lengths, weight_point, skip_input.shape),
+        )
+    else:
+        own_point, own_outer, own_skip, own_upsample, arrived_grad = sum_terms(
+            "sum_upper",
+            3,
+            [
+                (conv_flat, out_grad),
+                (hidden_low, block_low),
+                (skip_flat, joined_flat),
+                (third_low, lifted_grad),
+            ],
+            halves(0, r, half_width)
+            + halves(1, outer_weight.shape[0], half_width)
+            + halves(2, r, half_width)
+            + halves(3, r, half_width),
+            "in",
+            (mixed_grad,),
+        )
     query_own, own_side, other_side, bias_sums, relative_sum = attention_backward(
         info, rates, bias_gap, relative, mine, other, arrived_grad, mixed_wide, log_total, parts
     )
-    own_inner, own_mixing, heads_grad = sum_terms(
-        "sum_lower",
-        4,
-        [(second_low, before_low), (mixed_low, middle_low)],
-        halves(0, r, half_hidden) + halves(1, r, half_width),
-        "out",
-        (query_own, own_side, other_side),
-    )
-    packed_grad = jnp.concatenate(
-        [
-            by_row(heads_grad[:, :, :KD]),
-            by_row(heads_grad[:, :, KD : 2 * KD]),
-            by_row(heads_grad[:, :, 2 * KD :]),
-        ],
-        axis=1,
-    )
-    (packed_grad,) = tie(packed_grad)
-    normed_grad = (
-        times_transposed(packed_grad[:, : H * KD], weight_query)
-        + times_transposed(packed_grad[:, H * KD : keys_width], weight_key)
-        + times_transposed(packed_grad[:, keys_width:], weight_value)
-    )
-    input_part, grad_first = first_norm_back(normed_grad)
-    input_grad = (middle_grad + input_part).astype(jnp.bfloat16).reshape(windows, rows, width)
 
     def at_head(value):
         full = jnp.zeros((H,) + value.shape, jnp.float32)
         return lax.dynamic_update_index_in_dim(full, value, head, 0)
 
     pieces = [
-        grad_first,
         at_head(bias_sums[0, :, 0]).reshape(-1),
         at_head(bias_sums[1, :, 0]).reshape(-1),
         at_head(relative_sum).reshape(H * KD, RPF),
@@ -1717,24 +2367,69 @@
         grad_skip_bias,
         grad_depth,
     ]
-    packed = jnp.concatenate([p.reshape(devices, -1) for p in pieces], axis=1)
-    packed = jnp.pad(packed, ((0, 0), (0, -packed.shape[1] % 1024))).reshape(devices, -1, 128)
-    own_heads, small_total = sum_terms(
-        "sum_heads",
-        5,
-        [(normed_low, packed_grad)],
-        halves(0, r, packed_grad.shape[1] // 2),
-        small=packed,
-    )
+
+    def pack(pieces):
+        packed = jnp.concatenate([p.reshape(devices, -1) for p in pieces], axis=1)
+        return jnp.pad(packed, ((0, 0), (0, -packed.shape[1] % 1024))).reshape(devices, -1, 128)
+
+    lower = [(second_low, before_low), (mixed_low, middle_low)]
+    lower_groups = halves(0, r, half_hidden) + halves(1, r, half_width)
+    lower_heads = (query_own, own_side, other_side)
+    packed_width = keys_width + values_width
+    if r % 16 == 0:
+        right = jax.ShapeDtypeStruct((windows * rows, packed_width), BF)
+        own_inner, own_mixing, own_heads, small_total, input_grad = sum_terms(
+            "sum_lower",
+            4,
+            lower + [(normed_low, right)],
+            lower_groups + halves(2, r, packed_width // 2),
+            "out",
+            lower_heads,
+            pack(pieces),
+            (weight_query, weight_key, weight_value, inputs, middle_grad, gain_first[None, :]),
+        )
+        own_first = small_total[-8, : width // devices]
+        input_grad = input_grad.reshape(windows, rows, width)
+        names = pieces
+    else:
+        own_inner, own_mixing, heads_grad = sum_terms(
+            "sum_lower", 4, lower, lower_groups, "out", lower_heads
+        )
+        packed_grad = jnp.concatenate(
+            [
+                by_row(heads_grad[:, :, :KD]),
+                by_row(heads_grad[:, :, KD : 2 * KD]),
+                by_row(heads_grad[:, :, 2 * KD :]),
+            ],
+            axis=1,
+        )
+        (packed_grad,) = tie(packed_grad)
+        normed_grad = (
+            times_transposed(packed_grad[:, : H * KD], weight_query)
+            + times_transposed(packed_grad[:, H * KD : keys_width], weight_key)
+            + times_transposed(packed_grad[:, keys_width:], weight_value)
+        )
+        _, first_norm_back = jax.vjp(layer_norm, flat, gain_first)
+        input_part, grad_first = first_norm_back(normed_grad)
+        input_grad = (middle_grad + input_part).astype(jnp.bfloat16).reshape(windows, rows, width)
+        names = [grad_first] + pieces
+        own_heads, small_total = sum_terms(
+            "sum_heads",
+            5,
+            [(normed_low, packed_grad)],
+            halves(0, r, packed_width // 2),
+            small=pack(names),
+        )
     small_total, spot, small_grads = small_total.reshape(-1), 0, []
-    for p in pieces:
+    for p in names:
         size = p.size // devices
         small_grads.append(
             small_total[spot : spot + size].reshape((p.shape[0] // devices,) + p.shape[1:])
         )
         spot += size
+    if len(names) > len(pieces):
+        own_first = small_grads.pop(0)
     (
-        own_first,
         own_content,
         own_position,
         own_relative,

time: 938 us -> 846 us (0.902)
  matrix products: 125 us -> 11.1 us
  Pallas kernels: 685 us -> 773 us
  other arithmetic: 35.2 us -> 12.3 us
  starting transfers between devices: 27.1 us -> 4.32 us
  local copies, waits for them, and re-layouts: 58.3 us -> 44.5 us
    dot_general x10 -> x0, matrix products: 69.4 us -> none  [the longest x8 58.6 us: times_transposed(): lax.dot_general(left, right, (((1,), (1,)), ((), ())), preferred_element_...]
    pallas_call x0 -> x1, Pallas kernels: none -> 60.9 us  [block_pass(): pl.pallas_call(block_kernel, grid=(windows,), out_shape=[narrow, narrow,...]
    dot_general x6 -> x1, matrix products: 55 us -> 8.64 us  [matmul(): return jnp.dot(left, right, preferred_element_type=jnp.float32)]
    all_to_all x1 -> x0, starting transfers between devices: 13.9 us -> none  [exchange(): lax.all_to_all(array, 'seq', 0, 0, axis_index_groups=groups, tiled=True)]
    pallas_call x3, Pallas kernels: 334 us -> 348 us  [sum_terms(): pl.pallas_call(functools.partial(sums_kernel, plan, None), out_shape=out_...]
    reduce_sum x9 -> x0, other arithmetic: 11.6 us -> none  [the longest x2 4.53 us: layer_norm(): centered = values - mean]
    convert_element_type x5 -> x0, other arithmetic: 9.69 us -> none  [the longest x1 5.51 us: on_device(): (middle_grad + input_part).astype(jnp.bfloat16)]
  transfers between devices with their start and end apart: 5 -> 2, of which waited for: 0 -> 0; matrix products, arithmetic and copies ran while one was open for 8% -> 0% of each run, Pallas kernels for 0% -> 0%
where the time goes in v4:
time: 846 us; the launch traced here: 847 us
  Pallas kernels  773 us (91%)
  local copies, waits for them, and re-layouts  44.5 us (5%)
  other arithmetic  12.3 us (1%)
  matrix products  11.1 us (1%)
    pallas_call x3, Pallas kernels, sum_terms(): pl.pallas_call(functools.partial(sums_kernel, plan, None), out_shape=out_...  348 us
    pallas_call x1, Pallas kernels, use_links(): pl.pallas_call(functools.partial(links_kernel, pairs, (len(shards), len(a...  274 us
    pallas_call x1, Pallas kernels, block_pass(): pl.pallas_call(block_kernel, grid=(windows,), out_shape=[narrow, narrow,...  60.9 us
    pallas_call x1, Pallas kernels, attention_backward(): pl.pallas_call(functools.partial(backward_kernel, parts, per), grid=(wind...  53.6 us
    pallas_call x1, Pallas kernels, attention_forward(): pl.pallas_call(functools.partial(forward_kernel, parts, per), grid=(windo...  37.2 us
  transfers between devices with their start and end apart: 2, of which 0 were waited for; matrix products, arithmetic and copies ran while one was open for 0% of the time, Pallas kernels for 0%

profile of v4, /device:TPU:1, one launch (start us, length us, event | category | flops | bytes accessed | tf_op | source)
XLA Modules:
  0.0 846.8 jit_solution(16836578066879330830)
XLA Ops:
  6.0 0.7 pad.52
  6.7 0.7 pad.53
  8.1 0.7 fusion.8.refs_13_
  8.7 0.7 fusion.9.refs_12_.refs_16_
  9.4 0.8 fusion.4.refs_11_.refs_15_
  10.3 1.8 concatenate.40.refs_0_
  12.1 273.5 %gather_weights.1 = (bf16[2,4,2,2,32,128]{5,4,3,2,1,0:T(8,128)(2,1)}, bf16[2,4,2,2,48,512]{5,4,3,2,1,0:T(8,128)(2,1)}, bf16[2,4,2,2,48,512]{5,4,3,2,1,0:T(8,128)...) custom-call(bf16[32,128]{1,0:T(8,128)(2,1)} %concatenate.40.refs_0_,, ...), custom_call_target="tpu_custom_call" | custom-call | tf_op jit(solution)/shard_map/gather_weights/pallas_call | solution.py:1049
  285.6 1.0 bitcast_convert_fusion
  289.4 0.7 broadcast_in_dim_reshape_squeeze.17.inner_bias
  290.2 0.7 copy.70.bias_ref
  290.9 0.7 copy.69
  292.9 0.7 broadcast_in_dim_reshape_squeeze.15.second_gain
  293.6 37.2 %attention_forward.1 = (bf16[8,2,192,256]{3,2,1,0:T(8,128)(2,1)}, f32[8,2,192,256]{3,2,1,0:T(8,128)}, f32[8,2,8,256]{3,2,1,0:T(8,128)}) custom-call(s32[3]{0:T(128)} %pad_add_fusion.info, f32[16,1]{1,0:T(8,128)} %fusion.14.rates_ref, f32[1,128]{1,0:T(1,128)} %select_maximum_fusion.lanes_ref, f32[64,1]{1,0:T(8,128)} %copy.70.bias_ref, f32[32,64]{1,0:T(8,128)} %bitcast.89, ...), custom_call_target="tpu_custom_call" | custom-call | flops 9663676416 | bytes 20000000 | tf_op jit(solution)/shard_map/attention_forward/pallas_call | solution.py:436
  330.9 64.4 %sum_skip.1 = (f32[48,1536]{1,0:T(8,128)}, bf16[8,2,192,256]{3,2,1,0:T(8,128)(2,1)}) custom-call(bf16[1024,1536]{1,0:T(8,128)(2,1)} %bitcast.67, bf16[1024,1536]{1,0:T(8,128)(2,1)} %bitcast.77, bf16[8,2,192,256]{3,2,1,0:T(8,128)(2,1)} %get-tuple-element.79.refs_2_), custom_call_target="tpu_custom_call" | custom-call | tf_op jit(solution)/shard_map/sum_skip/pallas_call | solution.py:1795
  395.3 60.9 %block_pass.1 = (bf16[512,1536]{1,0:T(8,128)(2,1)}, bf16[512,1536]{1,0:T(8,128)(2,1)}, bf16[512,3072]{1,0:T(8,128)(2,1)}, bf16[512,1536]{1,0:T(8,128)(2,1)}, bf1...) custom-call(bf16[2,256,1536]{2,1,0:T(8,128)(2,1)} %refs_12_.1, ...), custom_call_target="tpu_custom_call" | custom-call | tf_op jit(solution)/shard_map/block_pass/pallas_call | solution.py:1962
  456.1 2.4 convolution_convert_fusion
  458.6 8.6 %fusion.3 = bf16[1024,1536]{1,0:T(8,128)(2,1)S(1)} fusion(f32[2,512,1536]{2,1,0:T(8,128)} %get-tuple-element.87, bf16[1024,1536]{1,0:T(8,128)(2,1)S(1)} %bitcast.76, bf16[1536,1536]{1,0:T(8,128)(2,1)} %bitcast.94), kind=kOutput, calls=%fused_computation.7 | convolution fusion | flops 4834983936 | bytes 17301504 | tf_op jit(solution)/shard_map/dot_general | solution.py:50
  467.3 1.9 collective-permute-start
  469.2 2.4 collective-permute-start.1
  471.7 0.9 slice.145
  472.9 0.7 broadcast_in_dim_reshape_squeeze.19.refs_14_
  475.1 0.9 maximum_convert_fusion
  476.1 0.9 copy-done.1
  477.0 4.7 fusion
  481.8 111.7 %sum_upper.1 = (f32[48,1536]{1,0:T(8,128)}, f32[96,1536]{1,0:T(8,128)}, f32[48,1536]{1,0:T(8,128)}, bf16[8,2,192,256]{3,2,1,0:T(8,128)(2,1)}, bf16[2,512,1536]{2,1,0:T(8,128)(2,1)}) custom-call(bf16[1024,1536]{1,0:T(8,128)(2,1)} %bitcast.68, bf16[1024,1536]{1,0:T(8,128)(2,1)} %bitcast.78, bf16[512,3072]{1,0:T(8,128)(2,1)} %get-tuple-element.89.refs_2_, ...), custom_call_target="tpu_custom_call" | custom-call | tf_op jit(solution)/shard_map/sum_upper/pallas_call | solution.py:1795
  593.4 53.6 %attention_backward.1 = (bf16[8,2,64,256]{3,2,1,0:T(8,128)(2,1)}, bf16[8,2,256,256]{3,2,1,0:T(8,128)(2,1)}, bf16[1,8,2,256,256]{4,3,2,1,0:T(8,128)(2,1)}, f32[2,64,1]{2,1,0:T(8,128)}, f32[64,32]{1,0:T(8,128)}) custom-call(s32[3]{0:T(128)} %pad_add_fusion.info, f32[16,1]{1,0:T(8,128)} %fusion.14.rates_ref, f32[1,128]{1,0:T(1,128)} %select_maximum_fusion.lanes_ref, ...), custom_call_target="tpu_custom_call" | custom-call | flops 32212254720 | bytes 20000000 | tf_op jit(solution)/shard_map/attention_backward/pallas_call | solution.py:478
  647.0 0.8 bitcast_dynamic-update-slice_fusion
  647.9 0.9 slice_reduce_fusion
  649.9 0.7 copy.76
  650.6 171.8 %sum_lower.1 = (f32[48,3072]{1,0:T(8,128)}, f32[48,1536]{1,0:T(8,128)}, f32[48,2560]{1,0:T(8,128)}, f32[16,128]{1,0:T(8,128)}, bf16[512,1536]{1,0:T(8,128)(2,1)}) custom-call(bf16[512,1536]{1,0:T(8,128)(2,1)} %get-tuple-element.95.refs_0_, bf16[512,3072]{1,0:T(8,128)(2,1)} %get-tuple-element.96.refs_1_, bf16[512,1536]{1,0:T(8,128)(2,1)} %get-tuple-element.97.refs_2_, ...), custom_call_target="tpu_custom_call" | custom-call | tf_op jit(solution)/shard_map/sum_lower/pallas_call | solution.py:1795
  822.4 1.2 slice_bitcast_fusion
  823.6 1.3 slice.156
  824.8 0.7 slice.160
  825.6 1.3 fusion.35
  826.9 1.4 fusion.34
  828.3 0.8 slice.127
  829.1 1.6 fusion.33
  830.7 1.7 slice.124
  833.8 3.9 copy.91
  837.7 1.1 copy.92
  838.8 1.3 copy-done
  840.2 1.7 copy.93
  841.8 0.7 copy.94
  842.5 0.8 copy.95
  843.4 0.8 copy.96
  844.2 0.7 copy.97
  844.9 0.7 copy.98
  845.6 0.7 copy.99
  (97 shorter events, 14.6 us)
Async XLA Ops:
  12.1 275.4 %copy-start.15 = (s32[2]{0:T(128)S(1)}, s32[2]{0:T(128)}, u32[]{:S(2)}) copy-start(s32[2]{0:T(128)} %refs_7_.3) | copy-start | bytes 28
  286.6 0.8 copy-start.2
  458.6 14.2 %copy-start.11 = (f32[1,1536]{1,0:T(1,128)S(1)}, f32[1,1536]{1,0:T(1,128)}, u32[]{:S(2)}) copy-start(f32[1,1536]{1,0:T(1,128)} %get-tuple-element.112) | copy-start | bytes 18436
  458.6 15.0 %copy-start.14 = (f32[1,1536]{1,0:T(1,128)S(1)}, f32[1,1536]{1,0:T(1,128)}, u32[]{:S(2)}) copy-start(f32[1,1536]{1,0:T(1,128)} %get-tuple-element.108) | copy-start | bytes 18436
  458.6 15.0 %copy-start.13 = (f32[1,1536]{1,0:T(1,128)S(1)}, f32[1,1536]{1,0:T(1,128)}, u32[]{:S(2)}) copy-start(f32[1,1536]{1,0:T(1,128)} %get-tuple-element.110) | copy-start | bytes 18436
  458.6 15.1 %copy-start.12 = (f32[1,1536]{1,0:T(1,128)S(1)}, f32[1,1536]{1,0:T(1,128)}, u32[]{:S(2)}) copy-start(f32[1,1536]{1,0:T(1,128)} %get-tuple-element.111) | copy-start | bytes 18436
  458.6 15.8 %copy-start.10 = (f32[1,3072]{1,0:T(1,128)S(1)}, f32[1,3072]{1,0:T(1,128)}, u32[]{:S(2)}) copy-start(f32[1,3072]{1,0:T(1,128)} %get-tuple-element.109) | copy-start | bytes 36868
  467.3 7.8 collective-permute-start
  469.2 5.9 collective-permute-start.1
  475.1 1.9 copy-start.1
  833.8 3.9 copy-start.3
  837.7 2.5 copy-start
  840.1 1.7 copy-start.9
  840.1 2.4 copy-start.5
  840.2 3.2 copy-start.4
  840.2 4.0 copy-start.8
  841.8 3.1 copy-start.6
  841.8 3.8 copy-start.7

commit v5 on v4

--- a/solution.py
+++ b/solution.py
@@ -1122,6 +1122,171 @@
     )
 
 
+def block_work(operands, outs, scratch, arrived, wait_heads):
+    values, third_grad, w_mixing, w_inner, w_outer = operands[:5]
+    second_gain, third_gain, inner_bias, outer_bias = operands[5:]
+    second_sum, third_sum, inner_sum, outer_sum = outs[9:]
+    mixing_v, inner_v, outer_v, values_v, third_grad_v, middle_v, block_v, slope_v = scratch[:8]
+    mixed_b, second_b, hidden_b, third_b, block_b, before_b, middle_b, back_b, heads_b = scratch[8:17]
+    weight_sem, load_sem, store_sem = scratch[17:]
+    windows, rows, width = values.shape
+    wide = slope_v.shape[1]
+    tile, chunk = 512, 32
+    weight_loads = [
+        pltpu.make_async_copy(source, target, weight_sem.at[k])
+        for k, (source, target) in enumerate(
+            ((w_mixing, mixing_v), (w_inner, inner_v), (w_outer, outer_v))
+        )
+    ]
+
+    def loads(w):
+        return [
+            pltpu.make_async_copy(values.at[w], values_v, load_sem.at[0]),
+            pltpu.make_async_copy(third_grad.at[pl.ds(w * rows, rows)], third_grad_v, load_sem.at[1]),
+        ]
+
+    buffers = (mixed_b, second_b, hidden_b, third_b, block_b, before_b, middle_b, back_b, heads_b)
+
+    def store(k, w):
+        target = outs[k].at[w] if k == 8 else outs[k].at[pl.ds(w * rows, rows)]
+        return pltpu.make_async_copy(buffers[k], target, store_sem.at[k])
+
+    def free(w, *numbers):
+        if w:
+            for k in numbers:
+                store(k, w - 1).wait()
+
+    def begin():
+        for load in weight_loads + loads(0):
+            load.start()
+        for total in (second_sum, third_sum, inner_sum, outer_sum):
+            total[...] = jnp.zeros(total.shape, F32)
+
+    def mix(w):
+        wait_heads(w)
+        free(w, 0)
+        for pair in range(H // 2):
+            both = jnp.concatenate([arrived[2 * pair + h, w] for h in range(2)], axis=0)
+            mixed_b[:, pair * 2 * VD : (pair + 1) * 2 * VD] = both.T
+        store(0, w).start()
+        if w == 0:
+            weight_loads[0].wait()
+        loads(w)[0].wait()
+        for k in range(0, width, tile):
+            cols = slice(k, k + tile)
+            middle_v[:, cols] = values_v[:, cols].astype(F32) + dot(mixed_b[...], mixing_v[:, cols])
+
+    def inner(w, part):
+        if part == 0:
+            free(w, 1, 2)
+
+            @pl.loop(0, rows // chunk)
+            def _(k):
+                at = pl.ds(pl.multiple_of(k * chunk, chunk), chunk)
+                unit, _ = norm_parts(middle_v[at, :])
+                second_b[at, :] = (unit * second_gain[...]).astype(BF)
+
+            store(1, w).start()
+            if w == 0:
+                weight_loads[1].wait()
+        for k in range(part * wide // 2, (part + 1) * wide // 2, tile):
+            cols = slice(k, k + tile)
+            before = dot(second_b[...], inner_v[:, cols]) + inner_bias[:, cols]
+            hidden, slope = gelu_parts(before)
+            hidden_b[:, cols] = hidden.astype(BF)
+            slope_v[:, cols] = slope.astype(BF)
+        if part == 1:
+            store(2, w).start()
+
+    def outer(w):
+        if w == 0:
+            weight_loads[2].wait()
+        for k in range(0, width, tile):
+            cols = slice(k, k + tile)
+            block_v[:, cols] = (
+                middle_v[:, cols] + dot(hidden_b[...], outer_v[:, cols]) + outer_bias[:, cols]
+            )
+
+    def turn(w):
+        free(w, 3, 4)
+        loads(w)[1].wait()
+
+        @pl.loop(0, rows // chunk)
+        def _(k):
+            at = pl.ds(pl.multiple_of(k * chunk, chunk), chunk)
+            unit, scale = norm_parts(block_v[at, :])
+            third, slope = gelu_parts(unit * third_gain[...])
+            third_b[at, :] = third.astype(BF)
+            grad = third_grad_v[at, :] * slope
+            third_sum[...] += jnp.sum(grad * unit, axis=0, keepdims=True)
+            back = norm_backward(unit, scale, grad, third_gain[...])
+            outer_sum[...] += jnp.sum(back, axis=0, keepdims=True)
+            block_v[at, :] = back
+            block_b[at, :] = back.astype(BF)
+
+        store(3, w).start()
+        store(4, w).start()
+        if w + 1 < windows:
+            for load in loads(w + 1):
+                load.start()
+
+    def before_grad(w):
+        free(w, 5)
+        for k in range(0, wide, tile):
+            cols = slice(k, k + tile)
+            grad = times_rows(block_b[...], outer_v[cols, :]) * slope_v[:, cols].astype(F32)
+            low = grad.astype(BF)
+            before_b[:, cols] = low
+            inner_sum[:, cols] += jnp.sum(low.astype(F32), axis=0, keepdims=True)
+        store(5, w).start()
+
+    def second_grad(w):
+        free(w, 7)
+        for k in range(0, width, tile):
+            cols = slice(k, k + tile)
+            back_b[:, cols] = times_rows(before_b[...], inner_v[cols, :])
+
+    def middle_grad(w):
+        free(w, 6, 8)
+
+        @pl.loop(0, rows // chunk)
+        def _(k):
+            at = pl.ds(pl.multiple_of(k * chunk, chunk), chunk)
+            unit, scale = norm_parts(middle_v[at, :])
+            grad = back_b[at, :]
+            second_sum[...] += jnp.sum(grad * unit, axis=0, keepdims=True)
+            back = block_v[at, :] + norm_backward(unit, scale, grad, second_gain[...])
+            back_b[at, :] = back
+            middle_b[at, :] = back.astype(BF)
+
+        store(6, w).start()
+        store(7, w).start()
+        for pair in range(H // 2):
+            cols = slice(pair * 2 * VD, (pair + 1) * 2 * VD)
+            turned = times_rows(middle_b[...], mixing_v[cols, :]).astype(BF).T
+            for h in range(2):
+                heads_b[2 * pair + h] = turned[h * VD : (h + 1) * VD]
+        store(8, w).start()
+
+    def finish():
+        for k in range(len(buffers)):
+            store(k, windows - 1).wait()
+
+    jobs = []
+    for w in range(windows):
+        jobs += [
+            functools.partial(mix, w),
+            functools.partial(inner, w, 0),
+            functools.partial(inner, w, 1),
+            functools.partial(outer, w),
+            functools.partial(turn, w),
+            functools.partial(before_grad, w),
+            functools.partial(second_grad, w),
+            functools.partial(middle_grad, w),
+        ]
+    return begin, jobs, finish
+
+
 def sums_kernel(plan, refs_spec, *refs):
     groups, n_terms, mode, parts, n_small, made_here, late, masked = plan
     refs = list(refs)
@@ -1131,19 +1296,23 @@
         return out
 
     terms = take(n_terms * (2 if made_here else 1) - (1 if late else 0))
-    head_in = take({None: 0, "in": 1, "back": 1, "out": 3}[mode])
+    head_in = take({None: 0, "in": 1, "block": 1, "out": 3}[mode])
     small_in = take(1 if n_small else 0)
     if late:
         w_query, w_key, w_value, values, middle_grad, gain, spread, pick = take(8)
     if masked:
         lengths, w_masked = take(2)
+    if mode == "block":
+        block_in = take(9)
     outs = take(n_terms)
-    head_out = take(0 if late or not mode else 1)
+    head_out = take(0 if late or not mode or mode == "block" else 1)
     small_out = take(1 if n_small else 0)
     if late:
         (input_grad,) = take(1)
     if masked:
         (masked_o,) = take(1)
+    if mode == "block":
+        block_out = take(13)
     own, arrived, result, back, hop1, hop2, line = [], [], [], [], [], [], []
     flat = [(side, unit) for group in groups for side in (0, 1) for unit in group[side]]
     count = len(flat)
@@ -1419,22 +1588,52 @@
             if not (late and array == n_terms - 1):
                 fetch_right(array).start()
 
-    if mode in ("in", "back"):
+    if mode == "in":
         head_send, head_recv, head_local = take(3)
         blocks, gathered = head_in[0], head_out[0]
-
-        def block_of(h):
-            return blocks.at[:, h] if mode == "in" else blocks.at[h]
-
         head_copies = [
-            remote(block_of(h), gathered.at[head], head_send.at[k], head_recv.at[k], p)
+            remote(blocks.at[:, h], gathered.at[head], head_send.at[k], head_recv.at[k], p)
             for k, (h, p) in enumerate(zip(head_of, head_peers, strict=True))
         ]
         head_own = [
-            pltpu.make_async_copy(block_of(head), gathered.at[head], head_local.at[0])
+            pltpu.make_async_copy(blocks.at[:, head], gathered.at[head], head_local.at[0])
         ]
         for copy in head_copies + head_own:
             copy.start()
+    if mode == "block":
+        head_send, head_recv, head_local, gathered = take(4)
+        blocks = head_in[0]
+        windows = blocks.shape[1]
+        by_window = [
+            [
+                remote(
+                    blocks.at[h, w],
+                    gathered.at[head, w],
+                    head_send.at[w, k],
+                    head_recv.at[w, k],
+                    p,
+                )
+                for k, (h, p) in enumerate(zip(head_of, head_peers, strict=True))
+            ]
+            for w in range(windows)
+        ]
+        head_copies = [copy for some in by_window for copy in some]
+        head_own = [
+            pltpu.make_async_copy(blocks.at[head, w], gathered.at[head, w], head_local.at[w])
+            for w in range(windows)
+        ]
+        for copy in by_window[0] + head_own:
+            copy.start()
+
+        def wait_heads(w):
+            head_own[w].wait()
+            for copy in by_window[w]:
+                copy.wait_recv()
+
+        begin_block, block_jobs, finish_block = block_work(
+            block_in, block_out, take(20), gathered, wait_heads
+        )
+        begin_block()
     if mode == "out":
         head_send, head_recv, head_local, part_send, part_recv, mine_kv, arrived_kv = take(7)
         query, pair_mine, pair_other = head_in
@@ -1591,6 +1790,10 @@
     ahead = 3
     for step in range(min(ahead, len(groups))):
         launch(step)
+    if mode == "block":
+        for some in by_window[1:]:
+            for copy in some:
+                copy.start()
     if mode == "out":
         for copy in part_copies:
             copy.wait_recv()
@@ -1632,6 +1835,12 @@
                             copy.start()
         if step + ahead < len(groups):
             launch(step + ahead)
+        if mode == "block":
+            steps = len(groups) + 4 * lag
+            for job in block_jobs[
+                step * len(block_jobs) // steps : (step + 1) * len(block_jobs) // steps
+            ]:
+                job()
         if masked and 0 <= step - (len(groups) - ahead) < terms[0].shape[0] // tile:
             masked_product(step - (len(groups) - ahead))
         if late and step >= len(groups) - ahead:
@@ -1656,8 +1865,10 @@
 
     if late:
         store_window(values.shape[0] - 1).wait()
+    if mode == "block":
+        finish_block()
     if mode:
-        if not late:
+        if not late and mode != "block":
             for copy in head_own:
                 copy.wait()
             for copy in head_copies:
@@ -1674,7 +1885,7 @@
                     copy.wait_send()
 
 
-def sum_terms(name, collective, pairs, groups, mode=None, heads=(), small=None, late=None, masked=None):
+def sum_terms(name, collective, pairs, groups, mode=None, heads=(), small=None, late=None, masked=None, block=None):
     ndp, nseq = lax.axis_size("dp"), lax.axis_size("seq")
     nhi, parts, devices = nseq // 4, nseq // H, ndp * nseq
     shares = [(left.shape[1] // devices, right.shape[1]) for left, right in pairs]
@@ -1725,14 +1936,55 @@
     hop = max(ndp - 1, 1)
     sizes = [(count,)] * 3 + [(count, hop)] * 4 + [(count, nhi - 1)] * 2 + [(count,)] * 2
     scratch += [pltpu.SemaphoreType.DMA(size) for size in sizes]
-    if mode in ("in", "back"):
-        windows = heads[0].shape[0 if mode == "in" else 1]
-        size, rows = heads[0].shape[2:]
+    if mode == "in":
+        windows, _, size, rows = heads[0].shape
         operands.append(heads[0])
         in_specs.append(pl.BlockSpec(memory_space=pl.ANY))
         out_shape.append(jax.ShapeDtypeStruct((H, windows, size, rows), BF))
         out_specs.append(pl.BlockSpec(memory_space=pl.ANY))
         scratch += [pltpu.SemaphoreType.DMA((n,)) for n in (H - 1, H - 1, 1)]
+    if mode == "block":
+        operands += [heads[0], *block]
+        in_specs += [pl.BlockSpec(memory_space=pl.ANY)] * 6
+        in_specs += [pl.BlockSpec(memory_space=pltpu.VMEM)] * 4
+        windows, rows, width = block[0].shape
+        wide = block[3].shape[1]
+        coarse, broad = (windows * rows, width), (windows * rows, wide)
+        out_shape += [
+            jax.ShapeDtypeStruct(s, BF)
+            for s in (coarse, coarse, broad, coarse, coarse, broad, coarse)
+        ]
+        out_shape.append(jax.ShapeDtypeStruct(coarse, F32))
+        out_shape.append(jax.ShapeDtypeStruct((windows, H, VD, rows), BF))
+        out_shape += [jax.ShapeDtypeStruct((1, n), F32) for n in (width, width, wide, width)]
+        out_specs += [pl.BlockSpec(memory_space=pl.ANY)] * 9
+        out_specs += [pl.BlockSpec(memory_space=pltpu.VMEM)] * 4
+        narrow, long = pltpu.VMEM((rows, width), BF), pltpu.VMEM((rows, wide), BF)
+        full_rows = pltpu.VMEM((rows, width), F32)
+        scratch += [
+            pltpu.SemaphoreType.DMA((windows, H - 1)),
+            pltpu.SemaphoreType.DMA((windows, H - 1)),
+            pltpu.SemaphoreType.DMA((windows,)),
+            pltpu.VMEM(heads[0].shape, BF),
+            *[pltpu.VMEM(w.shape, BF) for w in block[2:5]],
+            narrow,
+            full_rows,
+            full_rows,
+            full_rows,
+            long,
+            narrow,
+            narrow,
+            long,
+            narrow,
+            narrow,
+            long,
+            narrow,
+            full_rows,
+            pltpu.VMEM((H, VD, rows), BF),
+            pltpu.SemaphoreType.DMA((3,)),
+            pltpu.SemaphoreType.DMA((2,)),
+            pltpu.SemaphoreType.DMA((9,)),
+        ]
     if mode == "out":
         _, windows, _, rows = heads[0].shape
         operands += list(heads)
@@ -1845,154 +2097,6 @@
     return lax.dot_general(x, table, (((1,), (1,)), ((), ())), preferred_element_type=F32)
 
 
-def block_kernel(
-    values, arrived, third_grad, w_mixing, w_inner, w_outer,
-    second_gain, third_gain, inner_bias, outer_bias,
-    mixed_o, second_o, hidden_o, third_o, block_o, before_o, middle_o, middle_grad_o, mixed_grad_o,
-    second_sum, third_sum, inner_sum, outer_sum,
-    mixing_v, inner_v, outer_v, middle_v, block_v, slope_v, sem,
-):
-    first = pl.program_id(0) == 0
-    rows, width = middle_v.shape
-    wide = slope_v.shape[1]
-    tile = 512
-    loads = [
-        pltpu.make_async_copy(source, target, sem.at[k])
-        for k, (source, target) in enumerate(
-            ((w_mixing, mixing_v), (w_inner, inner_v), (w_outer, outer_v))
-        )
-    ]
-
-    @pl.when(first)
-    def _():
-        for load in loads:
-            load.start()
-        for total in (second_sum, third_sum, inner_sum, outer_sum):
-            total[...] = jnp.zeros(total.shape, F32)
-
-    def ready(k):
-        @pl.when(first)
-        def _():
-            loads[k].wait()
-
-    for pair in range(H // 2):
-        both = jnp.concatenate([arrived[2 * pair + h, 0] for h in range(2)], axis=0)
-        mixed_o[:, pair * 2 * VD : (pair + 1) * 2 * VD] = both.T
-    ready(0)
-    for k in range(0, width, tile):
-        cols = slice(k, k + tile)
-        middle_v[:, cols] = values[0][:, cols].astype(F32) + dot(mixed_o[...], mixing_v[:, cols])
-
-    chunk = 32
-
-    @pl.loop(0, rows // chunk)
-    def _(k):
-        at = pl.ds(pl.multiple_of(k * chunk, chunk), chunk)
-        unit, _ = norm_parts(middle_v[at, :])
-        second_o[at, :] = (unit * second_gain[...]).astype(BF)
-
-    ready(1)
-    for k in range(0, wide, tile):
-        cols = slice(k, k + tile)
-        before = dot(second_o[...], inner_v[:, cols]) + inner_bias[:, cols]
-        hidden, slope = gelu_parts(before)
-        hidden_o[:, cols] = hidden.astype(BF)
-        slope_v[:, cols] = slope.astype(BF)
-    ready(2)
-    for k in range(0, width, tile):
-        cols = slice(k, k + tile)
-        block_v[:, cols] = (
-            middle_v[:, cols] + dot(hidden_o[...], outer_v[:, cols]) + outer_bias[:, cols]
-        )
-
-    @pl.loop(0, rows // chunk)
-    def _(k):
-        at = pl.ds(pl.multiple_of(k * chunk, chunk), chunk)
-        unit, scale = norm_parts(block_v[at, :])
-        third, slope = gelu_parts(unit * third_gain[...])
-        third_o[at, :] = third.astype(BF)
-        grad = third_grad[at, :] * slope
-        third_sum[...] += jnp.sum(grad * unit, axis=0, keepdims=True)
-        back = norm_backward(unit, scale, grad, third_gain[...])
-        outer_sum[...] += jnp.sum(back, axis=0, keepdims=True)
-        block_v[at, :] = back
-        block_o[at, :] = back.astype(BF)
-
-    for k in range(0, wide, tile):
-        cols = slice(k, k + tile)
-        grad = times_rows(block_o[...], outer_v[cols, :]) * slope_v[:, cols].astype(F32)
-        low = grad.astype(BF)
-        before_o[:, cols] = low
-        inner_sum[:, cols] += jnp.sum(low.astype(F32), axis=0, keepdims=True)
-    for k in range(0, width, tile):
-        cols = slice(k, k + tile)
-        middle_grad_o[:, cols] = times_rows(before_o[...], inner_v[cols, :])
-
-    @pl.loop(0, rows // chunk)
-    def _(k):
-        at = pl.ds(pl.multiple_of(k * chunk, chunk), chunk)
-        unit, scale = norm_parts(middle_v[at, :])
-        grad = middle_grad_o[at, :]
-        second_sum[...] += jnp.sum(grad * unit, axis=0, keepdims=True)
-        back = block_v[at, :] + norm_backward(unit, scale, grad, second_gain[...])
-        middle_grad_o[at, :] = back
-        middle_o[at, :] = back.astype(BF)
-
-    for pair in range(H // 2):
-        cols = slice(pair * 2 * VD, (pair + 1) * 2 * VD)
-        turned = times_rows(middle_o[...], mixing_v[cols, :]).astype(BF).T
-        for h in range(2):
-            mixed_grad_o[0, 2 * pair + h] = turned[h * VD : (h + 1) * VD]
-
-
-def block_pass(values, arrived, third_grad, weights, gains, biases):
-    windows, rows, width = values.shape
-    wide = weights[1].shape[1]
-
-    def by_rows(columns):
-        return pl.BlockSpec((rows, columns), lambda w: (w, 0))
-
-    def line(columns):
-        return pl.BlockSpec((1, columns), lambda w: (0, 0))
-
-    narrow = jax.ShapeDtypeStruct((windows * rows, width), BF)
-    broad = jax.ShapeDtypeStruct((windows * rows, wide), BF)
-    sums = [jax.ShapeDtypeStruct((1, n), F32) for n in (width, width, wide, width)]
-    any_space = pl.BlockSpec(memory_space=pl.ANY)
-    return pl.pallas_call(
-        block_kernel,
-        grid=(windows,),
-        out_shape=[
-            narrow, narrow, broad, narrow, narrow, broad, narrow,
-            jax.ShapeDtypeStruct((windows * rows, width), F32),
-            jax.ShapeDtypeStruct((windows, H, VD, rows), BF),
-            *sums,
-        ],
-        in_specs=[
-            pl.BlockSpec((1, rows, width), lambda w: (w, 0, 0)),
-            pl.BlockSpec((H, 1, VD, rows), lambda w: (0, w, 0, 0)),
-            by_rows(width),
-            any_space, any_space, any_space,
-            line(width), line(width), line(wide), line(width),
-        ],
-        out_specs=[
-            by_rows(width), by_rows(width), by_rows(wide), by_rows(width), by_rows(width),
-            by_rows(wide), by_rows(width), by_rows(width),
-            pl.BlockSpec((1, H, VD, rows), lambda w: (w, 0, 0, 0)),
-            line(width), line(width), line(wide), line(width),
-        ],
-        scratch_shapes=[
-            *[pltpu.VMEM(w.shape, BF) for w in weights],
-            pltpu.VMEM((rows, width), F32),
-            pltpu.VMEM((rows, width), F32),
-            pltpu.VMEM((rows, wide), BF),
-            pltpu.SemaphoreType.DMA((3,)),
-        ],
-        compiler_params=pltpu.CompilerParams(vmem_limit_bytes=62 * 2**20),
-        name="block_pass",
-    )(values, arrived, third_grad, *weights, *gains, *biases)
-
-
 def weight_pairs(shapes, offset):
     def pieces(n, parts):
         rows, columns = shapes[n]
@@ -2191,18 +2295,8 @@
     )
     if r % 16 == 0:
         skip_flat = skip_input.reshape(windows * 2 * rows, width)
-        own_skip, mixed_arrived = sum_terms(
-            "sum_skip",
-            6,
-            [(skip_flat, joined_flat)],
-            halves(0, r, half_width),
-            "back",
-            (mixed_own,),
-        )
-    else:
-        mixed_arrived = exchange(mixed_own)
-    if r % 16 == 0:
         (
+            own_skip,
             mixed_low,
             second_low,
             hidden_low,
@@ -2213,17 +2307,28 @@
             middle_grad,
             mixed_grad,
             *block_sums,
-        ) = block_pass(
-            inputs,
-            mixed_arrived,
-            third_grad,
-            (weight_mixing, weight_inner, weight_outer),
-            (gain_second[None, :], gain_third[None, :]),
-            (bias_inner[None, :], bias_outer[None, :]),
+        ) = sum_terms(
+            "block_and_skip",
+            6,
+            [(skip_flat, joined_flat)],
+            halves(0, r, half_width),
+            "block",
+            (mixed_own,),
+            block=(
+                inputs,
+                third_grad,
+                weight_mixing,
+                weight_inner,
+                weight_outer,
+                gain_second[None, :],
+                gain_third[None, :],
+                bias_inner[None, :],
+                bias_outer[None, :],
+            ),
         )
         grad_second, grad_third, grad_inner_bias, grad_outer_bias = (s[0] for s in block_sums)
     else:
-        mixed_low = by_row(mixed_arrived)
+        mixed_low = by_row(exchange(mixed_own))
         middle = flat + matmul(mixed_low, weight_mixing)
         second, second_norm_back = jax.vjp(layer_norm, middle, gain_second)
         second_low = second.astype(jnp.bfloat16)

time: 846 us -> 818 us (0.967); the launches traced: 847 us -> 809 us
  Pallas kernels: 773 us -> 731 us
    pallas_call x1 -> x0, Pallas kernels: 60.9 us -> none  [block_pass(): pl.pallas_call(block_kernel, grid=(windows,), out_shape=[narrow, narrow,...]
    pallas_call x3, Pallas kernels: 348 us -> 366 us  [sum_terms(): pl.pallas_call(functools.partial(sums_kernel, plan, None), out_shape=out_...]
where the time goes in v5:
time: 818 us; the launch traced here: 809 us
  Pallas kernels  731 us (89%)
  local copies, waits for them, and re-layouts  44.5 us (5%)
  other arithmetic  12.2 us (1%)
  matrix products  11.1 us (1%)
  starting transfers between devices  8.53 us (1%)
    pallas_call x3, Pallas kernels, sum_terms(): pl.pallas_call(functools.partial(sums_kernel, plan, None), out_shape=out_...  366 us
    pallas_call x1, Pallas kernels, use_links(): pl.pallas_call(functools.partial(links_kernel, pairs, (len(shards), len(a...  274 us
    pallas_call x1, Pallas kernels, attention_backward(): pl.pallas_call(functools.partial(backward_kernel, parts, per), grid=(wind...  53.6 us
    pallas_call x1, Pallas kernels, attention_forward(): pl.pallas_call(functools.partial(forward_kernel, parts, per), grid=(windo...  37.2 us
  transfers between devices with their start and end apart: 2, of which 0 were waited for; matrix products, arithmetic and copies ran while one was open for 0% of the time, Pallas kernels for 0%

profile of v5, /device:TPU:1, one launch (start us, length us, event | category | flops | bytes accessed | tf_op | source)
XLA Modules:
  0.0 808.6 jit_solution(10241241170744618504)
XLA Ops:
  6.0 0.7 pad.52
  6.7 0.7 pad.53
  8.1 0.7 fusion.8.refs_13_
  8.7 0.7 fusion.9.refs_12_.refs_16_
  9.4 0.8 fusion.4.refs_11_.refs_15_
  10.3 1.8 concatenate.40.refs_0_
  12.1 273.6 %gather_weights.1 = (bf16[2,4,2,2,32,128]{5,4,3,2,1,0:T(8,128)(2,1)}, bf16[2,4,2,2,48,512]{5,4,3,2,1,0:T(8,128)(2,1)}, bf16[2,4,2,2,48,512]{5,4,3,2,1,0:T(8,128)...) custom-call(bf16[32,128]{1,0:T(8,128)(2,1)} %concatenate.40.refs_0_,, ...), custom_call_target="tpu_custom_call" | custom-call | tf_op jit(solution)/shard_map/gather_weights/pallas_call | solution.py:1049
  285.6 1.0 bitcast_convert_fusion
  289.4 0.7 broadcast_in_dim_reshape_squeeze.17.refs_10_
  290.2 0.7 copy.70.bias_ref
  290.9 0.7 copy.69
  291.6 0.7 broadcast_in_dim_reshape_squeeze.18.refs_11_
  292.3 0.7 broadcast_in_dim_reshape_squeeze.16.refs_9_
  293.6 37.2 %attention_forward.1 = (bf16[8,2,192,256]{3,2,1,0:T(8,128)(2,1)}, f32[8,2,192,256]{3,2,1,0:T(8,128)}, f32[8,2,8,256]{3,2,1,0:T(8,128)}) custom-call(s32[3]{0:T(128)} %pad_add_fusion.info, f32[16,1]{1,0:T(8,128)} %fusion.14.rates_ref, f32[1,128]{1,0:T(1,128)} %select_maximum_fusion.lanes_ref, f32[64,1]{1,0:T(8,128)} %copy.70.bias_ref, f32[32,64]{1,0:T(8,128)} %bitcast.89, ...), custom_call_target="tpu_custom_call" | custom-call | flops 9663676416 | bytes 20000000 | tf_op jit(solution)/shard_map/attention_forward/pallas_call | solution.py:436
  330.9 83.5 %block_and_skip.1 = (f32[48,1536]{1,0:T(8,128)}, bf16[512,1536]{1,0:T(8,128)(2,1)}, bf16[512,1536]{1,0:T(8,128)(2,1)}, bf16[512,3072]{1,0:T(8,128)(2,1)}, bf16[5...) custom-call(bf16[1024,1536]{1,0:T(8,128)(2,1)} %bitcast.67, ...), custom_call_target="tpu_custom_call" | custom-call | tf_op jit(solution)/shard_map/block_and_skip/pallas_call | solution.py:2047
  414.4 2.4 convolution_convert_fusion
  416.9 8.6 %fusion.3 = bf16[1024,1536]{1,0:T(8,128)(2,1)S(1)} fusion(f32[2,512,1536]{2,1,0:T(8,128)} %get-tuple-element.85, bf16[1024,1536]{1,0:T(8,128)(2,1)S(1)} %bitcast.77, bf16[1536,1536]{1,0:T(8,128)(2,1)} %bitcast.94), kind=kOutput, calls=%fused_computation.7 | convolution fusion | flops 4834983936 | bytes 17301504 | tf_op jit(solution)/shard_map/dot_general | solution.py:50
  425.6 6.6 collective-permute-start
  432.2 1.9 collective-permute-start.1
  434.1 0.9 slice.145
  435.3 0.7 broadcast_in_dim_reshape_squeeze.19.refs_14_
  437.6 0.9 maximum_convert_fusion
  438.5 0.9 copy-done.1
  439.5 4.6 fusion
  444.1 114.0 %sum_upper.1 = (f32[48,1536]{1,0:T(8,128)}, f32[96,1536]{1,0:T(8,128)}, f32[48,1536]{1,0:T(8,128)}, bf16[8,2,192,256]{3,2,1,0:T(8,128)(2,1)}, bf16[2,512,1536]{2,1,0:T(8,128)(2,1)}) custom-call(bf16[1024,1536]{1,0:T(8,128)(2,1)} %bitcast.68, bf16[1024,1536]{1,0:T(8,128)(2,1)} %bitcast.78, bf16[512,3072]{1,0:T(8,128)(2,1)} %get-tuple-element.87.refs_2_, ...), custom_call_target="tpu_custom_call" | custom-call | tf_op jit(solution)/shard_map/sum_upper/pallas_call | solution.py:2047
  558.1 53.6 %attention_backward.1 = (bf16[8,2,64,256]{3,2,1,0:T(8,128)(2,1)}, bf16[8,2,256,256]{3,2,1,0:T(8,128)(2,1)}, bf16[1,8,2,256,256]{4,3,2,1,0:T(8,128)(2,1)}, f32[2,64,1]{2,1,0:T(8,128)}, f32[64,32]{1,0:T(8,128)}) custom-call(s32[3]{0:T(128)} %pad_add_fusion.info, f32[16,1]{1,0:T(8,128)} %fusion.14.rates_ref, f32[1,128]{1,0:T(1,128)} %select_maximum_fusion.lanes_ref, ...), custom_call_target="tpu_custom_call" | custom-call | flops 32212254720 | bytes 20000000 | tf_op jit(solution)/shard_map/attention_backward/pallas_call | solution.py:478
  611.7 0.8 bitcast_dynamic-update-slice_fusion
  612.6 0.9 slice_reduce_fusion
  614.6 0.7 copy.76
  615.3 168.9 %sum_lower.1 = (f32[48,3072]{1,0:T(8,128)}, f32[48,1536]{1,0:T(8,128)}, f32[48,2560]{1,0:T(8,128)}, f32[16,128]{1,0:T(8,128)}, bf16[512,1536]{1,0:T(8,128)(2,1)}) custom-call(bf16[512,1536]{1,0:T(8,128)(2,1)} %get-tuple-element.93.refs_0_, bf16[512,3072]{1,0:T(8,128)(2,1)} %get-tuple-element.94.refs_1_, bf16[512,1536]{1,0:T(8,128)(2,1)} %get-tuple-element.95.refs_2_, ...), custom_call_target="tpu_custom_call" | custom-call | tf_op jit(solution)/shard_map/sum_lower/pallas_call | solution.py:2047
  784.2 1.2 slice_bitcast_fusion
  785.4 1.3 slice.156
  786.7 0.8 slice.160
  787.4 1.3 fusion.35
  788.8 1.4 fusion.34
  790.2 0.8 slice.127
  791.0 1.6 fusion.33
  792.6 1.7 slice.124
  795.7 3.9 copy.91
  799.5 1.1 copy.92
  800.7 1.3 copy-done
  802.0 1.7 copy.93
  803.7 0.7 copy.94
  804.4 0.8 copy.95
  805.2 0.8 copy.96
  806.0 0.7 copy.97
  806.7 0.7 copy.98
  807.5 0.7 copy.99
  (96 shorter events, 14.0 us)
Async XLA Ops:
  12.1 275.4 %copy-start.15 = (s32[2]{0:T(128)S(1)}, s32[2]{0:T(128)}, u32[]{:S(2)}) copy-start(s32[2]{0:T(128)} %refs_7_.3) | copy-start | bytes 28
  286.6 0.8 copy-start.2
  416.8 18.4 %copy-start.11 = (f32[1,1536]{1,0:T(1,128)S(1)}, f32[1,1536]{1,0:T(1,128)}, u32[]{:S(2)}) copy-start(f32[1,1536]{1,0:T(1,128)} %get-tuple-element.110) | copy-start | bytes 18436
  416.8 19.2 %copy-start.14 = (f32[1,1536]{1,0:T(1,128)S(1)}, f32[1,1536]{1,0:T(1,128)}, u32[]{:S(2)}) copy-start(f32[1,1536]{1,0:T(1,128)} %get-tuple-element.106) | copy-start | bytes 18436
  416.9 19.2 %copy-start.13 = (f32[1,1536]{1,0:T(1,128)S(1)}, f32[1,1536]{1,0:T(1,128)}, u32[]{:S(2)}) copy-start(f32[1,1536]{1,0:T(1,128)} %get-tuple-element.108) | copy-start | bytes 18436
  416.9 19.3 %copy-start.12 = (f32[1,1536]{1,0:T(1,128)S(1)}, f32[1,1536]{1,0:T(1,128)}, u32[]{:S(2)}) copy-start(f32[1,1536]{1,0:T(1,128)} %get-tuple-element.109) | copy-start | bytes 18436
  416.9 20.0 %copy-start.10 = (f32[1,3072]{1,0:T(1,128)S(1)}, f32[1,3072]{1,0:T(1,128)}, u32[]{:S(2)}) copy-start(f32[1,3072]{1,0:T(1,128)} %get-tuple-element.107) | copy-start | bytes 36868
  425.6 12.0 %collective-permute-start = (bf16[2,1,1536]{2,1,0:T(2,128)(2,1)S(1)}, bf16[2,1,1536]{2,1,0:T(2,128)(2,1)S(1)}, u32[]{:S(2)}, u32[]{:S(2)}) collective-permute-start(bf16[2,1,1536]{2,1,0:T(2,128)(2,1)S(1)} %get-tuple-element.205), channel_id=1, source_target_pairs={{0,1},{1,2},{2,3},{3,4},{4,5},{5,6},{6,7},{7,8},{8,9},{9,10},{10,1... | collective-permute-start | bytes 18440 | tf_op jit(solution)/shard_map/ppermute | solution.py:28
  432.2 5.4 collective-permute-start.1
  437.6 1.9 copy-start.1
  795.7 3.9 copy-start.3
  799.5 2.5 copy-start
  802.0 1.7 copy-start.9
  802.0 2.4 copy-start.5
  802.0 3.2 copy-start.4
  802.0 4.0 copy-start.8
  803.7 3.1 copy-start.6
  803.7 3.8 copy-start.7

commit v6 on v5

--- a/solution.py
+++ b/solution.py
@@ -902,6 +902,15 @@
             events.setdefault(spot + gap * (stage - 1), []).append((stage, spot))
     made_at = early + 2 if early else 0
     waited = []
+    exchange_at = made_at + len(head_copies) + 1
+
+    def exchange_parts():
+        head_own.wait()
+        for copy in head_copies:
+            copy.wait_recv()
+        for copy in part_copies:
+            copy.start()
+
     heads_at = [made_at + k for k in range(len(head_copies))]
     for step in range(min(ahead, len(pairs))):
         launch(step)
@@ -909,7 +918,7 @@
         own(array).start()
     for array in range(n_out):
         own(array).wait()
-    for step in range(max(list(events) + heads_at) + 1):
+    for step in range(max(list(events) + ([exchange_at] if early else heads_at)) + 1):
         for stage, spot in sorted(events.get(step, []), reverse=True):
             for chunk in step_chunks[spot]:
                 for copy in copies(chunk, stage - 1):
@@ -926,6 +935,8 @@
             make_blocks()
         if step in heads_at:
             head_copies[heads_at.index(step)].start()
+        if early and step == exchange_at:
+            exchange_parts()
         if early:
             for need, job in upper["jobs"].get(step, []):
                 for chunk in everything:
@@ -934,12 +945,8 @@
                             copy.wait_recv()
                         waited.append(chunk)
                 job()
-    if parts:
-        head_own.wait()
-        for copy in head_copies:
-            copy.wait_recv()
-        for copy in part_copies:
-            copy.start()
+    if parts and not early:
+        exchange_parts()
     for group in step_chunks[early:]:
         for chunk in group:
             if chunk not in waited:
@@ -1139,11 +1146,13 @@
         )
     ]
 
-    def loads(w):
-        return [
-            pltpu.make_async_copy(values.at[w], values_v, load_sem.at[0]),
-            pltpu.make_async_copy(third_grad.at[pl.ds(w * rows, rows)], third_grad_v, load_sem.at[1]),
-        ]
+    def load_values(w):
+        return pltpu.make_async_copy(values.at[w], values_v, load_sem.at[0])
+
+    def load_third(w):
+        return pltpu.make_async_copy(
+            third_grad.at[pl.ds(w * rows, rows)], third_grad_v, load_sem.at[1]
+        )
 
     buffers = (mixed_b, second_b, hidden_b, third_b, block_b, before_b, middle_b, back_b, heads_b)
 
@@ -1157,7 +1166,7 @@
                 store(k, w - 1).wait()
 
     def begin():
-        for load in weight_loads + loads(0):
+        for load in weight_loads + [load_values(0), load_third(0)]:
             load.start()
         for total in (second_sum, third_sum, inner_sum, outer_sum):
             total[...] = jnp.zeros(total.shape, F32)
@@ -1171,7 +1180,7 @@
         store(0, w).start()
         if w == 0:
             weight_loads[0].wait()
-        loads(w)[0].wait()
+        load_values(w).wait()
         for k in range(0, width, tile):
             cols = slice(k, k + tile)
             middle_v[:, cols] = values_v[:, cols].astype(F32) + dot(mixed_b[...], mixing_v[:, cols])
@@ -1209,7 +1218,7 @@
 
     def turn(w):
         free(w, 3, 4)
-        loads(w)[1].wait()
+        load_third(w).wait()
 
         @pl.loop(0, rows // chunk)
         def _(k):
@@ -1227,8 +1236,8 @@
         store(3, w).start()
         store(4, w).start()
         if w + 1 < windows:
-            for load in loads(w + 1):
-                load.start()
+            load_values(w + 1).start()
+            load_third(w + 1).start()
 
     def before_grad(w):
         free(w, 5)
@@ -1525,12 +1534,15 @@
                     packed[w * rows : (w + 1) * rows, at : at + 2 * size] = both.T
 
     def make(step):
+        if not numbers[step]:
+            return
         units = [flat[n][1] for n in numbers[step]]
         array, rows = units[0][0], units[0][2]
         first, size = units[0][3], sum(u[4] for u in units)
         left = terms[2 * array]
         tokens, slot = left.shape[0], array % 2
-        if step == 0 or flat[numbers[step - 1][0]][1][0] != array:
+        if array not in begun:
+            begun.append(array)
             fetch_left(array).wait()
 
             @pl.loop(0, left.shape[1] // 256)
@@ -1549,10 +1561,10 @@
             else:
                 fetch_right(array).wait()
 
-        if step >= 2:
-            for n in numbers[step - 2]:
-                for copy in over_core(n):
-                    copy.wait_send()
+        for n in unsent[step % 2]:
+            for copy in over_core(n):
+                copy.wait_send()
+        unsent[step % 2] = list(numbers[step])
         span = nhi * 4 * rows
         for whose in (1 - c, c):
             spot = pl.multiple_of(whose * half_of(array) + first, 128)
@@ -1572,6 +1584,8 @@
                 for n in numbers[step]:
                     for copy in over_core(n):
                         copy.start()
+
+    begun, unsent = [], [[], []]
 
     def launch(step):
         if made_here:
@@ -1787,13 +1801,6 @@
         if not late:
             start_small()
 
-    ahead = 3
-    for step in range(min(ahead, len(groups))):
-        launch(step)
-    if mode == "block":
-        for some in by_window[1:]:
-            for copy in some:
-                copy.start()
     if mode == "out":
         for copy in part_copies:
             copy.wait_recv()
@@ -1819,6 +1826,13 @@
         ]
         for copy in head_copies + head_own:
             copy.start()
+    ahead = 3
+    for step in range(min(ahead, len(groups))):
+        launch(step)
+    if mode == "block":
+        for some in by_window[1:]:
+            for copy in some:
+                copy.start()
     lag = 2
     for step in range(len(groups) + 4 * lag):
         for stage in (5, 4, 3, 2, 1):
@@ -1880,7 +1894,7 @@
             copy.wait_send()
     for n in range(count):
         for hop in hops:
-            if hop is not over_core or not made_here or n in tuple(numbers[-1]) + tuple(numbers[-2]):
+            if hop is not over_core or not made_here or n in unsent[0] + unsent[1]:
                 for copy in hop(n):
                     copy.wait_send()
 
@@ -2057,6 +2071,9 @@
     )(*operands)
 
 
+HOLD = 0
+
+
 def halves(array, rows, columns, size=128):
     out, spot = [], 0
     while spot < columns:
@@ -2487,7 +2504,7 @@
             "sum_lower",
             4,
             lower + [(normed_low, right)],
-            lower_groups + halves(2, r, packed_width // 2),
+            lower_groups + (((), ()),) * HOLD + halves(2, r, packed_width // 2),
             "out",
             lower_heads,
             pack(pieces),

time: 818 us -> 819 us (level)
  no operation moved by 1% of the time
where the time goes in v6:
time: 819 us; the launch traced here: 810 us
  Pallas kernels  731 us (89%)
  local copies, waits for them, and re-layouts  44.5 us (5%)
  other arithmetic  12.2 us (1%)
  matrix products  11.1 us (1%)
  starting transfers between devices  9.37 us (1%)
    pallas_call x3, Pallas kernels, sum_terms(): pl.pallas_call(functools.partial(sums_kernel, plan, None), out_shape=out_...  368 us
    pallas_call x1, Pallas kernels, use_links(): pl.pallas_call(functools.partial(links_kernel, pairs, (len(shards), len(a...  268 us
    pallas_call x1, Pallas kernels, attention_backward(): pl.pallas_call(functools.partial(backward_kernel, parts, per), grid=(wind...  56.5 us
    pallas_call x1, Pallas kernels, attention_forward(): pl.pallas_call(functools.partial(forward_kernel, parts, per), grid=(windo...  39.3 us
  transfers between devices with their start and end apart: 2, of which 0 were waited for; matrix products, arithmetic and copies ran while one was open for 0% of the time, Pallas kernels for 0%

profile of v6, /device:TPU:1, one launch (start us, length us, event | category | flops | bytes accessed | tf_op | source)
XLA Modules:
  0.0 809.7 jit_solution(12501368672128355354)
XLA Ops:
  6.0 0.7 pad.52
  6.7 0.7 pad.53
  8.1 0.7 fusion.8.refs_13_
  8.7 0.7 fusion.9.refs_12_.refs_16_
  9.4 0.8 fusion.4.refs_11_.refs_15_
  10.3 1.8 concatenate.40.refs_0_
  12.1 267.6 %gather_weights.1 = (bf16[2,4,2,2,32,128]{5,4,3,2,1,0:T(8,128)(2,1)}, bf16[2,4,2,2,48,512]{5,4,3,2,1,0:T(8,128)(2,1)}, bf16[2,4,2,2,48,512]{5,4,3,2,1,0:T(8,128)...) custom-call(bf16[32,128]{1,0:T(8,128)(2,1)} %concatenate.40.refs_0_,, ...), custom_call_target="tpu_custom_call" | custom-call | tf_op jit(solution)/shard_map/gather_weights/pallas_call | solution.py:1056
  279.7 1.0 bitcast_convert_fusion
  283.5 0.7 broadcast_in_dim_reshape_squeeze.17.refs_10_
  284.2 0.7 copy.70.bias_ref
  285.0 0.7 copy.69
  285.6 0.7 broadcast_in_dim_reshape_squeeze.18.refs_11_
  286.3 0.7 broadcast_in_dim_reshape_squeeze.16.refs_9_
  287.7 39.3 %attention_forward.1 = (bf16[8,2,192,256]{3,2,1,0:T(8,128)(2,1)}, f32[8,2,192,256]{3,2,1,0:T(8,128)}, f32[8,2,8,256]{3,2,1,0:T(8,128)}) custom-call(s32[3]{0:T(128)} %pad_add_fusion.info, f32[16,1]{1,0:T(8,128)} %fusion.14.rates_ref, f32[1,128]{1,0:T(1,128)} %select_maximum_fusion.lanes_ref, f32[64,1]{1,0:T(8,128)} %copy.70.bias_ref, f32[32,64]{1,0:T(8,128)} %bitcast.89, ...), custom_call_target="tpu_custom_call" | custom-call | flops 9663676416 | bytes 20000000 | tf_op jit(solution)/shard_map/attention_forward/pallas_call | solution.py:436
  327.0 85.2 %block_and_skip.1 = (f32[48,1536]{1,0:T(8,128)}, bf16[512,1536]{1,0:T(8,128)(2,1)}, bf16[512,1536]{1,0:T(8,128)(2,1)}, bf16[512,3072]{1,0:T(8,128)(2,1)}, bf16[5...) custom-call(bf16[1024,1536]{1,0:T(8,128)(2,1)} %bitcast.67, ...), custom_call_target="tpu_custom_call" | custom-call | tf_op jit(solution)/shard_map/block_and_skip/pallas_call | solution.py:2061
  412.3 2.4 convolution_convert_fusion
  414.7 8.6 %fusion.3 = bf16[1024,1536]{1,0:T(8,128)(2,1)S(1)} fusion(f32[2,512,1536]{2,1,0:T(8,128)} %get-tuple-element.85, bf16[1024,1536]{1,0:T(8,128)(2,1)S(1)} %bitcast.77, bf16[1536,1536]{1,0:T(8,128)(2,1)} %bitcast.94), kind=kOutput, calls=%fused_computation.7 | convolution fusion | flops 4834983936 | bytes 17301504 | tf_op jit(solution)/shard_map/dot_general | solution.py:50
  423.4 7.4 collective-permute-start
  430.9 1.9 collective-permute-start.1
  432.8 0.9 slice.145
  434.0 0.7 broadcast_in_dim_reshape_squeeze.19.refs_14_
  436.3 0.9 maximum_convert_fusion
  437.2 0.9 copy-done.1
  438.2 4.6 fusion
  442.8 114.6 %sum_upper.1 = (f32[48,1536]{1,0:T(8,128)}, f32[96,1536]{1,0:T(8,128)}, f32[48,1536]{1,0:T(8,128)}, bf16[8,2,192,256]{3,2,1,0:T(8,128)(2,1)}, bf16[2,512,1536]{2,1,0:T(8,128)(2,1)}) custom-call(bf16[1024,1536]{1,0:T(8,128)(2,1)} %bitcast.68, bf16[1024,1536]{1,0:T(8,128)(2,1)} %bitcast.78, bf16[512,3072]{1,0:T(8,128)(2,1)} %get-tuple-element.87.refs_2_, ...), custom_call_target="tpu_custom_call" | custom-call | tf_op jit(solution)/shard_map/sum_upper/pallas_call | solution.py:2061
  557.4 56.5 %attention_backward.1 = (bf16[8,2,64,256]{3,2,1,0:T(8,128)(2,1)}, bf16[8,2,256,256]{3,2,1,0:T(8,128)(2,1)}, bf16[1,8,2,256,256]{4,3,2,1,0:T(8,128)(2,1)}, f32[2,64,1]{2,1,0:T(8,128)}, f32[64,32]{1,0:T(8,128)}) custom-call(s32[3]{0:T(128)} %pad_add_fusion.info, f32[16,1]{1,0:T(8,128)} %fusion.14.rates_ref, f32[1,128]{1,0:T(1,128)} %select_maximum_fusion.lanes_ref, ...), custom_call_target="tpu_custom_call" | custom-call | flops 32212254720 | bytes 20000000 | tf_op jit(solution)/shard_map/attention_backward/pallas_call | solution.py:478
  613.9 0.8 bitcast_dynamic-update-slice_fusion
  614.8 0.9 slice_reduce_fusion
  616.8 0.7 copy.76
  617.5 167.8 %sum_lower.1 = (f32[48,3072]{1,0:T(8,128)}, f32[48,1536]{1,0:T(8,128)}, f32[48,2560]{1,0:T(8,128)}, f32[16,128]{1,0:T(8,128)}, bf16[512,1536]{1,0:T(8,128)(2,1)}) custom-call(bf16[512,1536]{1,0:T(8,128)(2,1)} %get-tuple-element.93.refs_0_, bf16[512,3072]{1,0:T(8,128)(2,1)} %get-tuple-element.94.refs_1_, bf16[512,1536]{1,0:T(8,128)(2,1)} %get-tuple-element.95.refs_2_, ...), custom_call_target="tpu_custom_call" | custom-call | tf_op jit(solution)/shard_map/sum_lower/pallas_call | solution.py:2061
  785.3 1.2 slice_bitcast_fusion
  786.5 1.3 slice.156
  787.8 0.8 slice.160
  788.5 1.3 fusion.35
  789.9 1.4 fusion.34
  791.3 0.8 slice.127
  792.1 1.6 fusion.33
  793.7 1.7 slice.124
  796.8 3.9 copy.91
  800.6 1.1 copy.92
  801.8 1.3 copy-done
  803.1 1.7 copy.93
  804.8 0.7 copy.94
  805.5 0.8 copy.95
  806.3 0.8 copy.96
  807.1 0.7 copy.97
  807.9 0.7 copy.98
  808.6 0.7 copy.99
  (96 shorter events, 14.0 us)
Async XLA Ops:
  12.1 269.4 %copy-start.15 = (s32[2]{0:T(128)S(1)}, s32[2]{0:T(128)}, u32[]{:S(2)}) copy-start(s32[2]{0:T(128)} %refs_7_.3) | copy-start | bytes 28
  280.7 0.8 copy-start.2
  414.7 19.2 %copy-start.11 = (f32[1,1536]{1,0:T(1,128)S(1)}, f32[1,1536]{1,0:T(1,128)}, u32[]{:S(2)}) copy-start(f32[1,1536]{1,0:T(1,128)} %get-tuple-element.110) | copy-start | bytes 18436
  414.7 20.0 %copy-start.14 = (f32[1,1536]{1,0:T(1,128)S(1)}, f32[1,1536]{1,0:T(1,128)}, u32[]{:S(2)}) copy-start(f32[1,1536]{1,0:T(1,128)} %get-tuple-element.106) | copy-start | bytes 18436
  414.7 20.1 %copy-start.13 = (f32[1,1536]{1,0:T(1,128)S(1)}, f32[1,1536]{1,0:T(1,128)}, u32[]{:S(2)}) copy-start(f32[1,1536]{1,0:T(1,128)} %get-tuple-element.108) | copy-start | bytes 18436
  414.7 20.1 %copy-start.12 = (f32[1,1536]{1,0:T(1,128)S(1)}, f32[1,1536]{1,0:T(1,128)}, u32[]{:S(2)}) copy-start(f32[1,1536]{1,0:T(1,128)} %get-tuple-element.109) | copy-start | bytes 18436
  414.7 20.8 %copy-start.10 = (f32[1,3072]{1,0:T(1,128)S(1)}, f32[1,3072]{1,0:T(1,128)}, u32[]{:S(2)}) copy-start(f32[1,3072]{1,0:T(1,128)} %get-tuple-element.107) | copy-start | bytes 36868
  423.4 12.9 %collective-permute-start = (bf16[2,1,1536]{2,1,0:T(2,128)(2,1)S(1)}, bf16[2,1,1536]{2,1,0:T(2,128)(2,1)S(1)}, u32[]{:S(2)}, u32[]{:S(2)}) collective-permute-start(bf16[2,1,1536]{2,1,0:T(2,128)(2,1)S(1)} %get-tuple-element.205), channel_id=1, source_target_pairs={{0,1},{1,2},{2,3},{3,4},{4,5},{5,6},{6,7},{7,8},{8,9},{9,10},{10,1... | collective-permute-start | bytes 18440 | tf_op jit(solution)/shard_map/ppermute | solution.py:28
  430.9 5.4 collective-permute-start.1
  436.3 1.9 copy-start.1
  796.8 3.9 copy-start.3
  800.6 2.5 copy-start
  803.1 1.7 copy-start.9
  803.1 2.4 copy-start.5
  803.1 3.2 copy-start.4
  803.1 4.0 copy-start.8
  804.8 3.1 copy-start.6
  804.8 3.8 copy-start.7

commit v7 on v6

--- a/solution.py
+++ b/solution.py
@@ -1066,6 +1066,29 @@
     )(*operands)
     flat = [out.reshape(-1, out.shape[-1]) for out in outs[: len(arrays)]]
     return flat + list(outs[len(arrays) :])
+
+
+def pack_kernel(*refs):
+    out, wide = refs[-2:]
+    wide[...] = jnp.zeros(wide.shape, F32)
+    spot = 0
+    for ref in refs[:-2]:
+        rows, columns = ref.shape
+        if rows >= 16:
+            spot = 16
+        wide[spot : spot + rows, :columns] = ref[...].astype(F32)
+        spot += rows
+    out[...] = wide[...].astype(BF)
+
+
+def pack_shards(shards):
+    rows = 16 + shards[-1].shape[0]
+    return pl.pallas_call(
+        pack_kernel,
+        out_shape=jax.ShapeDtypeStruct((rows, 128), BF),
+        scratch_shapes=[pltpu.VMEM((rows, 128), F32)],
+        name="pack_shards",
+    )(*shards)
 
 
 def tie(*values):
@@ -2071,9 +2094,6 @@
     )(*operands)
 
 
-HOLD = 0
-
-
 def halves(array, rows, columns, size=128):
     out, spot = [], 0
     while spot < columns:
@@ -2184,13 +2204,16 @@
         skip_bias,
     )
     small_rows = [v.reshape(1, -1) for v in vectors] + [depth_weight.T]
-    small_rows = [jnp.pad(v, ((0, 0), (0, 128 - v.shape[1]))) for v in small_rows]
-    small_rows.append(jnp.zeros((16 - len(vectors) - 3, 128), BF))
     relative_rows = relative_weight.shape[0]
-    small_rows.append(
-        jnp.pad(relative_weight, ((0, -relative_rows % 16), (0, 128 - relative_weight.shape[1])))
-    )
-    small_shard = jnp.concatenate(small_rows, axis=0)
+    if r % 16 == 0:
+        small_shard = pack_shards(small_rows + [relative_weight])
+    else:
+        small_rows = [jnp.pad(v, ((0, 0), (0, 128 - v.shape[1]))) for v in small_rows]
+        small_rows.append(jnp.zeros((16 - len(vectors) - 3, 128), BF))
+        small_rows.append(
+            jnp.pad(relative_weight, ((0, -relative_rows % 16), (0, 128 - relative_weight.shape[1])))
+        )
+        small_shard = jnp.concatenate(small_rows, axis=0)
     keys_width, values_width = 2 * H * KD, H * VD
     half_hidden, half_width = hidden_width // 2, width // 2
     head_shards = [small_shard, query_weight, key_weight, value_weight]
@@ -2504,7 +2527,7 @@
             "sum_lower",
             4,
             lower + [(normed_low, right)],
-            lower_groups + (((), ()),) * HOLD + halves(2, r, packed_width // 2),
+            lower_groups + halves(2, r, packed_width // 2),
             "out",
             lower_heads,
             pack(pieces),

time: 819 us -> 811 us (level)
  local copies, waits for them, and re-layouts: 44.5 us -> 36.1 us
where the time goes in v7:
time: 811 us; the launch traced here: 803 us
  Pallas kernels  733 us (90%)
  local copies, waits for them, and re-layouts  36.1 us (4%)
  other arithmetic  12.2 us (2%)
  matrix products  11.1 us (1%)
  starting transfers between devices  9.32 us (1%)
    pallas_call x3, Pallas kernels, sum_terms(): pl.pallas_call(functools.partial(sums_kernel, plan, None), out_shape=out_...  368 us
    pallas_call x1, Pallas kernels, use_links(): pl.pallas_call(functools.partial(links_kernel, pairs, (len(shards), len(a...  268 us
    pallas_call x1, Pallas kernels, attention_backward(): pl.pallas_call(functools.partial(backward_kernel, parts, per), grid=(wind...  56.5 us
    pallas_call x1, Pallas kernels, attention_forward(): pl.pallas_call(functools.partial(forward_kernel, parts, per), grid=(windo...  39.3 us
  transfers between devices with their start and end apart: 2, of which 0 were waited for; matrix products, arithmetic and copies ran while one was open for 0% of the time, Pallas kernels for 0%

profile of v7, /device:TPU:1, one launch (start us, length us, event | category | flops | bytes accessed | tf_op | source)
XLA Modules:
  0.0 802.7 jit_solution(5479700526953841460)
XLA Ops:
  1.4 0.7 fusion.8.refs_13_
  2.1 0.7 fusion.9.refs_12_.refs_16_
  2.8 0.8 fusion.4.refs_11_.refs_15_
  3.6 1.4 pack_shards.1.refs_0_
  5.0 267.6 %gather_weights.1 = (bf16[2,4,2,2,32,128]{5,4,3,2,1,0:T(8,128)(2,1)}, bf16[2,4,2,2,48,512]{5,4,3,2,1,0:T(8,128)(2,1)}, bf16[2,4,2,2,48,512]{5,4,3,2,1,0:T(8,128)...) custom-call(bf16[32,128]{1,0:T(8,128)(2,1)} %pack_shards.1.refs_0_, ...), custom_call_target="tpu_custom_call" | custom-call | tf_op jit(solution)/shard_map/gather_weights/pallas_call | solution.py:1056
  272.6 1.0 bitcast_convert_fusion
  276.4 0.7 broadcast_in_dim_reshape_squeeze.17.refs_10_
  277.2 0.7 copy.70.bias_ref
  277.9 0.7 copy.69
  278.6 0.7 broadcast_in_dim_reshape_squeeze.18.refs_11_
  279.3 0.7 broadcast_in_dim_reshape_squeeze.16.refs_9_
  280.0 0.7 broadcast_in_dim_reshape_squeeze.15.refs_8_
  280.6 39.3 %attention_forward.1 = (bf16[8,2,192,256]{3,2,1,0:T(8,128)(2,1)}, f32[8,2,192,256]{3,2,1,0:T(8,128)}, f32[8,2,8,256]{3,2,1,0:T(8,128)}) custom-call(s32[3]{0:T(128)} %pad_add_fusion.info, f32[16,1]{1,0:T(8,128)} %fusion.14.rates_ref, f32[1,128]{1,0:T(1,128)} %select_maximum_fusion.lanes_ref, f32[64,1]{1,0:T(8,128)} %copy.70.bias_ref, f32[32,64]{1,0:T(8,128)} %bitcast.89, ...), custom_call_target="tpu_custom_call" | custom-call | flops 9663676416 | bytes 20000000 | tf_op jit(solution)/shard_map/attention_forward/pallas_call | solution.py:436
  320.0 85.3 %block_and_skip.1 = (f32[48,1536]{1,0:T(8,128)}, bf16[512,1536]{1,0:T(8,128)(2,1)}, bf16[512,1536]{1,0:T(8,128)(2,1)}, bf16[512,3072]{1,0:T(8,128)(2,1)}, bf16[5...) custom-call(bf16[1024,1536]{1,0:T(8,128)(2,1)} %bitcast.67, ...), custom_call_target="tpu_custom_call" | custom-call | tf_op jit(solution)/shard_map/block_and_skip/pallas_call | solution.py:2084
  405.3 2.4 convolution_convert_fusion
  407.7 8.6 %fusion.3 = bf16[1024,1536]{1,0:T(8,128)(2,1)S(1)} fusion(f32[2,512,1536]{2,1,0:T(8,128)} %get-tuple-element.85, bf16[1024,1536]{1,0:T(8,128)(2,1)S(1)} %bitcast.77, bf16[1536,1536]{1,0:T(8,128)(2,1)} %bitcast.102), kind=kOutput, calls=%fused_computation.7 | convolution fusion | flops 4834983936 | bytes 17301504 | tf_op jit(solution)/shard_map/dot_general | solution.py:50
  416.4 7.4 collective-permute-start
  423.8 1.9 collective-permute-start.1
  425.7 0.9 slice.145
  427.0 0.7 broadcast_in_dim_reshape_squeeze.19.refs_14_
  428.5 0.7 reduce.41
  429.2 0.9 maximum_convert_fusion
  430.2 0.9 copy-done.1
  431.1 4.6 fusion
  435.8 114.6 %sum_upper.1 = (f32[48,1536]{1,0:T(8,128)}, f32[96,1536]{1,0:T(8,128)}, f32[48,1536]{1,0:T(8,128)}, bf16[8,2,192,256]{3,2,1,0:T(8,128)(2,1)}, bf16[2,512,1536]{2,1,0:T(8,128)(2,1)}) custom-call(bf16[1024,1536]{1,0:T(8,128)(2,1)} %bitcast.68, bf16[1024,1536]{1,0:T(8,128)(2,1)} %bitcast.78, bf16[512,3072]{1,0:T(8,128)(2,1)} %get-tuple-element.87.refs_2_, ...), custom_call_target="tpu_custom_call" | custom-call | tf_op jit(solution)/shard_map/sum_upper/pallas_call | solution.py:2084
  550.4 56.5 %attention_backward.1 = (bf16[8,2,64,256]{3,2,1,0:T(8,128)(2,1)}, bf16[8,2,256,256]{3,2,1,0:T(8,128)(2,1)}, bf16[1,8,2,256,256]{4,3,2,1,0:T(8,128)(2,1)}, f32[2,64,1]{2,1,0:T(8,128)}, f32[64,32]{1,0:T(8,128)}) custom-call(s32[3]{0:T(128)} %pad_add_fusion.info, f32[16,1]{1,0:T(8,128)} %fusion.14.rates_ref, f32[1,128]{1,0:T(1,128)} %select_maximum_fusion.lanes_ref, ...), custom_call_target="tpu_custom_call" | custom-call | flops 32212254720 | bytes 20000000 | tf_op jit(solution)/shard_map/attention_backward/pallas_call | solution.py:478
  606.9 0.8 bitcast_dynamic-update-slice_fusion
  607.8 0.9 slice_reduce_fusion
  609.8 0.7 copy.76
  610.4 167.8 %sum_lower.1 = (f32[48,3072]{1,0:T(8,128)}, f32[48,1536]{1,0:T(8,128)}, f32[48,2560]{1,0:T(8,128)}, f32[16,128]{1,0:T(8,128)}, bf16[512,1536]{1,0:T(8,128)(2,1)}) custom-call(bf16[512,1536]{1,0:T(8,128)(2,1)} %get-tuple-element.93.refs_0_, bf16[512,3072]{1,0:T(8,128)(2,1)} %get-tuple-element.94.refs_1_, bf16[512,1536]{1,0:T(8,128)(2,1)} %get-tuple-element.95.refs_2_, ...), custom_call_target="tpu_custom_call" | custom-call | tf_op jit(solution)/shard_map/sum_lower/pallas_call | solution.py:2084
  778.3 1.2 slice_bitcast_fusion
  779.5 1.3 slice.156
  780.7 0.8 slice.160
  781.5 1.3 fusion.35
  782.8 1.4 fusion.34
  784.3 0.8 slice.127
  785.0 1.6 fusion.33
  786.7 1.7 slice.124
  789.7 3.9 copy.91
  793.6 1.1 copy.92
  794.8 1.3 copy-done
  796.1 1.7 copy.93
  797.8 0.7 copy.94
  798.5 0.8 copy.95
  799.3 0.8 copy.96
  800.1 0.7 copy.97
  800.8 0.7 copy.98
  801.5 0.7 copy.99
  (85 shorter events, 7.3 us)
Async XLA Ops:
  5.0 269.4 %copy-start.15 = (s32[2]{0:T(128)S(1)}, s32[2]{0:T(128)}, u32[]{:S(2)}) copy-start(s32[2]{0:T(128)} %refs_7_.3) | copy-start | bytes 28
  273.6 0.8 copy-start.2
  407.7 19.2 %copy-start.11 = (f32[1,1536]{1,0:T(1,128)S(1)}, f32[1,1536]{1,0:T(1,128)}, u32[]{:S(2)}) copy-start(f32[1,1536]{1,0:T(1,128)} %get-tuple-element.110) | copy-start | bytes 18436
  407.7 19.9 %copy-start.14 = (f32[1,1536]{1,0:T(1,128)S(1)}, f32[1,1536]{1,0:T(1,128)}, u32[]{:S(2)}) copy-start(f32[1,1536]{1,0:T(1,128)} %get-tuple-element.106) | copy-start | bytes 18436
  407.7 20.0 %copy-start.13 = (f32[1,1536]{1,0:T(1,128)S(1)}, f32[1,1536]{1,0:T(1,128)}, u32[]{:S(2)}) copy-start(f32[1,1536]{1,0:T(1,128)} %get-tuple-element.108) | copy-start | bytes 18436
  407.7 20.1 %copy-start.12 = (f32[1,1536]{1,0:T(1,128)S(1)}, f32[1,1536]{1,0:T(1,128)}, u32[]{:S(2)}) copy-start(f32[1,1536]{1,0:T(1,128)} %get-tuple-element.109) | copy-start | bytes 18436
  407.7 20.7 %copy-start.10 = (f32[1,3072]{1,0:T(1,128)S(1)}, f32[1,3072]{1,0:T(1,128)}, u32[]{:S(2)}) copy-start(f32[1,3072]{1,0:T(1,128)} %get-tuple-element.107) | copy-start | bytes 36868
  416.4 12.8 %collective-permute-start = (bf16[2,1,1536]{2,1,0:T(2,128)(2,1)S(1)}, bf16[2,1,1536]{2,1,0:T(2,128)(2,1)S(1)}, u32[]{:S(2)}, u32[]{:S(2)}) collective-permute-start(bf16[2,1,1536]{2,1,0:T(2,128)(2,1)S(1)} %get-tuple-element.205), channel_id=1, source_target_pairs={{0,1},{1,2},{2,3},{3,4},{4,5},{5,6},{6,7},{7,8},{8,9},{9,10},{10,1... | collective-permute-start | bytes 18440 | tf_op jit(solution)/shard_map/ppermute | solution.py:28
  423.8 5.4 collective-permute-start.1
  429.2 1.9 copy-start.1
  789.7 3.9 copy-start.3
  793.6 2.5 copy-start
  796.1 1.7 copy-start.9
  796.1 2.4 copy-start.5
  796.1 3.2 copy-start.4
  796.1 4.0 copy-start.8
  797.8 3.1 copy-start.6
  797.8 3.8 copy-start.7
